TPU v7x, 256 devices: a whole 4x4x8 slice. The times are simulated.
256 devices in a mesh: row: 16 (over z, x_hi), col: 8 (over y, x_lo), layer: 2 (over core).
Axes of the slice: x: 4 (x_hi: 2, x_lo: 2; x = x_hi * 2 + x_lo), y: 4, z: 8, core: 2. Of those that a mesh axis runs over, the one named last changes fastest.
Arguments:
- t_amps: float32 [512, 131072], P('col', ('row', 'layer')), may hold values from -6 to 6
- v_tiles: float32 [16, 2, 16, 16, 4096], P('col', 'layer', 'row'), may hold values from -0.09375 to 0.09375
- v_where: int32 [16, 2, 16, 16], P('col', 'layer', 'row'), may hold values from -1 to 255, as said below
Outputs:
- residual_block: float32 [512, 4096], P('col', ('row', 'layer'))
Inputs may be any that keep to these rules, and one draw needn't show every extreme that they name: Within each list v_where[j, l, r, :] the live positions are distinct and come first, the unused slots (-1) after them; some list in every draw has all 16 slots live, and every list has at least one.
All inputs are finite; a program needn't handle non-finite values.
Results may differ from a plain program's by a relative error of at most 0.0003.
Values sent between devices are 32-bit elements; how exact they have to be, the bound alone decides.
No kernel may reach another device: no remote copies, remote signals or barrier semaphores. Data moves between devices by JAX's collectives and lax.ppermute only.
A program may use at most 64 MiB of HBM per device.

v0:
```python
import jax
import jax.numpy as jnp
from jax import lax
from jax.sharding import PartitionSpec as P

TILE = 64
AB_DEV = 128


def from_root(block, axis, holder):
    block = jnp.where(lax.axis_index(axis) == holder, block, jnp.zeros_like(block))
    return lax.psum(block, axis)


def shifted(block, axis, distance):
    devices = range(lax.axis_size(axis))
    route = [((i - distance) % len(devices), i) for i in devices]
    return lax.ppermute(block, axis, route)


def apply_tiles(totals, t_block, v_list, v_spots, ab_tiles):
    ij_rows = t_block.shape[0]
    t_shaped = t_block.reshape(ij_rows, t_block.shape[1] // TILE, TILE)
    is_live = v_spots >= 0
    v_safe = jnp.maximum(v_spots, 0)
    cd_tile = v_safe // ab_tiles
    ab_tile = v_safe % ab_tiles
    picked = jnp.take(t_shaped, cd_tile, axis=1)
    v_mats = v_list.reshape(v_list.shape[0], TILE, TILE)
    product = jnp.einsum("rtc,tca->rta", picked, v_mats, precision=lax.Precision.HIGHEST)
    onehot = (
        (ab_tile[:, None] == jnp.arange(ab_tiles, dtype=jnp.int32)[None, :]) & is_live[:, None]
    ).astype(jnp.float32)
    t_added = jnp.einsum("rta,tb->rba", product, onehot, precision=lax.Precision.HIGHEST)
    return totals + t_added.reshape(ij_rows, ab_tiles * TILE)


def contract_list(totals, t_block, v_list, v_spots, ab_tiles):
    return apply_tiles(totals, t_block, v_list, v_spots, ab_tiles)


def contract(totals, t_block, fine, v_tiles, v_where, ab_tiles):
    held_blocks = v_tiles.shape[0]
    own_list = lax.dynamic_index_in_dim(v_tiles[:, 0, 0], fine % held_blocks, 0, keepdims=False)
    own_spots = lax.dynamic_index_in_dim(v_where[:, 0, 0], fine % held_blocks, 0, keepdims=False)
    v_list, v_spots = (
        from_root(own_list, "col", fine // held_blocks),
        from_root(own_spots, "col", fine // held_blocks),
    )
    return contract_list(totals, t_block, v_list, v_spots, ab_tiles)


def on_device(t_amps, v_tiles, v_where):
    ij_rows = t_amps.shape[0]
    ab_tiles = AB_DEV * lax.axis_size("layer") // TILE
    loop_size = lax.axis_size("row")
    position = lax.axis_index("row")
    totals = jnp.zeros((ij_rows, ab_tiles * TILE), jnp.float32)

    def accumulate(running, t_block, fine):
        return contract(
            running, t_block, jnp.remainder(fine, loop_size), v_tiles, v_where, ab_tiles
        )

    def advance(step_id, carried):
        running, t_block = carried
        running = accumulate(running, t_block, position + step_id)
        t_block = shifted(t_block, "row", -1)
        return (running, t_block)

    totals, t_block = lax.fori_loop(0, loop_size - 1, advance, (totals, t_amps))
    totals = accumulate(totals, t_block, position + loop_size - 1)
    return lax.psum_scatter(totals, "layer", scatter_dimension=1, tiled=True)


def solution(mesh):
    return jax.shard_map(
        on_device,
        mesh=mesh,
        in_specs=(
            P("col", ("row", "layer")),
            P("col", "layer", "row", None, None),
            P("col", "layer", "row", None),
        ),
        out_specs=P("col", ("row", "layer")),
        check_vma=False,
    )
```

profile of v0, /device:TPU:1, one launch (start us, length us, event | category | flops | bytes accessed | tf_op | source)
XLA Modules:
  0.0 1548.0 jit_solution(526893026651830953)
XLA Ops:
  11.9 1425.1 %while.19 = (s32[]{:T(128)}, f32[64,256]{1,0:T(8,128)S(1)}, f32[64,4096]{1,0:T(8,128)}, s32[]{:T(128)}, s32[2,1,1,16]{3,2,1,0:T(1,128)S(1)}, /*index=5*/f32[2,1,...) while((s32[]{:T(128)}, f32[64,256]{1,0:T(8,128)S(1)}, ...), condition=%wide.region_3.5_spmd.clone, body=%wide.region_0.4_spmd.clone.sunk | while | flops 53708344 | bytes 16651624 | solution.py:71
  15.3 8.9 collective-permute-start
  24.2 10.6 psum.51
  35.7 2.6 copy.18
  40.4 66.5 %all-reduce.5.cloned.1.call-done = f32[16,64,64]{1,2,0:T(8,128)} async-done(((f32[16,64,64]{1,2,0:T(8,128)}), f32[16,64,64]{1,2,0:T(8,128)}) %all-reduce.5.cloned.1.call-update) | async-done | bytes 262160 | tf_op jit(solution)/shard_map/while/body/eval_jaxpr/psum | solution.py:12
  113.4 4.7 collective-permute-start
  118.0 8.8 psum.51
  127.7 2.6 copy.18
  132.5 69.3 %all-reduce.5.cloned.1.call-done = f32[16,64,64]{1,2,0:T(8,128)} async-done(((f32[16,64,64]{1,2,0:T(8,128)}), f32[16,64,64]{1,2,0:T(8,128)}) %all-reduce.5.cloned.1.call-update) | async-done | bytes 262160 | tf_op jit(solution)/shard_map/while/body/eval_jaxpr/psum | solution.py:12
  208.2 4.7 collective-permute-start
  212.8 8.8 psum.51
  222.5 2.6 copy.18
  227.3 69.3 %all-reduce.5.cloned.1.call-done = f32[16,64,64]{1,2,0:T(8,128)} async-done(((f32[16,64,64]{1,2,0:T(8,128)}), f32[16,64,64]{1,2,0:T(8,128)}) %all-reduce.5.cloned.1.call-update) | async-done | bytes 262160 | tf_op jit(solution)/shard_map/while/body/eval_jaxpr/psum | solution.py:12
  303.0 4.7 collective-permute-start
  307.6 8.8 psum.51
  317.3 2.6 copy.18
  322.0 69.3 %all-reduce.5.cloned.1.call-done = f32[16,64,64]{1,2,0:T(8,128)} async-done(((f32[16,64,64]{1,2,0:T(8,128)}), f32[16,64,64]{1,2,0:T(8,128)}) %all-reduce.5.cloned.1.call-update) | async-done | bytes 262160 | tf_op jit(solution)/shard_map/while/body/eval_jaxpr/psum | solution.py:12
  397.8 4.7 collective-permute-start
  402.4 8.8 psum.51
  412.1 2.6 copy.18
  416.8 69.3 %all-reduce.5.cloned.1.call-done = f32[16,64,64]{1,2,0:T(8,128)} async-done(((f32[16,64,64]{1,2,0:T(8,128)}), f32[16,64,64]{1,2,0:T(8,128)}) %all-reduce.5.cloned.1.call-update) | async-done | bytes 262160 | tf_op jit(solution)/shard_map/while/body/eval_jaxpr/psum | solution.py:12
  492.5 4.7 collective-permute-start
  497.2 8.8 psum.51
  506.9 2.6 copy.18
  511.6 69.3 %all-reduce.5.cloned.1.call-done = f32[16,64,64]{1,2,0:T(8,128)} async-done(((f32[16,64,64]{1,2,0:T(8,128)}), f32[16,64,64]{1,2,0:T(8,128)}) %all-reduce.5.cloned.1.call-update) | async-done | bytes 262160 | tf_op jit(solution)/shard_map/while/body/eval_jaxpr/psum | solution.py:12
  587.3 4.7 collective-permute-start
  592.0 8.8 psum.51
  601.7 2.6 copy.18
  606.4 69.3 %all-reduce.5.cloned.1.call-done = f32[16,64,64]{1,2,0:T(8,128)} async-done(((f32[16,64,64]{1,2,0:T(8,128)}), f32[16,64,64]{1,2,0:T(8,128)}) %all-reduce.5.cloned.1.call-update) | async-done | bytes 262160 | tf_op jit(solution)/shard_map/while/body/eval_jaxpr/psum | solution.py:12
  682.1 4.7 collective-permute-start
  686.8 8.8 psum.51
  696.5 2.6 copy.18
  701.2 69.3 %all-reduce.5.cloned.1.call-done = f32[16,64,64]{1,2,0:T(8,128)} async-done(((f32[16,64,64]{1,2,0:T(8,128)}), f32[16,64,64]{1,2,0:T(8,128)}) %all-reduce.5.cloned.1.call-update) | async-done | bytes 262160 | tf_op jit(solution)/shard_map/while/body/eval_jaxpr/psum | solution.py:12
  776.9 4.7 collective-permute-start
  781.6 8.8 psum.51
  791.3 2.6 copy.18
  796.0 69.3 %all-reduce.5.cloned.1.call-done = f32[16,64,64]{1,2,0:T(8,128)} async-done(((f32[16,64,64]{1,2,0:T(8,128)}), f32[16,64,64]{1,2,0:T(8,128)}) %all-reduce.5.cloned.1.call-update) | async-done | bytes 262160 | tf_op jit(solution)/shard_map/while/body/eval_jaxpr/psum | solution.py:12
  871.7 4.7 collective-permute-start
  876.4 8.8 psum.51
  886.1 2.6 copy.18
  890.8 69.3 %all-reduce.5.cloned.1.call-done = f32[16,64,64]{1,2,0:T(8,128)} async-done(((f32[16,64,64]{1,2,0:T(8,128)}), f32[16,64,64]{1,2,0:T(8,128)}) %all-reduce.5.cloned.1.call-update) | async-done | bytes 262160 | tf_op jit(solution)/shard_map/while/body/eval_jaxpr/psum | solution.py:12
  966.5 4.7 collective-permute-start
  971.2 8.8 psum.51
  980.8 2.6 copy.18
  985.6 69.3 %all-reduce.5.cloned.1.call-done = f32[16,64,64]{1,2,0:T(8,128)} async-done(((f32[16,64,64]{1,2,0:T(8,128)}), f32[16,64,64]{1,2,0:T(8,128)}) %all-reduce.5.cloned.1.call-update) | async-done | bytes 262160 | tf_op jit(solution)/shard_map/while/body/eval_jaxpr/psum | solution.py:12
  1061.3 4.7 collective-permute-start
  1066.0 8.8 psum.51
  1075.6 2.6 copy.18
  1080.4 69.3 %all-reduce.5.cloned.1.call-done = f32[16,64,64]{1,2,0:T(8,128)} async-done(((f32[16,64,64]{1,2,0:T(8,128)}), f32[16,64,64]{1,2,0:T(8,128)}) %all-reduce.5.cloned.1.call-update) | async-done | bytes 262160 | tf_op jit(solution)/shard_map/while/body/eval_jaxpr/psum | solution.py:12
  1156.1 4.7 collective-permute-start
  1160.8 8.8 psum.51
  1170.4 2.6 copy.18
  1175.2 69.3 %all-reduce.5.cloned.1.call-done = f32[16,64,64]{1,2,0:T(8,128)} async-done(((f32[16,64,64]{1,2,0:T(8,128)}), f32[16,64,64]{1,2,0:T(8,128)}) %all-reduce.5.cloned.1.call-update) | async-done | bytes 262160 | tf_op jit(solution)/shard_map/while/body/eval_jaxpr/psum | solution.py:12
  1250.9 4.7 collective-permute-start
  1255.6 8.8 psum.51
  1265.2 2.6 copy.18
  1270.0 69.3 %all-reduce.5.cloned.1.call-done = f32[16,64,64]{1,2,0:T(8,128)} async-done(((f32[16,64,64]{1,2,0:T(8,128)}), f32[16,64,64]{1,2,0:T(8,128)}) %all-reduce.5.cloned.1.call-update) | async-done | bytes 262160 | tf_op jit(solution)/shard_map/while/body/eval_jaxpr/psum | solution.py:12
  1345.7 4.7 collective-permute-start
  1350.4 8.8 psum.51
  1364.8 69.3 %all-reduce.5.cloned.1.call-done = f32[16,64,64]{1,2,0:T(8,128)} async-done(((f32[16,64,64]{1,2,0:T(8,128)}), f32[16,64,64]{1,2,0:T(8,128)}) %all-reduce.5.cloned.1.call-update) | async-done | bytes 262160 | tf_op jit(solution)/shard_map/while/body/eval_jaxpr/psum | solution.py:12
  1437.6 7.4 psum.44
  1447.0 2.6 copy.12
  1451.8 67.5 %all-reduce.3.cloned.1.call-done = f32[16,64,64]{1,2,0:T(8,128)} async-done(((f32[16,64,64]{1,2,0:T(8,128)}), f32[16,64,64]{1,2,0:T(8,128)}) %all-reduce.3.cloned.1.call-update) | async-done | bytes 262160 | tf_op jit(solution)/shard_map/psum | solution.py:12
  1522.7 18.2 %reduce-scatter.2.cloned.1.call-done = f32[64,128]{1,0:T(8,128)} async-done(((f32[64,256]{1,0:T(8,128)}), f32[64,128]{1,0:T(8,128)}) %reduce-scatter.2.cloned.1.call-update) | async-done | bytes 32784 | tf_op jit(solution)/shard_map/reduce_scatter | solution.py:73
  (293 shorter events, 154.6 us)
Async XLA Ops:
  7.4 4.5 copy-start
  11.9 95.1 %all-reduce.5.cloned.1.call-start = ((), (), s32[]{:S(2)}) async-start(), calls=%async_computation.3 | async-start | bytes 1048576 | tf_op jit(solution)/shard_map/while/body/eval_jaxpr/psum | solution.py:12
  15.3 94.5 %collective-permute-start = (f32[64,4096]{1,0:T(8,128)S(1)}, f32[64,4096]{1,0:T(8,128)}, u32[]{:S(2)}, u32[]{:S(2)}) collective-permute-start(f32[64,4096]{1,0:T(8,128)S(1)} %copy.26), channel_id=1, source_target_pairs={{16,0},{32,16},{48,32},{64,48},{80,64},{96,80},{112,96},{128,112},... | collective-permute-start | bytes 3145736 | tf_op jit(solution)/shard_map/while/body/eval_jaxpr/ppermute | solution.py:18
  109.8 92.0 %all-reduce.5.cloned.1.call-start = ((), (), s32[]{:S(2)}) async-start(), calls=%async_computation.3 | async-start | bytes 1048576 | tf_op jit(solution)/shard_map/while/body/eval_jaxpr/psum | solution.py:12
  113.4 91.2 %collective-permute-start = (f32[64,4096]{1,0:T(8,128)S(1)}, f32[64,4096]{1,0:T(8,128)}, u32[]{:S(2)}, u32[]{:S(2)}) collective-permute-start(f32[64,4096]{1,0:T(8,128)S(1)} %copy.26), channel_id=1, source_target_pairs={{16,0},{32,16},{48,32},{64,48},{80,64},{96,80},{112,96},{128,112},... | collective-permute-start | bytes 3145736 | tf_op jit(solution)/shard_map/while/body/eval_jaxpr/ppermute | solution.py:18
  204.6 91.9 %all-reduce.5.cloned.1.call-start = ((), (), s32[]{:S(2)}) async-start(), calls=%async_computation.3 | async-start | bytes 1048576 | tf_op jit(solution)/shard_map/while/body/eval_jaxpr/psum | solution.py:12
  208.2 91.2 %collective-permute-start = (f32[64,4096]{1,0:T(8,128)S(1)}, f32[64,4096]{1,0:T(8,128)}, u32[]{:S(2)}, u32[]{:S(2)}) collective-permute-start(f32[64,4096]{1,0:T(8,128)S(1)} %copy.26), channel_id=1, source_target_pairs={{16,0},{32,16},{48,32},{64,48},{80,64},{96,80},{112,96},{128,112},... | collective-permute-start | bytes 3145736 | tf_op jit(solution)/shard_map/while/body/eval_jaxpr/ppermute | solution.py:18
  299.4 91.9 %all-reduce.5.cloned.1.call-start = ((), (), s32[]{:S(2)}) async-start(), calls=%async_computation.3 | async-start | bytes 1048576 | tf_op jit(solution)/shard_map/while/body/eval_jaxpr/psum | solution.py:12
  303.0 91.2 %collective-permute-start = (f32[64,4096]{1,0:T(8,128)S(1)}, f32[64,4096]{1,0:T(8,128)}, u32[]{:S(2)}, u32[]{:S(2)}) collective-permute-start(f32[64,4096]{1,0:T(8,128)S(1)} %copy.26), channel_id=1, source_target_pairs={{16,0},{32,16},{48,32},{64,48},{80,64},{96,80},{112,96},{128,112},... | collective-permute-start | bytes 3145736 | tf_op jit(solution)/shard_map/while/body/eval_jaxpr/ppermute | solution.py:18
  394.2 92.0 %all-reduce.5.cloned.1.call-start = ((), (), s32[]{:S(2)}) async-start(), calls=%async_computation.3 | async-start | bytes 1048576 | tf_op jit(solution)/shard_map/while/body/eval_jaxpr/psum | solution.py:12
  397.8 91.2 %collective-permute-start = (f32[64,4096]{1,0:T(8,128)S(1)}, f32[64,4096]{1,0:T(8,128)}, u32[]{:S(2)}, u32[]{:S(2)}) collective-permute-start(f32[64,4096]{1,0:T(8,128)S(1)} %copy.26), channel_id=1, source_target_pairs={{16,0},{32,16},{48,32},{64,48},{80,64},{96,80},{112,96},{128,112},... | collective-permute-start | bytes 3145736 | tf_op jit(solution)/shard_map/while/body/eval_jaxpr/ppermute | solution.py:18
  489.0 91.9 %all-reduce.5.cloned.1.call-start = ((), (), s32[]{:S(2)}) async-start(), calls=%async_computation.3 | async-start | bytes 1048576 | tf_op jit(solution)/shard_map/while/body/eval_jaxpr/psum | solution.py:12
  492.5 91.2 %collective-permute-start = (f32[64,4096]{1,0:T(8,128)S(1)}, f32[64,4096]{1,0:T(8,128)}, u32[]{:S(2)}, u32[]{:S(2)}) collective-permute-start(f32[64,4096]{1,0:T(8,128)S(1)} %copy.26), channel_id=1, source_target_pairs={{16,0},{32,16},{48,32},{64,48},{80,64},{96,80},{112,96},{128,112},... | collective-permute-start | bytes 3145736 | tf_op jit(solution)/shard_map/while/body/eval_jaxpr/ppermute | solution.py:18
  583.8 92.0 %all-reduce.5.cloned.1.call-start = ((), (), s32[]{:S(2)}) async-start(), calls=%async_computation.3 | async-start | bytes 1048576 | tf_op jit(solution)/shard_map/while/body/eval_jaxpr/psum | solution.py:12
  587.3 91.2 %collective-permute-start = (f32[64,4096]{1,0:T(8,128)S(1)}, f32[64,4096]{1,0:T(8,128)}, u32[]{:S(2)}, u32[]{:S(2)}) collective-permute-start(f32[64,4096]{1,0:T(8,128)S(1)} %copy.26), channel_id=1, source_target_pairs={{16,0},{32,16},{48,32},{64,48},{80,64},{96,80},{112,96},{128,112},... | collective-permute-start | bytes 3145736 | tf_op jit(solution)/shard_map/while/body/eval_jaxpr/ppermute | solution.py:18
  678.6 92.0 %all-reduce.5.cloned.1.call-start = ((), (), s32[]{:S(2)}) async-start(), calls=%async_computation.3 | async-start | bytes 1048576 | tf_op jit(solution)/shard_map/while/body/eval_jaxpr/psum | solution.py:12
  682.1 91.2 %collective-permute-start = (f32[64,4096]{1,0:T(8,128)S(1)}, f32[64,4096]{1,0:T(8,128)}, u32[]{:S(2)}, u32[]{:S(2)}) collective-permute-start(f32[64,4096]{1,0:T(8,128)S(1)} %copy.26), channel_id=1, source_target_pairs={{16,0},{32,16},{48,32},{64,48},{80,64},{96,80},{112,96},{128,112},... | collective-permute-start | bytes 3145736 | tf_op jit(solution)/shard_map/while/body/eval_jaxpr/ppermute | solution.py:18
  773.4 92.0 %all-reduce.5.cloned.1.call-start = ((), (), s32[]{:S(2)}) async-start(), calls=%async_computation.3 | async-start | bytes 1048576 | tf_op jit(solution)/shard_map/while/body/eval_jaxpr/psum | solution.py:12
  776.9 91.2 %collective-permute-start = (f32[64,4096]{1,0:T(8,128)S(1)}, f32[64,4096]{1,0:T(8,128)}, u32[]{:S(2)}, u32[]{:S(2)}) collective-permute-start(f32[64,4096]{1,0:T(8,128)S(1)} %copy.26), channel_id=1, source_target_pairs={{16,0},{32,16},{48,32},{64,48},{80,64},{96,80},{112,96},{128,112},... | collective-permute-start | bytes 3145736 | tf_op jit(solution)/shard_map/while/body/eval_jaxpr/ppermute | solution.py:18
  868.2 92.0 %all-reduce.5.cloned.1.call-start = ((), (), s32[]{:S(2)}) async-start(), calls=%async_computation.3 | async-start | bytes 1048576 | tf_op jit(solution)/shard_map/while/body/eval_jaxpr/psum | solution.py:12
  871.7 91.2 %collective-permute-start = (f32[64,4096]{1,0:T(8,128)S(1)}, f32[64,4096]{1,0:T(8,128)}, u32[]{:S(2)}, u32[]{:S(2)}) collective-permute-start(f32[64,4096]{1,0:T(8,128)S(1)} %copy.26), channel_id=1, source_target_pairs={{16,0},{32,16},{48,32},{64,48},{80,64},{96,80},{112,96},{128,112},... | collective-permute-start | bytes 3145736 | tf_op jit(solution)/shard_map/while/body/eval_jaxpr/ppermute | solution.py:18
  963.0 91.9 %all-reduce.5.cloned.1.call-start = ((), (), s32[]{:S(2)}) async-start(), calls=%async_computation.3 | async-start | bytes 1048576 | tf_op jit(solution)/shard_map/while/body/eval_jaxpr/psum | solution.py:12
  966.5 91.2 %collective-permute-start = (f32[64,4096]{1,0:T(8,128)S(1)}, f32[64,4096]{1,0:T(8,128)}, u32[]{:S(2)}, u32[]{:S(2)}) collective-permute-start(f32[64,4096]{1,0:T(8,128)S(1)} %copy.26), channel_id=1, source_target_pairs={{16,0},{32,16},{48,32},{64,48},{80,64},{96,80},{112,96},{128,112},... | collective-permute-start | bytes 3145736 | tf_op jit(solution)/shard_map/while/body/eval_jaxpr/ppermute | solution.py:18
  1057.8 91.9 %all-reduce.5.cloned.1.call-start = ((), (), s32[]{:S(2)}) async-start(), calls=%async_computation.3 | async-start | bytes 1048576 | tf_op jit(solution)/shard_map/while/body/eval_jaxpr/psum | solution.py:12
  1061.3 91.2 %collective-permute-start = (f32[64,4096]{1,0:T(8,128)S(1)}, f32[64,4096]{1,0:T(8,128)}, u32[]{:S(2)}, u32[]{:S(2)}) collective-permute-start(f32[64,4096]{1,0:T(8,128)S(1)} %copy.26), channel_id=1, source_target_pairs={{16,0},{32,16},{48,32},{64,48},{80,64},{96,80},{112,96},{128,112},... | collective-permute-start | bytes 3145736 | tf_op jit(solution)/shard_map/while/body/eval_jaxpr/ppermute | solution.py:18
  1152.6 92.0 %all-reduce.5.cloned.1.call-start = ((), (), s32[]{:S(2)}) async-start(), calls=%async_computation.3 | async-start | bytes 1048576 | tf_op jit(solution)/shard_map/while/body/eval_jaxpr/psum | solution.py:12
  1156.1 91.2 %collective-permute-start = (f32[64,4096]{1,0:T(8,128)S(1)}, f32[64,4096]{1,0:T(8,128)}, u32[]{:S(2)}, u32[]{:S(2)}) collective-permute-start(f32[64,4096]{1,0:T(8,128)S(1)} %copy.26), channel_id=1, source_target_pairs={{16,0},{32,16},{48,32},{64,48},{80,64},{96,80},{112,96},{128,112},... | collective-permute-start | bytes 3145736 | tf_op jit(solution)/shard_map/while/body/eval_jaxpr/ppermute | solution.py:18
  1247.4 91.9 %all-reduce.5.cloned.1.call-start = ((), (), s32[]{:S(2)}) async-start(), calls=%async_computation.3 | async-start | bytes 1048576 | tf_op jit(solution)/shard_map/while/body/eval_jaxpr/psum | solution.py:12
  1250.9 91.2 %collective-permute-start = (f32[64,4096]{1,0:T(8,128)S(1)}, f32[64,4096]{1,0:T(8,128)}, u32[]{:S(2)}, u32[]{:S(2)}) collective-permute-start(f32[64,4096]{1,0:T(8,128)S(1)} %copy.26), channel_id=1, source_target_pairs={{16,0},{32,16},{48,32},{64,48},{80,64},{96,80},{112,96},{128,112},... | collective-permute-start | bytes 3145736 | tf_op jit(solution)/shard_map/while/body/eval_jaxpr/ppermute | solution.py:18
  1342.1 92.0 %all-reduce.5.cloned.1.call-start = ((), (), s32[]{:S(2)}) async-start(), calls=%async_computation.3 | async-start | bytes 1048576 | tf_op jit(solution)/shard_map/while/body/eval_jaxpr/psum | solution.py:12
  1345.7 91.2 %collective-permute-start = (f32[64,4096]{1,0:T(8,128)S(1)}, f32[64,4096]{1,0:T(8,128)}, u32[]{:S(2)}, u32[]{:S(2)}) collective-permute-start(f32[64,4096]{1,0:T(8,128)S(1)} %copy.26), channel_id=1, source_target_pairs={{16,0},{32,16},{48,32},{64,48},{80,64},{96,80},{112,96},{128,112},... | collective-permute-start | bytes 3145736 | tf_op jit(solution)/shard_map/while/body/eval_jaxpr/ppermute | solution.py:18
  1436.9 82.3 %all-reduce.3.cloned.1.call-start = ((), (), s32[]{:S(2)}) async-start(), calls=%async_computation.1 | async-start | bytes 1048576 | tf_op jit(solution)/shard_map/psum | solution.py:12
  1437.5 103.4 %reduce-scatter.2.cloned.1.call-start = ((), (), s32[]{:S(2)}) async-start(), calls=%async_computation.2 | async-start | bytes 98304 | tf_op jit(solution)/shard_map/reduce_scatter | solution.py:73
Sparse Core Ops, SparseCore 0:
  15.5 91.4 all-reduce.4
  113.5 88.2 all-reduce.4
  208.3 88.2 all-reduce.4
  302.8 88.5 all-reduce.4
  397.5 88.5 all-reduce.4
  492.3 88.5 all-reduce.4
  587.4 88.2 all-reduce.4
  682.2 88.2 all-reduce.4
  777.0 88.2 all-reduce.4
  871.5 88.5 all-reduce.4
  966.6 88.2 all-reduce.4
  1061.1 88.5 all-reduce.4
  1156.2 88.2 all-reduce.4
  1250.7 88.5 all-reduce.4
  1345.5 88.5 all-reduce.4
Sparse Core Ops, SparseCore 1:
  1440.0 79.2 all-reduce.2
  1522.8 18.0 reduce-scatter.1
where the time goes:
time: 1550 us
  waiting for transfers between devices  1120 us (72%)
  blocking collectives  141 us (9%)
  local copies, waits for them, and re-layouts  137 us (9%)
  starting transfers between devices  74.9 us (5%)
  matrix products  37.7 us (2%)
  other arithmetic  16.9 us (1%)
    psum x16, waiting for transfers between devices, from_root(): return lax.psum(block, axis)  1100 us
    psum x16, blocking collectives, from_root(): return lax.psum(block, axis)  141 us
    ppermute x15, starting transfers between devices, shifted(): return lax.ppermute(block, axis, route)  74.2 us
    reshape x32, local copies, waits for them, and re-layouts, apply_tiles(): t_shaped = t_block.reshape(ij_rows, t_block.shape[1] // TILE, TILE)  55.6 us
    gather x16, local copies, waits for them, and re-layouts, apply_tiles(): picked = jnp.take(t_shaped, cd_tile, axis=1)  34.7 us
    dot_general x16, matrix products, apply_tiles(): jnp.einsum('rtc,tca->rta', picked, v_mats, precision=lax.Precision.HIGHEST)  33 us
  transfers between devices with their start and end apart: 32, of which 17 were waited for; matrix products, arithmetic and copies ran while one was open for 10% of the time, Pallas kernels for 0%

commit v1 on v0

v1 whole, which is shorter than its diff:
```python
import jax
import jax.numpy as jnp
from jax import lax
from jax.experimental import pallas as pl
from jax.experimental.pallas import tpu as pltpu
from jax.sharding import PartitionSpec as P

TILE = 64
AB_DEV = 128
LANES = 128
HALF = TILE // 2


def split_rows(x):
    hi = x.astype(jnp.bfloat16)
    return hi, (x - hi.astype(jnp.float32)).astype(jnp.bfloat16)


def contract_kernel(spots_ref, t_ref, v_ref, out_ref, t_tiles, lhs, rhs):
    ij = t_ref.shape[0]
    pair = v_ref.shape[1] // HALF
    slots = v_ref.shape[0] * pair
    block = pl.program_id(0)

    @pl.when(block == 0)
    def _():
        row = lax.broadcasted_iota(jnp.int32, (LANES, 2 * LANES), 0)
        col = lax.broadcasted_iota(jnp.int32, (LANES, 2 * LANES), 1)
        source = (col // LANES) * TILE + 2 * (col % HALF) + (col % TILE) // HALF
        pick = (row == source).astype(jnp.bfloat16)
        for at in range(t_ref.shape[1] // LANES):
            hi, lo = split_rows(t_ref[:, at * LANES : (at + 1) * LANES])
            both = jnp.dot(
                jnp.concatenate([hi, lo], axis=0), pick, preferred_element_type=jnp.float32
            ).astype(jnp.bfloat16)
            t_tiles[2 * at] = both[:, :LANES]
            t_tiles[2 * at + 1] = both[:, LANES:]

    lane_half = lax.broadcasted_iota(jnp.int32, (HALF, LANES), 1) // TILE
    for t in range(slots):
        spot = spots_ref[block, t]
        live = spot >= 0
        safe = jnp.maximum(spot, 0)
        ab_half = safe & 1
        ab_pair = (safe >> 1) & 1
        lhs[:, t * LANES : (t + 1) * LANES] = t_tiles[safe >> 2]
        at = t % pair * HALF
        v = v_ref[t // pair, at : at + HALF]
        swapped = pltpu.roll(v, TILE, 1)
        upper = ab_half == 1
        even = jnp.where(upper, swapped, v)
        odd = jnp.where(upper, v, swapped)
        keep = (lane_half == ab_half) & live
        hi_e, lo_e = split_rows(jnp.where(keep, even, 0.0))
        hi_o, lo_o = split_rows(jnp.where(keep, odd, 0.0))
        rows = jnp.concatenate([hi_e, hi_o, lo_e, lo_o], axis=0)
        none = jnp.zeros_like(rows)
        rhs[t * LANES : (t + 1) * LANES, :LANES] = jnp.where(ab_pair == 0, rows, none)
        rhs[t * LANES : (t + 1) * LANES, LANES:] = jnp.where(ab_pair == 1, rows, none)
    total = jnp.dot(lhs[...], rhs[...], preferred_element_type=jnp.float32)
    total = total[:ij] + total[ij:]
    out_ref[0, 0] = total[:, :LANES]
    out_ref[1, 0] = total[:, LANES:]


def contract(t_block, shares, spots):
    ij, cd = t_block.shape
    blocks, slots = spots.shape
    cols = shares.shape[0]
    rows = slots // cols * HALF
    return pl.pallas_call(
        contract_kernel,
        out_shape=jax.ShapeDtypeStruct((2, blocks, ij, LANES), jnp.float32),
        grid_spec=pltpu.PrefetchScalarGridSpec(
            num_scalar_prefetch=1,
            grid=(blocks,),
            in_specs=[
                pl.BlockSpec((ij, cd), lambda i, _: (0, 0)),
                pl.BlockSpec((cols, rows, LANES), lambda i, _: (0, i, 0)),
            ],
            out_specs=pl.BlockSpec((2, 1, ij, LANES), lambda i, _: (0, i, 0, 0)),
            scratch_shapes=[
                pltpu.VMEM((cd // TILE, 2 * ij, LANES), jnp.bfloat16),
                pltpu.VMEM((2 * ij, slots * LANES), jnp.bfloat16),
                pltpu.VMEM((slots * LANES, 2 * LANES), jnp.bfloat16),
            ],
        ),
        compiler_params=pltpu.CompilerParams(vmem_limit_bytes=32 * 2**20),
        cost_estimate=pl.CostEstimate(
            flops=2 * blocks * 2 * ij * slots * LANES * 2 * LANES,
            bytes_accessed=6 * 2**20,
            transcendentals=0,
        ),
    )(spots, t_block, shares)


def on_device(t_amps, v_tiles, v_where):
    cols = lax.axis_size("col")
    blocks = lax.axis_size("row")
    held, slots = v_tiles.shape[0], v_tiles.shape[3]
    pair = slots // cols
    rows = pair * HALF

    tiles = v_tiles.reshape(held, cols, rows, LANES)
    spots = v_where.reshape(held, cols, 1, pair).astype(jnp.float32)
    spots = jnp.pad(spots, ((0, 0), (0, 0), (0, 7), (0, LANES - pair)))
    parts = jnp.concatenate([tiles, spots], axis=2).transpose(1, 0, 2, 3)
    parts = lax.all_to_all(parts, "col", 0, 0, tiled=True)
    parts = parts.reshape(held * cols, rows + 8, LANES)
    parts = lax.all_to_all(parts, "row", 0, 0, tiled=True)

    spots = jnp.pad(parts[:, rows, :pair].reshape(1, blocks * pair), ((0, 7), (0, LANES - blocks * pair)))
    share = jnp.concatenate([parts[:, :rows].reshape(blocks * rows, LANES), spots], axis=0)
    shares = jnp.broadcast_to(share, (cols, *share.shape))
    shares = lax.all_to_all(shares, "col", 0, 0, tiled=True)
    spots = shares[:, blocks * rows, : blocks * pair].astype(jnp.int32)
    spots = spots.reshape(cols, blocks, pair).transpose(1, 0, 2).reshape(blocks, slots)

    sums = contract(t_amps, shares, spots)
    sums = lax.all_to_all(sums, "layer", 0, 0, tiled=True)
    sums = sums[0] + sums[1]
    sums = lax.all_to_all(sums, "row", 0, 0, tiled=True)
    return jnp.sum(sums, axis=0)


def solution(mesh):
    return jax.shard_map(
        on_device,
        mesh=mesh,
        in_specs=(
            P("col", ("row", "layer")),
            P("col", "layer", "row", None, None),
            P("col", "layer", "row", None),
        ),
        out_specs=P("col", ("row", "layer")),
        check_vma=False,
    )
```

time: 1550 us -> 143 us (0.09)
  waiting for transfers between devices: 1120 us -> 0 us
  local copies, waits for them, and re-layouts: 137 us -> 6.03 us
  starting transfers between devices: 74.9 us -> 0 us
  matrix products: 37.7 us -> 0 us
  blocking collectives: 141 us -> 123 us
    psum x16 -> x0, waiting for transfers between devices: 1100 us -> none  [from_root(): return lax.psum(block, axis)]
    psum x16 -> x0, blocking collectives: 141 us -> none  [from_root(): return lax.psum(block, axis)]
    all_to_all x0 -> x5, blocking collectives: none -> 123 us  [the longest x1 48.3 us: on_device(): shares = lax.all_to_all(shares, 'col', 0, 0, tiled=True)]
    reshape x80 -> x2, local copies, waits for them, and re-layouts: 77.2 us -> 1.2 us  [the longest x1 1.13 us: on_device(): tiles = v_tiles.reshape(held, cols, rows, LANES)]
    ppermute x15 -> x0, starting transfers between devices: 74.2 us -> none  [shifted(): return lax.ppermute(block, axis, route)]
    dot_general x32 -> x0, matrix products: 37.7 us -> none  [the longest x16 33 us: apply_tiles(): jnp.einsum('rtc,tca->rta', picked, v_mats, precision=lax.Precision.HIGHEST)]
    gather x16 -> x0, local copies, waits for them, and re-layouts: 34.7 us -> none  [apply_tiles(): picked = jnp.take(t_shaped, cd_tile, axis=1)]
    while x15 -> x0, local copies, waits for them, and re-layouts: 18.4 us -> none
  transfers between devices with their start and end apart: 32 -> 0, of which waited for: 17 -> 0; matrix products, arithmetic and copies ran while one was open for 10% -> 0% of each run, Pallas kernels for 0% -> 0%
where the time goes in v1:
time: 143 us; the launch traced here: 142 us
  blocking collectives  123 us (86%)
  Pallas kernels  11.4 us (8%)
  local copies, waits for them, and re-layouts  6.03 us (4%)
  other arithmetic  1.49 us (1%)
    all_to_all x1, blocking collectives, on_device(): shares = lax.all_to_all(shares, 'col', 0, 0, tiled=True)  48.3 us
    all_to_all x1, blocking collectives, on_device(): parts = lax.all_to_all(parts, 'row', 0, 0, tiled=True)  28.2 us
    all_to_all x1, blocking collectives, on_device(): sums = lax.all_to_all(sums, 'row', 0, 0, tiled=True)  21.9 us
    all_to_all x1, blocking collectives, on_device(): parts = lax.all_to_all(parts, 'col', 0, 0, tiled=True)  15.5 us
    pallas_call x1, Pallas kernels, contract(): pl.pallas_call(contract_kernel, out_shape=jax.ShapeDtypeStruct((2, blocks...  11.4 us
    all_to_all x1, blocking collectives, on_device(): sums = lax.all_to_all(sums, 'layer', 0, 0, tiled=True)  9.39 us
    unnamed x7, local copies, waits for them, and re-layouts  4.16 us

profile of v1, /device:TPU:1, one launch (start us, length us, event | category | flops | bytes accessed | tf_op | source)
XLA Modules:
  0.0 142.3 jit_solution(387898231097013153)
XLA Ops:
  0.0 0.7 convert_reduce_fusion
  0.7 0.1 convert_element_type.26
  0.8 1.1 reshape.30
  2.0 15.5 %all_to_all.25 = f32[8,2,72,128]{3,2,1,0:T(8,128)S(1)} all-to-all(f32[8,2,72,128]{3,2,1,0:T(8,128)S(1)} %fusion), channel_id=1, replica_groups=mesh['row'=16,'col'=8,'layer'=2] {'col'}, dimensions={0} | all-to-all | bytes 1179648 | tf_op jit(solution)/shard_map/all_to_all | solution.py:108
  17.4 28.2 %all_to_all.26 = f32[16,72,128]{2,1,0:T(8,128)S(1)} all-to-all(f32[16,72,128]{2,1,0:T(8,128)S(1)} %bitcast.12), channel_id=1, replica_groups=mesh['row'=16,'col'=8,'layer'=2] {'row'}, dimensions={0} | all-to-all | bytes 1179648 | tf_op jit(solution)/shard_map/all_to_all | solution.py:110
  45.7 0.1 reshape_squeeze.3
  45.9 0.3 broadcast_in_dim.3
  46.2 0.0 copy-start.2
  46.2 48.3 %all_to_all.27.v_ref = f32[8,1032,128]{2,1,0:T(8,128)S(1)} all-to-all(f32[8,1032,128]{2,1,0:T(8,128)S(1)} %broadcast_in_dim.3), channel_id=1, replica_groups=mesh['row'=16,'col'=8,'layer'=2] {'col'}, dimensions={0} | all-to-all | bytes 8454144 | tf_op jit(solution)/shard_map/all_to_all | solution.py:115
  94.5 0.0 copy-start
  94.5 1.9 %copy-done = f32[8,1032,128]{2,1,0:T(8,128)} copy-done((f32[8,1032,128]{2,1,0:T(8,128)}, f32[8,1032,128]{2,1,0:T(8,128)S(1)}, u32[]{:S(2)}) %copy-start) | copy-done | bytes 4227096
  96.5 0.1 copy.14
  96.5 0.1 copy.15
  96.6 0.1 copy.16.spots_ref
  96.7 0.0 copy-done.2
  96.7 0.0 copy-start.1
  96.7 2.2 %copy-done.1 = f32[8,1032,128]{2,1,0:T(8,128)S(1)} copy-done((f32[8,1032,128]{2,1,0:T(8,128)S(1)}, f32[8,1032,128]{2,1,0:T(8,128)}, u32[]{:S(2)}) %copy-start.1) | copy-done | bytes 4227096
  98.9 11.4 %shard_map.37 = f32[2,16,64,128]{3,2,1,0:T(8,128)S(1)} custom-call(s32[16,16]{1,0:T(8,128)S(1)} %copy.16.spots_ref, f32[64,4096]{1,0:T(8,128)S(1)} %copy-done.2, f32[8,1032,128]{2,1,0:T(8,128)S(1)} %copy-done.1), custom_call_target="tpu_custom_call" | custom-call | flops 2147483648 | bytes 6291456 | tf_op jit(solution)/shard_map/pallas_call | solution.py:71
  110.3 9.4 %all_to_all.28 = f32[2,16,64,128]{3,2,1,0:T(8,128)S(1)} all-to-all(f32[2,16,64,128]{3,2,1,0:T(8,128)S(1)} %shard_map.37), channel_id=1, replica_groups=mesh['row'=16,'col'=8,'layer'=2] {'layer'}, dimensions={0} | all-to-all | bytes 2097152 | tf_op jit(solution)/shard_map/all_to_all | solution.py:120
  119.7 0.1 fusion.1
  119.8 21.9 %all_to_all.29 = f32[16,64,128]{2,1,0:T(8,128)S(1)} all-to-all(f32[16,64,128]{2,1,0:T(8,128)S(1)} %fusion.1), channel_id=1, replica_groups=mesh['row'=16,'col'=8,'layer'=2] {'row'}, dimensions={0} | all-to-all | bytes 1048576 | tf_op jit(solution)/shard_map/all_to_all | solution.py:122
  141.6 0.6 reduce_sum.9
  (6 shorter events, 0.2 us)
Async XLA Ops:
  46.2 50.5 %copy-start.2 = (f32[64,4096]{1,0:T(8,128)S(1)}, f32[64,4096]{1,0:T(8,128)}, u32[]{:S(2)}) copy-start(f32[64,4096]{1,0:T(8,128)} %t_ref.1) | copy-start | bytes 3145732
  94.5 1.9 %copy-start = (f32[8,1032,128]{2,1,0:T(8,128)}, f32[8,1032,128]{2,1,0:T(8,128)S(1)}, u32[]{:S(2)}) copy-start(f32[8,1032,128]{2,1,0:T(8,128)S(1)} %all_to_all.27.v_ref) | copy-start | bytes 12681220
  96.7 2.2 %copy-start.1 = (f32[8,1032,128]{2,1,0:T(8,128)S(1)}, f32[8,1032,128]{2,1,0:T(8,128)}, u32[]{:S(2)}) copy-start(f32[8,1032,128]{2,1,0:T(8,128)} %copy-done) | copy-start | bytes 12681220

commit v2 on v1

v2 whole, which is shorter than its diff:
```python
import jax
import jax.numpy as jnp
from jax import lax
from jax.experimental import pallas as pl
from jax.experimental.pallas import tpu as pltpu
from jax.sharding import PartitionSpec as P

TILE = 64
AB_DEV = 128
LANES = 128
HALF = TILE // 2
VMEM = pl.BlockSpec(memory_space=pltpu.VMEM)
SMEM = pl.BlockSpec(memory_space=pltpu.SMEM)


def split_rows(x):
    hi = x.astype(jnp.bfloat16)
    return hi, (x - hi.astype(jnp.float32)).astype(jnp.bfloat16)


def prepare_kernel(t_ref, t_tiles):
    row = lax.broadcasted_iota(jnp.int32, (LANES, 2 * LANES), 0)
    col = lax.broadcasted_iota(jnp.int32, (LANES, 2 * LANES), 1)
    source = (col // LANES) * TILE + 2 * (col % HALF) + (col % TILE) // HALF
    pick = (row == source).astype(jnp.bfloat16)
    for at in range(t_ref.shape[1] // LANES):
        hi, lo = split_rows(t_ref[:, at * LANES : (at + 1) * LANES])
        both = jnp.dot(
            jnp.concatenate([hi, lo], axis=0), pick, preferred_element_type=jnp.float32
        ).astype(jnp.bfloat16)
        t_tiles[2 * at] = both[:, :LANES]
        t_tiles[2 * at + 1] = both[:, LANES:]


def prepare(t_block):
    ij, cd = t_block.shape
    return pl.pallas_call(
        prepare_kernel,
        out_shape=jax.ShapeDtypeStruct((cd // TILE, 2 * ij, LANES), jnp.bfloat16),
        in_specs=[VMEM],
        out_specs=VMEM,
        compiler_params=pltpu.CompilerParams(vmem_limit_bytes=32 * 2**20),
        cost_estimate=pl.CostEstimate(flops=2 * 2 * ij * cd * 2 * LANES, bytes_accessed=3 * 2**20, transcendentals=0),
    )(t_block)


def slot_rows(v, spot):
    lane_half = lax.broadcasted_iota(jnp.int32, (HALF, LANES), 1) // TILE
    safe = jnp.maximum(spot, 0)
    ab_half = safe & 1
    ab_pair = (safe >> 1) & 1
    swapped = pltpu.roll(v, TILE, 1)
    upper = ab_half == 1
    keep = (lane_half == ab_half) & (spot >= 0)
    hi_e, lo_e = split_rows(jnp.where(keep, jnp.where(upper, swapped, v), 0.0))
    hi_o, lo_o = split_rows(jnp.where(keep, jnp.where(upper, v, swapped), 0.0))
    rows = jnp.concatenate([hi_e, hi_o, lo_e, lo_o], axis=0)
    none = jnp.zeros_like(rows)
    return jnp.where(ab_pair == 0, rows, none), jnp.where(ab_pair == 1, rows, none)


def contract_kernel(sources, fresh, pair, *refs):
    count = len(sources)
    starts = [first for first, _, _ in sources]
    place, spots, t_tiles = refs[:3]
    shares = refs[3 : 3 + count]
    if fresh:
        sums = None
        out, lhs, rhs = refs[3 + count :]
    else:
        sums, out, lhs, rhs = refs[3 + count :]
    layer = place[1]
    ij = out.shape[2]
    rows = pair * HALF
    cols = spots.shape[1] // pair
    columns = [((place[0] + shift) & (cols - 1)) ^ flip for _, shift, flip in sources]
    blocks = out.shape[1]
    for block in range(blocks):
        used = [
            n for n in range(count)
            if starts[n] <= block < starts[n] + shares[n].shape[0] // rows
        ]
        buffer = block % 2
        width = len(used) * pair * LANES
        for m, n in enumerate(used):
            base = (block - starts[n]) * rows
            for p in range(pair):
                spot = spots[block, columns[n] * pair + p]
                at = (m * pair + p) * LANES
                lhs[buffer, :, at : at + LANES] = t_tiles[jnp.maximum(spot, 0) >> 2]
                left, right = slot_rows(shares[n][base + p * HALF : base + (p + 1) * HALF], spot)
                rhs[buffer, at : at + LANES, :LANES] = left
                rhs[buffer, at : at + LANES, LANES:] = right
        total = jnp.dot(lhs[buffer, :, :width], rhs[buffer, :width], preferred_element_type=jnp.float32)
        total = total[:ij] + total[ij:]
        mine = total[:, :LANES]
        other = total[:, LANES:]
        if sums is not None:
            mine = mine + sums[layer, block]
            other = other + sums[1 - layer, block]
        out[layer, block] = mine
        out[1 - layer, block] = other


def contract(sums, t_tiles, spots, place, shares, pair):
    blocks = spots.shape[0]
    ij = t_tiles.shape[1] // 2
    sources = tuple(source for source, _ in shares)
    depth = len(shares) * pair * LANES
    given = [place, spots, t_tiles, *(share for _, share in shares)]
    specs = [SMEM, SMEM] + [VMEM] * (1 + len(shares))
    if sums is not None:
        given.append(sums)
        specs.append(VMEM)

    def kernel(*refs):
        contract_kernel(sources, sums is None, pair, *refs)

    return pl.pallas_call(
        kernel,
        out_shape=jax.ShapeDtypeStruct((2, blocks, ij, LANES), jnp.float32),
        in_specs=specs,
        out_specs=VMEM,
        scratch_shapes=[
            pltpu.VMEM((2, 2 * ij, depth), jnp.bfloat16),
            pltpu.VMEM((2, depth, 2 * LANES), jnp.bfloat16),
        ],
        input_output_aliases={} if sums is None else {len(given) - 1: 0},
        compiler_params=pltpu.CompilerParams(vmem_limit_bytes=32 * 2**20),
        cost_estimate=pl.CostEstimate(
            flops=2 * blocks * 2 * ij * depth * 2 * LANES,
            bytes_accessed=(len(shares) + 4) * 2**19,
            transcendentals=0,
        ),
    )(*given)


def on_device(t_amps, v_tiles, v_where):
    cols = lax.axis_size("col")
    blocks = lax.axis_size("row")
    held, slots = v_tiles.shape[0], v_tiles.shape[3]
    pair = slots // cols
    rows = pair * HALF
    place = jnp.stack([lax.axis_index("col"), lax.axis_index("layer")])

    tiles = v_tiles.reshape(held, cols, rows, LANES)
    spots = v_where.reshape(held, 1, 1, slots).astype(jnp.float32)
    spots = jnp.pad(spots, ((0, 0), (0, 0), (0, 7), (0, LANES - slots)))
    spots = jnp.broadcast_to(spots, (held, cols, 8, LANES))
    parts = jnp.concatenate([tiles, spots], axis=2).transpose(1, 0, 2, 3)
    parts = parts.reshape(cols, held * (rows + 8), LANES)
    parts = lax.all_to_all(parts, "col", 0, 0, tiled=True)
    parts = parts.reshape(held * cols, rows + 8, LANES)
    parts = lax.all_to_all(parts, "row", 0, 0, tiled=True)
    spots = parts[:, rows, :slots].astype(jnp.int32)
    own = parts[:, :rows].reshape(blocks * rows, LANES)

    def send(share, to):
        return lax.ppermute(share, "col", [(i, to(i)) for i in range(cols)])

    def up(i):
        return (i + 2) % cols

    def down(i):
        return (i - 2) % cols

    def across(i):
        return i ^ 1

    half = blocks * rows // 2
    partner = send(own, across)
    below = send(own, up)
    above = send(own, down)
    far_low = send(below[:half], up)
    far_high = send(above[half:], down)
    partner_below = send(partner, up)
    partner_above = send(partner, down)
    partner_far_low = send(far_low, across)
    partner_far_high = send(far_high, across)

    t_tiles = prepare(t_amps)

    def add(sums, *shares):
        return contract(sums, t_tiles, spots, place, shares, pair)

    middle = blocks // 2
    sums = add(None, ((0, 0, 0), own))
    sums = add(sums, ((0, 0, 1), partner), ((0, -2, 0), below), ((0, 2, 0), above))
    sums = add(
        sums,
        ((0, -2, 1), partner_below),
        ((0, 2, 1), partner_above),
        ((0, 4, 0), far_low),
        ((middle, 4, 0), far_high),
    )
    sums = add(sums, ((0, 4, 1), partner_far_low), ((middle, 4, 1), partner_far_high))
    sums = sums[0] + lax.ppermute(sums[1], "layer", [(0, 1), (1, 0)])
    sums = lax.all_to_all(sums, "row", 0, 0, tiled=True)
    return jnp.sum(sums, axis=0)


def solution(mesh):
    return jax.shard_map(
        on_device,
        mesh=mesh,
        in_specs=(
            P("col", ("row", "layer")),
            P("col", "layer", "row", None, None),
            P("col", "layer", "row", None),
        ),
        out_specs=P("col", ("row", "layer")),
        check_vma=False,
    )
```

time: 143 us -> 113 us (0.79)
  blocking collectives: 123 us -> 67.2 us
  starting transfers between devices: 0 us -> 15.5 us
  waiting for transfers between devices: 0 us -> 12 us
  local copies, waits for them, and re-layouts: 6.03 us -> 4.33 us
    all_to_all x2 -> x0, blocking collectives: 57.7 us -> none  [the longest x1 48.3 us: on_device(): shares = lax.all_to_all(shares, 'col', 0, 0, tiled=True)]
    ppermute x0 -> x10, starting transfers between devices: none -> 15.5 us  [the longest x9 9.49 us: send(): return lax.ppermute(share, 'col', [(i, to(i)) for i in range(cols)])]
    ppermute x0 -> x10, waiting for transfers between devices: none -> 12 us  [the longest x9 10.5 us: send(): return lax.ppermute(share, 'col', [(i, to(i)) for i in range(cols)])]
    unnamed x7 -> x4, local copies, waits for them, and re-layouts: 4.16 us -> 0.77 us
    slice x2 -> x4, local copies, waits for them, and re-layouts: 0.08 us -> 2.34 us  [the longest x1 0.84 us: on_device(): spots = parts[:, rows, :slots].astype(jnp.int32)]
    all_to_all x1, blocking collectives: 21.9 us -> 23.4 us  [on_device(): sums = lax.all_to_all(sums, 'row', 0, 0, tiled=True)]
    pallas_call x1 -> x5, Pallas kernels: 11.4 us -> 10.7 us  [the longest x4 10 us: contract(): pl.pallas_call(kernel, out_shape=jax.ShapeDtypeStruct((2, blocks, ij, LAN...]
  transfers between devices with their start and end apart: 0 -> 10, of which waited for: 0 -> 3; matrix products, arithmetic and copies ran while one was open for 0% -> 2% of each run, Pallas kernels for 0% -> 8%
where the time goes in v2:
time: 113 us; the launch traced here: 111 us
  blocking collectives  67.2 us (59%)
  starting transfers between devices  15.5 us (14%)
  waiting for transfers between devices  12 us (11%)
  Pallas kernels  10.7 us (9%)
  local copies, waits for them, and re-layouts  4.33 us (4%)
  other arithmetic  1.54 us (1%)
    all_to_all x1, blocking collectives, on_device(): parts = lax.all_to_all(parts, 'row', 0, 0, tiled=True)  28.2 us
    all_to_all x1, blocking collectives, on_device(): sums = lax.all_to_all(sums, 'row', 0, 0, tiled=True)  23.4 us
    all_to_all x1, blocking collectives, on_device(): parts = lax.all_to_all(parts, 'col', 0, 0, tiled=True)  15.6 us
    ppermute x9, waiting for transfers between devices, send(): return lax.ppermute(share, 'col', [(i, to(i)) for i in range(cols)])  10.5 us
    pallas_call x4, Pallas kernels, contract(): pl.pallas_call(kernel, out_shape=jax.ShapeDtypeStruct((2, blocks, ij, LAN...  10 us
    ppermute x9, starting transfers between devices, send(): return lax.ppermute(share, 'col', [(i, to(i)) for i in range(cols)])  9.49 us
    ppermute x1, starting transfers between devices, on_device(): sums = sums[0] + lax.ppermute(sums[1], 'layer', [(0, 1), (1, 0)])  6.03 us
  transfers between devices with their start and end apart: 10, of which 3 were waited for; matrix products, arithmetic and copies ran while one was open for 2% of the time, Pallas kernels for 8%

profile of v2, /device:TPU:1, one launch (start us, length us, event | category | flops | bytes accessed | tf_op | source)
XLA Modules:
  0.0 111.5 jit_solution(9574773503273963246)
XLA Ops:
  0.0 1.1 %reshape.13 = f32[2,8,64,128]{3,2,1,0:T(8,128)S(1)} reshape(f32[2,1,1,16,4096]{4,3,2,1,0:T(8,128)} %param.4) | data formatting | bytes 1048576 | tf_op jit(solution)/shard_map/reshape | solution.py:146
  1.1 0.7 convert_element_type.10
  1.9 0.0 copy-start
  1.9 15.6 %all_to_all.15 = f32[8,144,128]{2,1,0:T(8,128)S(1)} all-to-all(f32[8,144,128]{2,1,0:T(8,128)S(1)} %bitcast.24), channel_id=1, replica_groups=mesh['row'=16,'col'=8,'layer'=2] {'col'}, dimensions={0} | all-to-all | bytes 1179648 | tf_op jit(solution)/shard_map/all_to_all | solution.py:152
  17.5 28.2 %all_to_all.16 = f32[16,72,128]{2,1,0:T(8,128)S(1)} all-to-all(f32[16,72,128]{2,1,0:T(8,128)S(1)} %bitcast.25), channel_id=1, replica_groups=mesh['row'=16,'col'=8,'layer'=2] {'row'}, dimensions={0} | all-to-all | bytes 1179648 | tf_op jit(solution)/shard_map/all_to_all | solution.py:154
  45.8 0.0 copy-start.1
  45.8 0.8 copy-done.1
  46.6 0.0 collective-permute-start
  46.6 2.7 %collective-permute-start.3 = (f32[1024,128]{1,0:T(8,128)S(1)}, f32[1024,128]{1,0:T(8,128)S(1)}, u32[]{:S(2)}, u32[]{:S(2)}) collective-permute-start(f32[1024,128]{1,0:T(8,128)S(1)} %bitcast.21), channel_id=1, source_target_pairs={{0,12},{2,14},{4,0},{6,2},{8,4},{10,6},{12,8},{14,10},{1,13},{3,15... | collective-permute-start | bytes 1572872 | tf_op jit(solution)/shard_map/ppermute | solution.py:159
  49.3 0.0 collective-permute-start.6
  49.3 7.9 %collective-permute-done.refs_4_ = f32[1024,128]{1,0:T(8,128)S(1)} collective-permute-done((f32[1024,128]{1,0:T(8,128)S(1)}, f32[1024,128]{1,0:T(8,128)S(1)}, u32[]{:S(2)}, u32[]{:S(2)}) %collective-permute-start) | collective-permute-done | bytes 524320 | tf_op jit(solution)/shard_map/ppermute | solution.py:159
  57.2 0.7 slice.26
  57.9 0.0 collective-permute-start.1
  58.0 0.0 collective-permute-done.3.refs_5_
  58.0 0.7 slice.27
  58.7 2.7 %collective-permute-start.4 = (f32[512,128]{1,0:T(8,128)}, f32[512,128]{1,0:T(8,128)}, u32[]{:S(2)}, u32[]{:S(2)}) collective-permute-start(f32[512,128]{1,0:T(8,128)} %slice.27), channel_id=1, source_target_pairs={{0,12},{2,14},{4,0},{6,2},{8,4},{10,6},{12,8},{14,10},{1,13},{3,15... | collective-permute-start | bytes 786440 | tf_op jit(solution)/shard_map/ppermute | solution.py:159
  61.3 0.0 collective-permute-done.6.refs_3_
  61.3 0.0 collective-permute-start.7
  61.3 2.7 %collective-permute-start.8 = (f32[1024,128]{1,0:T(8,128)S(1)}, f32[1024,128]{1,0:T(8,128)}, u32[]{:S(2)}, u32[]{:S(2)}) collective-permute-start(f32[1024,128]{1,0:T(8,128)S(1)} %collective-permute-done.6.refs_3_), channel_id=1, source_target_pairs={{0,12},{2,14},{4,0},{6,2},{8,4},{10,6},{12,8},{14,10},{1,13},{3,15... | collective-permute-start | bytes 1572872 | tf_op jit(solution)/shard_map/ppermute | solution.py:159
  64.0 0.0 copy-done
  64.0 0.7 shard_map.37.refs_2_
  64.7 0.1 pad_add_fusion.refs_0_
  64.8 0.8 slice.24
  65.7 0.0 collective-permute-done.1.refs_5_
  65.7 0.0 collective-permute-start.2
  65.7 0.0 collective-permute-done.4.refs_6_
  65.7 1.5 %collective-permute-start.5 = (f32[512,128]{1,0:T(8,128)}, f32[512,128]{1,0:T(8,128)S(1)}, u32[]{:S(2)}, u32[]{:S(2)}) collective-permute-start(f32[512,128]{1,0:T(8,128)} %collective-permute-done.4.refs_6_), channel_id=1, source_target_pairs={{0,2},{2,0},{4,6},{6,4},{8,10},{10,8},{12,14},{14,12},{1,3},{3,1},... | collective-permute-start | bytes 786440 | tf_op jit(solution)/shard_map/ppermute | solution.py:159
  67.1 1.6 %shard_map.38.refs_6_ = f32[2,16,64,128]{3,2,1,0:T(8,128)S(1)} custom-call(s32[2]{0:T(128)S(1)} %pad_add_fusion.refs_0_, s32[16,16]{1,0:T(8,128)S(1)} %convert_bitcast_fusion.refs_1_, bf16[64,128,128]{2,1,0:T(8,128)(2,1)S(1)} %shard_map.37.refs_2_, f32[1024,128]{1,0:T(8,128)S(1)} %bitcast.23), custom_call_target="tpu_custom_call" | custom-call | flops 268435456 | bytes 2621440 | tf_op jit(solution)/shard_map/pallas_call | solution.py:119
  68.8 3.0 %shard_map.39.refs_7_ = f32[2,16,64,128]{3,2,1,0:T(8,128)S(1)} custom-call(s32[2]{0:T(128)S(1)} %pad_add_fusion.refs_0_, s32[16,16]{1,0:T(8,128)S(1)} %convert_bitcast_fusion.refs_1_, bf16[64,128,128]{2,1,0:T(8,128)(2,1)S(1)} %shard_map.37.refs_2_, f32[1024,128]{1,0:T(8,128)S(1)} %collective-permute-done.6.refs_3_, ...), custom_call_target="tpu_custom_call", output_to_operand_aliasing={{}: (6, {})} | custom-call | flops 805306368 | bytes 3670016 | tf_op jit(solution)/shard_map/pallas_call | solution.py:119
  71.8 2.5 %collective-permute-done.7.refs_3_ = f32[1024,128]{1,0:T(8,128)} collective-permute-done((f32[1024,128]{1,0:T(8,128)S(1)}, f32[1024,128]{1,0:T(8,128)}, u32[]{:S(2)}, u32[]{:S(2)}) %collective-permute-start.7) | collective-permute-done | bytes 524320 | tf_op jit(solution)/shard_map/ppermute | solution.py:159
  74.3 0.0 collective-permute-done.8.refs_4_
  74.3 3.8 %shard_map.40.refs_5_ = f32[2,16,64,128]{3,2,1,0:T(8,128)S(1)} custom-call(s32[2]{0:T(128)S(1)} %pad_add_fusion.refs_0_, s32[16,16]{1,0:T(8,128)S(1)} %convert_bitcast_fusion.refs_1_, bf16[64,128,128]{2,1,0:T(8,128)(2,1)S(1)} %shard_map.37.refs_2_, f32[1024,128]{1,0:T(8,128)} %collective-permute-done.7.refs_3_, ...), custom_call_target="tpu_custom_call", output_to_operand_aliasing={{}: (7, {})} | custom-call | flops 1073741824 | bytes 4194304 | tf_op jit(solution)/shard_map/pallas_call | solution.py:119
  78.1 0.0 collective-permute-done.2.refs_3_
  78.1 0.0 collective-permute-done.5.refs_4_
  78.1 1.6 %shard_map.41 = f32[2,16,64,128]{3,2,1,0:T(8,128)S(1)} custom-call(s32[2]{0:T(128)S(1)} %pad_add_fusion.refs_0_, s32[16,16]{1,0:T(8,128)S(1)} %convert_bitcast_fusion.refs_1_, bf16[64,128,128]{2,1,0:T(8,128)(2,1)S(1)} %shard_map.37.refs_2_, f32[512,128]{1,0:T(8,128)S(1)} %collective-permute-done.2.refs_3_, ...), custom_call_target="tpu_custom_call", output_to_operand_aliasing={{}: (5, {})} | custom-call | flops 536870912 | bytes 3145728 | tf_op jit(solution)/shard_map/pallas_call | solution.py:119
  79.8 6.0 %collective-permute-start.9 = (f32[16,64,128]{2,1,0:T(8,128)S(1)}, f32[16,64,128]{2,1,0:T(8,128)S(1)}, u32[]{:S(2)}, u32[]{:S(2)}) collective-permute-start(f32[16,64,128]{2,1,0:T(8,128)S(1)} %slice_bitcast_fusion), channel_id=1, source_target_pairs={{0,1},{1,0},{2,3},{3,2},{4,5},{5,4},{6,7},{7,6},{8,9},{9,8},{10,11... | collective-permute-start | bytes 1572872 | tf_op jit(solution)/shard_map/ppermute | solution.py:197
  85.8 1.5 %collective-permute-done.9 = f32[16,64,128]{2,1,0:T(8,128)S(1)} collective-permute-done((f32[16,64,128]{2,1,0:T(8,128)S(1)}, f32[16,64,128]{2,1,0:T(8,128)S(1)}, u32[]{:S(2)}, u32[]{:S(2)}) %collective-permute-start.9) | collective-permute-done | bytes 524320 | tf_op jit(solution)/shard_map/ppermute | solution.py:197
  87.4 0.1 fusion
  87.4 23.4 %all_to_all.17 = f32[16,64,128]{2,1,0:T(8,128)S(1)} all-to-all(f32[16,64,128]{2,1,0:T(8,128)S(1)} %fusion), channel_id=1, replica_groups=mesh['row'=16,'col'=8,'layer'=2] {'row'}, dimensions={0} | all-to-all | bytes 1048576 | tf_op jit(solution)/shard_map/all_to_all | solution.py:198
  110.8 0.6 reduce_sum.9
  (7 shorter events, 0.2 us)
Async XLA Ops:
  1.9 62.1 %copy-start = (f32[64,4096]{1,0:T(8,128)S(1)}, f32[64,4096]{1,0:T(8,128)}, u32[]{:S(2)}) copy-start(f32[64,4096]{1,0:T(8,128)} %t_ref.1) | copy-start | bytes 3145732
  45.8 0.8 copy-start.1
  46.6 10.6 %collective-permute-start = (f32[1024,128]{1,0:T(8,128)S(1)}, f32[1024,128]{1,0:T(8,128)S(1)}, u32[]{:S(2)}, u32[]{:S(2)}) collective-permute-start(f32[1024,128]{1,0:T(8,128)S(1)} %bitcast.20), channel_id=1, source_target_pairs={{0,4},{2,6},{4,8},{6,10},{8,12},{10,14},{12,0},{14,2},{1,5},{3,7},... | collective-permute-start | bytes 1572872 | tf_op jit(solution)/shard_map/ppermute | solution.py:159
  46.6 11.3 %collective-permute-start.3 = (f32[1024,128]{1,0:T(8,128)S(1)}, f32[1024,128]{1,0:T(8,128)S(1)}, u32[]{:S(2)}, u32[]{:S(2)}) collective-permute-start(f32[1024,128]{1,0:T(8,128)S(1)} %bitcast.21), channel_id=1, source_target_pairs={{0,12},{2,14},{4,0},{6,2},{8,4},{10,6},{12,8},{14,10},{1,13},{3,15... | collective-permute-start | bytes 1572872 | tf_op jit(solution)/shard_map/ppermute | solution.py:159
  49.3 12.1 %collective-permute-start.6 = (f32[1024,128]{1,0:T(8,128)S(1)}, f32[1024,128]{1,0:T(8,128)S(1)}, u32[]{:S(2)}, u32[]{:S(2)}) collective-permute-start(f32[1024,128]{1,0:T(8,128)S(1)} %bitcast.22), channel_id=1, source_target_pairs={{0,2},{2,0},{4,6},{6,4},{8,10},{10,8},{12,14},{14,12},{1,3},{3,1},... | collective-permute-start | bytes 1572872 | tf_op jit(solution)/shard_map/ppermute | solution.py:159
  57.9 7.7 %collective-permute-start.1 = (f32[512,128]{1,0:T(8,128)}, f32[512,128]{1,0:T(8,128)S(1)}, u32[]{:S(2)}, u32[]{:S(2)}) collective-permute-start(f32[512,128]{1,0:T(8,128)} %slice.26), channel_id=1, source_target_pairs={{0,4},{2,6},{4,8},{6,10},{8,12},{10,14},{12,0},{14,2},{1,5},{3,7},... | collective-permute-start | bytes 786440 | tf_op jit(solution)/shard_map/ppermute | solution.py:159
  58.7 7.0 %collective-permute-start.4 = (f32[512,128]{1,0:T(8,128)}, f32[512,128]{1,0:T(8,128)}, u32[]{:S(2)}, u32[]{:S(2)}) collective-permute-start(f32[512,128]{1,0:T(8,128)} %slice.27), channel_id=1, source_target_pairs={{0,12},{2,14},{4,0},{6,2},{8,4},{10,6},{12,8},{14,10},{1,13},{3,15... | collective-permute-start | bytes 786440 | tf_op jit(solution)/shard_map/ppermute | solution.py:159
  61.3 13.0 %collective-permute-start.7 = (f32[1024,128]{1,0:T(8,128)S(1)}, f32[1024,128]{1,0:T(8,128)}, u32[]{:S(2)}, u32[]{:S(2)}) collective-permute-start(f32[1024,128]{1,0:T(8,128)S(1)} %collective-permute-done.6.refs_3_), channel_id=1, source_target_pairs={{0,4},{2,6},{4,8},{6,10},{8,12},{10,14},{12,0},{14,2},{1,5},{3,7},... | collective-permute-start | bytes 1572872 | tf_op jit(solution)/shard_map/ppermute | solution.py:159
  61.3 13.0 %collective-permute-start.8 = (f32[1024,128]{1,0:T(8,128)S(1)}, f32[1024,128]{1,0:T(8,128)}, u32[]{:S(2)}, u32[]{:S(2)}) collective-permute-start(f32[1024,128]{1,0:T(8,128)S(1)} %collective-permute-done.6.refs_3_), channel_id=1, source_target_pairs={{0,12},{2,14},{4,0},{6,2},{8,4},{10,6},{12,8},{14,10},{1,13},{3,15... | collective-permute-start | bytes 1572872 | tf_op jit(solution)/shard_map/ppermute | solution.py:159
  65.7 12.4 %collective-permute-start.2 = (f32[512,128]{1,0:T(8,128)S(1)}, f32[512,128]{1,0:T(8,128)S(1)}, u32[]{:S(2)}, u32[]{:S(2)}) collective-permute-start(f32[512,128]{1,0:T(8,128)S(1)} %collective-permute-done.1.refs_5_), channel_id=1, source_target_pairs={{0,2},{2,0},{4,6},{6,4},{8,10},{10,8},{12,14},{14,12},{1,3},{3,1},... | collective-permute-start | bytes 786440 | tf_op jit(solution)/shard_map/ppermute | solution.py:159
  65.7 12.4 %collective-permute-start.5 = (f32[512,128]{1,0:T(8,128)}, f32[512,128]{1,0:T(8,128)S(1)}, u32[]{:S(2)}, u32[]{:S(2)}) collective-permute-start(f32[512,128]{1,0:T(8,128)} %collective-permute-done.4.refs_6_), channel_id=1, source_target_pairs={{0,2},{2,0},{4,6},{6,4},{8,10},{10,8},{12,14},{14,12},{1,3},{3,1},... | collective-permute-start | bytes 786440 | tf_op jit(solution)/shard_map/ppermute | solution.py:159
  79.8 7.6 %collective-permute-start.9 = (f32[16,64,128]{2,1,0:T(8,128)S(1)}, f32[16,64,128]{2,1,0:T(8,128)S(1)}, u32[]{:S(2)}, u32[]{:S(2)}) collective-permute-start(f32[16,64,128]{2,1,0:T(8,128)S(1)} %slice_bitcast_fusion), channel_id=1, source_target_pairs={{0,1},{1,0},{2,3},{3,2},{4,5},{5,4},{6,7},{7,6},{8,9},{9,8},{10,11... | collective-permute-start | bytes 1572872 | tf_op jit(solution)/shard_map/ppermute | solution.py:197

commit v3 on v2

--- a/solution.py
+++ b/solution.py
@@ -16,6 +16,38 @@
 def split_rows(x):
     hi = x.astype(jnp.bfloat16)
     return hi, (x - hi.astype(jnp.float32)).astype(jnp.bfloat16)
+
+
+def pack_kernel(spots, lists, out):
+    held, slots = spots.shape
+    cols = out.shape[0]
+    pair = slots // cols
+    rows = pair * HALF
+    lane = lax.broadcasted_iota(jnp.int32, (8, LANES), 1)
+    for b in range(held):
+        row = jnp.zeros((8, LANES), jnp.float32)
+        for s in range(slots):
+            row = jnp.where(lane == s, spots[b, s].astype(jnp.float32), row)
+        base = b * (rows + 8)
+        for c in range(cols):
+            for p in range(pair):
+                s = c * pair + p
+                out[c, base + p * HALF : base + (p + 1) * HALF] = lists[b, s // 8, pl.ds(s % 8, HALF, stride=8), :]
+            out[c, base + rows : base + rows + 8] = row
+
+
+def pack(v_tiles, v_where, cols):
+    held, slots = v_tiles.shape[0], v_tiles.shape[3]
+    lists = v_tiles.reshape(held, slots // 8, 8, HALF, LANES).transpose(0, 1, 3, 2, 4)
+    lists = lists.reshape(held, slots // 8, HALF * 8, LANES)
+    return pl.pallas_call(
+        pack_kernel,
+        out_shape=jax.ShapeDtypeStruct((cols, held * (slots // cols * HALF + 8), LANES), jnp.float32),
+        in_specs=[SMEM, VMEM],
+        out_specs=VMEM,
+        compiler_params=pltpu.CompilerParams(vmem_limit_bytes=16 * 2**20),
+        cost_estimate=pl.CostEstimate(flops=0, bytes_accessed=2**20, transcendentals=0),
+    )(v_where.reshape(held, slots), lists)
 
 
 def prepare_kernel(t_ref, t_tiles):
@@ -143,12 +175,7 @@
     rows = pair * HALF
     place = jnp.stack([lax.axis_index("col"), lax.axis_index("layer")])
 
-    tiles = v_tiles.reshape(held, cols, rows, LANES)
-    spots = v_where.reshape(held, 1, 1, slots).astype(jnp.float32)
-    spots = jnp.pad(spots, ((0, 0), (0, 0), (0, 7), (0, LANES - slots)))
-    spots = jnp.broadcast_to(spots, (held, cols, 8, LANES))
-    parts = jnp.concatenate([tiles, spots], axis=2).transpose(1, 0, 2, 3)
-    parts = parts.reshape(cols, held * (rows + 8), LANES)
+    parts = pack(v_tiles, v_where, cols)
     parts = lax.all_to_all(parts, "col", 0, 0, tiled=True)
     parts = parts.reshape(held * cols, rows + 8, LANES)
     parts = lax.all_to_all(parts, "row", 0, 0, tiled=True)
@@ -167,32 +194,27 @@
     def across(i):
         return i ^ 1
 
-    half = blocks * rows // 2
+    t_tiles = prepare(t_amps)
+
+    def add(sums, *shares):
+        return contract(sums, t_tiles, spots, place, shares, pair)
+
+    half, middle = blocks * rows // 2, blocks // 2
     partner = send(own, across)
     below = send(own, up)
     above = send(own, down)
+    sums = add(None, ((0, 0, 0), own))
+    sums, partner, below, above = lax.optimization_barrier((sums, partner, below, above))
+    partner_below = send(partner, up)
+    partner_above = send(partner, down)
     far_low = send(below[:half], up)
     far_high = send(above[half:], down)
-    partner_below = send(partner, up)
-    partner_above = send(partner, down)
+    sums = add(sums, ((0, 0, 1), partner), ((0, -2, 0), below), ((0, 2, 0), above))
+    sums, far_low, far_high = lax.optimization_barrier((sums, far_low, far_high))
     partner_far_low = send(far_low, across)
     partner_far_high = send(far_high, across)
-
-    t_tiles = prepare(t_amps)
-
-    def add(sums, *shares):
-        return contract(sums, t_tiles, spots, place, shares, pair)
-
-    middle = blocks // 2
-    sums = add(None, ((0, 0, 0), own))
-    sums = add(sums, ((0, 0, 1), partner), ((0, -2, 0), below), ((0, 2, 0), above))
-    sums = add(
-        sums,
-        ((0, -2, 1), partner_below),
-        ((0, 2, 1), partner_above),
-        ((0, 4, 0), far_low),
-        ((middle, 4, 0), far_high),
-    )
+    sums = add(sums, ((0, 4, 0), far_low), ((middle, 4, 0), far_high))
+    sums = add(sums, ((0, -2, 1), partner_below), ((0, 2, 1), partner_above))
     sums = add(sums, ((0, 4, 1), partner_far_low), ((middle, 4, 1), partner_far_high))
     sums = sums[0] + lax.ppermute(sums[1], "layer", [(0, 1), (1, 0)])
     sums = lax.all_to_all(sums, "row", 0, 0, tiled=True)

time: 113 us -> 120 us (1.062)
  waiting for transfers between devices: 12 us -> 18.9 us
  blocking collectives: 67.2 us -> 68.7 us
    ppermute x9, waiting for transfers between devices: 10.5 us -> 17.4 us  [send(): return lax.ppermute(share, 'col', [(i, to(i)) for i in range(cols)])]
    ppermute x9, starting transfers between devices: 9.49 us -> 7.15 us  [send(): return lax.ppermute(share, 'col', [(i, to(i)) for i in range(cols)])]
    ppermute x1, starting transfers between devices: 6.03 us -> 7.93 us  [on_device(): sums = sums[0] + lax.ppermute(sums[1], 'layer', [(0, 1), (1, 0)])]
    unnamed x4 -> x8, local copies, waits for them, and re-layouts: 0.77 us -> 2.48 us
    all_to_all x1, blocking collectives: 23.4 us -> 25 us  [on_device(): sums = lax.all_to_all(sums, 'row', 0, 0, tiled=True)]
    pallas_call x4 -> x5, Pallas kernels: 10 us -> 10.2 us  [contract(): pl.pallas_call(kernel, out_shape=jax.ShapeDtypeStruct((2, blocks, ij, LAN...]
  transfers between devices with their start and end apart: 10 -> 10, of which waited for: 3 -> 5; matrix products, arithmetic and copies ran while one was open for 2% -> 1% of each run, Pallas kernels for 8% -> 8%
where the time goes in v3:
time: 120 us; the launch traced here: 119 us
  blocking collectives  68.7 us (57%)
  waiting for transfers between devices  18.9 us (16%)
  starting transfers between devices  15.1 us (13%)
  Pallas kernels  11.6 us (10%)
  local copies, waits for them, and re-layouts  3.44 us (3%)
    all_to_all x1, blocking collectives, on_device(): parts = lax.all_to_all(parts, 'row', 0, 0, tiled=True)  28.2 us
    all_to_all x1, blocking collectives, on_device(): sums = lax.all_to_all(sums, 'row', 0, 0, tiled=True)  25 us
    ppermute x9, waiting for transfers between devices, send(): return lax.ppermute(share, 'col', [(i, to(i)) for i in range(cols)])  17.4 us
    all_to_all x1, blocking collectives, on_device(): parts = lax.all_to_all(parts, 'col', 0, 0, tiled=True)  15.5 us
    pallas_call x5, Pallas kernels, contract(): pl.pallas_call(kernel, out_shape=jax.ShapeDtypeStruct((2, blocks, ij, LAN...  10.2 us
    ppermute x1, starting transfers between devices, on_device(): sums = sums[0] + lax.ppermute(sums[1], 'layer', [(0, 1), (1, 0)])  7.93 us
    ppermute x9, starting transfers between devices, send(): return lax.ppermute(share, 'col', [(i, to(i)) for i in range(cols)])  7.15 us
    unnamed x8, local copies, waits for them, and re-layouts  2.48 us
  transfers between devices with their start and end apart: 10, of which 5 were waited for; matrix products, arithmetic and copies ran while one was open for 1% of the time, Pallas kernels for 8%

profile of v3, /device:TPU:1, one launch (start us, length us, event | category | flops | bytes accessed | tf_op | source)
XLA Modules:
  0.0 118.7 jit_solution(17315180441622695307)
XLA Ops:
  0.0 0.0 copy-start.1
  0.0 1.0 copy-done.1
  1.0 0.0 copy-start.2
  1.0 0.7 copy-done.2
  1.7 0.0 copy-start
  1.7 0.6 shard_map.37
  2.4 15.5 %all_to_all.15 = f32[8,144,128]{2,1,0:T(8,128)S(1)} all-to-all(f32[8,144,128]{2,1,0:T(8,128)S(1)} %shard_map.37), channel_id=1, replica_groups=mesh['row'=16,'col'=8,'layer'=2] {'col'}, dimensions={0} | all-to-all | bytes 1179648 | tf_op jit(solution)/shard_map/all_to_all | solution.py:179
  17.8 28.2 %all_to_all.16 = f32[16,72,128]{2,1,0:T(8,128)S(1)} all-to-all(f32[16,72,128]{2,1,0:T(8,128)S(1)} %bitcast.25), channel_id=1, replica_groups=mesh['row'=16,'col'=8,'layer'=2] {'row'}, dimensions={0} | all-to-all | bytes 1179648 | tf_op jit(solution)/shard_map/all_to_all | solution.py:181
  46.1 0.0 copy-start.3
  46.1 0.8 copy-done.3
  46.9 0.8 collective-permute-start.2
  47.7 0.6 collective-permute-start.1
  48.4 0.0 collective-permute-start
  48.4 0.0 copy-done
  48.4 0.7 shard_map.38.refs_2_
  49.1 0.1 pad_add_fusion.refs_0_
  49.2 0.8 slice.24
  50.0 1.6 %shard_map.39.refs_6_ = f32[2,16,64,128]{3,2,1,0:T(8,128)S(1)} custom-call(s32[2]{0:T(128)S(1)} %pad_add_fusion.refs_0_, s32[16,16]{1,0:T(8,128)S(1)} %convert_bitcast_fusion.refs_1_, bf16[64,128,128]{2,1,0:T(8,128)(2,1)S(1)} %shard_map.38.refs_2_, f32[1024,128]{1,0:T(8,128)S(1)} %bitcast.22), custom_call_target="tpu_custom_call" | custom-call | flops 268435456 | bytes 2621440 | tf_op jit(solution)/shard_map/pallas_call | solution.py:151
  51.6 4.7 %collective-permute-done.2.refs_5_ = f32[1024,128]{1,0:T(8,128)S(1)} collective-permute-done((f32[1024,128]{1,0:T(8,128)S(1)}, f32[1024,128]{1,0:T(8,128)S(1)}, u32[]{:S(2)}, u32[]{:S(2)}) %collective-permute-start.2) | collective-permute-done | bytes 524320 | tf_op jit(solution)/shard_map/ppermute | solution.py:186
  56.3 1.8 %collective-permute-done.1.refs_4_ = f32[1024,128]{1,0:T(8,128)S(1)} collective-permute-done((f32[1024,128]{1,0:T(8,128)S(1)}, f32[1024,128]{1,0:T(8,128)S(1)}, u32[]{:S(2)}, u32[]{:S(2)}) %collective-permute-start.1) | collective-permute-done | bytes 524320 | tf_op jit(solution)/shard_map/ppermute | solution.py:186
  58.1 0.0 collective-permute-done.refs_3_
  58.1 1.2 collective-permute-start.8
  59.3 0.3 collective-permute-start.7
  59.6 0.1 collective-permute-start.3
  59.7 2.7 %collective-permute-start.4 = (f32[512,128]{1,0:T(8,128)S(1)}, f32[512,128]{1,0:T(8,128)S(1)}, u32[]{:S(2)}, u32[]{:S(2)}) collective-permute-start(f32[512,128]{1,0:T(8,128)S(1)} %slice.21), channel_id=1, source_target_pairs={{0,12},{2,14},{4,0},{6,2},{8,4},{10,6},{12,8},{14,10},{1,13},{3,15... | collective-permute-start | bytes 786440 | tf_op jit(solution)/shard_map/ppermute | solution.py:186
  62.3 3.0 %shard_map.40.refs_5_ = f32[2,16,64,128]{3,2,1,0:T(8,128)S(1)} custom-call(s32[2]{0:T(128)S(1)} %pad_add_fusion.refs_0_, s32[16,16]{1,0:T(8,128)S(1)} %convert_bitcast_fusion.refs_1_, bf16[64,128,128]{2,1,0:T(8,128)(2,1)S(1)} %shard_map.38.refs_2_, f32[1024,128]{1,0:T(8,128)S(1)} %collective-permute-done.refs_3_, ...), custom_call_target="tpu_custom_call", output_to_operand_aliasing={{}: (6, {})} | custom-call | flops 805306368 | bytes 3670016 | tf_op jit(solution)/shard_map/pallas_call | solution.py:151
  65.4 8.4 %collective-permute-done.3.refs_3_ = f32[512,128]{1,0:T(8,128)S(1)} collective-permute-done((f32[512,128]{1,0:T(8,128)S(1)}, f32[512,128]{1,0:T(8,128)S(1)}, u32[]{:S(2)}, u32[]{:S(2)}) %collective-permute-start.3) | collective-permute-done | bytes 262176 | tf_op jit(solution)/shard_map/ppermute | solution.py:186
  73.7 0.0 collective-permute-done.4.refs_4_
  73.7 0.0 collective-permute-start.5
  73.7 1.5 %collective-permute-start.6 = (f32[512,128]{1,0:T(8,128)S(1)}, f32[512,128]{1,0:T(8,128)S(1)}, u32[]{:S(2)}, u32[]{:S(2)}) collective-permute-start(f32[512,128]{1,0:T(8,128)S(1)} %collective-permute-done.4.refs_4_), channel_id=1, source_target_pairs={{0,2},{2,0},{4,6},{6,4},{8,10},{10,8},{12,14},{14,12},{1,3},{3,1},... | collective-permute-start | bytes 786440 | tf_op jit(solution)/shard_map/ppermute | solution.py:186
  75.2 1.6 %shard_map.41.refs_5_ = f32[2,16,64,128]{3,2,1,0:T(8,128)S(1)} custom-call(s32[2]{0:T(128)S(1)} %pad_add_fusion.refs_0_, s32[16,16]{1,0:T(8,128)S(1)} %convert_bitcast_fusion.refs_1_, bf16[64,128,128]{2,1,0:T(8,128)(2,1)S(1)} %shard_map.38.refs_2_, f32[512,128]{1,0:T(8,128)S(1)} %collective-permute-done.3.refs_3_, ...), custom_call_target="tpu_custom_call", output_to_operand_aliasing={{}: (5, {})} | custom-call | flops 536870912 | bytes 3145728 | tf_op jit(solution)/shard_map/pallas_call | solution.py:151
  76.9 0.0 collective-permute-done.8.refs_4_
  76.9 0.0 collective-permute-done.7.refs_3_
  76.9 2.3 %shard_map.42.refs_5_ = f32[2,16,64,128]{3,2,1,0:T(8,128)S(1)} custom-call(s32[2]{0:T(128)S(1)} %pad_add_fusion.refs_0_, s32[16,16]{1,0:T(8,128)S(1)} %convert_bitcast_fusion.refs_1_, bf16[64,128,128]{2,1,0:T(8,128)(2,1)S(1)} %shard_map.38.refs_2_, f32[1024,128]{1,0:T(8,128)S(1)} %collective-permute-done.7.refs_3_, ...), custom_call_target="tpu_custom_call", output_to_operand_aliasing={{}: (5, {})} | custom-call | flops 536870912 | bytes 3145728 | tf_op jit(solution)/shard_map/pallas_call | solution.py:151
  79.2 0.0 collective-permute-done.5.refs_3_
  79.3 2.5 %collective-permute-done.6.refs_4_ = f32[512,128]{1,0:T(8,128)S(1)} collective-permute-done((f32[512,128]{1,0:T(8,128)S(1)}, f32[512,128]{1,0:T(8,128)S(1)}, u32[]{:S(2)}, u32[]{:S(2)}) %collective-permute-start.6) | collective-permute-done | bytes 262176 | tf_op jit(solution)/shard_map/ppermute | solution.py:186
  81.8 1.6 %shard_map.43 = f32[2,16,64,128]{3,2,1,0:T(8,128)S(1)} custom-call(s32[2]{0:T(128)S(1)} %pad_add_fusion.refs_0_, s32[16,16]{1,0:T(8,128)S(1)} %convert_bitcast_fusion.refs_1_, bf16[64,128,128]{2,1,0:T(8,128)(2,1)S(1)} %shard_map.38.refs_2_, f32[512,128]{1,0:T(8,128)S(1)} %collective-permute-done.5.refs_3_, ...), custom_call_target="tpu_custom_call", output_to_operand_aliasing={{}: (5, {})} | custom-call | flops 536870912 | bytes 3145728 | tf_op jit(solution)/shard_map/pallas_call | solution.py:151
  83.5 7.9 %collective-permute-start.9 = (f32[16,64,128]{2,1,0:T(8,128)S(1)}, f32[16,64,128]{2,1,0:T(8,128)S(1)}, u32[]{:S(2)}, u32[]{:S(2)}) collective-permute-start(f32[16,64,128]{2,1,0:T(8,128)S(1)} %slice_bitcast_fusion), channel_id=1, source_target_pairs={{0,1},{1,0},{2,3},{3,2},{4,5},{5,4},{6,7},{7,6},{8,9},{9,8},{10,11... | collective-permute-start | bytes 1572872 | tf_op jit(solution)/shard_map/ppermute | solution.py:219
  91.4 1.5 %collective-permute-done.9 = f32[16,64,128]{2,1,0:T(8,128)S(1)} collective-permute-done((f32[16,64,128]{2,1,0:T(8,128)S(1)}, f32[16,64,128]{2,1,0:T(8,128)S(1)}, u32[]{:S(2)}, u32[]{:S(2)}) %collective-permute-start.9) | collective-permute-done | bytes 524320 | tf_op jit(solution)/shard_map/ppermute | solution.py:219
  92.9 0.1 fusion
  93.0 25.0 %all_to_all.17 = f32[16,64,128]{2,1,0:T(8,128)S(1)} all-to-all(f32[16,64,128]{2,1,0:T(8,128)S(1)} %fusion), channel_id=1, replica_groups=mesh['row'=16,'col'=8,'layer'=2] {'row'}, dimensions={0} | all-to-all | bytes 1048576 | tf_op jit(solution)/shard_map/all_to_all | solution.py:220
  118.0 0.6 reduce_sum.9
  (5 shorter events, 0.1 us)
Async XLA Ops:
  0.0 1.0 copy-start.1
  1.0 0.7 copy-start.2
  1.7 46.7 %copy-start = (f32[64,4096]{1,0:T(8,128)S(1)}, f32[64,4096]{1,0:T(8,128)}, u32[]{:S(2)}) copy-start(f32[64,4096]{1,0:T(8,128)} %t_ref.1) | copy-start | bytes 3145732
  46.1 0.8 copy-start.3
  46.9 9.4 %collective-permute-start.2 = (f32[1024,128]{1,0:T(8,128)S(1)}, f32[1024,128]{1,0:T(8,128)S(1)}, u32[]{:S(2)}, u32[]{:S(2)}) collective-permute-start(f32[1024,128]{1,0:T(8,128)S(1)} %bitcast.19), channel_id=1, source_target_pairs={{0,12},{2,14},{4,0},{6,2},{8,4},{10,6},{12,8},{14,10},{1,13},{3,15... | collective-permute-start | bytes 1572872 | tf_op jit(solution)/shard_map/ppermute | solution.py:186
  47.7 10.3 %collective-permute-start.1 = (f32[1024,128]{1,0:T(8,128)S(1)}, f32[1024,128]{1,0:T(8,128)S(1)}, u32[]{:S(2)}, u32[]{:S(2)}) collective-permute-start(f32[1024,128]{1,0:T(8,128)S(1)} %bitcast.20), channel_id=1, source_target_pairs={{0,4},{2,6},{4,8},{6,10},{8,12},{10,14},{12,0},{14,2},{1,5},{3,7},... | collective-permute-start | bytes 1572872 | tf_op jit(solution)/shard_map/ppermute | solution.py:186
  48.4 9.7 %collective-permute-start = (f32[1024,128]{1,0:T(8,128)S(1)}, f32[1024,128]{1,0:T(8,128)S(1)}, u32[]{:S(2)}, u32[]{:S(2)}) collective-permute-start(f32[1024,128]{1,0:T(8,128)S(1)} %bitcast.21), channel_id=1, source_target_pairs={{0,2},{2,0},{4,6},{6,4},{8,10},{10,8},{12,14},{14,12},{1,3},{3,1},... | collective-permute-start | bytes 1572872 | tf_op jit(solution)/shard_map/ppermute | solution.py:186
  58.1 18.8 %collective-permute-start.8 = (f32[1024,128]{1,0:T(8,128)S(1)}, f32[1024,128]{1,0:T(8,128)S(1)}, u32[]{:S(2)}, u32[]{:S(2)}) collective-permute-start(f32[1024,128]{1,0:T(8,128)S(1)} %collective-permute-done.refs_3_), channel_id=1, source_target_pairs={{0,12},{2,14},{4,0},{6,2},{8,4},{10,6},{12,8},{14,10},{1,13},{3,15... | collective-permute-start | bytes 1572872 | tf_op jit(solution)/shard_map/ppermute | solution.py:186
  59.3 17.6 %collective-permute-start.7 = (f32[1024,128]{1,0:T(8,128)S(1)}, f32[1024,128]{1,0:T(8,128)S(1)}, u32[]{:S(2)}, u32[]{:S(2)}) collective-permute-start(f32[1024,128]{1,0:T(8,128)S(1)} %collective-permute-done.refs_3_), channel_id=1, source_target_pairs={{0,4},{2,6},{4,8},{6,10},{8,12},{10,14},{12,0},{14,2},{1,5},{3,7},... | collective-permute-start | bytes 1572872 | tf_op jit(solution)/shard_map/ppermute | solution.py:186
  59.6 14.1 %collective-permute-start.3 = (f32[512,128]{1,0:T(8,128)S(1)}, f32[512,128]{1,0:T(8,128)S(1)}, u32[]{:S(2)}, u32[]{:S(2)}) collective-permute-start(f32[512,128]{1,0:T(8,128)S(1)} %slice.20), channel_id=1, source_target_pairs={{0,4},{2,6},{4,8},{6,10},{8,12},{10,14},{12,0},{14,2},{1,5},{3,7},... | collective-permute-start | bytes 786440 | tf_op jit(solution)/shard_map/ppermute | solution.py:186
  59.7 14.1 %collective-permute-start.4 = (f32[512,128]{1,0:T(8,128)S(1)}, f32[512,128]{1,0:T(8,128)S(1)}, u32[]{:S(2)}, u32[]{:S(2)}) collective-permute-start(f32[512,128]{1,0:T(8,128)S(1)} %slice.21), channel_id=1, source_target_pairs={{0,12},{2,14},{4,0},{6,2},{8,4},{10,6},{12,8},{14,10},{1,13},{3,15... | collective-permute-start | bytes 786440 | tf_op jit(solution)/shard_map/ppermute | solution.py:186
  73.7 5.5 %collective-permute-start.5 = (f32[512,128]{1,0:T(8,128)S(1)}, f32[512,128]{1,0:T(8,128)S(1)}, u32[]{:S(2)}, u32[]{:S(2)}) collective-permute-start(f32[512,128]{1,0:T(8,128)S(1)} %collective-permute-done.3.refs_3_), channel_id=1, source_target_pairs={{0,2},{2,0},{4,6},{6,4},{8,10},{10,8},{12,14},{14,12},{1,3},{3,1},... | collective-permute-start | bytes 786440 | tf_op jit(solution)/shard_map/ppermute | solution.py:186
  73.7 8.0 %collective-permute-start.6 = (f32[512,128]{1,0:T(8,128)S(1)}, f32[512,128]{1,0:T(8,128)S(1)}, u32[]{:S(2)}, u32[]{:S(2)}) collective-permute-start(f32[512,128]{1,0:T(8,128)S(1)} %collective-permute-done.4.refs_4_), channel_id=1, source_target_pairs={{0,2},{2,0},{4,6},{6,4},{8,10},{10,8},{12,14},{14,12},{1,3},{3,1},... | collective-permute-start | bytes 786440 | tf_op jit(solution)/shard_map/ppermute | solution.py:186
  83.5 9.5 %collective-permute-start.9 = (f32[16,64,128]{2,1,0:T(8,128)S(1)}, f32[16,64,128]{2,1,0:T(8,128)S(1)}, u32[]{:S(2)}, u32[]{:S(2)}) collective-permute-start(f32[16,64,128]{2,1,0:T(8,128)S(1)} %slice_bitcast_fusion), channel_id=1, source_target_pairs={{0,1},{1,0},{2,3},{3,2},{4,5},{5,4},{6,7},{7,6},{8,9},{9,8},{10,11... | collective-permute-start | bytes 1572872 | tf_op jit(solution)/shard_map/ppermute | solution.py:219

commit v4 on v3

--- a/solution.py
+++ b/solution.py
@@ -8,6 +8,7 @@
 TILE = 64
 AB_DEV = 128
 LANES = 128
+GROUP = 4
 HALF = TILE // 2
 VMEM = pl.BlockSpec(memory_space=pltpu.VMEM)
 SMEM = pl.BlockSpec(memory_space=pltpu.SMEM)
@@ -91,39 +92,38 @@
     return jnp.where(ab_pair == 0, rows, none), jnp.where(ab_pair == 1, rows, none)
 
 
-def contract_kernel(sources, fresh, pair, *refs):
-    count = len(sources)
-    starts = [first for first, _, _ in sources]
-    place, spots, t_tiles = refs[:3]
-    shares = refs[3 : 3 + count]
-    if fresh:
-        sums = None
-        out, lhs, rhs = refs[3 + count :]
-    else:
-        sums, out, lhs, rhs = refs[3 + count :]
+def contract_kernel(sources, offsets, fresh, pair, group, *refs):
+    count, blocks_held = len(sources), len(offsets)
+    place, spots = refs[:2]
+    t_tiles = refs[2 : 2 + blocks_held]
+    shares = refs[2 + blocks_held : 2 + blocks_held + count]
+    rest = refs[2 + blocks_held + count :]
+    sums = None if fresh else rest[0]
+    out, lhs, rhs = rest[-3:]
     layer = place[1]
-    ij = out.shape[2]
+    blocks, ij = out.shape[1:3]
     rows = pair * HALF
     cols = spots.shape[1] // pair
     columns = [((place[0] + shift) & (cols - 1)) ^ flip for _, shift, flip in sources]
-    blocks = out.shape[1]
+    members = [place[2] ^ offset for offset in offsets]
     for block in range(blocks):
         used = [
             n for n in range(count)
-            if starts[n] <= block < starts[n] + shares[n].shape[0] // rows
+            if sources[n][0] <= block < sources[n][0] + shares[n].shape[0] // (group * rows)
         ]
         buffer = block % 2
-        width = len(used) * pair * LANES
-        for m, n in enumerate(used):
-            base = (block - starts[n]) * rows
-            for p in range(pair):
-                spot = spots[block, columns[n] * pair + p]
-                at = (m * pair + p) * LANES
-                lhs[buffer, :, at : at + LANES] = t_tiles[jnp.maximum(spot, 0) >> 2]
-                left, right = slot_rows(shares[n][base + p * HALF : base + (p + 1) * HALF], spot)
-                rhs[buffer, at : at + LANES, :LANES] = left
-                rhs[buffer, at : at + LANES, LANES:] = right
-        total = jnp.dot(lhs[buffer, :, :width], rhs[buffer, :width], preferred_element_type=jnp.float32)
+        at = 0
+        for n in used:
+            for held in range(blocks_held):
+                first = pl.multiple_of(((block - sources[n][0]) * group + members[held]) * rows, rows)
+                for p in range(pair):
+                    spot = spots[block * group + members[held], columns[n] * pair + p]
+                    lhs[buffer, :, at : at + LANES] = t_tiles[held][jnp.maximum(spot, 0) >> 2]
+                    left, right = slot_rows(shares[n][pl.ds(first + p * HALF, HALF), :], spot)
+                    rhs[buffer, at : at + LANES, :LANES] = left
+                    rhs[buffer, at : at + LANES, LANES:] = right
+                    at += LANES
+        total = jnp.dot(lhs[buffer, :, :at], rhs[buffer, :at], preferred_element_type=jnp.float32)
         total = total[:ij] + total[ij:]
         mine = total[:, :LANES]
         other = total[:, LANES:]
@@ -134,19 +134,21 @@
         out[1 - layer, block] = other
 
 
-def contract(sums, t_tiles, spots, place, shares, pair):
-    blocks = spots.shape[0]
-    ij = t_tiles.shape[1] // 2
+def contract(sums, place, spots, held, shares, pair):
+    group = GROUP
+    blocks = spots.shape[0] // group
+    ij = next(iter(held.values())).shape[1] // 2
     sources = tuple(source for source, _ in shares)
-    depth = len(shares) * pair * LANES
-    given = [place, spots, t_tiles, *(share for _, share in shares)]
-    specs = [SMEM, SMEM] + [VMEM] * (1 + len(shares))
+    offsets = tuple(held)
+    depth = len(shares) * len(held) * pair * LANES
+    given = [place, spots, *held.values(), *(share for _, share in shares)]
+    specs = [SMEM, SMEM] + [VMEM] * (len(given) - 2)
     if sums is not None:
         given.append(sums)
         specs.append(VMEM)
 
     def kernel(*refs):
-        contract_kernel(sources, sums is None, pair, *refs)
+        contract_kernel(sources, offsets, sums is None, pair, group, *refs)
 
     return pl.pallas_call(
         kernel,
@@ -158,7 +160,7 @@
             pltpu.VMEM((2, depth, 2 * LANES), jnp.bfloat16),
         ],
         input_output_aliases={} if sums is None else {len(given) - 1: 0},
-        compiler_params=pltpu.CompilerParams(vmem_limit_bytes=32 * 2**20),
+        compiler_params=pltpu.CompilerParams(vmem_limit_bytes=40 * 2**20),
         cost_estimate=pl.CostEstimate(
             flops=2 * blocks * 2 * ij * depth * 2 * LANES,
             bytes_accessed=(len(shares) + 4) * 2**19,
@@ -169,21 +171,30 @@
 
 def on_device(t_amps, v_tiles, v_where):
     cols = lax.axis_size("col")
-    blocks = lax.axis_size("row")
+    rows_axis = lax.axis_size("row")
     held, slots = v_tiles.shape[0], v_tiles.shape[3]
     pair = slots // cols
     rows = pair * HALF
-    place = jnp.stack([lax.axis_index("col"), lax.axis_index("layer")])
+    blocks = rows_axis // GROUP
+    across_m = [[GROUP * m + member for m in range(blocks)] for member in range(GROUP)]
+    place = jnp.stack([lax.axis_index("col"), lax.axis_index("layer"), lax.axis_index("row") % GROUP])
+
+    def send(share, to, axis="col", size=cols):
+        return lax.ppermute(share, axis, [(i, to(i)) for i in range(size)])
+
+    def send_t(t_block, offset):
+        return send(t_block, lambda i: i ^ offset, "row", rows_axis)
+
+    t_two = send_t(t_amps, 2)
+    t_one = send_t(t_amps, 1)
 
     parts = pack(v_tiles, v_where, cols)
     parts = lax.all_to_all(parts, "col", 0, 0, tiled=True)
-    parts = parts.reshape(held * cols, rows + 8, LANES)
-    parts = lax.all_to_all(parts, "row", 0, 0, tiled=True)
+    parts = parts.reshape(blocks, GROUP * (rows + 8), LANES)
+    parts = lax.all_to_all(parts, "row", 0, 0, tiled=True, axis_index_groups=across_m)
+    parts = parts.reshape(blocks * GROUP, rows + 8, LANES)
     spots = parts[:, rows, :slots].astype(jnp.int32)
-    own = parts[:, :rows].reshape(blocks * rows, LANES)
-
-    def send(share, to):
-        return lax.ppermute(share, "col", [(i, to(i)) for i in range(cols)])
+    own = parts[:, :rows].reshape(blocks * GROUP * rows, LANES)
 
     def up(i):
         return (i + 2) % cols
@@ -194,30 +205,37 @@
     def across(i):
         return i ^ 1
 
-    t_tiles = prepare(t_amps)
-
-    def add(sums, *shares):
-        return contract(sums, t_tiles, spots, place, shares, pair)
-
-    half, middle = blocks * rows // 2, blocks // 2
+    def add(sums, held, *shares):
+        return contract(sums, place, spots, held, shares, pair)
+
+    half, middle = own.shape[0] // 2, blocks // 2
     partner = send(own, across)
     below = send(own, up)
     above = send(own, down)
-    sums = add(None, ((0, 0, 0), own))
-    sums, partner, below, above = lax.optimization_barrier((sums, partner, below, above))
+    tiles = {0: prepare(t_amps), 2: prepare(t_two)}
+    sums = add(None, tiles, ((0, 0, 0), own))
+    t_three = send_t(t_one, 2)
+    far_low = send(below[:half], up)
+    far_high = send(above[half:], down)
     partner_below = send(partner, up)
     partner_above = send(partner, down)
-    far_low = send(below[:half], up)
-    far_high = send(above[half:], down)
-    sums = add(sums, ((0, 0, 1), partner), ((0, -2, 0), below), ((0, 2, 0), above))
-    sums, far_low, far_high = lax.optimization_barrier((sums, far_low, far_high))
+    sums = add(sums, tiles, ((0, 0, 1), partner), ((0, -2, 0), below), ((0, 2, 0), above))
     partner_far_low = send(far_low, across)
     partner_far_high = send(far_high, across)
-    sums = add(sums, ((0, 4, 0), far_low), ((middle, 4, 0), far_high))
-    sums = add(sums, ((0, -2, 1), partner_below), ((0, 2, 1), partner_above))
-    sums = add(sums, ((0, 4, 1), partner_far_low), ((middle, 4, 1), partner_far_high))
+    one = {1: prepare(t_one)}
+    here = [((0, 0, 0), own), ((0, 0, 1), partner), ((0, -2, 0), below), ((0, 2, 0), above)]
+    far = [((0, 4, 0), far_low), ((middle, 4, 0), far_high)]
+    beside = [((0, -2, 1), partner_below), ((0, 2, 1), partner_above)]
+    last = [((0, 4, 1), partner_far_low), ((middle, 4, 1), partner_far_high)]
+    sums = add(sums, one, *here)
+    three = {**tiles, **one}
+    sums = add(sums, three, *far)
+    sums = add(sums, three, *beside)
+    sums = add(sums, three, *last)
+    sums = add(sums, {3: prepare(t_three)}, *here, *far, *beside, *last)
+
     sums = sums[0] + lax.ppermute(sums[1], "layer", [(0, 1), (1, 0)])
-    sums = lax.all_to_all(sums, "row", 0, 0, tiled=True)
+    sums = lax.all_to_all(sums, "row", 0, 0, tiled=True, axis_index_groups=across_m)
     return jnp.sum(sums, axis=0)
 
 

time: 120 us -> 114 us (0.950)
  blocking collectives: 68.7 us -> 13.2 us
  waiting for transfers between devices: 18.9 us -> 40.7 us
  starting transfers between devices: 15.1 us -> 32 us
  Pallas kernels: 11.6 us -> 20.9 us
  local copies, waits for them, and re-layouts: 3.44 us -> 4.94 us
    all_to_all x3 -> x1, blocking collectives: 68.7 us -> 13.2 us  [on_device(): lax.all_to_all(sums, 'row', 0, 0, tiled=True, axis_index_groups=across_m)]
    all_to_all x0 -> x2, waiting for transfers between devices: none -> 16.7 us  [the longest x1 9.77 us: on_device(): lax.all_to_all(parts, 'row', 0, 0, tiled=True, axis_index_groups=across_m)]
    all_to_all x0 -> x2, starting transfers between devices: none -> 14.6 us  [the longest x1 8.64 us: on_device(): lax.all_to_all(parts, 'row', 0, 0, tiled=True, axis_index_groups=across_m)]
    ppermute x9 -> x12, starting transfers between devices: 7.15 us -> 13.7 us  [send(): return lax.ppermute(share, axis, [(i, to(i)) for i in range(size)])]
    pallas_call x1 -> x4, Pallas kernels: 0.7 us -> 6.46 us  [prepare(): pl.pallas_call(prepare_kernel, out_shape=jax.ShapeDtypeStruct((cd // TILE...]
    ppermute x9 -> x12, waiting for transfers between devices: 17.4 us -> 23 us  [send(): return lax.ppermute(share, axis, [(i, to(i)) for i in range(size)])]
    ppermute x1, starting transfers between devices: 7.93 us -> 3.74 us  [on_device(): sums = sums[0] + lax.ppermute(sums[1], 'layer', [(0, 1), (1, 0)])]
    pallas_call x5 -> x7, Pallas kernels: 10.2 us -> 12.9 us  [contract(): pl.pallas_call(kernel, out_shape=jax.ShapeDtypeStruct((2, blocks, ij, LAN...]
  transfers between devices with their start and end apart: 10 -> 15, of which waited for: 5 -> 7; matrix products, arithmetic and copies ran while one was open for 1% -> 2% of each run, Pallas kernels for 8% -> 13%
where the time goes in v4:
time: 114 us; the launch traced here: 113 us
  waiting for transfers between devices  40.7 us (36%)
  starting transfers between devices  32 us (28%)
  Pallas kernels  20.9 us (18%)
  blocking collectives  13.2 us (12%)
  local copies, waits for them, and re-layouts  4.94 us (4%)
    ppermute x12, waiting for transfers between devices, send(): return lax.ppermute(share, axis, [(i, to(i)) for i in range(size)])  23 us
    ppermute x12, starting transfers between devices, send(): return lax.ppermute(share, axis, [(i, to(i)) for i in range(size)])  13.7 us
    all_to_all x1, blocking collectives, on_device(): lax.all_to_all(sums, 'row', 0, 0, tiled=True, axis_index_groups=across_m)  13.2 us
    pallas_call x7, Pallas kernels, contract(): pl.pallas_call(kernel, out_shape=jax.ShapeDtypeStruct((2, blocks, ij, LAN...  12.9 us
    all_to_all x1, waiting for transfers between devices, on_device(): lax.all_to_all(parts, 'row', 0, 0, tiled=True, axis_index_groups=across_m)  9.77 us
    all_to_all x1, starting transfers between devices, on_device(): lax.all_to_all(parts, 'row', 0, 0, tiled=True, axis_index_groups=across_m)  8.64 us
    all_to_all x1, waiting for transfers between devices, on_device(): parts = lax.all_to_all(parts, 'col', 0, 0, tiled=True)  6.97 us
    pallas_call x4, Pallas kernels, prepare(): pl.pallas_call(prepare_kernel, out_shape=jax.ShapeDtypeStruct((cd // TILE...  6.46 us
  transfers between devices with their start and end apart: 15, of which 7 were waited for; matrix products, arithmetic and copies ran while one was open for 2% of the time, Pallas kernels for 13%

profile of v4, /device:TPU:1, one launch (start us, length us, event | category | flops | bytes accessed | tf_op | source)
XLA Modules:
  0.0 112.6 jit_solution(13229459349878118885)
XLA Ops:
  0.0 0.0 copy-start
  0.0 0.0 copy-start.1
  0.0 1.1 %copy-done.1 = f32[2,1,1,16,4096]{4,3,2,1,0:T(8,128)S(1)} copy-done((f32[2,1,1,16,4096]{4,3,2,1,0:T(8,128)S(1)}, f32[2,1,1,16,4096]{4,3,2,1,0:T(8,128)}, u32[]{:S(2)}) %copy-start.1) | copy-done | bytes 524312
  1.1 0.0 copy-start.2
  1.1 0.7 copy-done.2
  1.8 1.5 %shard_map.37 = f32[8,144,128]{2,1,0:T(8,128)} custom-call(s32[2,16]{1,0:T(2,128)S(1)} %bitcast.28, f32[2,2,256,128]{3,2,1,0:T(8,128)S(1)} %bitcast.27), custom_call_target="tpu_custom_call" | custom-call | bytes 1048576 | tf_op jit(solution)/shard_map/pallas_call | solution.py:44
  3.3 5.9 %all-to-all-start = ((f32[8,144,128]{2,1,0:T(8,128)}), f32[8,144,128]{2,1,0:T(8,128)}, u32[]{:S(2)}, u32[]{:S(2)}) async-start(f32[8,144,128]{2,1,0:T(8,128)} %shard_map.37), calls=%async_computation | async-start | bytes 1179648 | tf_op jit(solution)/shard_map/all_to_all | solution.py:192
  9.2 0.0 copy-done
  9.2 2.5 %collective-permute-start = (f32[64,4096]{1,0:T(8,128)S(1)}, f32[64,4096]{1,0:T(8,128)}, u32[]{:S(2)}, u32[]{:S(2)}) collective-permute-start(f32[64,4096]{1,0:T(8,128)S(1)} %copy-done), channel_id=1, source_target_pairs={{0,16},{16,0},{32,48},{48,32},{64,80},{80,64},{96,112},{112,96},{1... | collective-permute-start | bytes 3145736 | tf_op jit(solution)/shard_map/ppermute | solution.py:183
  11.8 7.0 %all-to-all-done = f32[8,144,128]{2,1,0:T(8,128)} async-done(((f32[8,144,128]{2,1,0:T(8,128)}), f32[8,144,128]{2,1,0:T(8,128)}, u32[]{:S(2)}, u32[]{:S(2)}) %all-to-all-start) | async-done | bytes 589856 | tf_op jit(solution)/shard_map/all_to_all | solution.py:192
  18.7 8.6 %all-to-all-start.1 = ((f32[4,288,128]{2,1,0:T(8,128)}), f32[4,288,128]{2,1,0:T(8,128)S(1)}, u32[]{:S(2)}, u32[]{:S(2)}) async-start(f32[4,288,128]{2,1,0:T(8,128)} %bitcast.7), calls=%async_computation.1 | async-start | bytes 1179648 | tf_op jit(solution)/shard_map/all_to_all | solution.py:194
  27.4 0.7 collective-permute-start.11
  28.1 9.8 %all-to-all-done.1 = f32[4,288,128]{2,1,0:T(8,128)S(1)} async-done(((f32[4,288,128]{2,1,0:T(8,128)}), f32[4,288,128]{2,1,0:T(8,128)S(1)}, u32[]{:S(2)}, u32[]{:S(2)}) %all-to-all-start.1) | async-done | bytes 589856 | tf_op jit(solution)/shard_map/all_to_all | solution.py:194
  37.9 0.0 copy-start.3
  37.9 0.8 copy-done.3
  38.7 0.6 collective-permute-start.4
  39.3 0.9 collective-permute-start.3
  40.2 0.7 collective-permute-done.t_ref
  40.9 1.6 %collective-permute-start.1 = (f32[64,4096]{1,0:T(8,128)}, f32[64,4096]{1,0:T(8,128)}, u32[]{:S(2)}, u32[]{:S(2)}) collective-permute-start(f32[64,4096]{1,0:T(8,128)} %collective-permute-done.t_ref), channel_id=1, source_target_pairs={{0,32},{16,48},{32,0},{48,16},{64,96},{80,112},{96,64},{112,80},{1... | collective-permute-start | bytes 3145736 | tf_op jit(solution)/shard_map/ppermute | solution.py:183
  42.5 1.4 %collective-permute-start.2 = (f32[1024,128]{1,0:T(8,128)S(1)}, f32[1024,128]{1,0:T(8,128)S(1)}, u32[]{:S(2)}, u32[]{:S(2)}) collective-permute-start(f32[1024,128]{1,0:T(8,128)S(1)} %bitcast.23), channel_id=1, source_target_pairs={{0,2},{2,0},{4,6},{6,4},{8,10},{10,8},{12,14},{14,12},{1,3},{3,1},... | collective-permute-start | bytes 1572872 | tf_op jit(solution)/shard_map/ppermute | solution.py:183
  43.9 3.2 %collective-permute-done.4.refs_6_ = f32[1024,128]{1,0:T(8,128)S(1)} collective-permute-done((f32[1024,128]{1,0:T(8,128)S(1)}, f32[1024,128]{1,0:T(8,128)S(1)}, u32[]{:S(2)}, u32[]{:S(2)}) %collective-permute-start.4) | collective-permute-done | bytes 524320 | tf_op jit(solution)/shard_map/ppermute | solution.py:183
  47.1 0.7 slice.27
  47.9 1.7 %collective-permute-start.6 = (f32[512,128]{1,0:T(8,128)}, f32[512,128]{1,0:T(8,128)S(1)}, u32[]{:S(2)}, u32[]{:S(2)}) collective-permute-start(f32[512,128]{1,0:T(8,128)} %slice.27), channel_id=1, source_target_pairs={{0,12},{2,14},{4,0},{6,2},{8,4},{10,6},{12,8},{14,10},{1,13},{3,15... | collective-permute-start | bytes 786440 | tf_op jit(solution)/shard_map/ppermute | solution.py:183
  49.6 0.0 collective-permute-done.3.refs_5_
  49.6 0.7 slice.26
  50.3 0.0 collective-permute-start.5
  50.3 0.7 shard_map.39.refs_2_
  51.0 0.0 collective-permute-done.2.refs_4_
  51.0 1.3 %collective-permute-start.7 = (f32[1024,128]{1,0:T(8,128)S(1)}, f32[1024,128]{1,0:T(8,128)S(1)}, u32[]{:S(2)}, u32[]{:S(2)}) collective-permute-start(f32[1024,128]{1,0:T(8,128)S(1)} %collective-permute-done.2.refs_4_), channel_id=1, source_target_pairs={{0,4},{2,6},{4,8},{6,10},{8,12},{10,14},{12,0},{14,2},{1,5},{3,7},... | collective-permute-start | bytes 1572872 | tf_op jit(solution)/shard_map/ppermute | solution.py:183
  52.3 9.2 %collective-permute-done.11.t_ref = f32[64,4096]{1,0:T(8,128)} collective-permute-done((f32[64,4096]{1,0:T(8,128)S(1)}, f32[64,4096]{1,0:T(8,128)}, u32[]{:S(2)}, u32[]{:S(2)}) %collective-permute-start.11) | collective-permute-done | bytes 1048608 | tf_op jit(solution)/shard_map/ppermute | solution.py:183
  61.6 0.6 collective-permute-start.8
  62.2 0.1 pad_add_fusion.refs_0_
  62.2 1.9 %shard_map.41.refs_2_.refs_4_ = bf16[64,128,128]{2,1,0:T(8,128)(2,1)S(1)} custom-call(f32[64,4096]{1,0:T(8,128)} %collective-permute-done.t_ref), custom_call_target="tpu_custom_call" | custom-call | flops 268435456 | bytes 3145728 | tf_op jit(solution)/shard_map/pallas_call | solution.py:70
  64.2 1.9 %shard_map.40.refs_3_ = bf16[64,128,128]{2,1,0:T(8,128)(2,1)S(1)} custom-call(f32[64,4096]{1,0:T(8,128)} %collective-permute-done.11.t_ref), custom_call_target="tpu_custom_call" | custom-call | flops 268435456 | bytes 3145728 | tf_op jit(solution)/shard_map/pallas_call | solution.py:70
  66.1 0.8 slice.24
  66.9 0.0 collective-permute-done.6.refs_6_.refs_8_
  66.9 2.1 %collective-permute-start.10 = (f32[512,128]{1,0:T(8,128)S(1)}, f32[512,128]{1,0:T(8,128)S(1)}, u32[]{:S(2)}, u32[]{:S(2)}) collective-permute-start(f32[512,128]{1,0:T(8,128)S(1)} %collective-permute-done.6.refs_6_.refs_8_), channel_id=1, source_target_pairs={{0,2},{2,0},{4,6},{6,4},{8,10},{10,8},{12,14},{14,12},{1,3},{3,1},... | collective-permute-start | bytes 786440 | tf_op jit(solution)/shard_map/ppermute | solution.py:183
  69.0 0.0 collective-permute-done.5.refs_5_.refs_7_
  69.0 0.3 collective-permute-start.9
  69.3 1.2 %shard_map.42.refs_7_ = f32[2,4,64,128]{3,2,1,0:T(8,128)S(1)} custom-call(s32[3]{0:T(128)S(1)} %pad_add_fusion.refs_0_, s32[16,16]{1,0:T(8,128)S(1)} %convert_bitcast_fusion.refs_1_, bf16[64,128,128]{2,1,0:T(8,128)(2,1)S(1)} %shard_map.39.refs_2_, bf16[64,128,128]{2,1,0:T(8,128)(2,1)S(1)} %shard_map.40.refs_3_, f32[1024,128]{1,0:T(8,128)S(1)} %bitcast.24), custom_call_target="tpu_custom_call" | custom-call | flops 134217728 | bytes 2621440 | tf_op jit(solution)/shard_map/pallas_call | solution.py:153
  70.6 2.0 %shard_map.43.refs_7_ = f32[2,4,64,128]{3,2,1,0:T(8,128)S(1)} custom-call(s32[3]{0:T(128)S(1)} %pad_add_fusion.refs_0_, s32[16,16]{1,0:T(8,128)S(1)} %convert_bitcast_fusion.refs_1_, bf16[64,128,128]{2,1,0:T(8,128)(2,1)S(1)} %shard_map.39.refs_2_, bf16[64,128,128]{2,1,0:T(8,128)(2,1)S(1)} %shard_map.40.refs_3_, ...), custom_call_target="tpu_custom_call", output_to_operand_aliasing={{}: (7, {})} | custom-call | flops 402653184 | bytes 3670016 | tf_op jit(solution)/shard_map/pallas_call | solution.py:153
  72.6 1.6 %shard_map.44.refs_7_ = f32[2,4,64,128]{3,2,1,0:T(8,128)S(1)} custom-call(s32[3]{0:T(128)S(1)} %pad_add_fusion.refs_0_, s32[16,16]{1,0:T(8,128)S(1)} %convert_bitcast_fusion.refs_1_, bf16[64,128,128]{2,1,0:T(8,128)(2,1)S(1)} %shard_map.41.refs_2_.refs_4_, f32[1024,128]{1,0:T(8,128)S(1)} %bitcast.25, ...), custom_call_target="tpu_custom_call", output_to_operand_aliasing={{}: (7, {})} | custom-call | flops 268435456 | bytes 4194304 | tf_op jit(solution)/shard_map/pallas_call | solution.py:153
  74.3 9.8 %collective-permute-done.1.t_ref = f32[64,4096]{1,0:T(8,128)} collective-permute-done((f32[64,4096]{1,0:T(8,128)}, f32[64,4096]{1,0:T(8,128)}, u32[]{:S(2)}, u32[]{:S(2)}) %collective-permute-start.1) | collective-permute-done | bytes 1048608 | tf_op jit(solution)/shard_map/ppermute | solution.py:183
  84.1 1.9 %shard_map.38.refs_2_ = bf16[64,128,128]{2,1,0:T(8,128)(2,1)S(1)} custom-call(f32[64,4096]{1,0:T(8,128)} %collective-permute-done.1.t_ref), custom_call_target="tpu_custom_call" | custom-call | flops 268435456 | bytes 3145728 | tf_op jit(solution)/shard_map/pallas_call | solution.py:70
  86.0 1.8 %shard_map.45.refs_7_ = f32[2,4,64,128]{3,2,1,0:T(8,128)S(1)} custom-call(s32[3]{0:T(128)S(1)} %pad_add_fusion.refs_0_, s32[16,16]{1,0:T(8,128)S(1)} %convert_bitcast_fusion.refs_1_, bf16[64,128,128]{2,1,0:T(8,128)(2,1)S(1)} %shard_map.39.refs_2_, bf16[64,128,128]{2,1,0:T(8,128)(2,1)S(1)} %shard_map.40.refs_3_, ...), custom_call_target="tpu_custom_call", output_to_operand_aliasing={{}: (7, {})} | custom-call | flops 402653184 | bytes 3145728 | tf_op jit(solution)/shard_map/pallas_call | solution.py:153
  87.7 0.0 collective-permute-done.7.refs_5_.refs_9_
  87.7 0.0 collective-permute-done.8.refs_6_.refs_10_
  87.8 2.0 %shard_map.46.refs_7_ = f32[2,4,64,128]{3,2,1,0:T(8,128)S(1)} custom-call(s32[3]{0:T(128)S(1)} %pad_add_fusion.refs_0_, s32[16,16]{1,0:T(8,128)S(1)} %convert_bitcast_fusion.refs_1_, bf16[64,128,128]{2,1,0:T(8,128)(2,1)S(1)} %shard_map.39.refs_2_, bf16[64,128,128]{2,1,0:T(8,128)(2,1)S(1)} %shard_map.40.refs_3_, ...), custom_call_target="tpu_custom_call", output_to_operand_aliasing={{}: (7, {})} | custom-call | flops 402653184 | bytes 3145728 | tf_op jit(solution)/shard_map/pallas_call | solution.py:153
  89.8 0.0 collective-permute-done.10.refs_6_.refs_12_
  89.8 0.0 collective-permute-done.9.refs_5_.refs_11_
  89.8 1.5 %shard_map.47.refs_13_ = f32[2,4,64,128]{3,2,1,0:T(8,128)S(1)} custom-call(s32[3]{0:T(128)S(1)} %pad_add_fusion.refs_0_, s32[16,16]{1,0:T(8,128)S(1)} %convert_bitcast_fusion.refs_1_, bf16[64,128,128]{2,1,0:T(8,128)(2,1)S(1)} %shard_map.39.refs_2_, bf16[64,128,128]{2,1,0:T(8,128)(2,1)S(1)} %shard_map.40.refs_3_, ...), custom_call_target="tpu_custom_call", output_to_operand_aliasing={{}: (7, {})} | custom-call | flops 402653184 | bytes 3145728 | tf_op jit(solution)/shard_map/pallas_call | solution.py:153
  91.3 2.7 %shard_map.48 = f32[2,4,64,128]{3,2,1,0:T(8,128)S(1)} custom-call(s32[3]{0:T(128)S(1)} %pad_add_fusion.refs_0_, s32[16,16]{1,0:T(8,128)S(1)} %convert_bitcast_fusion.refs_1_, bf16[64,128,128]{2,1,0:T(8,128)(2,1)S(1)} %shard_map.38.refs_2_, f32[1024,128]{1,0:T(8,128)S(1)} %bitcast.26, ...), custom_call_target="tpu_custom_call", output_to_operand_aliasing={{}: (13, {})} | custom-call | flops 671088640 | bytes 7340032 | tf_op jit(solution)/shard_map/pallas_call | solution.py:153
  94.1 3.7 %collective-permute-start.12 = (f32[4,64,128]{2,1,0:T(8,128)S(1)}, f32[4,64,128]{2,1,0:T(8,128)S(1)}, u32[]{:S(2)}, u32[]{:S(2)}) collective-permute-start(f32[4,64,128]{2,1,0:T(8,128)S(1)} %slice_bitcast_fusion), channel_id=1, source_target_pairs={{0,1},{1,0},{2,3},{3,2},{4,5},{5,4},{6,7},{7,6},{8,9},{9,8},{10,11... | collective-permute-start | bytes 393224 | tf_op jit(solution)/shard_map/ppermute | solution.py:237
  97.8 1.0 collective-permute-done.12
  98.8 13.2 %all_to_all.15 = f32[4,64,128]{2,1,0:T(8,128)S(1)} all-to-all(f32[4,64,128]{2,1,0:T(8,128)S(1)} %fusion), channel_id=1, replica_groups={{0,64,128,192},{16,80,144,208},{32,96,160,224},{48,112,176,240},{1,65,1..., dimensions={0} | all-to-all | bytes 262144 | tf_op jit(solution)/shard_map/all_to_all | solution.py:238
  112.0 0.6 reduce_sum.9
  (4 shorter events, 0.1 us)
Async XLA Ops:
  0.0 9.2 %copy-start = (f32[64,4096]{1,0:T(8,128)S(1)}, f32[64,4096]{1,0:T(8,128)}, u32[]{:S(2)}) copy-start(f32[64,4096]{1,0:T(8,128)} %t_ref.1) | copy-start | bytes 3145732
  0.0 1.1 %copy-start.1 = (f32[2,1,1,16,4096]{4,3,2,1,0:T(8,128)S(1)}, f32[2,1,1,16,4096]{4,3,2,1,0:T(8,128)}, u32[]{:S(2)}) copy-start(f32[2,1,1,16,4096]{4,3,2,1,0:T(8,128)} %param.4) | copy-start | bytes 1572868
  1.1 0.7 copy-start.2
  3.3 15.5 %all-to-all-start = ((f32[8,144,128]{2,1,0:T(8,128)}), f32[8,144,128]{2,1,0:T(8,128)}, u32[]{:S(2)}, u32[]{:S(2)}) async-start(f32[8,144,128]{2,1,0:T(8,128)} %shard_map.37), calls=%async_computation | async-start | bytes 1179648 | tf_op jit(solution)/shard_map/all_to_all | solution.py:192
  9.2 31.6 %collective-permute-start = (f32[64,4096]{1,0:T(8,128)S(1)}, f32[64,4096]{1,0:T(8,128)}, u32[]{:S(2)}, u32[]{:S(2)}) collective-permute-start(f32[64,4096]{1,0:T(8,128)S(1)} %copy-done), channel_id=1, source_target_pairs={{0,16},{16,0},{32,48},{48,32},{64,80},{80,64},{96,112},{112,96},{1... | collective-permute-start | bytes 3145736 | tf_op jit(solution)/shard_map/ppermute | solution.py:183
  18.7 19.2 %all-to-all-start.1 = ((f32[4,288,128]{2,1,0:T(8,128)}), f32[4,288,128]{2,1,0:T(8,128)S(1)}, u32[]{:S(2)}, u32[]{:S(2)}) async-start(f32[4,288,128]{2,1,0:T(8,128)} %bitcast.7), calls=%async_computation.1 | async-start | bytes 1179648 | tf_op jit(solution)/shard_map/all_to_all | solution.py:194
  27.4 34.2 %collective-permute-start.11 = (f32[64,4096]{1,0:T(8,128)S(1)}, f32[64,4096]{1,0:T(8,128)}, u32[]{:S(2)}, u32[]{:S(2)}) collective-permute-start(f32[64,4096]{1,0:T(8,128)S(1)} %copy-done), channel_id=1, source_target_pairs={{0,32},{16,48},{32,0},{48,16},{64,96},{80,112},{96,64},{112,80},{1... | collective-permute-start | bytes 3145736 | tf_op jit(solution)/shard_map/ppermute | solution.py:183
  37.9 0.8 copy-start.3
  38.7 8.4 %collective-permute-start.4 = (f32[1024,128]{1,0:T(8,128)S(1)}, f32[1024,128]{1,0:T(8,128)S(1)}, u32[]{:S(2)}, u32[]{:S(2)}) collective-permute-start(f32[1024,128]{1,0:T(8,128)S(1)} %bitcast.21), channel_id=1, source_target_pairs={{0,12},{2,14},{4,0},{6,2},{8,4},{10,6},{12,8},{14,10},{1,13},{3,15... | collective-permute-start | bytes 1572872 | tf_op jit(solution)/shard_map/ppermute | solution.py:183
  39.3 10.3 %collective-permute-start.3 = (f32[1024,128]{1,0:T(8,128)S(1)}, f32[1024,128]{1,0:T(8,128)S(1)}, u32[]{:S(2)}, u32[]{:S(2)}) collective-permute-start(f32[1024,128]{1,0:T(8,128)S(1)} %bitcast.22), channel_id=1, source_target_pairs={{0,4},{2,6},{4,8},{6,10},{8,12},{10,14},{12,0},{14,2},{1,5},{3,7},... | collective-permute-start | bytes 1572872 | tf_op jit(solution)/shard_map/ppermute | solution.py:183
  40.9 43.2 %collective-permute-start.1 = (f32[64,4096]{1,0:T(8,128)}, f32[64,4096]{1,0:T(8,128)}, u32[]{:S(2)}, u32[]{:S(2)}) collective-permute-start(f32[64,4096]{1,0:T(8,128)} %collective-permute-done.t_ref), channel_id=1, source_target_pairs={{0,32},{16,48},{32,0},{48,16},{64,96},{80,112},{96,64},{112,80},{1... | collective-permute-start | bytes 3145736 | tf_op jit(solution)/shard_map/ppermute | solution.py:183
  42.5 8.5 %collective-permute-start.2 = (f32[1024,128]{1,0:T(8,128)S(1)}, f32[1024,128]{1,0:T(8,128)S(1)}, u32[]{:S(2)}, u32[]{:S(2)}) collective-permute-start(f32[1024,128]{1,0:T(8,128)S(1)} %bitcast.23), channel_id=1, source_target_pairs={{0,2},{2,0},{4,6},{6,4},{8,10},{10,8},{12,14},{14,12},{1,3},{3,1},... | collective-permute-start | bytes 1572872 | tf_op jit(solution)/shard_map/ppermute | solution.py:183
  47.9 19.1 %collective-permute-start.6 = (f32[512,128]{1,0:T(8,128)}, f32[512,128]{1,0:T(8,128)S(1)}, u32[]{:S(2)}, u32[]{:S(2)}) collective-permute-start(f32[512,128]{1,0:T(8,128)} %slice.27), channel_id=1, source_target_pairs={{0,12},{2,14},{4,0},{6,2},{8,4},{10,6},{12,8},{14,10},{1,13},{3,15... | collective-permute-start | bytes 786440 | tf_op jit(solution)/shard_map/ppermute | solution.py:183
  50.3 18.7 %collective-permute-start.5 = (f32[512,128]{1,0:T(8,128)}, f32[512,128]{1,0:T(8,128)}, u32[]{:S(2)}, u32[]{:S(2)}) collective-permute-start(f32[512,128]{1,0:T(8,128)} %slice.26), channel_id=1, source_target_pairs={{0,4},{2,6},{4,8},{6,10},{8,12},{10,14},{12,0},{14,2},{1,5},{3,7},... | collective-permute-start | bytes 786440 | tf_op jit(solution)/shard_map/ppermute | solution.py:183
  51.0 36.7 %collective-permute-start.7 = (f32[1024,128]{1,0:T(8,128)S(1)}, f32[1024,128]{1,0:T(8,128)S(1)}, u32[]{:S(2)}, u32[]{:S(2)}) collective-permute-start(f32[1024,128]{1,0:T(8,128)S(1)} %collective-permute-done.2.refs_4_), channel_id=1, source_target_pairs={{0,4},{2,6},{4,8},{6,10},{8,12},{10,14},{12,0},{14,2},{1,5},{3,7},... | collective-permute-start | bytes 1572872 | tf_op jit(solution)/shard_map/ppermute | solution.py:183
  61.6 26.2 %collective-permute-start.8 = (f32[1024,128]{1,0:T(8,128)S(1)}, f32[1024,128]{1,0:T(8,128)S(1)}, u32[]{:S(2)}, u32[]{:S(2)}) collective-permute-start(f32[1024,128]{1,0:T(8,128)S(1)} %collective-permute-done.2.refs_4_), channel_id=1, source_target_pairs={{0,12},{2,14},{4,0},{6,2},{8,4},{10,6},{12,8},{14,10},{1,13},{3,15... | collective-permute-start | bytes 1572872 | tf_op jit(solution)/shard_map/ppermute | solution.py:183
  66.9 22.9 %collective-permute-start.10 = (f32[512,128]{1,0:T(8,128)S(1)}, f32[512,128]{1,0:T(8,128)S(1)}, u32[]{:S(2)}, u32[]{:S(2)}) collective-permute-start(f32[512,128]{1,0:T(8,128)S(1)} %collective-permute-done.6.refs_6_.refs_8_), channel_id=1, source_target_pairs={{0,2},{2,0},{4,6},{6,4},{8,10},{10,8},{12,14},{14,12},{1,3},{3,1},... | collective-permute-start | bytes 786440 | tf_op jit(solution)/shard_map/ppermute | solution.py:183
  69.0 20.8 %collective-permute-start.9 = (f32[512,128]{1,0:T(8,128)}, f32[512,128]{1,0:T(8,128)S(1)}, u32[]{:S(2)}, u32[]{:S(2)}) collective-permute-start(f32[512,128]{1,0:T(8,128)} %collective-permute-done.5.refs_5_.refs_7_), channel_id=1, source_target_pairs={{0,2},{2,0},{4,6},{6,4},{8,10},{10,8},{12,14},{14,12},{1,3},{3,1},... | collective-permute-start | bytes 786440 | tf_op jit(solution)/shard_map/ppermute | solution.py:183
  94.1 4.7 %collective-permute-start.12 = (f32[4,64,128]{2,1,0:T(8,128)S(1)}, f32[4,64,128]{2,1,0:T(8,128)S(1)}, u32[]{:S(2)}, u32[]{:S(2)}) collective-permute-start(f32[4,64,128]{2,1,0:T(8,128)S(1)} %slice_bitcast_fusion), channel_id=1, source_target_pairs={{0,1},{1,0},{2,3},{3,2},{4,5},{5,4},{6,7},{7,6},{8,9},{9,8},{10,11... | collective-permute-start | bytes 393224 | tf_op jit(solution)/shard_map/ppermute | solution.py:237

commit v5 on v4

--- a/solution.py
+++ b/solution.py
@@ -8,7 +8,7 @@
 TILE = 64
 AB_DEV = 128
 LANES = 128
-GROUP = 4
+GROUP = 2
 HALF = TILE // 2
 VMEM = pl.BlockSpec(memory_space=pltpu.VMEM)
 SMEM = pl.BlockSpec(memory_space=pltpu.SMEM)
@@ -185,8 +185,7 @@
     def send_t(t_block, offset):
         return send(t_block, lambda i: i ^ offset, "row", rows_axis)
 
-    t_two = send_t(t_amps, 2)
-    t_one = send_t(t_amps, 1)
+    t_other = send_t(t_amps, 1)
 
     parts = pack(v_tiles, v_where, cols)
     parts = lax.all_to_all(parts, "col", 0, 0, tiled=True)
@@ -212,27 +211,23 @@
     partner = send(own, across)
     below = send(own, up)
     above = send(own, down)
-    tiles = {0: prepare(t_amps), 2: prepare(t_two)}
+    tiles = {0: prepare(t_amps)}
     sums = add(None, tiles, ((0, 0, 0), own))
-    t_three = send_t(t_one, 2)
+    sums, partner = lax.optimization_barrier((sums, partner))
     far_low = send(below[:half], up)
     far_high = send(above[half:], down)
     partner_below = send(partner, up)
     partner_above = send(partner, down)
-    sums = add(sums, tiles, ((0, 0, 1), partner), ((0, -2, 0), below), ((0, 2, 0), above))
+    other = {1: prepare(t_other)}
+    both = {**tiles, **other}
+    sums = add(sums, both, ((0, 0, 1), partner), ((0, -2, 0), below), ((0, 2, 0), above))
+    sums, far_low, far_high = lax.optimization_barrier((sums, far_low, far_high))
     partner_far_low = send(far_low, across)
     partner_far_high = send(far_high, across)
-    one = {1: prepare(t_one)}
-    here = [((0, 0, 0), own), ((0, 0, 1), partner), ((0, -2, 0), below), ((0, 2, 0), above)]
-    far = [((0, 4, 0), far_low), ((middle, 4, 0), far_high)]
-    beside = [((0, -2, 1), partner_below), ((0, 2, 1), partner_above)]
-    last = [((0, 4, 1), partner_far_low), ((middle, 4, 1), partner_far_high)]
-    sums = add(sums, one, *here)
-    three = {**tiles, **one}
-    sums = add(sums, three, *far)
-    sums = add(sums, three, *beside)
-    sums = add(sums, three, *last)
-    sums = add(sums, {3: prepare(t_three)}, *here, *far, *beside, *last)
+    sums = add(sums, other, ((0, 0, 0), own))
+    sums = add(sums, both, ((0, 4, 0), far_low), ((middle, 4, 0), far_high))
+    sums = add(sums, both, ((0, -2, 1), partner_below), ((0, 2, 1), partner_above))
+    sums = add(sums, both, ((0, 4, 1), partner_far_low), ((middle, 4, 1), partner_far_high))
 
     sums = sums[0] + lax.ppermute(sums[1], "layer", [(0, 1), (1, 0)])
     sums = lax.all_to_all(sums, "row", 0, 0, tiled=True, axis_index_groups=across_m)

time: 114 us -> 114 us (level); the launches traced: 113 us -> 114 us
  blocking collectives: 13.2 us -> 32.4 us
  starting transfers between devices: 32 us -> 23.7 us
  Pallas kernels: 20.9 us -> 14.7 us
  waiting for transfers between devices: 40.7 us -> 38.5 us
  local copies, waits for them, and re-layouts: 4.94 us -> 3.56 us
    all_to_all x0 -> x1, blocking collectives: none -> 15.6 us  [on_device(): parts = lax.all_to_all(parts, 'col', 0, 0, tiled=True)]
    all_to_all x1 -> x0, waiting for transfers between devices: 6.97 us -> none  [on_device(): parts = lax.all_to_all(parts, 'col', 0, 0, tiled=True)]
    all_to_all x1 -> x0, starting transfers between devices: 5.95 us -> none  [on_device(): parts = lax.all_to_all(parts, 'col', 0, 0, tiled=True)]
    all_to_all x1, waiting for transfers between devices: 9.77 us -> 14.3 us  [on_device(): lax.all_to_all(parts, 'row', 0, 0, tiled=True, axis_index_groups=across_m)]
    pallas_call x4 -> x2, Pallas kernels: 6.46 us -> 2.63 us  [prepare(): pl.pallas_call(prepare_kernel, out_shape=jax.ShapeDtypeStruct((cd // TILE...]
    all_to_all x1, blocking collectives: 13.2 us -> 16.9 us  [on_device(): lax.all_to_all(sums, 'row', 0, 0, tiled=True, axis_index_groups=across_m)]
    ppermute x12 -> x10, starting transfers between devices: 13.7 us -> 10.2 us  [send(): return lax.ppermute(share, axis, [(i, to(i)) for i in range(size)])]
    ppermute x1, starting transfers between devices: 3.74 us -> 5.31 us  [on_device(): sums = sums[0] + lax.ppermute(sums[1], 'layer', [(0, 1), (1, 0)])]
  transfers between devices with their start and end apart: 15 -> 12, of which waited for: 7 -> 6; matrix products, arithmetic and copies ran while one was open for 2% -> 1% of each run, Pallas kernels for 13% -> 11%
where the time goes in v5:
time: 114 us
  waiting for transfers between devices  38.5 us (34%)
  blocking collectives  32.4 us (28%)
  starting transfers between devices  23.7 us (21%)
  Pallas kernels  14.7 us (13%)
  local copies, waits for them, and re-layouts  3.56 us (3%)
    ppermute x10, waiting for transfers between devices, send(): return lax.ppermute(share, axis, [(i, to(i)) for i in range(size)])  23.1 us
    all_to_all x1, blocking collectives, on_device(): lax.all_to_all(sums, 'row', 0, 0, tiled=True, axis_index_groups=across_m)  16.9 us
    all_to_all x1, blocking collectives, on_device(): parts = lax.all_to_all(parts, 'col', 0, 0, tiled=True)  15.6 us
    all_to_all x1, waiting for transfers between devices, on_device(): lax.all_to_all(parts, 'row', 0, 0, tiled=True, axis_index_groups=across_m)  14.3 us
    pallas_call x6, Pallas kernels, contract(): pl.pallas_call(kernel, out_shape=jax.ShapeDtypeStruct((2, blocks, ij, LAN...  11.4 us
    ppermute x10, starting transfers between devices, send(): return lax.ppermute(share, axis, [(i, to(i)) for i in range(size)])  10.2 us
    all_to_all x1, starting transfers between devices, on_device(): lax.all_to_all(parts, 'row', 0, 0, tiled=True, axis_index_groups=across_m)  8.19 us
    ppermute x1, starting transfers between devices, on_device(): sums = sums[0] + lax.ppermute(sums[1], 'layer', [(0, 1), (1, 0)])  5.31 us
  transfers between devices with their start and end apart: 12, of which 6 were waited for; matrix products, arithmetic and copies ran while one was open for 1% of the time, Pallas kernels for 11%

profile of v5, /device:TPU:1, one launch (start us, length us, event | category | flops | bytes accessed | tf_op | source)
XLA Modules:
  0.0 113.8 jit_solution(10308564156660847580)
XLA Ops:
  0.0 0.0 copy-start
  0.0 0.0 copy-start.1
  0.0 1.1 copy-done.1
  1.1 0.0 copy-start.2
  1.1 0.7 copy-done.2
  1.8 0.6 shard_map.37
  2.5 15.6 %all_to_all.15 = f32[8,144,128]{2,1,0:T(8,128)} all-to-all(f32[8,144,128]{2,1,0:T(8,128)S(1)} %shard_map.37), channel_id=1, replica_groups=mesh['row'=16,'col'=8,'layer'=2] {'col'}, dimensions={0} | all-to-all | bytes 1179648 | tf_op jit(solution)/shard_map/all_to_all | solution.py:191
  18.0 8.2 %all-to-all-start.1 = ((f32[8,144,128]{2,1,0:T(8,128)}), f32[8,144,128]{2,1,0:T(8,128)S(1)}, u32[]{:S(2)}, u32[]{:S(2)}) async-start(f32[8,144,128]{2,1,0:T(8,128)} %all_to_all.15), calls=%async_computation.1 | async-start | bytes 1179648 | tf_op jit(solution)/shard_map/all_to_all | solution.py:193
  26.2 0.0 copy-done
  26.2 2.5 %collective-permute-start = (f32[64,4096]{1,0:T(8,128)S(1)}, f32[64,4096]{1,0:T(8,128)}, u32[]{:S(2)}, u32[]{:S(2)}) collective-permute-start(f32[64,4096]{1,0:T(8,128)S(1)} %copy-done), channel_id=1, source_target_pairs={{0,16},{16,0},{32,48},{48,32},{64,80},{80,64},{96,112},{112,96},{1... | collective-permute-start | bytes 3145736 | tf_op jit(solution)/shard_map/ppermute | solution.py:183
  28.8 14.3 %all-to-all-done.1 = f32[8,144,128]{2,1,0:T(8,128)S(1)} async-done(((f32[8,144,128]{2,1,0:T(8,128)}), f32[8,144,128]{2,1,0:T(8,128)S(1)}, u32[]{:S(2)}, u32[]{:S(2)}) %all-to-all-start.1) | async-done | bytes 589856 | tf_op jit(solution)/shard_map/all_to_all | solution.py:193
  43.0 0.0 copy-start.3
  43.1 0.8 copy-done.3
  43.9 0.6 collective-permute-start.1
  44.5 1.3 %collective-permute-start.3 = (f32[1024,128]{1,0:T(8,128)S(1)}, f32[1024,128]{1,0:T(8,128)S(1)}, u32[]{:S(2)}, u32[]{:S(2)}) collective-permute-start(f32[1024,128]{1,0:T(8,128)S(1)} %bitcast.21), channel_id=1, source_target_pairs={{0,12},{2,14},{4,0},{6,2},{8,4},{10,6},{12,8},{14,10},{1,13},{3,15... | collective-permute-start | bytes 1572872 | tf_op jit(solution)/shard_map/ppermute | solution.py:183
  45.8 0.1 collective-permute-start.2
  45.9 0.7 shard_map.38.refs_2_
  46.6 0.1 pad_add_fusion.refs_0_
  46.7 0.8 slice.24
  47.6 1.2 %shard_map.40.refs_7_ = f32[2,8,64,128]{3,2,1,0:T(8,128)S(1)} custom-call(s32[3]{0:T(128)S(1)} %pad_add_fusion.refs_0_, s32[16,16]{1,0:T(8,128)S(1)} %convert_bitcast_fusion.refs_1_, bf16[64,128,128]{2,1,0:T(8,128)(2,1)S(1)} %shard_map.38.refs_2_, f32[1024,128]{1,0:T(8,128)S(1)} %bitcast.23), custom_call_target="tpu_custom_call" | custom-call | flops 134217728 | bytes 2621440 | tf_op jit(solution)/shard_map/pallas_call | solution.py:153
  48.8 11.9 %collective-permute-done.1.refs_4_ = f32[1024,128]{1,0:T(8,128)S(1)} collective-permute-done((f32[1024,128]{1,0:T(8,128)S(1)}, f32[1024,128]{1,0:T(8,128)S(1)}, u32[]{:S(2)}, u32[]{:S(2)}) %collective-permute-start.1) | collective-permute-done | bytes 524320 | tf_op jit(solution)/shard_map/ppermute | solution.py:183
  60.7 1.3 %collective-permute-start.9 = (f32[1024,128]{1,0:T(8,128)S(1)}, f32[1024,128]{1,0:T(8,128)S(1)}, u32[]{:S(2)}, u32[]{:S(2)}) collective-permute-start(f32[1024,128]{1,0:T(8,128)S(1)} %collective-permute-done.1.refs_4_), channel_id=1, source_target_pairs={{0,12},{2,14},{4,0},{6,2},{8,4},{10,6},{12,8},{14,10},{1,13},{3,15... | collective-permute-start | bytes 1572872 | tf_op jit(solution)/shard_map/ppermute | solution.py:183
  62.1 0.1 collective-permute-start.8
  62.2 0.0 collective-permute-done.3.refs_6_
  62.2 2.6 %collective-permute-start.5 = (f32[512,128]{1,0:T(8,128)S(1)}, f32[512,128]{1,0:T(8,128)S(1)}, u32[]{:S(2)}, u32[]{:S(2)}) collective-permute-start(f32[512,128]{1,0:T(8,128)S(1)} %slice.27), channel_id=1, source_target_pairs={{0,12},{2,14},{4,0},{6,2},{8,4},{10,6},{12,8},{14,10},{1,13},{3,15... | collective-permute-start | bytes 786440 | tf_op jit(solution)/shard_map/ppermute | solution.py:183
  64.8 0.0 collective-permute-done.2.refs_5_
  64.9 0.1 collective-permute-start.4
  65.0 0.0 collective-permute-done.t_ref
  65.0 1.9 %shard_map.39.refs_3_.refs_2_ = bf16[64,128,128]{2,1,0:T(8,128)(2,1)S(1)} custom-call(f32[64,4096]{1,0:T(8,128)} %collective-permute-done.t_ref), custom_call_target="tpu_custom_call" | custom-call | flops 268435456 | bytes 3145728 | tf_op jit(solution)/shard_map/pallas_call | solution.py:70
  66.9 3.1 %shard_map.41.refs_4_ = f32[2,8,64,128]{3,2,1,0:T(8,128)S(1)} custom-call(s32[3]{0:T(128)S(1)} %pad_add_fusion.refs_0_, s32[16,16]{1,0:T(8,128)S(1)} %convert_bitcast_fusion.refs_1_, bf16[64,128,128]{2,1,0:T(8,128)(2,1)S(1)} %shard_map.38.refs_2_, bf16[64,128,128]{2,1,0:T(8,128)(2,1)S(1)} %shard_map.39.refs_3_.refs_2_, ...), custom_call_target="tpu_custom_call", output_to_operand_aliasing={{}: (7, {})} | custom-call | flops 805306368 | bytes 3670016 | tf_op jit(solution)/shard_map/pallas_call | solution.py:153
  70.0 6.4 %collective-permute-done.5.refs_5_ = f32[512,128]{1,0:T(8,128)S(1)} collective-permute-done((f32[512,128]{1,0:T(8,128)S(1)}, f32[512,128]{1,0:T(8,128)S(1)}, u32[]{:S(2)}, u32[]{:S(2)}) %collective-permute-start.5) | collective-permute-done | bytes 262176 | tf_op jit(solution)/shard_map/ppermute | solution.py:183
  76.5 2.5 %collective-permute-done.4.refs_4_ = f32[512,128]{1,0:T(8,128)S(1)} collective-permute-done((f32[512,128]{1,0:T(8,128)S(1)}, f32[512,128]{1,0:T(8,128)S(1)}, u32[]{:S(2)}, u32[]{:S(2)}) %collective-permute-start.4) | collective-permute-done | bytes 262176 | tf_op jit(solution)/shard_map/ppermute | solution.py:183
  78.9 0.5 collective-permute-start.6
  79.5 0.9 collective-permute-start.7
  80.4 1.2 %shard_map.42.refs_6_ = f32[2,8,64,128]{3,2,1,0:T(8,128)S(1)} custom-call(s32[3]{0:T(128)S(1)} %pad_add_fusion.refs_0_, s32[16,16]{1,0:T(8,128)S(1)} %convert_bitcast_fusion.refs_1_, bf16[64,128,128]{2,1,0:T(8,128)(2,1)S(1)} %shard_map.39.refs_3_.refs_2_, f32[1024,128]{1,0:T(8,128)S(1)} %bitcast.24, ...), custom_call_target="tpu_custom_call", output_to_operand_aliasing={{}: (4, {})} | custom-call | flops 134217728 | bytes 2621440 | tf_op jit(solution)/shard_map/pallas_call | solution.py:153
  81.6 1.7 %shard_map.43.refs_6_ = f32[2,8,64,128]{3,2,1,0:T(8,128)S(1)} custom-call(s32[3]{0:T(128)S(1)} %pad_add_fusion.refs_0_, s32[16,16]{1,0:T(8,128)S(1)} %convert_bitcast_fusion.refs_1_, bf16[64,128,128]{2,1,0:T(8,128)(2,1)S(1)} %shard_map.38.refs_2_, bf16[64,128,128]{2,1,0:T(8,128)(2,1)S(1)} %shard_map.39.refs_3_.refs_2_, ...), custom_call_target="tpu_custom_call", output_to_operand_aliasing={{}: (6, {})} | custom-call | flops 536870912 | bytes 3145728 | tf_op jit(solution)/shard_map/pallas_call | solution.py:153
  83.3 0.0 collective-permute-done.9.refs_5_
  83.3 0.0 collective-permute-done.8.refs_4_
  83.3 2.5 %shard_map.44.refs_6_ = f32[2,8,64,128]{3,2,1,0:T(8,128)S(1)} custom-call(s32[3]{0:T(128)S(1)} %pad_add_fusion.refs_0_, s32[16,16]{1,0:T(8,128)S(1)} %convert_bitcast_fusion.refs_1_, bf16[64,128,128]{2,1,0:T(8,128)(2,1)S(1)} %shard_map.38.refs_2_, bf16[64,128,128]{2,1,0:T(8,128)(2,1)S(1)} %shard_map.39.refs_3_.refs_2_, ...), custom_call_target="tpu_custom_call", output_to_operand_aliasing={{}: (6, {})} | custom-call | flops 536870912 | bytes 3145728 | tf_op jit(solution)/shard_map/pallas_call | solution.py:153
  85.8 0.0 collective-permute-done.6.refs_4_
  85.8 2.2 %collective-permute-done.7.refs_5_ = f32[512,128]{1,0:T(8,128)S(1)} collective-permute-done((f32[512,128]{1,0:T(8,128)S(1)}, f32[512,128]{1,0:T(8,128)S(1)}, u32[]{:S(2)}, u32[]{:S(2)}) %collective-permute-start.7) | collective-permute-done | bytes 262176 | tf_op jit(solution)/shard_map/ppermute | solution.py:183
  88.1 1.7 %shard_map.45 = f32[2,8,64,128]{3,2,1,0:T(8,128)S(1)} custom-call(s32[3]{0:T(128)S(1)} %pad_add_fusion.refs_0_, s32[16,16]{1,0:T(8,128)S(1)} %convert_bitcast_fusion.refs_1_, bf16[64,128,128]{2,1,0:T(8,128)(2,1)S(1)} %shard_map.38.refs_2_, bf16[64,128,128]{2,1,0:T(8,128)(2,1)S(1)} %shard_map.39.refs_3_.refs_2_, ...), custom_call_target="tpu_custom_call", output_to_operand_aliasing={{}: (6, {})} | custom-call | flops 536870912 | bytes 3145728 | tf_op jit(solution)/shard_map/pallas_call | solution.py:153
  89.8 5.3 %collective-permute-start.10 = (f32[8,64,128]{2,1,0:T(8,128)S(1)}, f32[8,64,128]{2,1,0:T(8,128)S(1)}, u32[]{:S(2)}, u32[]{:S(2)}) collective-permute-start(f32[8,64,128]{2,1,0:T(8,128)S(1)} %slice_bitcast_fusion), channel_id=1, source_target_pairs={{0,1},{1,0},{2,3},{3,2},{4,5},{5,4},{6,7},{7,6},{8,9},{9,8},{10,11... | collective-permute-start | bytes 786440 | tf_op jit(solution)/shard_map/ppermute | solution.py:232
  95.1 1.2 %collective-permute-done.10 = f32[8,64,128]{2,1,0:T(8,128)S(1)} collective-permute-done((f32[8,64,128]{2,1,0:T(8,128)S(1)}, f32[8,64,128]{2,1,0:T(8,128)S(1)}, u32[]{:S(2)}, u32[]{:S(2)}) %collective-permute-start.10) | collective-permute-done | bytes 262176 | tf_op jit(solution)/shard_map/ppermute | solution.py:232
  96.3 16.9 %all_to_all.16 = f32[8,64,128]{2,1,0:T(8,128)S(1)} all-to-all(f32[8,64,128]{2,1,0:T(8,128)S(1)} %fusion), channel_id=1, replica_groups={{0,32,64,96,128,160,192,224},{16,48,80,112,144,176,208,240},{1,33,65,97..., dimensions={0} | all-to-all | bytes 524288 | tf_op jit(solution)/shard_map/all_to_all | solution.py:233
  113.1 0.6 reduce_sum.9
  (6 shorter events, 0.1 us)
Async XLA Ops:
  0.0 26.2 %copy-start = (f32[64,4096]{1,0:T(8,128)S(1)}, f32[64,4096]{1,0:T(8,128)}, u32[]{:S(2)}) copy-start(f32[64,4096]{1,0:T(8,128)} %t_ref.1) | copy-start | bytes 3145732
  0.0 1.1 copy-start.1
  1.1 0.7 copy-start.2
  18.0 25.0 %all-to-all-start.1 = ((f32[8,144,128]{2,1,0:T(8,128)}), f32[8,144,128]{2,1,0:T(8,128)S(1)}, u32[]{:S(2)}, u32[]{:S(2)}) async-start(f32[8,144,128]{2,1,0:T(8,128)} %all_to_all.15), calls=%async_computation.1 | async-start | bytes 1179648 | tf_op jit(solution)/shard_map/all_to_all | solution.py:193
  26.2 38.7 %collective-permute-start = (f32[64,4096]{1,0:T(8,128)S(1)}, f32[64,4096]{1,0:T(8,128)}, u32[]{:S(2)}, u32[]{:S(2)}) collective-permute-start(f32[64,4096]{1,0:T(8,128)S(1)} %copy-done), channel_id=1, source_target_pairs={{0,16},{16,0},{32,48},{48,32},{64,80},{80,64},{96,112},{112,96},{1... | collective-permute-start | bytes 3145736 | tf_op jit(solution)/shard_map/ppermute | solution.py:183
  43.0 0.9 copy-start.3
  43.9 16.8 %collective-permute-start.1 = (f32[1024,128]{1,0:T(8,128)S(1)}, f32[1024,128]{1,0:T(8,128)S(1)}, u32[]{:S(2)}, u32[]{:S(2)}) collective-permute-start(f32[1024,128]{1,0:T(8,128)S(1)} %bitcast.20), channel_id=1, source_target_pairs={{0,2},{2,0},{4,6},{6,4},{8,10},{10,8},{12,14},{14,12},{1,3},{3,1},... | collective-permute-start | bytes 1572872 | tf_op jit(solution)/shard_map/ppermute | solution.py:183
  44.5 17.7 %collective-permute-start.3 = (f32[1024,128]{1,0:T(8,128)S(1)}, f32[1024,128]{1,0:T(8,128)S(1)}, u32[]{:S(2)}, u32[]{:S(2)}) collective-permute-start(f32[1024,128]{1,0:T(8,128)S(1)} %bitcast.21), channel_id=1, source_target_pairs={{0,12},{2,14},{4,0},{6,2},{8,4},{10,6},{12,8},{14,10},{1,13},{3,15... | collective-permute-start | bytes 1572872 | tf_op jit(solution)/shard_map/ppermute | solution.py:183
  45.8 19.0 %collective-permute-start.2 = (f32[1024,128]{1,0:T(8,128)S(1)}, f32[1024,128]{1,0:T(8,128)S(1)}, u32[]{:S(2)}, u32[]{:S(2)}) collective-permute-start(f32[1024,128]{1,0:T(8,128)S(1)} %bitcast.22), channel_id=1, source_target_pairs={{0,4},{2,6},{4,8},{6,10},{8,12},{10,14},{12,0},{14,2},{1,5},{3,7},... | collective-permute-start | bytes 1572872 | tf_op jit(solution)/shard_map/ppermute | solution.py:183
  60.7 22.6 %collective-permute-start.9 = (f32[1024,128]{1,0:T(8,128)S(1)}, f32[1024,128]{1,0:T(8,128)S(1)}, u32[]{:S(2)}, u32[]{:S(2)}) collective-permute-start(f32[1024,128]{1,0:T(8,128)S(1)} %collective-permute-done.1.refs_4_), channel_id=1, source_target_pairs={{0,12},{2,14},{4,0},{6,2},{8,4},{10,6},{12,8},{14,10},{1,13},{3,15... | collective-permute-start | bytes 1572872 | tf_op jit(solution)/shard_map/ppermute | solution.py:183
  62.1 21.3 %collective-permute-start.8 = (f32[1024,128]{1,0:T(8,128)S(1)}, f32[1024,128]{1,0:T(8,128)S(1)}, u32[]{:S(2)}, u32[]{:S(2)}) collective-permute-start(f32[1024,128]{1,0:T(8,128)S(1)} %collective-permute-done.1.refs_4_), channel_id=1, source_target_pairs={{0,4},{2,6},{4,8},{6,10},{8,12},{10,14},{12,0},{14,2},{1,5},{3,7},... | collective-permute-start | bytes 1572872 | tf_op jit(solution)/shard_map/ppermute | solution.py:183
  62.2 14.3 %collective-permute-start.5 = (f32[512,128]{1,0:T(8,128)S(1)}, f32[512,128]{1,0:T(8,128)S(1)}, u32[]{:S(2)}, u32[]{:S(2)}) collective-permute-start(f32[512,128]{1,0:T(8,128)S(1)} %slice.27), channel_id=1, source_target_pairs={{0,12},{2,14},{4,0},{6,2},{8,4},{10,6},{12,8},{14,10},{1,13},{3,15... | collective-permute-start | bytes 786440 | tf_op jit(solution)/shard_map/ppermute | solution.py:183
  64.9 14.1 %collective-permute-start.4 = (f32[512,128]{1,0:T(8,128)S(1)}, f32[512,128]{1,0:T(8,128)S(1)}, u32[]{:S(2)}, u32[]{:S(2)}) collective-permute-start(f32[512,128]{1,0:T(8,128)S(1)} %slice.26), channel_id=1, source_target_pairs={{0,4},{2,6},{4,8},{6,10},{8,12},{10,14},{12,0},{14,2},{1,5},{3,7},... | collective-permute-start | bytes 786440 | tf_op jit(solution)/shard_map/ppermute | solution.py:183
  78.9 6.9 %collective-permute-start.6 = (f32[512,128]{1,0:T(8,128)S(1)}, f32[512,128]{1,0:T(8,128)S(1)}, u32[]{:S(2)}, u32[]{:S(2)}) collective-permute-start(f32[512,128]{1,0:T(8,128)S(1)} %collective-permute-done.4.refs_4_), channel_id=1, source_target_pairs={{0,2},{2,0},{4,6},{6,4},{8,10},{10,8},{12,14},{14,12},{1,3},{3,1},... | collective-permute-start | bytes 786440 | tf_op jit(solution)/shard_map/ppermute | solution.py:183
  79.5 8.6 %collective-permute-start.7 = (f32[512,128]{1,0:T(8,128)S(1)}, f32[512,128]{1,0:T(8,128)S(1)}, u32[]{:S(2)}, u32[]{:S(2)}) collective-permute-start(f32[512,128]{1,0:T(8,128)S(1)} %collective-permute-done.5.refs_5_), channel_id=1, source_target_pairs={{0,2},{2,0},{4,6},{6,4},{8,10},{10,8},{12,14},{14,12},{1,3},{3,1},... | collective-permute-start | bytes 786440 | tf_op jit(solution)/shard_map/ppermute | solution.py:183
  89.8 6.5 %collective-permute-start.10 = (f32[8,64,128]{2,1,0:T(8,128)S(1)}, f32[8,64,128]{2,1,0:T(8,128)S(1)}, u32[]{:S(2)}, u32[]{:S(2)}) collective-permute-start(f32[8,64,128]{2,1,0:T(8,128)S(1)} %slice_bitcast_fusion), channel_id=1, source_target_pairs={{0,1},{1,0},{2,3},{3,2},{4,5},{5,4},{6,7},{7,6},{8,9},{9,8},{10,11... | collective-permute-start | bytes 786440 | tf_op jit(solution)/shard_map/ppermute | solution.py:232

commit v6 on v5

--- a/solution.py
+++ b/solution.py
@@ -46,35 +46,35 @@
         out_shape=jax.ShapeDtypeStruct((cols, held * (slots // cols * HALF + 8), LANES), jnp.float32),
         in_specs=[SMEM, VMEM],
         out_specs=VMEM,
-        compiler_params=pltpu.CompilerParams(vmem_limit_bytes=16 * 2**20),
+        compiler_params=pltpu.CompilerParams(vmem_limit_bytes=14 * 2**20),
         cost_estimate=pl.CostEstimate(flops=0, bytes_accessed=2**20, transcendentals=0),
     )(v_where.reshape(held, slots), lists)
 
 
-def prepare_kernel(t_ref, t_tiles):
+def prepare_kernel(*refs):
+    *halves, t_tiles = refs
     row = lax.broadcasted_iota(jnp.int32, (LANES, 2 * LANES), 0)
     col = lax.broadcasted_iota(jnp.int32, (LANES, 2 * LANES), 1)
     source = (col // LANES) * TILE + 2 * (col % HALF) + (col % TILE) // HALF
     pick = (row == source).astype(jnp.bfloat16)
-    for at in range(t_ref.shape[1] // LANES):
-        hi, lo = split_rows(t_ref[:, at * LANES : (at + 1) * LANES])
-        both = jnp.dot(
-            jnp.concatenate([hi, lo], axis=0), pick, preferred_element_type=jnp.float32
-        ).astype(jnp.bfloat16)
+    for at in range(halves[0].shape[1] // LANES):
+        split = [split_rows(half[:, at * LANES : (at + 1) * LANES]) for half in halves]
+        rows = jnp.concatenate([hi for hi, _ in split] + [lo for _, lo in split], axis=0)
+        both = jnp.dot(rows, pick, preferred_element_type=jnp.float32).astype(jnp.bfloat16)
         t_tiles[2 * at] = both[:, :LANES]
         t_tiles[2 * at + 1] = both[:, LANES:]
 
 
-def prepare(t_block):
-    ij, cd = t_block.shape
+def prepare(*halves):
+    ij, cd = sum(half.shape[0] for half in halves), halves[0].shape[1]
     return pl.pallas_call(
         prepare_kernel,
         out_shape=jax.ShapeDtypeStruct((cd // TILE, 2 * ij, LANES), jnp.bfloat16),
-        in_specs=[VMEM],
+        in_specs=[VMEM] * len(halves),
         out_specs=VMEM,
-        compiler_params=pltpu.CompilerParams(vmem_limit_bytes=32 * 2**20),
+        compiler_params=pltpu.CompilerParams(vmem_limit_bytes=14 * 2**20),
         cost_estimate=pl.CostEstimate(flops=2 * 2 * ij * cd * 2 * LANES, bytes_accessed=3 * 2**20, transcendentals=0),
-    )(t_block)
+    )(*halves)
 
 
 def slot_rows(v, spot):
@@ -160,7 +160,7 @@
             pltpu.VMEM((2, depth, 2 * LANES), jnp.bfloat16),
         ],
         input_output_aliases={} if sums is None else {len(given) - 1: 0},
-        compiler_params=pltpu.CompilerParams(vmem_limit_bytes=40 * 2**20),
+        compiler_params=pltpu.CompilerParams(vmem_limit_bytes=14 * 2**20),
         cost_estimate=pl.CostEstimate(
             flops=2 * blocks * 2 * ij * depth * 2 * LANES,
             bytes_accessed=(len(shares) + 4) * 2**19,
@@ -176,24 +176,27 @@
     pair = slots // cols
     rows = pair * HALF
     blocks = rows_axis // GROUP
-    across_m = [[GROUP * m + member for m in range(blocks)] for member in range(GROUP)]
-    place = jnp.stack([lax.axis_index("col"), lax.axis_index("layer"), lax.axis_index("row") % GROUP])
+    ranks = [[2 * (GROUP * m + member) + x for m in range(blocks // 2) for x in range(2)] for member in range(GROUP)]
+    place = jnp.stack([lax.axis_index("col"), lax.axis_index("layer"), lax.axis_index("row") // 2 % GROUP])
 
     def send(share, to, axis="col", size=cols):
         return lax.ppermute(share, axis, [(i, to(i)) for i in range(size)])
 
-    def send_t(t_block, offset):
-        return send(t_block, lambda i: i ^ offset, "row", rows_axis)
-
-    t_other = send_t(t_amps, 1)
-
+    def send_t(t_block):
+        return send(t_block, lambda i: i ^ 2, "row", rows_axis)
+
+    ij_half = t_amps.shape[0] // 2
+    t_first = send_t(t_amps[:ij_half])
     parts = pack(v_tiles, v_where, cols)
     parts = lax.all_to_all(parts, "col", 0, 0, tiled=True)
+    parts, t_first = lax.optimization_barrier((parts, t_first))
+    parts = parts.reshape(blocks // 2, GROUP, 2, rows + 8, LANES).transpose(0, 2, 1, 3, 4)
     parts = parts.reshape(blocks, GROUP * (rows + 8), LANES)
-    parts = lax.all_to_all(parts, "row", 0, 0, tiled=True, axis_index_groups=across_m)
+    parts = lax.all_to_all(parts, "row", 0, 0, tiled=True, axis_index_groups=ranks)
     parts = parts.reshape(blocks * GROUP, rows + 8, LANES)
     spots = parts[:, rows, :slots].astype(jnp.int32)
     own = parts[:, :rows].reshape(blocks * GROUP * rows, LANES)
+    own, t_rest = lax.optimization_barrier((own, t_amps[ij_half:]))
 
     def up(i):
         return (i + 2) % cols
@@ -211,26 +214,25 @@
     partner = send(own, across)
     below = send(own, up)
     above = send(own, down)
+    t_rest = send_t(t_rest)
     tiles = {0: prepare(t_amps)}
-    sums = add(None, tiles, ((0, 0, 0), own))
-    sums, partner = lax.optimization_barrier((sums, partner))
     far_low = send(below[:half], up)
     far_high = send(above[half:], down)
     partner_below = send(partner, up)
     partner_above = send(partner, down)
-    other = {1: prepare(t_other)}
-    both = {**tiles, **other}
-    sums = add(sums, both, ((0, 0, 1), partner), ((0, -2, 0), below), ((0, 2, 0), above))
-    sums, far_low, far_high = lax.optimization_barrier((sums, far_low, far_high))
     partner_far_low = send(far_low, across)
     partner_far_high = send(far_high, across)
-    sums = add(sums, other, ((0, 0, 0), own))
+    near = [((0, 0, 0), own), ((0, 0, 1), partner), ((0, -2, 0), below), ((0, 2, 0), above)]
+    sums = add(None, tiles, *near)
+    other = {1: prepare(t_first, t_rest)}
+    sums = add(sums, other, *near)
+    both = {**tiles, **other}
     sums = add(sums, both, ((0, 4, 0), far_low), ((middle, 4, 0), far_high))
     sums = add(sums, both, ((0, -2, 1), partner_below), ((0, 2, 1), partner_above))
     sums = add(sums, both, ((0, 4, 1), partner_far_low), ((middle, 4, 1), partner_far_high))
 
     sums = sums[0] + lax.ppermute(sums[1], "layer", [(0, 1), (1, 0)])
-    sums = lax.all_to_all(sums, "row", 0, 0, tiled=True, axis_index_groups=across_m)
+    sums = lax.all_to_all(sums, "row", 0, 0, tiled=True, axis_index_groups=ranks)
     return jnp.sum(sums, axis=0)
 
 

time: 114 us -> 108 us (0.947); the launches traced: 114 us -> 106 us
  waiting for transfers between devices: 38.5 us -> 9.6 us
  blocking collectives: 32.4 us -> 54 us
  starting transfers between devices: 23.7 us -> 19.8 us
  local copies, waits for them, and re-layouts: 3.56 us -> 6.48 us
    all_to_all x1 -> x2, blocking collectives: 16.9 us -> 39.5 us  [the longest x1 26.2 us: on_device(): lax.all_to_all(parts, 'row', 0, 0, tiled=True, axis_index_groups=ranks)]
    ppermute x10 -> x11, waiting for transfers between devices: 23.1 us -> 8.44 us  [send(): return lax.ppermute(share, axis, [(i, to(i)) for i in range(size)])]
    all_to_all x1 -> x0, waiting for transfers between devices: 14.3 us -> none  [on_device(): lax.all_to_all(parts, 'row', 0, 0, tiled=True, axis_index_groups=across_m)]
    all_to_all x1 -> x0, starting transfers between devices: 8.19 us -> none  [on_device(): lax.all_to_all(parts, 'row', 0, 0, tiled=True, axis_index_groups=across_m)]
    ppermute x1, starting transfers between devices: 5.31 us -> 9.5 us  [on_device(): sums = sums[0] + lax.ppermute(sums[1], 'layer', [(0, 1), (1, 0)])]
    slice x0 -> x1, local copies, waits for them, and re-layouts: none -> 2.13 us  [on_device(): own, t_rest = lax.optimization_barrier((own, t_amps[ij_half:]))]
    pallas_call x6 -> x5, Pallas kernels: 11.4 us -> 12.2 us  [contract(): pl.pallas_call(kernel, out_shape=jax.ShapeDtypeStruct((2, blocks, ij, LAN...]
    unnamed x8 -> x16, local copies, waits for them, and re-layouts: 2.61 us -> 1.84 us
  transfers between devices with their start and end apart: 12 -> 12, of which waited for: 6 -> 3; matrix products, arithmetic and copies ran while one was open for 1% -> 2% of each run, Pallas kernels for 11% -> 13%
where the time goes in v6:
time: 108 us; the launch traced here: 106 us
  blocking collectives  54 us (50%)
  starting transfers between devices  19.8 us (18%)
  Pallas kernels  15.3 us (14%)
  waiting for transfers between devices  9.6 us (9%)
  local copies, waits for them, and re-layouts  6.48 us (6%)
    all_to_all x1, blocking collectives, on_device(): lax.all_to_all(parts, 'row', 0, 0, tiled=True, axis_index_groups=ranks)  26.2 us
    all_to_all x1, blocking collectives, on_device(): parts = lax.all_to_all(parts, 'col', 0, 0, tiled=True)  14.5 us
    all_to_all x1, blocking collectives, on_device(): lax.all_to_all(sums, 'row', 0, 0, tiled=True, axis_index_groups=ranks)  13.3 us
    pallas_call x5, Pallas kernels, contract(): pl.pallas_call(kernel, out_shape=jax.ShapeDtypeStruct((2, blocks, ij, LAN...  12.2 us
    ppermute x11, starting transfers between devices, send(): return lax.ppermute(share, axis, [(i, to(i)) for i in range(size)])  10.3 us
    ppermute x1, starting transfers between devices, on_device(): sums = sums[0] + lax.ppermute(sums[1], 'layer', [(0, 1), (1, 0)])  9.5 us
    ppermute x11, waiting for transfers between devices, send(): return lax.ppermute(share, axis, [(i, to(i)) for i in range(size)])  8.44 us
    pallas_call x2, Pallas kernels, prepare(): pl.pallas_call(prepare_kernel, out_shape=jax.ShapeDtypeStruct((cd // TILE...  2.45 us
  transfers between devices with their start and end apart: 12, of which 3 were waited for; matrix products, arithmetic and copies ran while one was open for 2% of the time, Pallas kernels for 13%

profile of v6, /device:TPU:1, one launch (start us, length us, event | category | flops | bytes accessed | tf_op | source)
XLA Modules:
  0.0 106.1 jit_solution(7887350103115396309)
XLA Ops:
  0.0 0.0 copy-start.6
  0.0 0.0 copy-start.3
  0.0 2.1 %fusion.1 = (f32[32,4096]{1,0:T(8,128)}, f32[32,4096]{1,0:T(8,128)S(1)}) fusion(f32[64,4096]{1,0:T(8,128)} %refs_0_.1), kind=kLoop, calls=%fused_computation.5 | loop fusion | bytes 2097152 | tf_op jit(solution)/shard_map/slice | solution.py:199
  2.1 2.5 %collective-permute-start = (f32[32,4096]{1,0:T(8,128)S(1)}, f32[32,4096]{1,0:T(8,128)S(1)}, u32[]{:S(2)}, u32[]{:S(2)}) collective-permute-start(f32[32,4096]{1,0:T(8,128)S(1)} %get-tuple-element.14), channel_id=1, source_target_pairs={{0,32},{16,48},{32,0},{48,16},{64,96},{80,112},{96,64},{112,80},{1... | collective-permute-start | bytes 1572872 | tf_op jit(solution)/shard_map/ppermute | solution.py:183
  4.6 0.0 copy-done.6
  4.6 0.0 copy-done.3
  4.6 0.6 shard_map.37
  5.3 14.5 %all_to_all.15 = f32[8,144,128]{2,1,0:T(8,128)S(1)} all-to-all(f32[8,144,128]{2,1,0:T(8,128)S(1)} %shard_map.37), channel_id=1, replica_groups=mesh['row'=16,'col'=8,'layer'=2] {'col'}, dimensions={0} | all-to-all | bytes 1179648 | tf_op jit(solution)/shard_map/all_to_all | solution.py:191
  19.8 0.0 collective-permute-done.refs_0_
  19.8 0.0 copy-start.4
  19.8 0.0 copy-start
  19.8 26.2 %all_to_all.16 = f32[8,144,128]{2,1,0:T(8,128)S(1)} all-to-all(f32[8,144,128]{2,1,0:T(8,128)S(1)} %bitcast.32), channel_id=1, replica_groups={{0,16,64,80,128,144,192,208},{32,48,96,112,160,176,224,240},{1,17,65,81..., dimensions={0} | all-to-all | bytes 1179648 | tf_op jit(solution)/shard_map/all_to_all | solution.py:195
  46.0 0.0 copy-start.7
  46.1 0.8 copy-done.7
  46.9 0.0 collective-permute-start.2
  46.9 2.7 %collective-permute-start.5 = (f32[1024,128]{1,0:T(8,128)S(1)}, f32[1024,128]{1,0:T(8,128)S(1)}, u32[]{:S(2)}, u32[]{:S(2)}) collective-permute-start(f32[1024,128]{1,0:T(8,128)S(1)} %bitcast.25), channel_id=1, source_target_pairs={{0,12},{2,14},{4,0},{6,2},{8,4},{10,6},{12,8},{14,10},{1,13},{3,15... | collective-permute-start | bytes 1572872 | tf_op jit(solution)/shard_map/ppermute | solution.py:183
  49.5 0.0 collective-permute-start.8
  49.5 0.0 collective-permute-start.1
  49.5 8.0 %collective-permute-done.2.refs_5_ = f32[1024,128]{1,0:T(8,128)S(1)} collective-permute-done((f32[1024,128]{1,0:T(8,128)S(1)}, f32[1024,128]{1,0:T(8,128)S(1)}, u32[]{:S(2)}, u32[]{:S(2)}) %collective-permute-start.2) | collective-permute-done | bytes 524320 | tf_op jit(solution)/shard_map/ppermute | solution.py:183
  57.5 0.7 slice.34
  58.3 0.0 collective-permute-start.3
  58.3 0.0 collective-permute-done.5.refs_6_
  58.3 0.0 copy-start.1
  58.3 0.8 slice.35
  59.1 0.0 copy-done.4
  59.1 2.7 %collective-permute-start.6 = (f32[512,128]{1,0:T(8,128)}, f32[512,128]{1,0:T(8,128)}, u32[]{:S(2)}, u32[]{:S(2)}) collective-permute-start(f32[512,128]{1,0:T(8,128)} %slice.35), channel_id=1, source_target_pairs={{0,12},{2,14},{4,0},{6,2},{8,4},{10,6},{12,8},{14,10},{1,13},{3,15... | collective-permute-start | bytes 786440 | tf_op jit(solution)/shard_map/ppermute | solution.py:183
  61.7 0.0 collective-permute-done.8.refs_4_
  61.8 0.1 collective-permute-start.10
  61.8 0.0 copy-done.1
  61.8 1.4 %collective-permute-start.9 = (f32[1024,128]{1,0:T(8,128)}, f32[1024,128]{1,0:T(8,128)}, u32[]{:S(2)}, u32[]{:S(2)}) collective-permute-start(f32[1024,128]{1,0:T(8,128)} %collective-permute-done.8.refs_4_), channel_id=1, source_target_pairs={{0,4},{2,6},{4,8},{6,10},{8,12},{10,14},{12,0},{14,2},{1,5},{3,7},... | collective-permute-start | bytes 1572872 | tf_op jit(solution)/shard_map/ppermute | solution.py:183
  63.2 0.0 copy-done
  63.2 0.7 shard_map.38.refs_2_
  64.0 0.0 copy-start.2
  64.0 0.1 pad_add_fusion.refs_0_
  64.1 0.9 slice.32
  64.9 0.0 collective-permute-done.3.refs_4_
  65.0 0.0 collective-permute-start.4
  65.0 0.4 collective-permute-done.6.refs_5_
  65.4 1.0 collective-permute-start.7
  66.4 0.0 collective-permute-done.1.refs_1_
  66.4 0.0 copy-start.5
  66.4 1.0 copy-done.5
  67.5 1.7 %shard_map.39.refs_2_.refs_3_ = bf16[64,128,128]{2,1,0:T(8,128)(2,1)S(1)} custom-call(f32[32,4096]{1,0:T(8,128)S(1)} %copy-done.5, f32[32,4096]{1,0:T(8,128)} %collective-permute-done.1.refs_1_), custom_call_target="tpu_custom_call" | custom-call | flops 268435456 | bytes 3145728 | tf_op jit(solution)/shard_map/pallas_call | solution.py:70
  69.2 0.0 copy-done.2
  69.2 2.7 %shard_map.40.refs_7_ = f32[2,8,64,128]{3,2,1,0:T(8,128)S(1)} custom-call(s32[3]{0:T(128)S(1)} %pad_add_fusion.refs_0_, s32[16,16]{1,0:T(8,128)S(1)} %convert_bitcast_fusion.refs_1_, bf16[64,128,128]{2,1,0:T(8,128)(2,1)S(1)} %shard_map.38.refs_2_, f32[1024,128]{1,0:T(8,128)S(1)} %bitcast.27, f32[1024,128]{1,0:T(8,128)} %collective-permute-done.8.refs_4_, ...), custom_call_target="tpu_custom_call" | custom-call | flops 536870912 | bytes 4194304 | tf_op jit(solution)/shard_map/pallas_call | solution.py:153
  72.0 2.9 %shard_map.41.refs_6_ = f32[2,8,64,128]{3,2,1,0:T(8,128)S(1)} custom-call(s32[3]{0:T(128)S(1)} %pad_add_fusion.refs_0_, s32[16,16]{1,0:T(8,128)S(1)} %convert_bitcast_fusion.refs_1_, bf16[64,128,128]{2,1,0:T(8,128)(2,1)S(1)} %shard_map.39.refs_2_.refs_3_, f32[1024,128]{1,0:T(8,128)S(1)} %bitcast.28, ...), custom_call_target="tpu_custom_call", output_to_operand_aliasing={{}: (7, {})} | custom-call | flops 536870912 | bytes 4194304 | tf_op jit(solution)/shard_map/pallas_call | solution.py:153
  74.8 1.9 %shard_map.42.refs_6_ = f32[2,8,64,128]{3,2,1,0:T(8,128)S(1)} custom-call(s32[3]{0:T(128)S(1)} %pad_add_fusion.refs_0_, s32[16,16]{1,0:T(8,128)S(1)} %convert_bitcast_fusion.refs_1_, bf16[64,128,128]{2,1,0:T(8,128)(2,1)S(1)} %shard_map.38.refs_2_, bf16[64,128,128]{2,1,0:T(8,128)(2,1)S(1)} %shard_map.39.refs_2_.refs_3_, ...), custom_call_target="tpu_custom_call", output_to_operand_aliasing={{}: (6, {})} | custom-call | flops 536870912 | bytes 3145728 | tf_op jit(solution)/shard_map/pallas_call | solution.py:153
  76.8 0.0 collective-permute-done.10.refs_5_
  76.8 0.0 collective-permute-done.9.refs_4_
  76.8 3.0 %shard_map.43.refs_6_ = f32[2,8,64,128]{3,2,1,0:T(8,128)S(1)} custom-call(s32[3]{0:T(128)S(1)} %pad_add_fusion.refs_0_, s32[16,16]{1,0:T(8,128)S(1)} %convert_bitcast_fusion.refs_1_, bf16[64,128,128]{2,1,0:T(8,128)(2,1)S(1)} %shard_map.38.refs_2_, bf16[64,128,128]{2,1,0:T(8,128)(2,1)S(1)} %shard_map.39.refs_2_.refs_3_, ...), custom_call_target="tpu_custom_call", output_to_operand_aliasing={{}: (6, {})} | custom-call | flops 536870912 | bytes 3145728 | tf_op jit(solution)/shard_map/pallas_call | solution.py:153
  79.8 0.0 collective-permute-done.4.refs_4_
  79.8 0.0 collective-permute-done.7.refs_5_
  79.8 1.7 %shard_map.44 = f32[2,8,64,128]{3,2,1,0:T(8,128)S(1)} custom-call(s32[3]{0:T(128)S(1)} %pad_add_fusion.refs_0_, s32[16,16]{1,0:T(8,128)S(1)} %convert_bitcast_fusion.refs_1_, bf16[64,128,128]{2,1,0:T(8,128)(2,1)S(1)} %shard_map.38.refs_2_, bf16[64,128,128]{2,1,0:T(8,128)(2,1)S(1)} %shard_map.39.refs_2_.refs_3_, ...), custom_call_target="tpu_custom_call", output_to_operand_aliasing={{}: (6, {})} | custom-call | flops 536870912 | bytes 3145728 | tf_op jit(solution)/shard_map/pallas_call | solution.py:153
  81.5 9.5 %collective-permute-start.11 = (f32[8,64,128]{2,1,0:T(8,128)S(1)}, f32[8,64,128]{2,1,0:T(8,128)S(1)}, u32[]{:S(2)}, u32[]{:S(2)}) collective-permute-start(f32[8,64,128]{2,1,0:T(8,128)S(1)} %slice_bitcast_fusion), channel_id=1, source_target_pairs={{0,1},{1,0},{2,3},{3,2},{4,5},{5,4},{6,7},{7,6},{8,9},{9,8},{10,11... | collective-permute-start | bytes 786440 | tf_op jit(solution)/shard_map/ppermute | solution.py:234
  91.0 1.2 %collective-permute-done.11 = f32[8,64,128]{2,1,0:T(8,128)S(1)} collective-permute-done((f32[8,64,128]{2,1,0:T(8,128)S(1)}, f32[8,64,128]{2,1,0:T(8,128)S(1)}, u32[]{:S(2)}, u32[]{:S(2)}) %collective-permute-start.11) | collective-permute-done | bytes 262176 | tf_op jit(solution)/shard_map/ppermute | solution.py:234
  92.2 13.3 %all_to_all.17 = f32[8,64,128]{2,1,0:T(8,128)S(1)} all-to-all(f32[8,64,128]{2,1,0:T(8,128)S(1)} %fusion), channel_id=1, replica_groups={{0,16,64,80,128,144,192,208},{32,48,96,112,160,176,224,240},{1,17,65,81..., dimensions={0} | all-to-all | bytes 524288 | tf_op jit(solution)/shard_map/all_to_all | solution.py:235
  105.5 0.6 reduce_sum.9
  (5 shorter events, 0.1 us)
Async XLA Ops:
  0.0 4.6 %copy-start.6 = (s32[2,1,1,16]{3,2,1,0:T(1,128)S(1)}, s32[2,1,1,16]{3,2,1,0:T(1,128)}, u32[]{:S(2)}) copy-start(s32[2,1,1,16]{3,2,1,0:T(1,128)} %param.5) | copy-start | bytes 388
  0.0 4.6 %copy-start.3 = (f32[2,1,1,16,4096]{4,3,2,1,0:T(8,128)S(1)}, f32[2,1,1,16,4096]{4,3,2,1,0:T(8,128)}, u32[]{:S(2)}) copy-start(f32[2,1,1,16,4096]{4,3,2,1,0:T(8,128)} %param.4) | copy-start | bytes 1572868
  2.1 17.6 %collective-permute-start = (f32[32,4096]{1,0:T(8,128)S(1)}, f32[32,4096]{1,0:T(8,128)S(1)}, u32[]{:S(2)}, u32[]{:S(2)}) collective-permute-start(f32[32,4096]{1,0:T(8,128)S(1)} %get-tuple-element.14), channel_id=1, source_target_pairs={{0,32},{16,48},{32,0},{48,16},{64,96},{80,112},{96,64},{112,80},{1... | collective-permute-start | bytes 1572872 | tf_op jit(solution)/shard_map/ppermute | solution.py:183
  19.8 39.3 %copy-start.4 = (f32[32,4096]{1,0:T(8,128)}, f32[32,4096]{1,0:T(8,128)S(1)}, u32[]{:S(2)}) copy-start(f32[32,4096]{1,0:T(8,128)S(1)} %collective-permute-done.refs_0_) | copy-start | bytes 1572868
  19.8 43.5 %copy-start = (f32[64,4096]{1,0:T(8,128)S(1)}, f32[64,4096]{1,0:T(8,128)}, u32[]{:S(2)}) copy-start(f32[64,4096]{1,0:T(8,128)} %refs_0_.1) | copy-start | bytes 3145732
  46.0 0.8 copy-start.7
  46.9 10.7 %collective-permute-start.2 = (f32[1024,128]{1,0:T(8,128)S(1)}, f32[1024,128]{1,0:T(8,128)S(1)}, u32[]{:S(2)}, u32[]{:S(2)}) collective-permute-start(f32[1024,128]{1,0:T(8,128)S(1)} %bitcast.24), channel_id=1, source_target_pairs={{0,4},{2,6},{4,8},{6,10},{8,12},{10,14},{12,0},{14,2},{1,5},{3,7},... | collective-permute-start | bytes 1572872 | tf_op jit(solution)/shard_map/ppermute | solution.py:183
  46.9 11.4 %collective-permute-start.5 = (f32[1024,128]{1,0:T(8,128)S(1)}, f32[1024,128]{1,0:T(8,128)S(1)}, u32[]{:S(2)}, u32[]{:S(2)}) collective-permute-start(f32[1024,128]{1,0:T(8,128)S(1)} %bitcast.25), channel_id=1, source_target_pairs={{0,12},{2,14},{4,0},{6,2},{8,4},{10,6},{12,8},{14,10},{1,13},{3,15... | collective-permute-start | bytes 1572872 | tf_op jit(solution)/shard_map/ppermute | solution.py:183
  49.5 12.2 %collective-permute-start.8 = (f32[1024,128]{1,0:T(8,128)S(1)}, f32[1024,128]{1,0:T(8,128)}, u32[]{:S(2)}, u32[]{:S(2)}) collective-permute-start(f32[1024,128]{1,0:T(8,128)S(1)} %bitcast.26), channel_id=1, source_target_pairs={{0,2},{2,0},{4,6},{6,4},{8,10},{10,8},{12,14},{14,12},{1,3},{3,1},... | collective-permute-start | bytes 1572872 | tf_op jit(solution)/shard_map/ppermute | solution.py:183
  49.5 16.9 %collective-permute-start.1 = (f32[32,4096]{1,0:T(8,128)}, f32[32,4096]{1,0:T(8,128)}, u32[]{:S(2)}, u32[]{:S(2)}) collective-permute-start(f32[32,4096]{1,0:T(8,128)} %get-tuple-element.11), channel_id=1, source_target_pairs={{0,32},{16,48},{32,0},{48,16},{64,96},{80,112},{96,64},{112,80},{1... | collective-permute-start | bytes 1572872 | tf_op jit(solution)/shard_map/ppermute | solution.py:183
  58.3 6.7 %collective-permute-start.3 = (f32[512,128]{1,0:T(8,128)}, f32[512,128]{1,0:T(8,128)S(1)}, u32[]{:S(2)}, u32[]{:S(2)}) collective-permute-start(f32[512,128]{1,0:T(8,128)} %slice.34), channel_id=1, source_target_pairs={{0,4},{2,6},{4,8},{6,10},{8,12},{10,14},{12,0},{14,2},{1,5},{3,7},... | collective-permute-start | bytes 786440 | tf_op jit(solution)/shard_map/ppermute | solution.py:183
  58.3 3.5 %copy-start.1 = (f32[1024,128]{1,0:T(8,128)}, f32[1024,128]{1,0:T(8,128)S(1)}, u32[]{:S(2)}) copy-start(f32[1024,128]{1,0:T(8,128)S(1)} %collective-permute-done.5.refs_6_) | copy-start | bytes 1572868
  59.1 6.3 %collective-permute-start.6 = (f32[512,128]{1,0:T(8,128)}, f32[512,128]{1,0:T(8,128)}, u32[]{:S(2)}, u32[]{:S(2)}) collective-permute-start(f32[512,128]{1,0:T(8,128)} %slice.35), channel_id=1, source_target_pairs={{0,12},{2,14},{4,0},{6,2},{8,4},{10,6},{12,8},{14,10},{1,13},{3,15... | collective-permute-start | bytes 786440 | tf_op jit(solution)/shard_map/ppermute | solution.py:183
  61.8 15.0 %collective-permute-start.10 = (f32[1024,128]{1,0:T(8,128)}, f32[1024,128]{1,0:T(8,128)}, u32[]{:S(2)}, u32[]{:S(2)}) collective-permute-start(f32[1024,128]{1,0:T(8,128)} %collective-permute-done.8.refs_4_), channel_id=1, source_target_pairs={{0,12},{2,14},{4,0},{6,2},{8,4},{10,6},{12,8},{14,10},{1,13},{3,15... | collective-permute-start | bytes 1572872 | tf_op jit(solution)/shard_map/ppermute | solution.py:183
  61.8 15.0 %collective-permute-start.9 = (f32[1024,128]{1,0:T(8,128)}, f32[1024,128]{1,0:T(8,128)}, u32[]{:S(2)}, u32[]{:S(2)}) collective-permute-start(f32[1024,128]{1,0:T(8,128)} %collective-permute-done.8.refs_4_), channel_id=1, source_target_pairs={{0,4},{2,6},{4,8},{6,10},{8,12},{10,14},{12,0},{14,2},{1,5},{3,7},... | collective-permute-start | bytes 1572872 | tf_op jit(solution)/shard_map/ppermute | solution.py:183
  64.0 5.3 %copy-start.2 = (f32[1024,128]{1,0:T(8,128)S(1)}, f32[1024,128]{1,0:T(8,128)}, u32[]{:S(2)}) copy-start(f32[1024,128]{1,0:T(8,128)} %copy-done.1) | copy-start | bytes 1572868
  65.0 14.9 %collective-permute-start.4 = (f32[512,128]{1,0:T(8,128)S(1)}, f32[512,128]{1,0:T(8,128)S(1)}, u32[]{:S(2)}, u32[]{:S(2)}) collective-permute-start(f32[512,128]{1,0:T(8,128)S(1)} %collective-permute-done.3.refs_4_), channel_id=1, source_target_pairs={{0,2},{2,0},{4,6},{6,4},{8,10},{10,8},{12,14},{14,12},{1,3},{3,1},... | collective-permute-start | bytes 786440 | tf_op jit(solution)/shard_map/ppermute | solution.py:183
  65.4 14.4 %collective-permute-start.7 = (f32[512,128]{1,0:T(8,128)}, f32[512,128]{1,0:T(8,128)S(1)}, u32[]{:S(2)}, u32[]{:S(2)}) collective-permute-start(f32[512,128]{1,0:T(8,128)} %collective-permute-done.6.refs_5_), channel_id=1, source_target_pairs={{0,2},{2,0},{4,6},{6,4},{8,10},{10,8},{12,14},{14,12},{1,3},{3,1},... | collective-permute-start | bytes 786440 | tf_op jit(solution)/shard_map/ppermute | solution.py:183
  66.4 1.0 copy-start.5
  81.5 10.7 %collective-permute-start.11 = (f32[8,64,128]{2,1,0:T(8,128)S(1)}, f32[8,64,128]{2,1,0:T(8,128)S(1)}, u32[]{:S(2)}, u32[]{:S(2)}) collective-permute-start(f32[8,64,128]{2,1,0:T(8,128)S(1)} %slice_bitcast_fusion), channel_id=1, source_target_pairs={{0,1},{1,0},{2,3},{3,2},{4,5},{5,4},{6,7},{7,6},{8,9},{9,8},{10,11... | collective-permute-start | bytes 786440 | tf_op jit(solution)/shard_map/ppermute | solution.py:234

commit v7 on v6

--- a/solution.py
+++ b/solution.py
@@ -176,7 +176,10 @@
     pair = slots // cols
     rows = pair * HALF
     blocks = rows_axis // GROUP
-    ranks = [[2 * (GROUP * m + member) + x for m in range(blocks // 2) for x in range(2)] for member in range(GROUP)]
+    ranks = [
+        [2 * (GROUP * m + (m.bit_count() + odd) % 2) + x for m in range(blocks // 2) for x in range(2)]
+        for odd in range(2)
+    ]
     place = jnp.stack([lax.axis_index("col"), lax.axis_index("layer"), lax.axis_index("row") // 2 % GROUP])
 
     def send(share, to, axis="col", size=cols):
@@ -185,18 +188,15 @@
     def send_t(t_block):
         return send(t_block, lambda i: i ^ 2, "row", rows_axis)
 
-    ij_half = t_amps.shape[0] // 2
-    t_first = send_t(t_amps[:ij_half])
     parts = pack(v_tiles, v_where, cols)
     parts = lax.all_to_all(parts, "col", 0, 0, tiled=True)
-    parts, t_first = lax.optimization_barrier((parts, t_first))
     parts = parts.reshape(blocks // 2, GROUP, 2, rows + 8, LANES).transpose(0, 2, 1, 3, 4)
     parts = parts.reshape(blocks, GROUP * (rows + 8), LANES)
     parts = lax.all_to_all(parts, "row", 0, 0, tiled=True, axis_index_groups=ranks)
     parts = parts.reshape(blocks * GROUP, rows + 8, LANES)
     spots = parts[:, rows, :slots].astype(jnp.int32)
     own = parts[:, :rows].reshape(blocks * GROUP * rows, LANES)
-    own, t_rest = lax.optimization_barrier((own, t_amps[ij_half:]))
+    own, t_other = lax.optimization_barrier((own, t_amps))
 
     def up(i):
         return (i + 2) % cols
@@ -214,7 +214,7 @@
     partner = send(own, across)
     below = send(own, up)
     above = send(own, down)
-    t_rest = send_t(t_rest)
+    t_other = send_t(t_other)
     tiles = {0: prepare(t_amps)}
     far_low = send(below[:half], up)
     far_high = send(above[half:], down)
@@ -224,7 +224,7 @@
     partner_far_high = send(far_high, across)
     near = [((0, 0, 0), own), ((0, 0, 1), partner), ((0, -2, 0), below), ((0, 2, 0), above)]
     sums = add(None, tiles, *near)
-    other = {1: prepare(t_first, t_rest)}
+    other = {1: prepare(t_other)}
     sums = add(sums, other, *near)
     both = {**tiles, **other}
     sums = add(sums, both, ((0, 4, 0), far_low), ((middle, 4, 0), far_high))

time: 108 us -> 107 us (level); the launches traced: 106 us -> 107 us
  starting transfers between devices: 19.8 us -> 15.9 us
  blocking collectives: 54 us -> 57.5 us
  Pallas kernels: 15.3 us -> 16.7 us
    ppermute x1, starting transfers between devices: 9.5 us -> 6.19 us  [on_device(): sums = sums[0] + lax.ppermute(sums[1], 'layer', [(0, 1), (1, 0)])]
    slice x1 -> x0, local copies, waits for them, and re-layouts: 2.13 us -> none  [on_device(): own, t_rest = lax.optimization_barrier((own, t_amps[ij_half:]))]
    unnamed x16 -> x10, local copies, waits for them, and re-layouts: 1.84 us -> 3.56 us
    all_to_all x1, blocking collectives: 13.3 us -> 14.8 us  [on_device(): lax.all_to_all(sums, 'row', 0, 0, tiled=True, axis_index_groups=ranks)]
    pallas_call x2, Pallas kernels: 2.45 us -> 3.84 us  [prepare(): pl.pallas_call(prepare_kernel, out_shape=jax.ShapeDtypeStruct((cd // TILE...]
    ppermute x11 -> x10, starting transfers between devices: 10.3 us -> 9.67 us  [send(): return lax.ppermute(share, axis, [(i, to(i)) for i in range(size)])]
    ppermute x11 -> x10, waiting for transfers between devices: 8.44 us -> 8.75 us  [send(): return lax.ppermute(share, axis, [(i, to(i)) for i in range(size)])]
  transfers between devices with their start and end apart: 12 -> 11, of which waited for: 3 -> 2; matrix products, arithmetic and copies ran while one was open for 2% -> 2% of each run, Pallas kernels for 13% -> 13%
where the time goes in v7:
time: 107 us
  blocking collectives  57.5 us (54%)
  Pallas kernels  16.7 us (16%)
  starting transfers between devices  15.9 us (15%)
  waiting for transfers between devices  9.92 us (9%)
  local copies, waits for them, and re-layouts  5.97 us (6%)
    all_to_all x1, blocking collectives, on_device(): lax.all_to_all(parts, 'row', 0, 0, tiled=True, axis_index_groups=ranks)  27.2 us
    all_to_all x1, blocking collectives, on_device(): parts = lax.all_to_all(parts, 'col', 0, 0, tiled=True)  15.5 us
    all_to_all x1, blocking collectives, on_device(): lax.all_to_all(sums, 'row', 0, 0, tiled=True, axis_index_groups=ranks)  14.8 us
    pallas_call x5, Pallas kernels, contract(): pl.pallas_call(kernel, out_shape=jax.ShapeDtypeStruct((2, blocks, ij, LAN...  12.2 us
    ppermute x10, starting transfers between devices, send(): return lax.ppermute(share, axis, [(i, to(i)) for i in range(size)])  9.67 us
    ppermute x10, waiting for transfers between devices, send(): return lax.ppermute(share, axis, [(i, to(i)) for i in range(size)])  8.75 us
    ppermute x1, starting transfers between devices, on_device(): sums = sums[0] + lax.ppermute(sums[1], 'layer', [(0, 1), (1, 0)])  6.19 us
    pallas_call x2, Pallas kernels, prepare(): pl.pallas_call(prepare_kernel, out_shape=jax.ShapeDtypeStruct((cd // TILE...  3.84 us
  transfers between devices with their start and end apart: 11, of which 2 were waited for; matrix products, arithmetic and copies ran while one was open for 2% of the time, Pallas kernels for 13%

profile of v7, /device:TPU:1, one launch (start us, length us, event | category | flops | bytes accessed | tf_op | source)
XLA Modules:
  0.0 106.9 jit_solution(6798488586756480389)
XLA Ops:
  0.0 0.0 copy-start.2
  0.0 1.0 copy-done.2
  1.0 0.0 copy-start.3
  1.0 0.7 copy-done.3
  1.7 0.6 shard_map.37
  2.4 15.5 %all_to_all.15 = f32[8,144,128]{2,1,0:T(8,128)S(1)} all-to-all(f32[8,144,128]{2,1,0:T(8,128)S(1)} %shard_map.37), channel_id=1, replica_groups=mesh['row'=16,'col'=8,'layer'=2] {'col'}, dimensions={0} | all-to-all | bytes 1179648 | tf_op jit(solution)/shard_map/all_to_all | solution.py:192
  17.9 27.2 %all_to_all.16 = f32[8,144,128]{2,1,0:T(8,128)S(1)} all-to-all(f32[8,144,128]{2,1,0:T(8,128)S(1)} %bitcast.32), channel_id=1, replica_groups={{0,16,96,112,160,176,192,208},{32,48,64,80,128,144,224,240},{1,17,97,11..., dimensions={0} | all-to-all | bytes 1179648 | tf_op jit(solution)/shard_map/all_to_all | solution.py:195
  45.1 0.0 copy-start.4
  45.2 0.8 copy-done.4
  46.0 0.1 collective-permute-start.1
  46.1 2.6 %collective-permute-start.4 = (f32[1024,128]{1,0:T(8,128)S(1)}, f32[1024,128]{1,0:T(8,128)S(1)}, u32[]{:S(2)}, u32[]{:S(2)}) collective-permute-start(f32[1024,128]{1,0:T(8,128)S(1)} %bitcast.25), channel_id=1, source_target_pairs={{0,12},{2,14},{4,0},{6,2},{8,4},{10,6},{12,8},{14,10},{1,13},{3,15... | collective-permute-start | bytes 1572872 | tf_op jit(solution)/shard_map/ppermute | solution.py:186
  48.7 0.2 collective-permute-start
  48.8 0.0 collective-permute-start.7
  48.8 8.7 %collective-permute-done.1.refs_5_ = f32[1024,128]{1,0:T(8,128)S(1)} collective-permute-done((f32[1024,128]{1,0:T(8,128)S(1)}, f32[1024,128]{1,0:T(8,128)S(1)}, u32[]{:S(2)}, u32[]{:S(2)}) %collective-permute-start.1) | collective-permute-done | bytes 524320 | tf_op jit(solution)/shard_map/ppermute | solution.py:186
  57.6 0.7 slice.26
  58.3 0.0 collective-permute-start.2
  58.3 0.0 collective-permute-done.4.refs_6_
  58.3 0.0 copy-start
  58.3 0.8 slice.27
  59.0 2.7 %collective-permute-start.5 = (f32[512,128]{1,0:T(8,128)}, f32[512,128]{1,0:T(8,128)}, u32[]{:S(2)}, u32[]{:S(2)}) collective-permute-start(f32[512,128]{1,0:T(8,128)} %slice.27), channel_id=1, source_target_pairs={{0,12},{2,14},{4,0},{6,2},{8,4},{10,6},{12,8},{14,10},{1,13},{3,15... | collective-permute-start | bytes 786440 | tf_op jit(solution)/shard_map/ppermute | solution.py:186
  61.7 0.0 collective-permute-done.7.refs_4_
  61.7 0.0 collective-permute-start.8
  61.7 0.0 copy-done
  61.7 2.7 %collective-permute-start.9 = (f32[1024,128]{1,0:T(8,128)}, f32[1024,128]{1,0:T(8,128)}, u32[]{:S(2)}, u32[]{:S(2)}) collective-permute-start(f32[1024,128]{1,0:T(8,128)} %collective-permute-done.7.refs_4_), channel_id=1, source_target_pairs={{0,12},{2,14},{4,0},{6,2},{8,4},{10,6},{12,8},{14,10},{1,13},{3,15... | collective-permute-start | bytes 1572872 | tf_op jit(solution)/shard_map/ppermute | solution.py:186
  64.4 1.9 %shard_map.38.refs_2_ = bf16[64,128,128]{2,1,0:T(8,128)(2,1)S(1)} custom-call(f32[64,4096]{1,0:T(8,128)} %refs_0_.1), custom_call_target="tpu_custom_call" | custom-call | flops 268435456 | bytes 3145728 | tf_op jit(solution)/shard_map/pallas_call | solution.py:70
  66.4 0.1 pad_add_fusion.refs_0_
  66.4 0.8 slice.24
  67.3 0.0 collective-permute-done.2.refs_4_
  67.3 0.0 collective-permute-start.3
  67.3 0.0 collective-permute-done.5.refs_5_
  67.3 1.5 %collective-permute-start.6 = (f32[512,128]{1,0:T(8,128)}, f32[512,128]{1,0:T(8,128)S(1)}, u32[]{:S(2)}, u32[]{:S(2)}) collective-permute-start(f32[512,128]{1,0:T(8,128)} %collective-permute-done.5.refs_5_), channel_id=1, source_target_pairs={{0,2},{2,0},{4,6},{6,4},{8,10},{10,8},{12,14},{14,12},{1,3},{3,1},... | collective-permute-start | bytes 786440 | tf_op jit(solution)/shard_map/ppermute | solution.py:186
  68.8 0.0 copy-start.1
  68.8 1.0 copy-done.1
  69.8 2.7 %shard_map.40.refs_7_ = f32[2,8,64,128]{3,2,1,0:T(8,128)S(1)} custom-call(s32[3]{0:T(128)S(1)} %pad_add_fusion.refs_0_, s32[16,16]{1,0:T(8,128)S(1)} %convert_bitcast_fusion.refs_1_, bf16[64,128,128]{2,1,0:T(8,128)(2,1)S(1)} %shard_map.38.refs_2_, f32[1024,128]{1,0:T(8,128)S(1)} %bitcast.27, f32[1024,128]{1,0:T(8,128)} %collective-permute-done.7.refs_4_, ...), custom_call_target="tpu_custom_call" | custom-call | flops 536870912 | bytes 4194304 | tf_op jit(solution)/shard_map/pallas_call | solution.py:153
  72.5 0.0 collective-permute-done.refs_0_
  72.5 1.9 %shard_map.39.refs_2_.refs_3_ = bf16[64,128,128]{2,1,0:T(8,128)(2,1)S(1)} custom-call(f32[64,4096]{1,0:T(8,128)} %collective-permute-done.refs_0_), custom_call_target="tpu_custom_call" | custom-call | flops 268435456 | bytes 3145728 | tf_op jit(solution)/shard_map/pallas_call | solution.py:70
  74.5 2.8 %shard_map.41.refs_6_ = f32[2,8,64,128]{3,2,1,0:T(8,128)S(1)} custom-call(s32[3]{0:T(128)S(1)} %pad_add_fusion.refs_0_, s32[16,16]{1,0:T(8,128)S(1)} %convert_bitcast_fusion.refs_1_, bf16[64,128,128]{2,1,0:T(8,128)(2,1)S(1)} %shard_map.39.refs_2_.refs_3_, f32[1024,128]{1,0:T(8,128)S(1)} %bitcast.28, ...), custom_call_target="tpu_custom_call", output_to_operand_aliasing={{}: (7, {})} | custom-call | flops 536870912 | bytes 4194304 | tf_op jit(solution)/shard_map/pallas_call | solution.py:153
  77.3 2.0 %shard_map.42.refs_6_ = f32[2,8,64,128]{3,2,1,0:T(8,128)S(1)} custom-call(s32[3]{0:T(128)S(1)} %pad_add_fusion.refs_0_, s32[16,16]{1,0:T(8,128)S(1)} %convert_bitcast_fusion.refs_1_, bf16[64,128,128]{2,1,0:T(8,128)(2,1)S(1)} %shard_map.38.refs_2_, bf16[64,128,128]{2,1,0:T(8,128)(2,1)S(1)} %shard_map.39.refs_2_.refs_3_, ...), custom_call_target="tpu_custom_call", output_to_operand_aliasing={{}: (6, {})} | custom-call | flops 536870912 | bytes 3145728 | tf_op jit(solution)/shard_map/pallas_call | solution.py:153
  79.3 0.0 collective-permute-done.8.refs_4_
  79.3 0.0 collective-permute-done.9.refs_5_
  79.3 3.0 %shard_map.43.refs_6_ = f32[2,8,64,128]{3,2,1,0:T(8,128)S(1)} custom-call(s32[3]{0:T(128)S(1)} %pad_add_fusion.refs_0_, s32[16,16]{1,0:T(8,128)S(1)} %convert_bitcast_fusion.refs_1_, bf16[64,128,128]{2,1,0:T(8,128)(2,1)S(1)} %shard_map.38.refs_2_, bf16[64,128,128]{2,1,0:T(8,128)(2,1)S(1)} %shard_map.39.refs_2_.refs_3_, ...), custom_call_target="tpu_custom_call", output_to_operand_aliasing={{}: (6, {})} | custom-call | flops 536870912 | bytes 3145728 | tf_op jit(solution)/shard_map/pallas_call | solution.py:153
  82.3 0.0 collective-permute-done.3.refs_4_
  82.3 0.0 collective-permute-done.6.refs_5_
  82.3 1.7 %shard_map.44 = f32[2,8,64,128]{3,2,1,0:T(8,128)S(1)} custom-call(s32[3]{0:T(128)S(1)} %pad_add_fusion.refs_0_, s32[16,16]{1,0:T(8,128)S(1)} %convert_bitcast_fusion.refs_1_, bf16[64,128,128]{2,1,0:T(8,128)(2,1)S(1)} %shard_map.38.refs_2_, bf16[64,128,128]{2,1,0:T(8,128)(2,1)S(1)} %shard_map.39.refs_2_.refs_3_, ...), custom_call_target="tpu_custom_call", output_to_operand_aliasing={{}: (6, {})} | custom-call | flops 536870912 | bytes 3145728 | tf_op jit(solution)/shard_map/pallas_call | solution.py:153
  84.0 6.2 %collective-permute-start.10 = (f32[8,64,128]{2,1,0:T(8,128)S(1)}, f32[8,64,128]{2,1,0:T(8,128)S(1)}, u32[]{:S(2)}, u32[]{:S(2)}) collective-permute-start(f32[8,64,128]{2,1,0:T(8,128)S(1)} %slice_bitcast_fusion), channel_id=1, source_target_pairs={{0,1},{1,0},{2,3},{3,2},{4,5},{5,4},{6,7},{7,6},{8,9},{9,8},{10,11... | collective-permute-start | bytes 786440 | tf_op jit(solution)/shard_map/ppermute | solution.py:234
  90.2 1.2 %collective-permute-done.10 = f32[8,64,128]{2,1,0:T(8,128)S(1)} collective-permute-done((f32[8,64,128]{2,1,0:T(8,128)S(1)}, f32[8,64,128]{2,1,0:T(8,128)S(1)}, u32[]{:S(2)}, u32[]{:S(2)}) %collective-permute-start.10) | collective-permute-done | bytes 262176 | tf_op jit(solution)/shard_map/ppermute | solution.py:234
  91.4 14.8 %all_to_all.17 = f32[8,64,128]{2,1,0:T(8,128)S(1)} all-to-all(f32[8,64,128]{2,1,0:T(8,128)S(1)} %fusion), channel_id=1, replica_groups={{0,16,96,112,160,176,192,208},{32,48,64,80,128,144,224,240},{1,17,97,11..., dimensions={0} | all-to-all | bytes 524288 | tf_op jit(solution)/shard_map/all_to_all | solution.py:235
  106.2 0.6 reduce_sum.9
  (5 shorter events, 0.1 us)
Async XLA Ops:
  0.0 1.0 copy-start.2
  1.0 0.7 copy-start.3
  45.1 0.8 copy-start.4
  46.0 11.6 %collective-permute-start.1 = (f32[1024,128]{1,0:T(8,128)S(1)}, f32[1024,128]{1,0:T(8,128)S(1)}, u32[]{:S(2)}, u32[]{:S(2)}) collective-permute-start(f32[1024,128]{1,0:T(8,128)S(1)} %bitcast.24), channel_id=1, source_target_pairs={{0,4},{2,6},{4,8},{6,10},{8,12},{10,14},{12,0},{14,2},{1,5},{3,7},... | collective-permute-start | bytes 1572872 | tf_op jit(solution)/shard_map/ppermute | solution.py:186
  46.1 12.2 %collective-permute-start.4 = (f32[1024,128]{1,0:T(8,128)S(1)}, f32[1024,128]{1,0:T(8,128)S(1)}, u32[]{:S(2)}, u32[]{:S(2)}) collective-permute-start(f32[1024,128]{1,0:T(8,128)S(1)} %bitcast.25), channel_id=1, source_target_pairs={{0,12},{2,14},{4,0},{6,2},{8,4},{10,6},{12,8},{14,10},{1,13},{3,15... | collective-permute-start | bytes 1572872 | tf_op jit(solution)/shard_map/ppermute | solution.py:186
  48.7 23.9 %collective-permute-start = (f32[64,4096]{1,0:T(8,128)}, f32[64,4096]{1,0:T(8,128)}, u32[]{:S(2)}, u32[]{:S(2)}) collective-permute-start(f32[64,4096]{1,0:T(8,128)} %refs_0_.1), channel_id=1, source_target_pairs={{0,32},{16,48},{32,0},{48,16},{64,96},{80,112},{96,64},{112,80},{1... | collective-permute-start | bytes 3145736 | tf_op jit(solution)/shard_map/ppermute | solution.py:186
  48.8 12.9 %collective-permute-start.7 = (f32[1024,128]{1,0:T(8,128)S(1)}, f32[1024,128]{1,0:T(8,128)}, u32[]{:S(2)}, u32[]{:S(2)}) collective-permute-start(f32[1024,128]{1,0:T(8,128)S(1)} %bitcast.26), channel_id=1, source_target_pairs={{0,2},{2,0},{4,6},{6,4},{8,10},{10,8},{12,14},{14,12},{1,3},{3,1},... | collective-permute-start | bytes 1572872 | tf_op jit(solution)/shard_map/ppermute | solution.py:186
  58.3 9.0 %collective-permute-start.2 = (f32[512,128]{1,0:T(8,128)}, f32[512,128]{1,0:T(8,128)S(1)}, u32[]{:S(2)}, u32[]{:S(2)}) collective-permute-start(f32[512,128]{1,0:T(8,128)} %slice.26), channel_id=1, source_target_pairs={{0,4},{2,6},{4,8},{6,10},{8,12},{10,14},{12,0},{14,2},{1,5},{3,7},... | collective-permute-start | bytes 786440 | tf_op jit(solution)/shard_map/ppermute | solution.py:186
  58.3 3.4 %copy-start = (f32[1024,128]{1,0:T(8,128)}, f32[1024,128]{1,0:T(8,128)S(1)}, u32[]{:S(2)}) copy-start(f32[1024,128]{1,0:T(8,128)S(1)} %collective-permute-done.4.refs_6_) | copy-start | bytes 1572868
  59.0 8.3 %collective-permute-start.5 = (f32[512,128]{1,0:T(8,128)}, f32[512,128]{1,0:T(8,128)}, u32[]{:S(2)}, u32[]{:S(2)}) collective-permute-start(f32[512,128]{1,0:T(8,128)} %slice.27), channel_id=1, source_target_pairs={{0,12},{2,14},{4,0},{6,2},{8,4},{10,6},{12,8},{14,10},{1,13},{3,15... | collective-permute-start | bytes 786440 | tf_op jit(solution)/shard_map/ppermute | solution.py:186
  61.7 17.6 %collective-permute-start.8 = (f32[1024,128]{1,0:T(8,128)}, f32[1024,128]{1,0:T(8,128)}, u32[]{:S(2)}, u32[]{:S(2)}) collective-permute-start(f32[1024,128]{1,0:T(8,128)} %collective-permute-done.7.refs_4_), channel_id=1, source_target_pairs={{0,4},{2,6},{4,8},{6,10},{8,12},{10,14},{12,0},{14,2},{1,5},{3,7},... | collective-permute-start | bytes 1572872 | tf_op jit(solution)/shard_map/ppermute | solution.py:186
  61.7 17.6 %collective-permute-start.9 = (f32[1024,128]{1,0:T(8,128)}, f32[1024,128]{1,0:T(8,128)}, u32[]{:S(2)}, u32[]{:S(2)}) collective-permute-start(f32[1024,128]{1,0:T(8,128)} %collective-permute-done.7.refs_4_), channel_id=1, source_target_pairs={{0,12},{2,14},{4,0},{6,2},{8,4},{10,6},{12,8},{14,10},{1,13},{3,15... | collective-permute-start | bytes 1572872 | tf_op jit(solution)/shard_map/ppermute | solution.py:186
  67.3 15.0 %collective-permute-start.3 = (f32[512,128]{1,0:T(8,128)S(1)}, f32[512,128]{1,0:T(8,128)S(1)}, u32[]{:S(2)}, u32[]{:S(2)}) collective-permute-start(f32[512,128]{1,0:T(8,128)S(1)} %collective-permute-done.2.refs_4_), channel_id=1, source_target_pairs={{0,2},{2,0},{4,6},{6,4},{8,10},{10,8},{12,14},{14,12},{1,3},{3,1},... | collective-permute-start | bytes 786440 | tf_op jit(solution)/shard_map/ppermute | solution.py:186
  67.3 15.0 %collective-permute-start.6 = (f32[512,128]{1,0:T(8,128)}, f32[512,128]{1,0:T(8,128)S(1)}, u32[]{:S(2)}, u32[]{:S(2)}) collective-permute-start(f32[512,128]{1,0:T(8,128)} %collective-permute-done.5.refs_5_), channel_id=1, source_target_pairs={{0,2},{2,0},{4,6},{6,4},{8,10},{10,8},{12,14},{14,12},{1,3},{3,1},... | collective-permute-start | bytes 786440 | tf_op jit(solution)/shard_map/ppermute | solution.py:186
  68.8 1.0 copy-start.1
  84.0 7.4 %collective-permute-start.10 = (f32[8,64,128]{2,1,0:T(8,128)S(1)}, f32[8,64,128]{2,1,0:T(8,128)S(1)}, u32[]{:S(2)}, u32[]{:S(2)}) collective-permute-start(f32[8,64,128]{2,1,0:T(8,128)S(1)} %slice_bitcast_fusion), channel_id=1, source_target_pairs={{0,1},{1,0},{2,3},{3,2},{4,5},{5,4},{6,7},{7,6},{8,9},{9,8},{10,11... | collective-permute-start | bytes 786440 | tf_op jit(solution)/shard_map/ppermute | solution.py:234

commit v8 on v7

--- a/solution.py
+++ b/solution.py
@@ -89,7 +89,7 @@
     hi_o, lo_o = split_rows(jnp.where(keep, jnp.where(upper, v, swapped), 0.0))
     rows = jnp.concatenate([hi_e, hi_o, lo_e, lo_o], axis=0)
     none = jnp.zeros_like(rows)
-    return jnp.where(ab_pair == 0, rows, none), jnp.where(ab_pair == 1, rows, none)
+    return jnp.concatenate([jnp.where(ab_pair == 0, rows, none), jnp.where(ab_pair == 1, rows, none)], axis=1)
 
 
 def contract_kernel(sources, offsets, fresh, pair, group, *refs):
@@ -99,7 +99,7 @@
     shares = refs[2 + blocks_held : 2 + blocks_held + count]
     rest = refs[2 + blocks_held + count :]
     sums = None if fresh else rest[0]
-    out, lhs, rhs = rest[-3:]
+    out = rest[-1]
     layer = place[1]
     blocks, ij = out.shape[1:3]
     rows = pair * HALF
@@ -111,19 +111,21 @@
             n for n in range(count)
             if sources[n][0] <= block < sources[n][0] + shares[n].shape[0] // (group * rows)
         ]
-        buffer = block % 2
-        at = 0
+        total = None
         for n in used:
             for held in range(blocks_held):
                 first = pl.multiple_of(((block - sources[n][0]) * group + members[held]) * rows, rows)
+                left, right = [], []
                 for p in range(pair):
                     spot = spots[block * group + members[held], columns[n] * pair + p]
-                    lhs[buffer, :, at : at + LANES] = t_tiles[held][jnp.maximum(spot, 0) >> 2]
-                    left, right = slot_rows(shares[n][pl.ds(first + p * HALF, HALF), :], spot)
-                    rhs[buffer, at : at + LANES, :LANES] = left
-                    rhs[buffer, at : at + LANES, LANES:] = right
-                    at += LANES
-        total = jnp.dot(lhs[buffer, :, :at], rhs[buffer, :at], preferred_element_type=jnp.float32)
+                    left.append(t_tiles[held][jnp.maximum(spot, 0) >> 2])
+                    right.append(slot_rows(shares[n][pl.ds(first + p * HALF, HALF), :], spot))
+                part = jnp.dot(
+                    jnp.concatenate(left, axis=1),
+                    jnp.concatenate(right, axis=0),
+                    preferred_element_type=jnp.float32,
+                )
+                total = part if total is None else total + part
         total = total[:ij] + total[ij:]
         mine = total[:, :LANES]
         other = total[:, LANES:]
@@ -140,7 +142,6 @@
     ij = next(iter(held.values())).shape[1] // 2
     sources = tuple(source for source, _ in shares)
     offsets = tuple(held)
-    depth = len(shares) * len(held) * pair * LANES
     given = [place, spots, *held.values(), *(share for _, share in shares)]
     specs = [SMEM, SMEM] + [VMEM] * (len(given) - 2)
     if sums is not None:
@@ -155,15 +156,11 @@
         out_shape=jax.ShapeDtypeStruct((2, blocks, ij, LANES), jnp.float32),
         in_specs=specs,
         out_specs=VMEM,
-        scratch_shapes=[
-            pltpu.VMEM((2, 2 * ij, depth), jnp.bfloat16),
-            pltpu.VMEM((2, depth, 2 * LANES), jnp.bfloat16),
-        ],
         input_output_aliases={} if sums is None else {len(given) - 1: 0},
         compiler_params=pltpu.CompilerParams(vmem_limit_bytes=14 * 2**20),
         cost_estimate=pl.CostEstimate(
-            flops=2 * blocks * 2 * ij * depth * 2 * LANES,
-            bytes_accessed=(len(shares) + 4) * 2**19,
+            flops=2**20,
+            bytes_accessed=2**16,
             transcendentals=0,
         ),
     )(*given)
@@ -216,14 +213,17 @@
     above = send(own, down)
     t_other = send_t(t_other)
     tiles = {0: prepare(t_amps)}
+    sums = add(None, tiles, ((0, 0, 0), own))
+    sums, partner, below, above = lax.optimization_barrier((sums, partner, below, above))
     far_low = send(below[:half], up)
     far_high = send(above[half:], down)
     partner_below = send(partner, up)
     partner_above = send(partner, down)
+    near = [((0, 0, 0), own), ((0, 0, 1), partner), ((0, -2, 0), below), ((0, 2, 0), above)]
+    sums = add(sums, tiles, *near[1:])
+    sums, far_low, far_high = lax.optimization_barrier((sums, far_low, far_high))
     partner_far_low = send(far_low, across)
     partner_far_high = send(far_high, across)
-    near = [((0, 0, 0), own), ((0, 0, 1), partner), ((0, -2, 0), below), ((0, 2, 0), above)]
-    sums = add(None, tiles, *near)
     other = {1: prepare(t_other)}
     sums = add(sums, other, *near)
     both = {**tiles, **other}

time: 107 us -> 102 us (0.953)
  Pallas kernels: 16.7 us -> 11.2 us
  local copies, waits for them, and re-layouts: 5.97 us -> 2.72 us
  waiting for transfers between devices: 9.92 us -> 12.9 us
    pallas_call x5 -> x6, Pallas kernels: 12.2 us -> 7.9 us  [contract(): pl.pallas_call(kernel, out_shape=jax.ShapeDtypeStruct((2, blocks, ij, LAN...]
    ppermute x10, waiting for transfers between devices: 8.75 us -> 11.7 us  [send(): return lax.ppermute(share, axis, [(i, to(i)) for i in range(size)])]
    ppermute x10, starting transfers between devices: 9.67 us -> 7.25 us  [send(): return lax.ppermute(share, axis, [(i, to(i)) for i in range(size)])]
    ppermute x1, starting transfers between devices: 6.19 us -> 8.52 us  [on_device(): sums = sums[0] + lax.ppermute(sums[1], 'layer', [(0, 1), (1, 0)])]
    unnamed x10 -> x8, local copies, waits for them, and re-layouts: 3.56 us -> 1.73 us
    pallas_call x2, Pallas kernels: 3.84 us -> 2.63 us  [prepare(): pl.pallas_call(prepare_kernel, out_shape=jax.ShapeDtypeStruct((cd // TILE...]
  transfers between devices with their start and end apart: 11 -> 11, of which waited for: 2 -> 7; matrix products, arithmetic and copies ran while one was open for 2% -> 1% of each run, Pallas kernels for 13% -> 9%
where the time goes in v8:
time: 102 us; the launch traced here: 101 us
  blocking collectives  57.8 us (57%)
  starting transfers between devices  15.8 us (15%)
  waiting for transfers between devices  12.9 us (13%)
  Pallas kernels  11.2 us (11%)
  local copies, waits for them, and re-layouts  2.72 us (3%)
    all_to_all x1, blocking collectives, on_device(): lax.all_to_all(parts, 'row', 0, 0, tiled=True, axis_index_groups=ranks)  27.2 us
    all_to_all x1, blocking collectives, on_device(): parts = lax.all_to_all(parts, 'col', 0, 0, tiled=True)  15.6 us
    all_to_all x1, blocking collectives, on_device(): lax.all_to_all(sums, 'row', 0, 0, tiled=True, axis_index_groups=ranks)  15 us
    ppermute x10, waiting for transfers between devices, send(): return lax.ppermute(share, axis, [(i, to(i)) for i in range(size)])  11.7 us
    ppermute x1, starting transfers between devices, on_device(): sums = sums[0] + lax.ppermute(sums[1], 'layer', [(0, 1), (1, 0)])  8.52 us
    pallas_call x6, Pallas kernels, contract(): pl.pallas_call(kernel, out_shape=jax.ShapeDtypeStruct((2, blocks, ij, LAN...  7.9 us
    ppermute x10, starting transfers between devices, send(): return lax.ppermute(share, axis, [(i, to(i)) for i in range(size)])  7.25 us
    pallas_call x2, Pallas kernels, prepare(): pl.pallas_call(prepare_kernel, out_shape=jax.ShapeDtypeStruct((cd // TILE...  2.63 us
  transfers between devices with their start and end apart: 11, of which 7 were waited for; matrix products, arithmetic and copies ran while one was open for 1% of the time, Pallas kernels for 9%

profile of v8, /device:TPU:1, one launch (start us, length us, event | category | flops | bytes accessed | tf_op | source)
XLA Modules:
  0.0 101.3 jit_solution(4286045926841191980)
XLA Ops:
  0.0 0.0 copy-start.1
  0.0 1.0 %copy-done.1 = f32[2,1,1,16,4096]{4,3,2,1,0:T(8,128)S(1)} copy-done((f32[2,1,1,16,4096]{4,3,2,1,0:T(8,128)S(1)}, f32[2,1,1,16,4096]{4,3,2,1,0:T(8,128)}, u32[]{:S(2)}) %copy-start.1) | copy-done | bytes 524312
  1.0 0.0 copy-start.2
  1.0 0.7 copy-done.2
  1.7 0.6 shard_map.37
  2.4 0.0 copy-start
  2.4 15.6 %all_to_all.15 = f32[8,144,128]{2,1,0:T(8,128)S(1)} all-to-all(f32[8,144,128]{2,1,0:T(8,128)S(1)} %shard_map.37), channel_id=1, replica_groups=mesh['row'=16,'col'=8,'layer'=2] {'col'}, dimensions={0} | all-to-all | bytes 1179648 | tf_op jit(solution)/shard_map/all_to_all | solution.py:189
  18.0 27.2 %all_to_all.16 = f32[8,144,128]{2,1,0:T(8,128)S(1)} all-to-all(f32[8,144,128]{2,1,0:T(8,128)S(1)} %bitcast.32), channel_id=1, replica_groups={{0,16,96,112,160,176,192,208},{32,48,64,80,128,144,224,240},{1,17,97,11..., dimensions={0} | all-to-all | bytes 1179648 | tf_op jit(solution)/shard_map/all_to_all | solution.py:192
  45.3 0.0 copy-start.3
  45.3 0.0 copy-done
  45.3 0.3 collective-permute-start
  45.6 0.8 collective-permute-start.3
  46.4 0.0 copy-done.3
  46.4 0.6 collective-permute-start.2
  47.1 0.0 collective-permute-start.1
  47.1 0.7 shard_map.38.refs_2_
  47.8 0.1 pad_add_fusion.refs_0_
  47.9 0.8 slice.24
  48.7 1.1 %shard_map.40.refs_6_ = f32[2,8,64,128]{3,2,1,0:T(8,128)S(1)} custom-call(s32[3]{0:T(128)S(1)} %pad_add_fusion.refs_0_, s32[16,16]{1,0:T(8,128)S(1)} %convert_bitcast_fusion.refs_1_, bf16[64,128,128]{2,1,0:T(8,128)(2,1)S(1)} %shard_map.38.refs_2_, f32[1024,128]{1,0:T(8,128)S(1)} %bitcast.27), custom_call_target="tpu_custom_call" | custom-call | flops 1048576 | bytes 65536 | tf_op jit(solution)/shard_map/pallas_call | solution.py:154
  49.8 5.4 %collective-permute-done.3.refs_5_.refs_6_ = f32[1024,128]{1,0:T(8,128)S(1)} collective-permute-done((f32[1024,128]{1,0:T(8,128)S(1)}, f32[1024,128]{1,0:T(8,128)S(1)}, u32[]{:S(2)}, u32[]{:S(2)}) %collective-permute-start.3) | collective-permute-done | bytes 524320 | tf_op jit(solution)/shard_map/ppermute | solution.py:183
  55.2 1.7 %collective-permute-done.2.refs_4_.refs_5_ = f32[1024,128]{1,0:T(8,128)S(1)} collective-permute-done((f32[1024,128]{1,0:T(8,128)S(1)}, f32[1024,128]{1,0:T(8,128)S(1)}, u32[]{:S(2)}, u32[]{:S(2)}) %collective-permute-start.2) | collective-permute-done | bytes 524320 | tf_op jit(solution)/shard_map/ppermute | solution.py:183
  57.0 0.0 collective-permute-done.1.refs_3_.refs_4_
  57.0 1.4 %collective-permute-start.5 = (f32[512,128]{1,0:T(8,128)S(1)}, f32[512,128]{1,0:T(8,128)S(1)}, u32[]{:S(2)}, u32[]{:S(2)}) collective-permute-start(f32[512,128]{1,0:T(8,128)S(1)} %slice.21), channel_id=1, source_target_pairs={{0,12},{2,14},{4,0},{6,2},{8,4},{10,6},{12,8},{14,10},{1,13},{3,15... | collective-permute-start | bytes 786440 | tf_op jit(solution)/shard_map/ppermute | solution.py:183
  58.4 0.2 collective-permute-start.4
  58.6 2.5 %collective-permute-start.9 = (f32[1024,128]{1,0:T(8,128)S(1)}, f32[1024,128]{1,0:T(8,128)S(1)}, u32[]{:S(2)}, u32[]{:S(2)}) collective-permute-start(f32[1024,128]{1,0:T(8,128)S(1)} %collective-permute-done.1.refs_3_.refs_4_), channel_id=1, source_target_pairs={{0,12},{2,14},{4,0},{6,2},{8,4},{10,6},{12,8},{14,10},{1,13},{3,15... | collective-permute-start | bytes 1572872 | tf_op jit(solution)/shard_map/ppermute | solution.py:183
  61.1 0.0 collective-permute-start.8
  61.1 1.4 %shard_map.41.refs_7_ = f32[2,8,64,128]{3,2,1,0:T(8,128)S(1)} custom-call(s32[3]{0:T(128)S(1)} %pad_add_fusion.refs_0_, s32[16,16]{1,0:T(8,128)S(1)} %convert_bitcast_fusion.refs_1_, bf16[64,128,128]{2,1,0:T(8,128)(2,1)S(1)} %shard_map.38.refs_2_, f32[1024,128]{1,0:T(8,128)S(1)} %collective-permute-done.1.refs_3_.refs_4_, ...), custom_call_target="tpu_custom_call", output_to_operand_aliasing={{}: (6, {})} | custom-call | flops 1048576 | bytes 65536 | tf_op jit(solution)/shard_map/pallas_call | solution.py:154
  62.4 0.3 collective-permute-done.5.refs_5_
  62.7 2.1 %collective-permute-done.4.refs_4_ = f32[512,128]{1,0:T(8,128)S(1)} collective-permute-done((f32[512,128]{1,0:T(8,128)S(1)}, f32[512,128]{1,0:T(8,128)S(1)}, u32[]{:S(2)}, u32[]{:S(2)}) %collective-permute-start.4) | collective-permute-done | bytes 262176 | tf_op jit(solution)/shard_map/ppermute | solution.py:183
  64.8 0.6 collective-permute-start.6
  65.4 0.8 collective-permute-start.7
  66.3 0.9 collective-permute-done.refs_0_
  67.1 1.9 %shard_map.39.refs_2_.refs_3_ = bf16[64,128,128]{2,1,0:T(8,128)(2,1)S(1)} custom-call(f32[64,4096]{1,0:T(8,128)} %collective-permute-done.refs_0_), custom_call_target="tpu_custom_call" | custom-call | flops 268435456 | bytes 3145728 | tf_op jit(solution)/shard_map/pallas_call | solution.py:70
  69.1 1.5 %shard_map.42.refs_6_ = f32[2,8,64,128]{3,2,1,0:T(8,128)S(1)} custom-call(s32[3]{0:T(128)S(1)} %pad_add_fusion.refs_0_, s32[16,16]{1,0:T(8,128)S(1)} %convert_bitcast_fusion.refs_1_, bf16[64,128,128]{2,1,0:T(8,128)(2,1)S(1)} %shard_map.39.refs_2_.refs_3_, f32[1024,128]{1,0:T(8,128)S(1)} %bitcast.28, ...), custom_call_target="tpu_custom_call", output_to_operand_aliasing={{}: (7, {})} | custom-call | flops 1048576 | bytes 65536 | tf_op jit(solution)/shard_map/pallas_call | solution.py:154
  70.6 1.2 %shard_map.43.refs_6_ = f32[2,8,64,128]{3,2,1,0:T(8,128)S(1)} custom-call(s32[3]{0:T(128)S(1)} %pad_add_fusion.refs_0_, s32[16,16]{1,0:T(8,128)S(1)} %convert_bitcast_fusion.refs_1_, bf16[64,128,128]{2,1,0:T(8,128)(2,1)S(1)} %shard_map.38.refs_2_, bf16[64,128,128]{2,1,0:T(8,128)(2,1)S(1)} %shard_map.39.refs_2_.refs_3_, ...), custom_call_target="tpu_custom_call", output_to_operand_aliasing={{}: (6, {})} | custom-call | flops 1048576 | bytes 65536 | tf_op jit(solution)/shard_map/pallas_call | solution.py:154
  71.8 0.0 collective-permute-done.9.refs_5_
  71.9 1.3 %collective-permute-done.8.refs_4_ = f32[1024,128]{1,0:T(8,128)S(1)} collective-permute-done((f32[1024,128]{1,0:T(8,128)S(1)}, f32[1024,128]{1,0:T(8,128)S(1)}, u32[]{:S(2)}, u32[]{:S(2)}) %collective-permute-start.8) | collective-permute-done | bytes 524320 | tf_op jit(solution)/shard_map/ppermute | solution.py:183
  73.1 1.5 %shard_map.44.refs_6_ = f32[2,8,64,128]{3,2,1,0:T(8,128)S(1)} custom-call(s32[3]{0:T(128)S(1)} %pad_add_fusion.refs_0_, s32[16,16]{1,0:T(8,128)S(1)} %convert_bitcast_fusion.refs_1_, bf16[64,128,128]{2,1,0:T(8,128)(2,1)S(1)} %shard_map.38.refs_2_, bf16[64,128,128]{2,1,0:T(8,128)(2,1)S(1)} %shard_map.39.refs_2_.refs_3_, ...), custom_call_target="tpu_custom_call", output_to_operand_aliasing={{}: (6, {})} | custom-call | flops 1048576 | bytes 65536 | tf_op jit(solution)/shard_map/pallas_call | solution.py:154
  74.7 0.0 collective-permute-done.6.refs_4_
  74.7 0.0 collective-permute-done.7.refs_5_
  74.7 1.2 %shard_map.45 = f32[2,8,64,128]{3,2,1,0:T(8,128)S(1)} custom-call(s32[3]{0:T(128)S(1)} %pad_add_fusion.refs_0_, s32[16,16]{1,0:T(8,128)S(1)} %convert_bitcast_fusion.refs_1_, bf16[64,128,128]{2,1,0:T(8,128)(2,1)S(1)} %shard_map.38.refs_2_, bf16[64,128,128]{2,1,0:T(8,128)(2,1)S(1)} %shard_map.39.refs_2_.refs_3_, ...), custom_call_target="tpu_custom_call", output_to_operand_aliasing={{}: (6, {})} | custom-call | flops 1048576 | bytes 65536 | tf_op jit(solution)/shard_map/pallas_call | solution.py:154
  75.9 8.5 %collective-permute-start.10 = (f32[8,64,128]{2,1,0:T(8,128)S(1)}, f32[8,64,128]{2,1,0:T(8,128)S(1)}, u32[]{:S(2)}, u32[]{:S(2)}) collective-permute-start(f32[8,64,128]{2,1,0:T(8,128)S(1)} %slice_bitcast_fusion), channel_id=1, source_target_pairs={{0,1},{1,0},{2,3},{3,2},{4,5},{5,4},{6,7},{7,6},{8,9},{9,8},{10,11... | collective-permute-start | bytes 786440 | tf_op jit(solution)/shard_map/ppermute | solution.py:234
  84.4 1.2 %collective-permute-done.10 = f32[8,64,128]{2,1,0:T(8,128)S(1)} collective-permute-done((f32[8,64,128]{2,1,0:T(8,128)S(1)}, f32[8,64,128]{2,1,0:T(8,128)S(1)}, u32[]{:S(2)}, u32[]{:S(2)}) %collective-permute-start.10) | collective-permute-done | bytes 262176 | tf_op jit(solution)/shard_map/ppermute | solution.py:234
  85.6 15.0 %all_to_all.17 = f32[8,64,128]{2,1,0:T(8,128)S(1)} all-to-all(f32[8,64,128]{2,1,0:T(8,128)S(1)} %fusion), channel_id=1, replica_groups={{0,16,96,112,160,176,192,208},{32,48,64,80,128,144,224,240},{1,17,97,11..., dimensions={0} | all-to-all | bytes 524288 | tf_op jit(solution)/shard_map/all_to_all | solution.py:235
  100.6 0.6 reduce_sum.9
  (7 shorter events, 0.2 us)
Async XLA Ops:
  0.0 1.0 %copy-start.1 = (f32[2,1,1,16,4096]{4,3,2,1,0:T(8,128)S(1)}, f32[2,1,1,16,4096]{4,3,2,1,0:T(8,128)}, u32[]{:S(2)}) copy-start(f32[2,1,1,16,4096]{4,3,2,1,0:T(8,128)} %param.4) | copy-start | bytes 1572868
  1.0 0.7 copy-start.2
  2.4 43.0 %copy-start = (f32[64,4096]{1,0:T(8,128)S(1)}, f32[64,4096]{1,0:T(8,128)}, u32[]{:S(2)}) copy-start(f32[64,4096]{1,0:T(8,128)} %refs_0_.1) | copy-start | bytes 3145732
  45.3 1.2 %copy-start.3 = (f32[8,144,128]{2,1,0:T(8,128)}, f32[8,144,128]{2,1,0:T(8,128)S(1)}, u32[]{:S(2)}) copy-start(f32[8,144,128]{2,1,0:T(8,128)S(1)} %all_to_all.16) | copy-start | bytes 1769476
  45.3 21.8 %collective-permute-start = (f32[64,4096]{1,0:T(8,128)S(1)}, f32[64,4096]{1,0:T(8,128)}, u32[]{:S(2)}, u32[]{:S(2)}) collective-permute-start(f32[64,4096]{1,0:T(8,128)S(1)} %copy-done), channel_id=1, source_target_pairs={{0,32},{16,48},{32,0},{48,16},{64,96},{80,112},{96,64},{112,80},{1... | collective-permute-start | bytes 3145736 | tf_op jit(solution)/shard_map/ppermute | solution.py:183
  45.6 9.6 %collective-permute-start.3 = (f32[1024,128]{1,0:T(8,128)S(1)}, f32[1024,128]{1,0:T(8,128)S(1)}, u32[]{:S(2)}, u32[]{:S(2)}) collective-permute-start(f32[1024,128]{1,0:T(8,128)S(1)} %bitcast.24), channel_id=1, source_target_pairs={{0,12},{2,14},{4,0},{6,2},{8,4},{10,6},{12,8},{14,10},{1,13},{3,15... | collective-permute-start | bytes 1572872 | tf_op jit(solution)/shard_map/ppermute | solution.py:183
  46.4 10.5 %collective-permute-start.2 = (f32[1024,128]{1,0:T(8,128)S(1)}, f32[1024,128]{1,0:T(8,128)S(1)}, u32[]{:S(2)}, u32[]{:S(2)}) collective-permute-start(f32[1024,128]{1,0:T(8,128)S(1)} %bitcast.25), channel_id=1, source_target_pairs={{0,4},{2,6},{4,8},{6,10},{8,12},{10,14},{12,0},{14,2},{1,5},{3,7},... | collective-permute-start | bytes 1572872 | tf_op jit(solution)/shard_map/ppermute | solution.py:183
  47.1 9.9 %collective-permute-start.1 = (f32[1024,128]{1,0:T(8,128)S(1)}, f32[1024,128]{1,0:T(8,128)S(1)}, u32[]{:S(2)}, u32[]{:S(2)}) collective-permute-start(f32[1024,128]{1,0:T(8,128)S(1)} %bitcast.26), channel_id=1, source_target_pairs={{0,2},{2,0},{4,6},{6,4},{8,10},{10,8},{12,14},{14,12},{1,3},{3,1},... | collective-permute-start | bytes 1572872 | tf_op jit(solution)/shard_map/ppermute | solution.py:183
  57.0 5.7 %collective-permute-start.5 = (f32[512,128]{1,0:T(8,128)S(1)}, f32[512,128]{1,0:T(8,128)S(1)}, u32[]{:S(2)}, u32[]{:S(2)}) collective-permute-start(f32[512,128]{1,0:T(8,128)S(1)} %slice.21), channel_id=1, source_target_pairs={{0,12},{2,14},{4,0},{6,2},{8,4},{10,6},{12,8},{14,10},{1,13},{3,15... | collective-permute-start | bytes 786440 | tf_op jit(solution)/shard_map/ppermute | solution.py:183
  58.4 6.4 %collective-permute-start.4 = (f32[512,128]{1,0:T(8,128)S(1)}, f32[512,128]{1,0:T(8,128)S(1)}, u32[]{:S(2)}, u32[]{:S(2)}) collective-permute-start(f32[512,128]{1,0:T(8,128)S(1)} %slice.20), channel_id=1, source_target_pairs={{0,4},{2,6},{4,8},{6,10},{8,12},{10,14},{12,0},{14,2},{1,5},{3,7},... | collective-permute-start | bytes 786440 | tf_op jit(solution)/shard_map/ppermute | solution.py:183
  58.6 13.3 %collective-permute-start.9 = (f32[1024,128]{1,0:T(8,128)S(1)}, f32[1024,128]{1,0:T(8,128)S(1)}, u32[]{:S(2)}, u32[]{:S(2)}) collective-permute-start(f32[1024,128]{1,0:T(8,128)S(1)} %collective-permute-done.1.refs_3_.refs_4_), channel_id=1, source_target_pairs={{0,12},{2,14},{4,0},{6,2},{8,4},{10,6},{12,8},{14,10},{1,13},{3,15... | collective-permute-start | bytes 1572872 | tf_op jit(solution)/shard_map/ppermute | solution.py:183
  61.1 12.1 %collective-permute-start.8 = (f32[1024,128]{1,0:T(8,128)S(1)}, f32[1024,128]{1,0:T(8,128)S(1)}, u32[]{:S(2)}, u32[]{:S(2)}) collective-permute-start(f32[1024,128]{1,0:T(8,128)S(1)} %collective-permute-done.1.refs_3_.refs_4_), channel_id=1, source_target_pairs={{0,4},{2,6},{4,8},{6,10},{8,12},{10,14},{12,0},{14,2},{1,5},{3,7},... | collective-permute-start | bytes 1572872 | tf_op jit(solution)/shard_map/ppermute | solution.py:183
  64.8 9.8 %collective-permute-start.6 = (f32[512,128]{1,0:T(8,128)S(1)}, f32[512,128]{1,0:T(8,128)S(1)}, u32[]{:S(2)}, u32[]{:S(2)}) collective-permute-start(f32[512,128]{1,0:T(8,128)S(1)} %collective-permute-done.4.refs_4_), channel_id=1, source_target_pairs={{0,2},{2,0},{4,6},{6,4},{8,10},{10,8},{12,14},{14,12},{1,3},{3,1},... | collective-permute-start | bytes 786440 | tf_op jit(solution)/shard_map/ppermute | solution.py:183
  65.4 9.2 %collective-permute-start.7 = (f32[512,128]{1,0:T(8,128)S(1)}, f32[512,128]{1,0:T(8,128)S(1)}, u32[]{:S(2)}, u32[]{:S(2)}) collective-permute-start(f32[512,128]{1,0:T(8,128)S(1)} %collective-permute-done.5.refs_5_), channel_id=1, source_target_pairs={{0,2},{2,0},{4,6},{6,4},{8,10},{10,8},{12,14},{14,12},{1,3},{3,1},... | collective-permute-start | bytes 786440 | tf_op jit(solution)/shard_map/ppermute | solution.py:183
  75.9 9.7 %collective-permute-start.10 = (f32[8,64,128]{2,1,0:T(8,128)S(1)}, f32[8,64,128]{2,1,0:T(8,128)S(1)}, u32[]{:S(2)}, u32[]{:S(2)}) collective-permute-start(f32[8,64,128]{2,1,0:T(8,128)S(1)} %slice_bitcast_fusion), channel_id=1, source_target_pairs={{0,1},{1,0},{2,3},{3,2},{4,5},{5,4},{6,7},{7,6},{8,9},{9,8},{10,11... | collective-permute-start | bytes 786440 | tf_op jit(solution)/shard_map/ppermute | solution.py:234

commit v9 on v8

--- a/solution.py
+++ b/solution.py
@@ -8,7 +8,7 @@
 TILE = 64
 AB_DEV = 128
 LANES = 128
-GROUP = 2
+GROUP = 4
 HALF = TILE // 2
 VMEM = pl.BlockSpec(memory_space=pltpu.VMEM)
 SMEM = pl.BlockSpec(memory_space=pltpu.SMEM)
@@ -159,41 +159,96 @@
         input_output_aliases={} if sums is None else {len(given) - 1: 0},
         compiler_params=pltpu.CompilerParams(vmem_limit_bytes=14 * 2**20),
         cost_estimate=pl.CostEstimate(
-            flops=2**20,
-            bytes_accessed=2**16,
+            flops=2**12,
+            bytes_accessed=2**10,
             transcendentals=0,
         ),
     )(*given)
 
 
+def sort_kernel(rows, slots, place, parts, *chunks):
+    m = place[3]
+    for k in range(len(chunks)):
+        for n in range(GROUP):
+            base = n * (rows + 8)
+            chunks[k][n * rows : (n + 1) * rows] = parts[m ^ k, base : base + rows]
+        at = lax.broadcasted_iota(jnp.int32, (8, LANES), 0)
+        spots = jnp.zeros((8, LANES), jnp.float32)
+        for n in range(GROUP):
+            base = n * (rows + 8) + rows
+            spots = jnp.where(at == n, parts[m ^ k, base : base + 8], spots)
+        chunks[k][GROUP * rows :] = spots
+
+
+def sort(place, parts, blocks, rows, slots):
+    def kernel(*refs):
+        sort_kernel(rows, slots, *refs)
+
+    return pl.pallas_call(
+        kernel,
+        out_shape=[jax.ShapeDtypeStruct((GROUP * rows + 8, LANES), jnp.float32)] * blocks,
+        in_specs=[SMEM, VMEM],
+        out_specs=[VMEM] * blocks,
+        compiler_params=pltpu.CompilerParams(vmem_limit_bytes=14 * 2**20),
+        cost_estimate=pl.CostEstimate(flops=0, bytes_accessed=2**16, transcendentals=0),
+    )(place, parts)
+
+
+def join_kernel(*refs):
+    *chunks, own, spots = refs
+    for k, chunk in enumerate(chunks):
+        size = chunk.shape[0] - 8
+        own[k * size : (k + 1) * size] = chunk[:size]
+        spots[k] = chunk[size:].astype(jnp.int32)
+
+
+def join(chunks):
+    size = chunks[0].shape[0] - 8
+    return pl.pallas_call(
+        join_kernel,
+        out_shape=[
+            jax.ShapeDtypeStruct((len(chunks) * size, LANES), jnp.float32),
+            jax.ShapeDtypeStruct((len(chunks), 8, LANES), jnp.int32),
+        ],
+        in_specs=[VMEM] * len(chunks),
+        out_specs=[VMEM] * 2,
+        compiler_params=pltpu.CompilerParams(vmem_limit_bytes=14 * 2**20),
+        cost_estimate=pl.CostEstimate(flops=0, bytes_accessed=2**16, transcendentals=0),
+    )(*chunks)
+
+
 def on_device(t_amps, v_tiles, v_where):
     cols = lax.axis_size("col")
     rows_axis = lax.axis_size("row")
-    held, slots = v_tiles.shape[0], v_tiles.shape[3]
+    slots = v_tiles.shape[3]
     pair = slots // cols
     rows = pair * HALF
     blocks = rows_axis // GROUP
-    ranks = [
-        [2 * (GROUP * m + (m.bit_count() + odd) % 2) + x for m in range(blocks // 2) for x in range(2)]
-        for odd in range(2)
-    ]
-    place = jnp.stack([lax.axis_index("col"), lax.axis_index("layer"), lax.axis_index("row") // 2 % GROUP])
+    row = lax.axis_index("row")
+    place = jnp.stack([lax.axis_index("col"), lax.axis_index("layer"), row % GROUP, row // GROUP])
 
     def send(share, to, axis="col", size=cols):
         return lax.ppermute(share, axis, [(i, to(i)) for i in range(size)])
 
-    def send_t(t_block):
-        return send(t_block, lambda i: i ^ 2, "row", rows_axis)
-
+    def send_t(t_block, offset):
+        return send(t_block, lambda i: i ^ offset, "row", rows_axis)
+
+    def send_m(chunk, k):
+        def to(i):
+            return i ^ (GROUP * k) ^ (2 * (k.bit_count() % 2))
+
+        return send(chunk, to, "row", rows_axis)
+
+    t_one, t_two = send_t(t_amps, 1), send_t(t_amps, 2)
     parts = pack(v_tiles, v_where, cols)
     parts = lax.all_to_all(parts, "col", 0, 0, tiled=True)
-    parts = parts.reshape(blocks // 2, GROUP, 2, rows + 8, LANES).transpose(0, 2, 1, 3, 4)
+    parts, t_two = lax.optimization_barrier((parts, t_two))
     parts = parts.reshape(blocks, GROUP * (rows + 8), LANES)
-    parts = lax.all_to_all(parts, "row", 0, 0, tiled=True, axis_index_groups=ranks)
-    parts = parts.reshape(blocks * GROUP, rows + 8, LANES)
-    spots = parts[:, rows, :slots].astype(jnp.int32)
-    own = parts[:, :rows].reshape(blocks * GROUP * rows, LANES)
-    own, t_other = lax.optimization_barrier((own, t_amps))
+    chunks = sort(place, parts, blocks, rows, slots)
+    chunks = [chunks[0]] + [send_m(chunks[k], k) for k in range(1, blocks)]
+    own, spots = join(chunks)
+    spots = spots[:, :GROUP, :slots].reshape(blocks * GROUP, slots)
+    own, t_one = lax.optimization_barrier((own, t_one))
 
     def up(i):
         return (i + 2) % cols
@@ -211,29 +266,35 @@
     partner = send(own, across)
     below = send(own, up)
     above = send(own, down)
-    t_other = send_t(t_other)
-    tiles = {0: prepare(t_amps)}
-    sums = add(None, tiles, ((0, 0, 0), own))
+    t_three = send_t(t_one, 2)
+    early = {0: prepare(t_amps), 2: prepare(t_two)}
+    sums = add(None, early, ((0, 0, 0), own))
     sums, partner, below, above = lax.optimization_barrier((sums, partner, below, above))
     far_low = send(below[:half], up)
     far_high = send(above[half:], down)
     partner_below = send(partner, up)
     partner_above = send(partner, down)
     near = [((0, 0, 0), own), ((0, 0, 1), partner), ((0, -2, 0), below), ((0, 2, 0), above)]
-    sums = add(sums, tiles, *near[1:])
+    sums = add(sums, early, *near[1:])
     sums, far_low, far_high = lax.optimization_barrier((sums, far_low, far_high))
     partner_far_low = send(far_low, across)
     partner_far_high = send(far_high, across)
-    other = {1: prepare(t_other)}
-    sums = add(sums, other, *near)
-    both = {**tiles, **other}
-    sums = add(sums, both, ((0, 4, 0), far_low), ((middle, 4, 0), far_high))
-    sums = add(sums, both, ((0, -2, 1), partner_below), ((0, 2, 1), partner_above))
-    sums = add(sums, both, ((0, 4, 1), partner_far_low), ((middle, 4, 1), partner_far_high))
+    one = {1: prepare(t_one)}
+    most = {**early, **one}
+    far = [((0, 4, 0), far_low), ((middle, 4, 0), far_high)]
+    beside = [((0, -2, 1), partner_below), ((0, 2, 1), partner_above)]
+    last = [((0, 4, 1), partner_far_low), ((middle, 4, 1), partner_far_high)]
+    sums = add(sums, one, *near)
+    sums = add(sums, most, *far)
+    sums = add(sums, most, *beside)
+    sums, t_three = lax.optimization_barrier((sums, t_three))
+    three = {3: prepare(t_three)}
+    sums = add(sums, three, *near, *far, *beside)
+    sums = add(sums, {**most, **three}, *last)
 
     sums = sums[0] + lax.ppermute(sums[1], "layer", [(0, 1), (1, 0)])
-    sums = lax.all_to_all(sums, "row", 0, 0, tiled=True, axis_index_groups=ranks)
-    return jnp.sum(sums, axis=0)
+    received = [send_m(sums[k], k) for k in range(1, blocks)]
+    return sum(received, sums[0])
 
 
 def solution(mesh):

time: 102 us -> 113 us (1.11)
  blocking collectives: 57.8 us -> 0 us
  waiting for transfers between devices: 12.9 us -> 55.4 us
  starting transfers between devices: 15.8 us -> 39.3 us
  Pallas kernels: 11.2 us -> 15 us
    all_to_all x3 -> x0, blocking collectives: 57.8 us -> none  [the longest x1 27.2 us: on_device(): lax.all_to_all(parts, 'row', 0, 0, tiled=True, axis_index_groups=ranks)]
    all_to_all x0 -> x1, waiting for transfers between devices: none -> 24 us  [on_device(): parts = lax.all_to_all(parts, 'col', 0, 0, tiled=True)]
    ppermute x10 -> x18, starting transfers between devices: 7.25 us -> 30.4 us  [send(): return lax.ppermute(share, axis, [(i, to(i)) for i in range(size)])]
    ppermute x10 -> x18, waiting for transfers between devices: 11.7 us -> 30.4 us  [send(): return lax.ppermute(share, axis, [(i, to(i)) for i in range(size)])]
    all_to_all x0 -> x1, starting transfers between devices: none -> 4.22 us  [on_device(): parts = lax.all_to_all(parts, 'col', 0, 0, tiled=True)]
    ppermute x1, starting transfers between devices: 8.52 us -> 4.76 us  [on_device(): sums = sums[0] + lax.ppermute(sums[1], 'layer', [(0, 1), (1, 0)])]
    pallas_call x2 -> x4, Pallas kernels: 2.63 us -> 4.03 us  [prepare(): pl.pallas_call(prepare_kernel, out_shape=jax.ShapeDtypeStruct((cd // TILE...]
    pallas_call x6 -> x7, Pallas kernels: 7.9 us -> 8.8 us  [contract(): pl.pallas_call(kernel, out_shape=jax.ShapeDtypeStruct((2, blocks, ij, LAN...]
  transfers between devices with their start and end apart: 11 -> 20, of which waited for: 7 -> 10; matrix products, arithmetic and copies ran while one was open for 1% -> 0% of each run, Pallas kernels for 9% -> 12%
where the time goes in v9:
time: 113 us; the launch traced here: 112 us
  waiting for transfers between devices  55.4 us (49%)
  starting transfers between devices  39.3 us (35%)
  Pallas kernels  15 us (13%)
  local copies, waits for them, and re-layouts  1.78 us (2%)
    ppermute x18, waiting for transfers between devices, send(): return lax.ppermute(share, axis, [(i, to(i)) for i in range(size)])  30.4 us
    ppermute x18, starting transfers between devices, send(): return lax.ppermute(share, axis, [(i, to(i)) for i in range(size)])  30.4 us
    all_to_all x1, waiting for transfers between devices, on_device(): parts = lax.all_to_all(parts, 'col', 0, 0, tiled=True)  24 us
    pallas_call x7, Pallas kernels, contract(): pl.pallas_call(kernel, out_shape=jax.ShapeDtypeStruct((2, blocks, ij, LAN...  8.8 us
    ppermute x1, starting transfers between devices, on_device(): sums = sums[0] + lax.ppermute(sums[1], 'layer', [(0, 1), (1, 0)])  4.76 us
    all_to_all x1, starting transfers between devices, on_device(): parts = lax.all_to_all(parts, 'col', 0, 0, tiled=True)  4.22 us
    pallas_call x4, Pallas kernels, prepare(): pl.pallas_call(prepare_kernel, out_shape=jax.ShapeDtypeStruct((cd // TILE...  4.03 us
  transfers between devices with their start and end apart: 20, of which 10 were waited for; matrix products, arithmetic and copies ran while one was open for 0% of the time, Pallas kernels for 12%

profile of v9, /device:TPU:1, one launch (start us, length us, event | category | flops | bytes accessed | tf_op | source)
XLA Modules:
  0.0 112.4 jit_solution(18056132044920894944)
XLA Ops:
  0.0 0.0 copy-start
  0.0 2.5 %collective-permute-start = (f32[64,4096]{1,0:T(8,128)}, f32[64,4096]{1,0:T(8,128)}, u32[]{:S(2)}, u32[]{:S(2)}) collective-permute-start(f32[64,4096]{1,0:T(8,128)} %refs_0_.1), channel_id=1, source_target_pairs={{0,32},{16,48},{32,0},{48,16},{64,96},{80,112},{96,64},{112,80},{1... | collective-permute-start | bytes 3145736 | tf_op jit(solution)/shard_map/ppermute | solution.py:231
  2.5 2.7 %collective-permute-start.4 = (f32[64,4096]{1,0:T(8,128)}, f32[64,4096]{1,0:T(8,128)S(1)}, u32[]{:S(2)}, u32[]{:S(2)}) collective-permute-start(f32[64,4096]{1,0:T(8,128)} %refs_0_.1), channel_id=1, source_target_pairs={{0,16},{16,0},{32,48},{48,32},{64,80},{80,64},{96,112},{112,96},{1... | collective-permute-start | bytes 3145736 | tf_op jit(solution)/shard_map/ppermute | solution.py:231
  5.2 0.0 copy-start.1
  5.2 1.0 copy-done.1
  6.3 0.0 copy-start.2
  6.3 0.7 copy-done.2
  6.9 1.5 %shard_map.37 = f32[8,144,128]{2,1,0:T(8,128)} custom-call(s32[2,16]{1,0:T(2,128)S(1)} %bitcast.41, f32[2,2,256,128]{3,2,1,0:T(8,128)S(1)} %bitcast.33), custom_call_target="tpu_custom_call" | custom-call | bytes 1048576 | tf_op jit(solution)/shard_map/pallas_call | solution.py:44
  8.4 4.2 %all-to-all-start = ((f32[8,144,128]{2,1,0:T(8,128)}), f32[8,144,128]{2,1,0:T(8,128)S(1)}, u32[]{:S(2)}, u32[]{:S(2)}) async-start(f32[8,144,128]{2,1,0:T(8,128)} %shard_map.37), calls=%async_computation | async-start | bytes 1179648 | tf_op jit(solution)/shard_map/all_to_all | solution.py:244
  12.7 0.1 pad_add_fusion.refs_0_
  12.7 24.0 %all-to-all-done = f32[8,144,128]{2,1,0:T(8,128)S(1)} async-done(((f32[8,144,128]{2,1,0:T(8,128)}), f32[8,144,128]{2,1,0:T(8,128)S(1)}, u32[]{:S(2)}, u32[]{:S(2)}) %all-to-all-start) | async-done | bytes 589856 | tf_op jit(solution)/shard_map/all_to_all | solution.py:244
  36.7 0.0 collective-permute-done.refs_0_
  36.7 0.6 shard_map.38
  37.3 2.9 %collective-permute-start.1 = (f32[264,128]{1,0:T(8,128)S(1)}, f32[264,128]{1,0:T(8,128)S(1)}, u32[]{:S(2)}, u32[]{:S(2)}) collective-permute-start(f32[264,128]{1,0:T(8,128)S(1)} %get-tuple-element.26), channel_id=1, source_target_pairs={{0,96},{16,112},{32,64},{48,80},{64,32},{80,48},{96,0},{112,16},{1... | collective-permute-start | bytes 405512 | tf_op jit(solution)/shard_map/ppermute | solution.py:231
  40.2 3.5 %collective-permute-start.2 = (f32[264,128]{1,0:T(8,128)S(1)}, f32[264,128]{1,0:T(8,128)S(1)}, u32[]{:S(2)}, u32[]{:S(2)}) collective-permute-start(f32[264,128]{1,0:T(8,128)S(1)} %get-tuple-element.27), channel_id=1, source_target_pairs={{0,160},{16,176},{32,128},{48,144},{64,224},{80,240},{96,192},{112... | collective-permute-start | bytes 405512 | tf_op jit(solution)/shard_map/ppermute | solution.py:231
  43.7 0.0 collective-permute-start.3
  43.7 0.0 collective-permute-done.1.refs_1_
  43.7 10.1 %collective-permute-done.2.refs_2_ = f32[264,128]{1,0:T(8,128)S(1)} collective-permute-done((f32[264,128]{1,0:T(8,128)S(1)}, f32[264,128]{1,0:T(8,128)S(1)}, u32[]{:S(2)}, u32[]{:S(2)}) %collective-permute-start.2) | collective-permute-done | bytes 135200 | tf_op jit(solution)/shard_map/ppermute | solution.py:231
  53.8 0.4 collective-permute-done.3.refs_3_
  54.3 0.0 collective-permute-done.4.refs_0_
  54.3 0.1 collective-permute-start.5
  54.4 0.1 collective-permute-start.6
  54.5 2.7 %collective-permute-start.7 = (f32[1024,128]{1,0:T(8,128)S(1)}, f32[1024,128]{1,0:T(8,128)S(1)}, u32[]{:S(2)}, u32[]{:S(2)}) collective-permute-start(f32[1024,128]{1,0:T(8,128)S(1)} %get-tuple-element.33.refs_4_.refs_3_), channel_id=1, source_target_pairs={{0,12},{2,14},{4,0},{6,2},{8,4},{10,6},{12,8},{14,10},{1,13},{3,15... | collective-permute-start | bytes 1572872 | tf_op jit(solution)/shard_map/ppermute | solution.py:231
  57.2 3.2 %collective-permute-start.12 = (f32[64,4096]{1,0:T(8,128)S(1)}, f32[64,4096]{1,0:T(8,128)S(1)}, u32[]{:S(2)}, u32[]{:S(2)}) collective-permute-start(f32[64,4096]{1,0:T(8,128)S(1)} %collective-permute-done.4.refs_0_), channel_id=1, source_target_pairs={{0,32},{16,48},{32,0},{48,16},{64,96},{80,112},{96,64},{112,80},{1... | collective-permute-start | bytes 3145736 | tf_op jit(solution)/shard_map/ppermute | solution.py:231
  60.4 0.0 copy-done
  60.4 0.7 shard_map.40.refs_2_
  61.1 1.9 %shard_map.41.refs_3_ = bf16[64,128,128]{2,1,0:T(8,128)(2,1)S(1)} custom-call(f32[64,4096]{1,0:T(8,128)} %collective-permute-done.refs_0_), custom_call_target="tpu_custom_call" | custom-call | flops 268435456 | bytes 3145728 | tf_op jit(solution)/shard_map/pallas_call | solution.py:70
  63.0 1.1 shard_map.43.refs_7_
  64.1 1.8 %collective-permute-done.5.refs_4_ = f32[1024,128]{1,0:T(8,128)S(1)} collective-permute-done((f32[1024,128]{1,0:T(8,128)S(1)}, f32[1024,128]{1,0:T(8,128)S(1)}, u32[]{:S(2)}, u32[]{:S(2)}) %collective-permute-start.5) | collective-permute-done | bytes 524320 | tf_op jit(solution)/shard_map/ppermute | solution.py:231
  65.9 1.3 %collective-permute-done.6.refs_5_ = f32[1024,128]{1,0:T(8,128)S(1)} collective-permute-done((f32[1024,128]{1,0:T(8,128)S(1)}, f32[1024,128]{1,0:T(8,128)S(1)}, u32[]{:S(2)}, u32[]{:S(2)}) %collective-permute-start.6) | collective-permute-done | bytes 524320 | tf_op jit(solution)/shard_map/ppermute | solution.py:231
  67.2 0.0 collective-permute-done.7.refs_6_
  67.2 0.0 collective-permute-start.8
  67.2 2.7 %collective-permute-start.9 = (f32[1024,128]{1,0:T(8,128)S(1)}, f32[1024,128]{1,0:T(8,128)S(1)}, u32[]{:S(2)}, u32[]{:S(2)}) collective-permute-start(f32[1024,128]{1,0:T(8,128)S(1)} %collective-permute-done.5.refs_4_), channel_id=1, source_target_pairs={{0,12},{2,14},{4,0},{6,2},{8,4},{10,6},{12,8},{14,10},{1,13},{3,15... | collective-permute-start | bytes 1572872 | tf_op jit(solution)/shard_map/ppermute | solution.py:231
  69.9 0.1 collective-permute-start.10
  70.0 2.7 %collective-permute-start.11 = (f32[512,128]{1,0:T(8,128)S(1)}, f32[512,128]{1,0:T(8,128)S(1)}, u32[]{:S(2)}, u32[]{:S(2)}) collective-permute-start(f32[512,128]{1,0:T(8,128)S(1)} %slice.29), channel_id=1, source_target_pairs={{0,12},{2,14},{4,0},{6,2},{8,4},{10,6},{12,8},{14,10},{1,13},{3,15... | collective-permute-start | bytes 786440 | tf_op jit(solution)/shard_map/ppermute | solution.py:231
  72.8 1.4 %shard_map.44.refs_7_ = f32[2,4,64,128]{3,2,1,0:T(8,128)S(1)} custom-call(s32[4]{0:T(128)S(1)} %pad_add_fusion.refs_0_, s32[16,16]{1,0:T(8,128)S(1)} %bitcast.35, bf16[64,128,128]{2,1,0:T(8,128)(2,1)S(1)} %shard_map.40.refs_2_, bf16[64,128,128]{2,1,0:T(8,128)(2,1)S(1)} %shard_map.41.refs_3_, ...), custom_call_target="tpu_custom_call", output_to_operand_aliasing={{}: (7, {})} | custom-call | flops 4096 | bytes 1024 | tf_op jit(solution)/shard_map/pallas_call | solution.py:154
  74.2 10.5 %collective-permute-done.10.refs_5_.refs_7_ = f32[512,128]{1,0:T(8,128)S(1)} collective-permute-done((f32[512,128]{1,0:T(8,128)S(1)}, f32[512,128]{1,0:T(8,128)S(1)}, u32[]{:S(2)}, u32[]{:S(2)}) %collective-permute-start.10) | collective-permute-done | bytes 262176 | tf_op jit(solution)/shard_map/ppermute | solution.py:231
  84.6 0.0 collective-permute-done.11.refs_6_.refs_8_
  84.6 0.8 collective-permute-start.13
  85.5 0.7 collective-permute-start.14
  86.1 0.7 shard_map.42.refs_2_.refs_4_
  86.8 1.2 %shard_map.45.refs_7_ = f32[2,4,64,128]{3,2,1,0:T(8,128)S(1)} custom-call(s32[4]{0:T(128)S(1)} %pad_add_fusion.refs_0_, s32[16,16]{1,0:T(8,128)S(1)} %bitcast.36, bf16[64,128,128]{2,1,0:T(8,128)(2,1)S(1)} %shard_map.42.refs_2_.refs_4_, f32[1024,128]{1,0:T(8,128)S(1)} %get-tuple-element.33.refs_4_.refs_3_, ...), custom_call_target="tpu_custom_call", output_to_operand_aliasing={{}: (7, {})} | custom-call | flops 4096 | bytes 1024 | tf_op jit(solution)/shard_map/pallas_call | solution.py:154
  88.0 1.1 %shard_map.46.refs_7_ = f32[2,4,64,128]{3,2,1,0:T(8,128)S(1)} custom-call(s32[4]{0:T(128)S(1)} %pad_add_fusion.refs_0_, s32[16,16]{1,0:T(8,128)S(1)} %bitcast.37, bf16[64,128,128]{2,1,0:T(8,128)(2,1)S(1)} %shard_map.40.refs_2_, bf16[64,128,128]{2,1,0:T(8,128)(2,1)S(1)} %shard_map.41.refs_3_, ...), custom_call_target="tpu_custom_call", output_to_operand_aliasing={{}: (7, {})} | custom-call | flops 4096 | bytes 1024 | tf_op jit(solution)/shard_map/pallas_call | solution.py:154
  89.2 0.0 collective-permute-done.8.refs_5_.refs_9_
  89.2 0.0 collective-permute-done.9.refs_6_.refs_10_
  89.2 1.4 %shard_map.47.refs_11_ = f32[2,4,64,128]{3,2,1,0:T(8,128)S(1)} custom-call(s32[4]{0:T(128)S(1)} %pad_add_fusion.refs_0_, s32[16,16]{1,0:T(8,128)S(1)} %bitcast.38, bf16[64,128,128]{2,1,0:T(8,128)(2,1)S(1)} %shard_map.40.refs_2_, bf16[64,128,128]{2,1,0:T(8,128)(2,1)S(1)} %shard_map.41.refs_3_, ...), custom_call_target="tpu_custom_call", output_to_operand_aliasing={{}: (7, {})} | custom-call | flops 4096 | bytes 1024 | tf_op jit(solution)/shard_map/pallas_call | solution.py:154
  90.6 0.0 collective-permute-done.12.refs_0_
  90.6 0.7 shard_map.48.refs_2_.refs_5_
  91.3 1.4 %shard_map.49.refs_8_ = f32[2,4,64,128]{3,2,1,0:T(8,128)S(1)} custom-call(s32[4]{0:T(128)S(1)} %pad_add_fusion.refs_0_, s32[16,16]{1,0:T(8,128)S(1)} %bitcast.39, bf16[64,128,128]{2,1,0:T(8,128)(2,1)S(1)} %shard_map.48.refs_2_.refs_5_, f32[1024,128]{1,0:T(8,128)S(1)} %get-tuple-element.33.refs_4_.refs_3_, ...), custom_call_target="tpu_custom_call", output_to_operand_aliasing={{}: (11, {})} | custom-call | flops 4096 | bytes 1024 | tf_op jit(solution)/shard_map/pallas_call | solution.py:154
  92.8 0.0 collective-permute-done.13.refs_6_
  92.8 1.5 %collective-permute-done.14.refs_7_ = f32[512,128]{1,0:T(8,128)S(1)} collective-permute-done((f32[512,128]{1,0:T(8,128)S(1)}, f32[512,128]{1,0:T(8,128)S(1)}, u32[]{:S(2)}, u32[]{:S(2)}) %collective-permute-start.14) | collective-permute-done | bytes 262176 | tf_op jit(solution)/shard_map/ppermute | solution.py:231
  94.3 1.2 %shard_map.50 = f32[2,4,64,128]{3,2,1,0:T(8,128)S(1)} custom-call(s32[4]{0:T(128)S(1)} %pad_add_fusion.refs_0_, s32[16,16]{1,0:T(8,128)S(1)} %bitcast.40, bf16[64,128,128]{2,1,0:T(8,128)(2,1)S(1)} %shard_map.40.refs_2_, bf16[64,128,128]{2,1,0:T(8,128)(2,1)S(1)} %shard_map.41.refs_3_, ...), custom_call_target="tpu_custom_call", output_to_operand_aliasing={{}: (8, {})} | custom-call | flops 4096 | bytes 1024 | tf_op jit(solution)/shard_map/pallas_call | solution.py:154
  95.5 4.8 %collective-permute-start.15 = (f32[4,64,128]{2,1,0:T(8,128)S(1)}, f32[4,64,128]{2,1,0:T(8,128)S(1)}, u32[]{:S(2)}, u32[]{:S(2)}) collective-permute-start(f32[4,64,128]{2,1,0:T(8,128)S(1)} %slice_bitcast_fusion), channel_id=1, source_target_pairs={{0,1},{1,0},{2,3},{3,2},{4,5},{5,4},{6,7},{7,6},{8,9},{9,8},{10,11... | collective-permute-start | bytes 393224 | tf_op jit(solution)/shard_map/ppermute | solution.py:295
  100.3 1.0 collective-permute-done.15
  101.3 1.2 %collective-permute-start.16 = (f32[64,128]{1,0:T(8,128)S(1)}, f32[64,128]{1,0:T(8,128)S(1)}, u32[]{:S(2)}, u32[]{:S(2)}) collective-permute-start(f32[64,128]{1,0:T(8,128)S(1)} %get-tuple-element.43), channel_id=1, source_target_pairs={{0,96},{16,112},{32,64},{48,80},{64,32},{80,48},{96,0},{112,16},{1... | collective-permute-start | bytes 98312 | tf_op jit(solution)/shard_map/ppermute | solution.py:231
  102.6 4.3 %collective-permute-start.17 = (f32[64,128]{1,0:T(8,128)S(1)}, f32[64,128]{1,0:T(8,128)S(1)}, u32[]{:S(2)}, u32[]{:S(2)}) collective-permute-start(f32[64,128]{1,0:T(8,128)S(1)} %get-tuple-element.45), channel_id=1, source_target_pairs={{0,160},{16,176},{32,128},{48,144},{64,224},{80,240},{96,192},{112... | collective-permute-start | bytes 98312 | tf_op jit(solution)/shard_map/ppermute | solution.py:231
  106.9 0.2 collective-permute-start.18
  107.1 0.0 collective-permute-done.16
  107.1 1.5 %collective-permute-done.17 = f32[64,128]{1,0:T(8,128)S(1)} collective-permute-done((f32[64,128]{1,0:T(8,128)S(1)}, f32[64,128]{1,0:T(8,128)S(1)}, u32[]{:S(2)}, u32[]{:S(2)}) %collective-permute-start.17) | collective-permute-done | bytes 32800 | tf_op jit(solution)/shard_map/ppermute | solution.py:231
  108.6 3.2 %collective-permute-done.18 = f32[64,128]{1,0:T(8,128)S(1)} collective-permute-done((f32[64,128]{1,0:T(8,128)S(1)}, f32[64,128]{1,0:T(8,128)S(1)}, u32[]{:S(2)}, u32[]{:S(2)}) %collective-permute-start.18) | collective-permute-done | bytes 32800 | tf_op jit(solution)/shard_map/ppermute | solution.py:231
  111.8 0.6 fusion.3
  (7 shorter events, 0.1 us)
Async XLA Ops:
  0.0 60.4 %copy-start = (f32[64,4096]{1,0:T(8,128)S(1)}, f32[64,4096]{1,0:T(8,128)}, u32[]{:S(2)}) copy-start(f32[64,4096]{1,0:T(8,128)} %refs_0_.1) | copy-start | bytes 3145732
  0.0 36.7 %collective-permute-start = (f32[64,4096]{1,0:T(8,128)}, f32[64,4096]{1,0:T(8,128)}, u32[]{:S(2)}, u32[]{:S(2)}) collective-permute-start(f32[64,4096]{1,0:T(8,128)} %refs_0_.1), channel_id=1, source_target_pairs={{0,32},{16,48},{32,0},{48,16},{64,96},{80,112},{96,64},{112,80},{1... | collective-permute-start | bytes 3145736 | tf_op jit(solution)/shard_map/ppermute | solution.py:231
  2.5 51.8 %collective-permute-start.4 = (f32[64,4096]{1,0:T(8,128)}, f32[64,4096]{1,0:T(8,128)S(1)}, u32[]{:S(2)}, u32[]{:S(2)}) collective-permute-start(f32[64,4096]{1,0:T(8,128)} %refs_0_.1), channel_id=1, source_target_pairs={{0,16},{16,0},{32,48},{48,32},{64,80},{80,64},{96,112},{112,96},{1... | collective-permute-start | bytes 3145736 | tf_op jit(solution)/shard_map/ppermute | solution.py:231
  5.2 1.0 copy-start.1
  6.3 0.7 copy-start.2
  8.4 28.3 %all-to-all-start = ((f32[8,144,128]{2,1,0:T(8,128)}), f32[8,144,128]{2,1,0:T(8,128)S(1)}, u32[]{:S(2)}, u32[]{:S(2)}) async-start(f32[8,144,128]{2,1,0:T(8,128)} %shard_map.37), calls=%async_computation | async-start | bytes 1179648 | tf_op jit(solution)/shard_map/all_to_all | solution.py:244
  37.3 6.4 %collective-permute-start.1 = (f32[264,128]{1,0:T(8,128)S(1)}, f32[264,128]{1,0:T(8,128)S(1)}, u32[]{:S(2)}, u32[]{:S(2)}) collective-permute-start(f32[264,128]{1,0:T(8,128)S(1)} %get-tuple-element.26), channel_id=1, source_target_pairs={{0,96},{16,112},{32,64},{48,80},{64,32},{80,48},{96,0},{112,16},{1... | collective-permute-start | bytes 405512 | tf_op jit(solution)/shard_map/ppermute | solution.py:231
  40.2 13.6 %collective-permute-start.2 = (f32[264,128]{1,0:T(8,128)S(1)}, f32[264,128]{1,0:T(8,128)S(1)}, u32[]{:S(2)}, u32[]{:S(2)}) collective-permute-start(f32[264,128]{1,0:T(8,128)S(1)} %get-tuple-element.27), channel_id=1, source_target_pairs={{0,160},{16,176},{32,128},{48,144},{64,224},{80,240},{96,192},{112... | collective-permute-start | bytes 405512 | tf_op jit(solution)/shard_map/ppermute | solution.py:231
  43.7 10.6 %collective-permute-start.3 = (f32[264,128]{1,0:T(8,128)S(1)}, f32[264,128]{1,0:T(8,128)S(1)}, u32[]{:S(2)}, u32[]{:S(2)}) collective-permute-start(f32[264,128]{1,0:T(8,128)S(1)} %get-tuple-element.28), channel_id=1, source_target_pairs={{0,192},{16,208},{32,224},{48,240},{64,128},{80,144},{96,160},{112... | collective-permute-start | bytes 405512 | tf_op jit(solution)/shard_map/ppermute | solution.py:231
  54.3 11.6 %collective-permute-start.5 = (f32[1024,128]{1,0:T(8,128)S(1)}, f32[1024,128]{1,0:T(8,128)S(1)}, u32[]{:S(2)}, u32[]{:S(2)}) collective-permute-start(f32[1024,128]{1,0:T(8,128)S(1)} %get-tuple-element.33.refs_4_.refs_3_), channel_id=1, source_target_pairs={{0,2},{2,0},{4,6},{6,4},{8,10},{10,8},{12,14},{14,12},{1,3},{3,1},... | collective-permute-start | bytes 1572872 | tf_op jit(solution)/shard_map/ppermute | solution.py:231
  54.4 12.8 %collective-permute-start.6 = (f32[1024,128]{1,0:T(8,128)S(1)}, f32[1024,128]{1,0:T(8,128)S(1)}, u32[]{:S(2)}, u32[]{:S(2)}) collective-permute-start(f32[1024,128]{1,0:T(8,128)S(1)} %get-tuple-element.33.refs_4_.refs_3_), channel_id=1, source_target_pairs={{0,4},{2,6},{4,8},{6,10},{8,12},{10,14},{12,0},{14,2},{1,5},{3,7},... | collective-permute-start | bytes 1572872 | tf_op jit(solution)/shard_map/ppermute | solution.py:231
  54.5 12.7 %collective-permute-start.7 = (f32[1024,128]{1,0:T(8,128)S(1)}, f32[1024,128]{1,0:T(8,128)S(1)}, u32[]{:S(2)}, u32[]{:S(2)}) collective-permute-start(f32[1024,128]{1,0:T(8,128)S(1)} %get-tuple-element.33.refs_4_.refs_3_), channel_id=1, source_target_pairs={{0,12},{2,14},{4,0},{6,2},{8,4},{10,6},{12,8},{14,10},{1,13},{3,15... | collective-permute-start | bytes 1572872 | tf_op jit(solution)/shard_map/ppermute | solution.py:231
  57.2 33.4 %collective-permute-start.12 = (f32[64,4096]{1,0:T(8,128)S(1)}, f32[64,4096]{1,0:T(8,128)S(1)}, u32[]{:S(2)}, u32[]{:S(2)}) collective-permute-start(f32[64,4096]{1,0:T(8,128)S(1)} %collective-permute-done.4.refs_0_), channel_id=1, source_target_pairs={{0,32},{16,48},{32,0},{48,16},{64,96},{80,112},{96,64},{112,80},{1... | collective-permute-start | bytes 3145736 | tf_op jit(solution)/shard_map/ppermute | solution.py:231
  67.2 22.0 %collective-permute-start.8 = (f32[1024,128]{1,0:T(8,128)S(1)}, f32[1024,128]{1,0:T(8,128)S(1)}, u32[]{:S(2)}, u32[]{:S(2)}) collective-permute-start(f32[1024,128]{1,0:T(8,128)S(1)} %collective-permute-done.5.refs_4_), channel_id=1, source_target_pairs={{0,4},{2,6},{4,8},{6,10},{8,12},{10,14},{12,0},{14,2},{1,5},{3,7},... | collective-permute-start | bytes 1572872 | tf_op jit(solution)/shard_map/ppermute | solution.py:231
  67.2 22.0 %collective-permute-start.9 = (f32[1024,128]{1,0:T(8,128)S(1)}, f32[1024,128]{1,0:T(8,128)S(1)}, u32[]{:S(2)}, u32[]{:S(2)}) collective-permute-start(f32[1024,128]{1,0:T(8,128)S(1)} %collective-permute-done.5.refs_4_), channel_id=1, source_target_pairs={{0,12},{2,14},{4,0},{6,2},{8,4},{10,6},{12,8},{14,10},{1,13},{3,15... | collective-permute-start | bytes 1572872 | tf_op jit(solution)/shard_map/ppermute | solution.py:231
  69.9 14.7 %collective-permute-start.10 = (f32[512,128]{1,0:T(8,128)S(1)}, f32[512,128]{1,0:T(8,128)S(1)}, u32[]{:S(2)}, u32[]{:S(2)}) collective-permute-start(f32[512,128]{1,0:T(8,128)S(1)} %slice.28), channel_id=1, source_target_pairs={{0,4},{2,6},{4,8},{6,10},{8,12},{10,14},{12,0},{14,2},{1,5},{3,7},... | collective-permute-start | bytes 786440 | tf_op jit(solution)/shard_map/ppermute | solution.py:231
  70.0 14.6 %collective-permute-start.11 = (f32[512,128]{1,0:T(8,128)S(1)}, f32[512,128]{1,0:T(8,128)S(1)}, u32[]{:S(2)}, u32[]{:S(2)}) collective-permute-start(f32[512,128]{1,0:T(8,128)S(1)} %slice.29), channel_id=1, source_target_pairs={{0,12},{2,14},{4,0},{6,2},{8,4},{10,6},{12,8},{14,10},{1,13},{3,15... | collective-permute-start | bytes 786440 | tf_op jit(solution)/shard_map/ppermute | solution.py:231
  84.6 8.1 %collective-permute-start.13 = (f32[512,128]{1,0:T(8,128)S(1)}, f32[512,128]{1,0:T(8,128)S(1)}, u32[]{:S(2)}, u32[]{:S(2)}) collective-permute-start(f32[512,128]{1,0:T(8,128)S(1)} %collective-permute-done.10.refs_5_.refs_7_), channel_id=1, source_target_pairs={{0,2},{2,0},{4,6},{6,4},{8,10},{10,8},{12,14},{14,12},{1,3},{3,1},... | collective-permute-start | bytes 786440 | tf_op jit(solution)/shard_map/ppermute | solution.py:231
  85.5 8.8 %collective-permute-start.14 = (f32[512,128]{1,0:T(8,128)S(1)}, f32[512,128]{1,0:T(8,128)S(1)}, u32[]{:S(2)}, u32[]{:S(2)}) collective-permute-start(f32[512,128]{1,0:T(8,128)S(1)} %collective-permute-done.11.refs_6_.refs_8_), channel_id=1, source_target_pairs={{0,2},{2,0},{4,6},{6,4},{8,10},{10,8},{12,14},{14,12},{1,3},{3,1},... | collective-permute-start | bytes 786440 | tf_op jit(solution)/shard_map/ppermute | solution.py:231
  95.5 5.7 %collective-permute-start.15 = (f32[4,64,128]{2,1,0:T(8,128)S(1)}, f32[4,64,128]{2,1,0:T(8,128)S(1)}, u32[]{:S(2)}, u32[]{:S(2)}) collective-permute-start(f32[4,64,128]{2,1,0:T(8,128)S(1)} %slice_bitcast_fusion), channel_id=1, source_target_pairs={{0,1},{1,0},{2,3},{3,2},{4,5},{5,4},{6,7},{7,6},{8,9},{9,8},{10,11... | collective-permute-start | bytes 393224 | tf_op jit(solution)/shard_map/ppermute | solution.py:295
  101.3 5.7 %collective-permute-start.16 = (f32[64,128]{1,0:T(8,128)S(1)}, f32[64,128]{1,0:T(8,128)S(1)}, u32[]{:S(2)}, u32[]{:S(2)}) collective-permute-start(f32[64,128]{1,0:T(8,128)S(1)} %get-tuple-element.43), channel_id=1, source_target_pairs={{0,96},{16,112},{32,64},{48,80},{64,32},{80,48},{96,0},{112,16},{1... | collective-permute-start | bytes 98312 | tf_op jit(solution)/shard_map/ppermute | solution.py:231
  102.6 6.0 %collective-permute-start.17 = (f32[64,128]{1,0:T(8,128)S(1)}, f32[64,128]{1,0:T(8,128)S(1)}, u32[]{:S(2)}, u32[]{:S(2)}) collective-permute-start(f32[64,128]{1,0:T(8,128)S(1)} %get-tuple-element.45), channel_id=1, source_target_pairs={{0,160},{16,176},{32,128},{48,144},{64,224},{80,240},{96,192},{112... | collective-permute-start | bytes 98312 | tf_op jit(solution)/shard_map/ppermute | solution.py:231
  106.9 4.9 %collective-permute-start.18 = (f32[64,128]{1,0:T(8,128)S(1)}, f32[64,128]{1,0:T(8,128)S(1)}, u32[]{:S(2)}, u32[]{:S(2)}) collective-permute-start(f32[64,128]{1,0:T(8,128)S(1)} %get-tuple-element.44), channel_id=1, source_target_pairs={{0,192},{16,208},{32,224},{48,240},{64,128},{80,144},{96,160},{112... | collective-permute-start | bytes 98312 | tf_op jit(solution)/shard_map/ppermute | solution.py:231

commit v10 on v8

--- a/solution.py
+++ b/solution.py
@@ -129,11 +129,12 @@
         total = total[:ij] + total[ij:]
         mine = total[:, :LANES]
         other = total[:, LANES:]
+        to = place[3] ^ block
         if sums is not None:
-            mine = mine + sums[layer, block]
-            other = other + sums[1 - layer, block]
-        out[layer, block] = mine
-        out[1 - layer, block] = other
+            mine = mine + sums[layer, to]
+            other = other + sums[1 - layer, to]
+        out[layer, to] = mine
+        out[1 - layer, to] = other
 
 
 def contract(sums, place, spots, held, shares, pair):
@@ -166,6 +167,56 @@
     )(*given)
 
 
+def sort_kernel(rows, place, parts, *chunks):
+    for n in range(len(chunks)):
+        to = place[3] ^ n
+        base = pl.multiple_of((to & 1) * (rows + 8), 8)
+        at = lax.broadcasted_iota(jnp.int32, (8, LANES), 0)
+        spots = jnp.zeros((8, LANES), jnp.float32)
+        for e in range(GROUP):
+            source = (to >> 1) * GROUP + e
+            chunks[n][e * rows : (e + 1) * rows] = parts[source, pl.ds(base, rows), :]
+            spots = jnp.where(at == e, parts[source, pl.ds(base + rows, 8), :], spots)
+        chunks[n][GROUP * rows :] = spots
+
+
+def sort(place, parts, blocks, rows):
+    def kernel(*refs):
+        sort_kernel(rows, *refs)
+
+    return pl.pallas_call(
+        kernel,
+        out_shape=[jax.ShapeDtypeStruct((GROUP * rows + 8, LANES), jnp.float32)] * blocks,
+        in_specs=[SMEM, VMEM],
+        out_specs=[VMEM] * blocks,
+        compiler_params=pltpu.CompilerParams(vmem_limit_bytes=14 * 2**20),
+        cost_estimate=pl.CostEstimate(flops=0, bytes_accessed=2**16, transcendentals=0),
+    )(place, parts)
+
+
+def join_kernel(*refs):
+    *chunks, own, spots = refs
+    for k, chunk in enumerate(chunks):
+        size = chunk.shape[0] - 8
+        own[k * size : (k + 1) * size] = chunk[:size]
+        spots[k] = chunk[size:].astype(jnp.int32)
+
+
+def join(chunks):
+    size = chunks[0].shape[0] - 8
+    return pl.pallas_call(
+        join_kernel,
+        out_shape=[
+            jax.ShapeDtypeStruct((len(chunks) * size, LANES), jnp.float32),
+            jax.ShapeDtypeStruct((len(chunks), 8, LANES), jnp.int32),
+        ],
+        in_specs=[VMEM] * len(chunks),
+        out_specs=[VMEM] * 2,
+        compiler_params=pltpu.CompilerParams(vmem_limit_bytes=14 * 2**20),
+        cost_estimate=pl.CostEstimate(flops=0, bytes_accessed=2**16, transcendentals=0),
+    )(*chunks)
+
+
 def on_device(t_amps, v_tiles, v_where):
     cols = lax.axis_size("col")
     rows_axis = lax.axis_size("row")
@@ -177,7 +228,10 @@
         [2 * (GROUP * m + (m.bit_count() + odd) % 2) + x for m in range(blocks // 2) for x in range(2)]
         for odd in range(2)
     ]
-    place = jnp.stack([lax.axis_index("col"), lax.axis_index("layer"), lax.axis_index("row") // 2 % GROUP])
+    row = lax.axis_index("row")
+    place = jnp.stack(
+        [lax.axis_index("col"), lax.axis_index("layer"), row // 2 % GROUP, row // (2 * GROUP) * 2 + row % 2]
+    )
 
     def send(share, to, axis="col", size=cols):
         return lax.ppermute(share, axis, [(i, to(i)) for i in range(size)])
@@ -187,12 +241,14 @@
 
     parts = pack(v_tiles, v_where, cols)
     parts = lax.all_to_all(parts, "col", 0, 0, tiled=True)
-    parts = parts.reshape(blocks // 2, GROUP, 2, rows + 8, LANES).transpose(0, 2, 1, 3, 4)
-    parts = parts.reshape(blocks, GROUP * (rows + 8), LANES)
-    parts = lax.all_to_all(parts, "row", 0, 0, tiled=True, axis_index_groups=ranks)
-    parts = parts.reshape(blocks * GROUP, rows + 8, LANES)
-    spots = parts[:, rows, :slots].astype(jnp.int32)
-    own = parts[:, :rows].reshape(blocks * GROUP * rows, LANES)
+    chunks = sort(place, parts, blocks, rows)
+
+    def send_block(chunk, n):
+        m, x = n // 2, n % 2
+        return send(chunk, lambda i: i ^ (2 * GROUP * m) ^ (2 * (m.bit_count() % 2)) ^ x, "row", rows_axis)
+
+    own, spots = join([chunks[0]] + [send_block(chunks[n], n) for n in range(1, blocks)])
+    spots = spots[:, :GROUP, :slots].reshape(blocks * GROUP, slots)
     own, t_other = lax.optimization_barrier((own, t_amps))
 
     def up(i):

time: 102 us -> 107 us (1.049)
  blocking collectives: 57.8 us -> 18.2 us
  starting transfers between devices: 15.8 us -> 43.5 us
  waiting for transfers between devices: 12.9 us -> 30.6 us
    all_to_all x2 -> x0, blocking collectives: 42.8 us -> none  [the longest x1 27.2 us: on_device(): lax.all_to_all(parts, 'row', 0, 0, tiled=True, axis_index_groups=ranks)]
    ppermute x10 -> x17, starting transfers between devices: 7.25 us -> 28.8 us  [send(): return lax.ppermute(share, axis, [(i, to(i)) for i in range(size)])]
    all_to_all x0 -> x1, waiting for transfers between devices: none -> 9.8 us  [on_device(): parts = lax.all_to_all(parts, 'col', 0, 0, tiled=True)]
    ppermute x10 -> x17, waiting for transfers between devices: 11.7 us -> 19.6 us  [send(): return lax.ppermute(share, axis, [(i, to(i)) for i in range(size)])]
    all_to_all x0 -> x1, starting transfers between devices: none -> 5.95 us  [on_device(): parts = lax.all_to_all(parts, 'col', 0, 0, tiled=True)]
    all_to_all x1, blocking collectives: 15 us -> 18.2 us  [on_device(): lax.all_to_all(sums, 'row', 0, 0, tiled=True, axis_index_groups=ranks)]
    pallas_call x2, Pallas kernels: 2.63 us -> 1.4 us  [prepare(): pl.pallas_call(prepare_kernel, out_shape=jax.ShapeDtypeStruct((cd // TILE...]
  transfers between devices with their start and end apart: 11 -> 19, of which waited for: 7 -> 11; matrix products, arithmetic and copies ran while one was open for 1% -> 0% of each run, Pallas kernels for 9% -> 8%
where the time goes in v10:
time: 107 us; the launch traced here: 106 us
  starting transfers between devices  43.5 us (41%)
  waiting for transfers between devices  30.6 us (29%)
  blocking collectives  18.2 us (17%)
  Pallas kernels  11.4 us (11%)
  local copies, waits for them, and re-layouts  1.87 us (2%)
    ppermute x17, starting transfers between devices, send(): return lax.ppermute(share, axis, [(i, to(i)) for i in range(size)])  28.8 us
    ppermute x17, waiting for transfers between devices, send(): return lax.ppermute(share, axis, [(i, to(i)) for i in range(size)])  19.6 us
    all_to_all x1, blocking collectives, on_device(): lax.all_to_all(sums, 'row', 0, 0, tiled=True, axis_index_groups=ranks)  18.2 us
    all_to_all x1, waiting for transfers between devices, on_device(): parts = lax.all_to_all(parts, 'col', 0, 0, tiled=True)  9.8 us
    ppermute x1, starting transfers between devices, on_device(): sums = sums[0] + lax.ppermute(sums[1], 'layer', [(0, 1), (1, 0)])  8.68 us
    pallas_call x6, Pallas kernels, contract(): pl.pallas_call(kernel, out_shape=jax.ShapeDtypeStruct((2, blocks, ij, LAN...  7.93 us
    all_to_all x1, starting transfers between devices, on_device(): parts = lax.all_to_all(parts, 'col', 0, 0, tiled=True)  5.95 us
  transfers between devices with their start and end apart: 19, of which 11 were waited for; matrix products, arithmetic and copies ran while one was open for 0% of the time, Pallas kernels for 8%

profile of v10, /device:TPU:1, one launch (start us, length us, event | category | flops | bytes accessed | tf_op | source)
XLA Modules:
  0.0 106.5 jit_solution(16497978232967050591)
XLA Ops:
  0.0 0.0 copy-start
  0.0 0.0 copy-start.1
  0.0 1.1 %copy-done.1 = f32[2,1,1,16,4096]{4,3,2,1,0:T(8,128)S(1)} copy-done((f32[2,1,1,16,4096]{4,3,2,1,0:T(8,128)S(1)}, f32[2,1,1,16,4096]{4,3,2,1,0:T(8,128)}, u32[]{:S(2)}) %copy-start.1) | copy-done | bytes 524312
  1.1 0.0 copy-start.2
  1.1 0.7 copy-done.2
  1.8 1.5 %shard_map.37 = f32[8,144,128]{2,1,0:T(8,128)} custom-call(s32[2,16]{1,0:T(2,128)S(1)} %bitcast.24, f32[2,2,256,128]{3,2,1,0:T(8,128)S(1)} %bitcast.17), custom_call_target="tpu_custom_call" | custom-call | bytes 1048576 | tf_op jit(solution)/shard_map/pallas_call | solution.py:44
  3.3 5.9 %all-to-all-start = ((f32[8,144,128]{2,1,0:T(8,128)}), f32[8,144,128]{2,1,0:T(8,128)S(1)}, u32[]{:S(2)}, u32[]{:S(2)}) async-start(f32[8,144,128]{2,1,0:T(8,128)} %shard_map.37), calls=%async_computation | async-start | bytes 1179648 | tf_op jit(solution)/shard_map/all_to_all | solution.py:243
  9.2 0.1 pad_add_fusion.refs_0_
  9.3 9.8 %all-to-all-done.refs_1_ = f32[8,144,128]{2,1,0:T(8,128)S(1)} async-done(((f32[8,144,128]{2,1,0:T(8,128)}), f32[8,144,128]{2,1,0:T(8,128)S(1)}, u32[]{:S(2)}, u32[]{:S(2)}) %all-to-all-start) | async-done | bytes 589856 | tf_op jit(solution)/shard_map/all_to_all | solution.py:243
  19.1 0.6 shard_map.38
  19.7 2.5 %collective-permute-start = (f32[136,128]{1,0:T(8,128)S(1)}, f32[136,128]{1,0:T(8,128)S(1)}, u32[]{:S(2)}, u32[]{:S(2)}) collective-permute-start(f32[136,128]{1,0:T(8,128)S(1)} %get-tuple-element.25), channel_id=1, source_target_pairs={{0,16},{16,0},{32,48},{48,32},{64,80},{80,64},{96,112},{112,96},{1... | collective-permute-start | bytes 208904 | tf_op jit(solution)/shard_map/ppermute | solution.py:237
  22.2 4.3 %collective-permute-start.1 = (f32[136,128]{1,0:T(8,128)S(1)}, f32[136,128]{1,0:T(8,128)S(1)}, u32[]{:S(2)}, u32[]{:S(2)}) collective-permute-start(f32[136,128]{1,0:T(8,128)S(1)} %get-tuple-element.26), channel_id=1, source_target_pairs={{0,96},{16,112},{32,64},{48,80},{64,32},{80,48},{96,0},{112,16},{1... | collective-permute-start | bytes 208904 | tf_op jit(solution)/shard_map/ppermute | solution.py:237
  26.6 0.2 collective-permute-start.2
  26.8 3.6 %collective-permute-start.3 = (f32[136,128]{1,0:T(8,128)S(1)}, f32[136,128]{1,0:T(8,128)S(1)}, u32[]{:S(2)}, u32[]{:S(2)}) collective-permute-start(f32[136,128]{1,0:T(8,128)S(1)} %get-tuple-element.28), channel_id=1, source_target_pairs={{0,160},{16,176},{32,128},{48,144},{64,224},{80,240},{96,192},{112... | collective-permute-start | bytes 208904 | tf_op jit(solution)/shard_map/ppermute | solution.py:237
  30.4 3.1 %collective-permute-start.4 = (f32[136,128]{1,0:T(8,128)S(1)}, f32[136,128]{1,0:T(8,128)S(1)}, u32[]{:S(2)}, u32[]{:S(2)}) collective-permute-start(f32[136,128]{1,0:T(8,128)S(1)} %get-tuple-element.29), channel_id=1, source_target_pairs={{0,176},{16,160},{32,144},{48,128},{64,240},{80,224},{96,208},{112... | collective-permute-start | bytes 208904 | tf_op jit(solution)/shard_map/ppermute | solution.py:237
  33.5 0.0 collective-permute-done.refs_1_
  33.5 3.1 %collective-permute-start.5 = (f32[136,128]{1,0:T(8,128)S(1)}, f32[136,128]{1,0:T(8,128)S(1)}, u32[]{:S(2)}, u32[]{:S(2)}) collective-permute-start(f32[136,128]{1,0:T(8,128)S(1)} %get-tuple-element.30), channel_id=1, source_target_pairs={{0,192},{16,208},{32,224},{48,240},{64,128},{80,144},{96,160},{112... | collective-permute-start | bytes 208904 | tf_op jit(solution)/shard_map/ppermute | solution.py:237
  36.6 0.0 collective-permute-done.1.refs_2_
  36.6 0.7 collective-permute-start.6
  37.3 0.0 collective-permute-done.2.refs_3_
  37.3 0.0 collective-permute-done.3.refs_4_
  37.3 3.4 %collective-permute-done.4.refs_5_ = f32[136,128]{1,0:T(8,128)S(1)} collective-permute-done((f32[136,128]{1,0:T(8,128)S(1)}, f32[136,128]{1,0:T(8,128)S(1)}, u32[]{:S(2)}, u32[]{:S(2)}) %collective-permute-start.4) | collective-permute-done | bytes 69664 | tf_op jit(solution)/shard_map/ppermute | solution.py:237
  40.7 0.8 collective-permute-done.5.refs_6_
  41.6 2.9 %collective-permute-done.6.refs_7_ = f32[136,128]{1,0:T(8,128)S(1)} collective-permute-done((f32[136,128]{1,0:T(8,128)S(1)}, f32[136,128]{1,0:T(8,128)S(1)}, u32[]{:S(2)}, u32[]{:S(2)}) %collective-permute-start.6) | collective-permute-done | bytes 69664 | tf_op jit(solution)/shard_map/ppermute | solution.py:237
  44.5 0.0 copy-done
  44.5 3.5 %collective-permute-start.7 = (f32[64,4096]{1,0:T(8,128)S(1)}, f32[64,4096]{1,0:T(8,128)S(1)}, u32[]{:S(2)}, u32[]{:S(2)}) collective-permute-start(f32[64,4096]{1,0:T(8,128)S(1)} %copy-done), channel_id=1, source_target_pairs={{0,32},{16,48},{32,0},{48,16},{64,96},{80,112},{96,64},{112,80},{1... | collective-permute-start | bytes 3145736 | tf_op jit(solution)/shard_map/ppermute | solution.py:237
  48.0 0.6 collective-permute-start.10
  48.6 0.9 collective-permute-start.9
  49.5 0.3 collective-permute-start.8
  49.8 0.7 shard_map.40.refs_2_
  50.5 1.1 %shard_map.42.refs_6_ = f32[2,8,64,128]{3,2,1,0:T(8,128)S(1)} custom-call(s32[4]{0:T(128)S(1)} %pad_add_fusion.refs_0_, s32[16,16]{1,0:T(8,128)S(1)} %bitcast.18, bf16[64,128,128]{2,1,0:T(8,128)(2,1)S(1)} %shard_map.40.refs_2_, f32[1024,128]{1,0:T(8,128)S(1)} %get-tuple-element.35.refs_3_), custom_call_target="tpu_custom_call" | custom-call | flops 1048576 | bytes 65536 | tf_op jit(solution)/shard_map/pallas_call | solution.py:155
  51.6 6.0 %collective-permute-done.10.refs_5_.refs_6_ = f32[1024,128]{1,0:T(8,128)S(1)} collective-permute-done((f32[1024,128]{1,0:T(8,128)S(1)}, f32[1024,128]{1,0:T(8,128)S(1)}, u32[]{:S(2)}, u32[]{:S(2)}) %collective-permute-start.10) | collective-permute-done | bytes 524320 | tf_op jit(solution)/shard_map/ppermute | solution.py:237
  57.5 1.5 %collective-permute-done.9.refs_4_.refs_5_ = f32[1024,128]{1,0:T(8,128)S(1)} collective-permute-done((f32[1024,128]{1,0:T(8,128)S(1)}, f32[1024,128]{1,0:T(8,128)S(1)}, u32[]{:S(2)}, u32[]{:S(2)}) %collective-permute-start.9) | collective-permute-done | bytes 524320 | tf_op jit(solution)/shard_map/ppermute | solution.py:237
  59.0 0.0 collective-permute-done.8.refs_3_.refs_4_
  59.1 1.3 %collective-permute-start.12 = (f32[512,128]{1,0:T(8,128)S(1)}, f32[512,128]{1,0:T(8,128)S(1)}, u32[]{:S(2)}, u32[]{:S(2)}) collective-permute-start(f32[512,128]{1,0:T(8,128)S(1)} %slice.17), channel_id=1, source_target_pairs={{0,12},{2,14},{4,0},{6,2},{8,4},{10,6},{12,8},{14,10},{1,13},{3,15... | collective-permute-start | bytes 786440 | tf_op jit(solution)/shard_map/ppermute | solution.py:237
  60.3 0.3 collective-permute-start.11
  60.6 2.4 %collective-permute-start.16 = (f32[1024,128]{1,0:T(8,128)S(1)}, f32[1024,128]{1,0:T(8,128)S(1)}, u32[]{:S(2)}, u32[]{:S(2)}) collective-permute-start(f32[1024,128]{1,0:T(8,128)S(1)} %collective-permute-done.8.refs_3_.refs_4_), channel_id=1, source_target_pairs={{0,12},{2,14},{4,0},{6,2},{8,4},{10,6},{12,8},{14,10},{1,13},{3,15... | collective-permute-start | bytes 1572872 | tf_op jit(solution)/shard_map/ppermute | solution.py:237
  63.0 0.0 collective-permute-start.15
  63.0 1.4 %shard_map.43.refs_7_ = f32[2,8,64,128]{3,2,1,0:T(8,128)S(1)} custom-call(s32[4]{0:T(128)S(1)} %pad_add_fusion.refs_0_, s32[16,16]{1,0:T(8,128)S(1)} %bitcast.19, bf16[64,128,128]{2,1,0:T(8,128)(2,1)S(1)} %shard_map.40.refs_2_, f32[1024,128]{1,0:T(8,128)S(1)} %collective-permute-done.8.refs_3_.refs_4_, ...), custom_call_target="tpu_custom_call", output_to_operand_aliasing={{}: (6, {})} | custom-call | flops 1048576 | bytes 65536 | tf_op jit(solution)/shard_map/pallas_call | solution.py:155
  64.4 0.4 collective-permute-done.12.refs_5_
  64.8 2.0 %collective-permute-done.11.refs_4_ = f32[512,128]{1,0:T(8,128)S(1)} collective-permute-done((f32[512,128]{1,0:T(8,128)S(1)}, f32[512,128]{1,0:T(8,128)S(1)}, u32[]{:S(2)}, u32[]{:S(2)}) %collective-permute-start.11) | collective-permute-done | bytes 262176 | tf_op jit(solution)/shard_map/ppermute | solution.py:237
  66.8 2.0 %collective-permute-start.13 = (f32[512,128]{1,0:T(8,128)S(1)}, f32[512,128]{1,0:T(8,128)S(1)}, u32[]{:S(2)}, u32[]{:S(2)}) collective-permute-start(f32[512,128]{1,0:T(8,128)S(1)} %collective-permute-done.11.refs_4_), channel_id=1, source_target_pairs={{0,2},{2,0},{4,6},{6,4},{8,10},{10,8},{12,14},{14,12},{1,3},{3,1},... | collective-permute-start | bytes 786440 | tf_op jit(solution)/shard_map/ppermute | solution.py:237
  68.8 0.0 collective-permute-start.14
  68.8 0.0 collective-permute-done.7.refs_0_
  68.9 0.7 shard_map.41.refs_2_.refs_3_
  69.6 1.5 %shard_map.44.refs_6_ = f32[2,8,64,128]{3,2,1,0:T(8,128)S(1)} custom-call(s32[4]{0:T(128)S(1)} %pad_add_fusion.refs_0_, s32[16,16]{1,0:T(8,128)S(1)} %bitcast.20, bf16[64,128,128]{2,1,0:T(8,128)(2,1)S(1)} %shard_map.41.refs_2_.refs_3_, f32[1024,128]{1,0:T(8,128)S(1)} %get-tuple-element.35.refs_3_, ...), custom_call_target="tpu_custom_call", output_to_operand_aliasing={{}: (7, {})} | custom-call | flops 1048576 | bytes 65536 | tf_op jit(solution)/shard_map/pallas_call | solution.py:155
  71.1 1.2 %shard_map.45.refs_6_ = f32[2,8,64,128]{3,2,1,0:T(8,128)S(1)} custom-call(s32[4]{0:T(128)S(1)} %pad_add_fusion.refs_0_, s32[16,16]{1,0:T(8,128)S(1)} %bitcast.21, bf16[64,128,128]{2,1,0:T(8,128)(2,1)S(1)} %shard_map.40.refs_2_, bf16[64,128,128]{2,1,0:T(8,128)(2,1)S(1)} %shard_map.41.refs_2_.refs_3_, ...), custom_call_target="tpu_custom_call", output_to_operand_aliasing={{}: (6, {})} | custom-call | flops 1048576 | bytes 65536 | tf_op jit(solution)/shard_map/pallas_call | solution.py:155
  72.3 0.9 collective-permute-done.16.refs_5_
  73.3 1.6 %collective-permute-done.15.refs_4_ = f32[1024,128]{1,0:T(8,128)S(1)} collective-permute-done((f32[1024,128]{1,0:T(8,128)S(1)}, f32[1024,128]{1,0:T(8,128)S(1)}, u32[]{:S(2)}, u32[]{:S(2)}) %collective-permute-start.15) | collective-permute-done | bytes 524320 | tf_op jit(solution)/shard_map/ppermute | solution.py:237
  74.9 1.5 %shard_map.46.refs_6_ = f32[2,8,64,128]{3,2,1,0:T(8,128)S(1)} custom-call(s32[4]{0:T(128)S(1)} %pad_add_fusion.refs_0_, s32[16,16]{1,0:T(8,128)S(1)} %bitcast.22, bf16[64,128,128]{2,1,0:T(8,128)(2,1)S(1)} %shard_map.40.refs_2_, bf16[64,128,128]{2,1,0:T(8,128)(2,1)S(1)} %shard_map.41.refs_2_.refs_3_, ...), custom_call_target="tpu_custom_call", output_to_operand_aliasing={{}: (6, {})} | custom-call | flops 1048576 | bytes 65536 | tf_op jit(solution)/shard_map/pallas_call | solution.py:155
  76.4 0.0 collective-permute-done.13.refs_4_
  76.5 0.0 collective-permute-done.14.refs_5_
  76.5 1.2 %shard_map.47 = f32[2,8,64,128]{3,2,1,0:T(8,128)S(1)} custom-call(s32[4]{0:T(128)S(1)} %pad_add_fusion.refs_0_, s32[16,16]{1,0:T(8,128)S(1)} %bitcast.23, bf16[64,128,128]{2,1,0:T(8,128)(2,1)S(1)} %shard_map.40.refs_2_, bf16[64,128,128]{2,1,0:T(8,128)(2,1)S(1)} %shard_map.41.refs_2_.refs_3_, ...), custom_call_target="tpu_custom_call", output_to_operand_aliasing={{}: (6, {})} | custom-call | flops 1048576 | bytes 65536 | tf_op jit(solution)/shard_map/pallas_call | solution.py:155
  77.7 8.7 %collective-permute-start.17 = (f32[8,64,128]{2,1,0:T(8,128)S(1)}, f32[8,64,128]{2,1,0:T(8,128)S(1)}, u32[]{:S(2)}, u32[]{:S(2)}) collective-permute-start(f32[8,64,128]{2,1,0:T(8,128)S(1)} %slice_bitcast_fusion), channel_id=1, source_target_pairs={{0,1},{1,0},{2,3},{3,2},{4,5},{5,4},{6,7},{7,6},{8,9},{9,8},{10,11... | collective-permute-start | bytes 786440 | tf_op jit(solution)/shard_map/ppermute | solution.py:290
  86.4 1.2 %collective-permute-done.17 = f32[8,64,128]{2,1,0:T(8,128)S(1)} collective-permute-done((f32[8,64,128]{2,1,0:T(8,128)S(1)}, f32[8,64,128]{2,1,0:T(8,128)S(1)}, u32[]{:S(2)}, u32[]{:S(2)}) %collective-permute-start.17) | collective-permute-done | bytes 262176 | tf_op jit(solution)/shard_map/ppermute | solution.py:290
  87.6 18.2 %all_to_all.10 = f32[8,64,128]{2,1,0:T(8,128)S(1)} all-to-all(f32[8,64,128]{2,1,0:T(8,128)S(1)} %fusion), channel_id=1, replica_groups={{0,16,96,112,160,176,192,208},{32,48,64,80,128,144,224,240},{1,17,97,11..., dimensions={0} | all-to-all | bytes 524288 | tf_op jit(solution)/shard_map/all_to_all | solution.py:291
  105.8 0.6 reduce_sum.9
  (6 shorter events, 0.1 us)
Async XLA Ops:
  0.0 44.5 %copy-start = (f32[64,4096]{1,0:T(8,128)S(1)}, f32[64,4096]{1,0:T(8,128)}, u32[]{:S(2)}) copy-start(f32[64,4096]{1,0:T(8,128)} %refs_0_.1) | copy-start | bytes 3145732
  0.0 1.1 %copy-start.1 = (f32[2,1,1,16,4096]{4,3,2,1,0:T(8,128)S(1)}, f32[2,1,1,16,4096]{4,3,2,1,0:T(8,128)}, u32[]{:S(2)}) copy-start(f32[2,1,1,16,4096]{4,3,2,1,0:T(8,128)} %param.4) | copy-start | bytes 1572868
  1.1 0.7 copy-start.2
  3.3 15.8 %all-to-all-start = ((f32[8,144,128]{2,1,0:T(8,128)}), f32[8,144,128]{2,1,0:T(8,128)S(1)}, u32[]{:S(2)}, u32[]{:S(2)}) async-start(f32[8,144,128]{2,1,0:T(8,128)} %shard_map.37), calls=%async_computation | async-start | bytes 1179648 | tf_op jit(solution)/shard_map/all_to_all | solution.py:243
  19.7 13.8 %collective-permute-start = (f32[136,128]{1,0:T(8,128)S(1)}, f32[136,128]{1,0:T(8,128)S(1)}, u32[]{:S(2)}, u32[]{:S(2)}) collective-permute-start(f32[136,128]{1,0:T(8,128)S(1)} %get-tuple-element.25), channel_id=1, source_target_pairs={{0,16},{16,0},{32,48},{48,32},{64,80},{80,64},{96,112},{112,96},{1... | collective-permute-start | bytes 208904 | tf_op jit(solution)/shard_map/ppermute | solution.py:237
  22.2 14.4 %collective-permute-start.1 = (f32[136,128]{1,0:T(8,128)S(1)}, f32[136,128]{1,0:T(8,128)S(1)}, u32[]{:S(2)}, u32[]{:S(2)}) collective-permute-start(f32[136,128]{1,0:T(8,128)S(1)} %get-tuple-element.26), channel_id=1, source_target_pairs={{0,96},{16,112},{32,64},{48,80},{64,32},{80,48},{96,0},{112,16},{1... | collective-permute-start | bytes 208904 | tf_op jit(solution)/shard_map/ppermute | solution.py:237
  26.6 10.7 %collective-permute-start.2 = (f32[136,128]{1,0:T(8,128)S(1)}, f32[136,128]{1,0:T(8,128)S(1)}, u32[]{:S(2)}, u32[]{:S(2)}) collective-permute-start(f32[136,128]{1,0:T(8,128)S(1)} %get-tuple-element.27), channel_id=1, source_target_pairs={{0,112},{16,96},{32,80},{48,64},{64,48},{80,32},{96,16},{112,0},{1... | collective-permute-start | bytes 208904 | tf_op jit(solution)/shard_map/ppermute | solution.py:237
  26.8 10.5 %collective-permute-start.3 = (f32[136,128]{1,0:T(8,128)S(1)}, f32[136,128]{1,0:T(8,128)S(1)}, u32[]{:S(2)}, u32[]{:S(2)}) collective-permute-start(f32[136,128]{1,0:T(8,128)S(1)} %get-tuple-element.28), channel_id=1, source_target_pairs={{0,160},{16,176},{32,128},{48,144},{64,224},{80,240},{96,192},{112... | collective-permute-start | bytes 208904 | tf_op jit(solution)/shard_map/ppermute | solution.py:237
  30.4 10.3 %collective-permute-start.4 = (f32[136,128]{1,0:T(8,128)S(1)}, f32[136,128]{1,0:T(8,128)S(1)}, u32[]{:S(2)}, u32[]{:S(2)}) collective-permute-start(f32[136,128]{1,0:T(8,128)S(1)} %get-tuple-element.29), channel_id=1, source_target_pairs={{0,176},{16,160},{32,144},{48,128},{64,240},{80,224},{96,208},{112... | collective-permute-start | bytes 208904 | tf_op jit(solution)/shard_map/ppermute | solution.py:237
  33.5 8.1 %collective-permute-start.5 = (f32[136,128]{1,0:T(8,128)S(1)}, f32[136,128]{1,0:T(8,128)S(1)}, u32[]{:S(2)}, u32[]{:S(2)}) collective-permute-start(f32[136,128]{1,0:T(8,128)S(1)} %get-tuple-element.30), channel_id=1, source_target_pairs={{0,192},{16,208},{32,224},{48,240},{64,128},{80,144},{96,160},{112... | collective-permute-start | bytes 208904 | tf_op jit(solution)/shard_map/ppermute | solution.py:237
  36.6 7.9 %collective-permute-start.6 = (f32[136,128]{1,0:T(8,128)S(1)}, f32[136,128]{1,0:T(8,128)S(1)}, u32[]{:S(2)}, u32[]{:S(2)}) collective-permute-start(f32[136,128]{1,0:T(8,128)S(1)} %get-tuple-element.31), channel_id=1, source_target_pairs={{0,208},{16,192},{32,240},{48,224},{64,144},{80,128},{96,176},{112... | collective-permute-start | bytes 208904 | tf_op jit(solution)/shard_map/ppermute | solution.py:237
  44.5 24.3 %collective-permute-start.7 = (f32[64,4096]{1,0:T(8,128)S(1)}, f32[64,4096]{1,0:T(8,128)S(1)}, u32[]{:S(2)}, u32[]{:S(2)}) collective-permute-start(f32[64,4096]{1,0:T(8,128)S(1)} %copy-done), channel_id=1, source_target_pairs={{0,32},{16,48},{32,0},{48,16},{64,96},{80,112},{96,64},{112,80},{1... | collective-permute-start | bytes 3145736 | tf_op jit(solution)/shard_map/ppermute | solution.py:237
  48.0 9.5 %collective-permute-start.10 = (f32[1024,128]{1,0:T(8,128)S(1)}, f32[1024,128]{1,0:T(8,128)S(1)}, u32[]{:S(2)}, u32[]{:S(2)}) collective-permute-start(f32[1024,128]{1,0:T(8,128)S(1)} %get-tuple-element.35.refs_3_), channel_id=1, source_target_pairs={{0,12},{2,14},{4,0},{6,2},{8,4},{10,6},{12,8},{14,10},{1,13},{3,15... | collective-permute-start | bytes 1572872 | tf_op jit(solution)/shard_map/ppermute | solution.py:237
  48.6 10.4 %collective-permute-start.9 = (f32[1024,128]{1,0:T(8,128)S(1)}, f32[1024,128]{1,0:T(8,128)S(1)}, u32[]{:S(2)}, u32[]{:S(2)}) collective-permute-start(f32[1024,128]{1,0:T(8,128)S(1)} %get-tuple-element.35.refs_3_), channel_id=1, source_target_pairs={{0,4},{2,6},{4,8},{6,10},{8,12},{10,14},{12,0},{14,2},{1,5},{3,7},... | collective-permute-start | bytes 1572872 | tf_op jit(solution)/shard_map/ppermute | solution.py:237
  49.5 9.5 %collective-permute-start.8 = (f32[1024,128]{1,0:T(8,128)S(1)}, f32[1024,128]{1,0:T(8,128)S(1)}, u32[]{:S(2)}, u32[]{:S(2)}) collective-permute-start(f32[1024,128]{1,0:T(8,128)S(1)} %get-tuple-element.35.refs_3_), channel_id=1, source_target_pairs={{0,2},{2,0},{4,6},{6,4},{8,10},{10,8},{12,14},{14,12},{1,3},{3,1},... | collective-permute-start | bytes 1572872 | tf_op jit(solution)/shard_map/ppermute | solution.py:237
  59.1 5.7 %collective-permute-start.12 = (f32[512,128]{1,0:T(8,128)S(1)}, f32[512,128]{1,0:T(8,128)S(1)}, u32[]{:S(2)}, u32[]{:S(2)}) collective-permute-start(f32[512,128]{1,0:T(8,128)S(1)} %slice.17), channel_id=1, source_target_pairs={{0,12},{2,14},{4,0},{6,2},{8,4},{10,6},{12,8},{14,10},{1,13},{3,15... | collective-permute-start | bytes 786440 | tf_op jit(solution)/shard_map/ppermute | solution.py:237
  60.3 6.4 %collective-permute-start.11 = (f32[512,128]{1,0:T(8,128)S(1)}, f32[512,128]{1,0:T(8,128)S(1)}, u32[]{:S(2)}, u32[]{:S(2)}) collective-permute-start(f32[512,128]{1,0:T(8,128)S(1)} %slice.16), channel_id=1, source_target_pairs={{0,4},{2,6},{4,8},{6,10},{8,12},{10,14},{12,0},{14,2},{1,5},{3,7},... | collective-permute-start | bytes 786440 | tf_op jit(solution)/shard_map/ppermute | solution.py:237
  60.6 12.6 %collective-permute-start.16 = (f32[1024,128]{1,0:T(8,128)S(1)}, f32[1024,128]{1,0:T(8,128)S(1)}, u32[]{:S(2)}, u32[]{:S(2)}) collective-permute-start(f32[1024,128]{1,0:T(8,128)S(1)} %collective-permute-done.8.refs_3_.refs_4_), channel_id=1, source_target_pairs={{0,12},{2,14},{4,0},{6,2},{8,4},{10,6},{12,8},{14,10},{1,13},{3,15... | collective-permute-start | bytes 1572872 | tf_op jit(solution)/shard_map/ppermute | solution.py:237
  63.0 11.9 %collective-permute-start.15 = (f32[1024,128]{1,0:T(8,128)S(1)}, f32[1024,128]{1,0:T(8,128)S(1)}, u32[]{:S(2)}, u32[]{:S(2)}) collective-permute-start(f32[1024,128]{1,0:T(8,128)S(1)} %collective-permute-done.8.refs_3_.refs_4_), channel_id=1, source_target_pairs={{0,4},{2,6},{4,8},{6,10},{8,12},{10,14},{12,0},{14,2},{1,5},{3,7},... | collective-permute-start | bytes 1572872 | tf_op jit(solution)/shard_map/ppermute | solution.py:237
  66.8 9.7 %collective-permute-start.13 = (f32[512,128]{1,0:T(8,128)S(1)}, f32[512,128]{1,0:T(8,128)S(1)}, u32[]{:S(2)}, u32[]{:S(2)}) collective-permute-start(f32[512,128]{1,0:T(8,128)S(1)} %collective-permute-done.11.refs_4_), channel_id=1, source_target_pairs={{0,2},{2,0},{4,6},{6,4},{8,10},{10,8},{12,14},{14,12},{1,3},{3,1},... | collective-permute-start | bytes 786440 | tf_op jit(solution)/shard_map/ppermute | solution.py:237
  68.8 7.6 %collective-permute-start.14 = (f32[512,128]{1,0:T(8,128)S(1)}, f32[512,128]{1,0:T(8,128)S(1)}, u32[]{:S(2)}, u32[]{:S(2)}) collective-permute-start(f32[512,128]{1,0:T(8,128)S(1)} %collective-permute-done.12.refs_5_), channel_id=1, source_target_pairs={{0,2},{2,0},{4,6},{6,4},{8,10},{10,8},{12,14},{14,12},{1,3},{3,1},... | collective-permute-start | bytes 786440 | tf_op jit(solution)/shard_map/ppermute | solution.py:237
  77.7 9.8 %collective-permute-start.17 = (f32[8,64,128]{2,1,0:T(8,128)S(1)}, f32[8,64,128]{2,1,0:T(8,128)S(1)}, u32[]{:S(2)}, u32[]{:S(2)}) collective-permute-start(f32[8,64,128]{2,1,0:T(8,128)S(1)} %slice_bitcast_fusion), channel_id=1, source_target_pairs={{0,1},{1,0},{2,3},{3,2},{4,5},{5,4},{6,7},{7,6},{8,9},{9,8},{10,11... | collective-permute-start | bytes 786440 | tf_op jit(solution)/shard_map/ppermute | solution.py:290

commit v11 on v10

--- a/solution.py
+++ b/solution.py
@@ -21,7 +21,7 @@
 
 def pack_kernel(spots, lists, out):
     held, slots = spots.shape
-    cols = out.shape[0]
+    cols = out.shape[0] // held
     pair = slots // cols
     rows = pair * HALF
     lane = lax.broadcasted_iota(jnp.int32, (8, LANES), 1)
@@ -29,12 +29,11 @@
         row = jnp.zeros((8, LANES), jnp.float32)
         for s in range(slots):
             row = jnp.where(lane == s, spots[b, s].astype(jnp.float32), row)
-        base = b * (rows + 8)
         for c in range(cols):
             for p in range(pair):
                 s = c * pair + p
-                out[c, base + p * HALF : base + (p + 1) * HALF] = lists[b, s // 8, pl.ds(s % 8, HALF, stride=8), :]
-            out[c, base + rows : base + rows + 8] = row
+                out[b * cols + c, p * HALF : (p + 1) * HALF] = lists[b, s // 8, pl.ds(s % 8, HALF, stride=8), :]
+            out[b * cols + c, rows:] = row
 
 
 def pack(v_tiles, v_where, cols):
@@ -43,7 +42,7 @@
     lists = lists.reshape(held, slots // 8, HALF * 8, LANES)
     return pl.pallas_call(
         pack_kernel,
-        out_shape=jax.ShapeDtypeStruct((cols, held * (slots // cols * HALF + 8), LANES), jnp.float32),
+        out_shape=jax.ShapeDtypeStruct((held * cols, slots // cols * HALF + 8, LANES), jnp.float32),
         in_specs=[SMEM, VMEM],
         out_specs=VMEM,
         compiler_params=pltpu.CompilerParams(vmem_limit_bytes=14 * 2**20),
@@ -167,28 +166,28 @@
     )(*given)
 
 
-def sort_kernel(rows, place, parts, *chunks):
-    for n in range(len(chunks)):
-        to = place[3] ^ n
-        base = pl.multiple_of((to & 1) * (rows + 8), 8)
+def sort_kernel(place, parts, *chunks):
+    cols = parts.shape[0] // 2
+    rows = parts.shape[1] - 8
+    for k in range(len(chunks)):
+        first = ((place[3] >> 1) ^ k) * GROUP
         at = lax.broadcasted_iota(jnp.int32, (8, LANES), 0)
         spots = jnp.zeros((8, LANES), jnp.float32)
-        for e in range(GROUP):
-            source = (to >> 1) * GROUP + e
-            chunks[n][e * rows : (e + 1) * rows] = parts[source, pl.ds(base, rows), :]
-            spots = jnp.where(at == e, parts[source, pl.ds(base + rows, 8), :], spots)
-        chunks[n][GROUP * rows :] = spots
-
-
-def sort(place, parts, blocks, rows):
-    def kernel(*refs):
-        sort_kernel(rows, *refs)
-
-    return pl.pallas_call(
-        kernel,
-        out_shape=[jax.ShapeDtypeStruct((GROUP * rows + 8, LANES), jnp.float32)] * blocks,
+        for x in range(2):
+            for e in range(GROUP):
+                n, source = x * GROUP + e, x * cols + first + e
+                chunks[k][n * rows : (n + 1) * rows] = parts[source, :rows]
+                spots = jnp.where(at == n, parts[source, rows:], spots)
+        chunks[k][2 * GROUP * rows :] = spots
+
+
+def sort(place, parts, count):
+    rows = parts.shape[1] - 8
+    return pl.pallas_call(
+        sort_kernel,
+        out_shape=[jax.ShapeDtypeStruct((2 * GROUP * rows + 8, LANES), jnp.float32)] * count,
         in_specs=[SMEM, VMEM],
-        out_specs=[VMEM] * blocks,
+        out_specs=[VMEM] * count,
         compiler_params=pltpu.CompilerParams(vmem_limit_bytes=14 * 2**20),
         cost_estimate=pl.CostEstimate(flops=0, bytes_accessed=2**16, transcendentals=0),
     )(place, parts)
@@ -230,7 +229,7 @@
     ]
     row = lax.axis_index("row")
     place = jnp.stack(
-        [lax.axis_index("col"), lax.axis_index("layer"), row // 2 % GROUP, row // (2 * GROUP) * 2 + row % 2]
+        [lax.axis_index("col"), lax.axis_index("layer"), row // 2 % GROUP, row // (2 * GROUP) * 2]
     )
 
     def send(share, to, axis="col", size=cols):
@@ -239,16 +238,18 @@
     def send_t(t_block):
         return send(t_block, lambda i: i ^ 2, "row", rows_axis)
 
+    planes = [
+        [(2 * z + x) * cols + c for x in range(2) for c in range(cols)] for z in range(rows_axis // 2)
+    ]
     parts = pack(v_tiles, v_where, cols)
-    parts = lax.all_to_all(parts, "col", 0, 0, tiled=True)
-    chunks = sort(place, parts, blocks, rows)
-
-    def send_block(chunk, n):
-        m, x = n // 2, n % 2
-        return send(chunk, lambda i: i ^ (2 * GROUP * m) ^ (2 * (m.bit_count() % 2)) ^ x, "row", rows_axis)
-
-    own, spots = join([chunks[0]] + [send_block(chunks[n], n) for n in range(1, blocks)])
-    spots = spots[:, :GROUP, :slots].reshape(blocks * GROUP, slots)
+    parts = lax.all_to_all(parts, ("row", "col"), 0, 0, tiled=True, axis_index_groups=planes)
+    chunks = sort(place, parts, blocks // 2)
+
+    def send_m(chunk, k):
+        return send(chunk, lambda i: i ^ (2 * GROUP * k) ^ (2 * (k.bit_count() % 2)), "row", rows_axis)
+
+    own, spots = join([chunks[0]] + [send_m(chunks[k], k) for k in range(1, blocks // 2)])
+    spots = spots[:, : 2 * GROUP, :slots].reshape(blocks * GROUP, slots)
     own, t_other = lax.optimization_barrier((own, t_amps))
 
     def up(i):

time: 107 us -> 101 us (0.944)
  starting transfers between devices: 43.5 us -> 30.5 us
  waiting for transfers between devices: 30.6 us -> 42 us
  blocking collectives: 18.2 us -> 14.1 us
    ppermute x17 -> x13, waiting for transfers between devices: 19.6 us -> 29.9 us  [send(): return lax.ppermute(share, axis, [(i, to(i)) for i in range(size)])]
    ppermute x17 -> x13, starting transfers between devices: 28.8 us -> 18.9 us  [send(): return lax.ppermute(share, axis, [(i, to(i)) for i in range(size)])]
    ppermute x1, starting transfers between devices: 8.68 us -> 4.02 us  [on_device(): sums = sums[0] + lax.ppermute(sums[1], 'layer', [(0, 1), (1, 0)])]
    all_to_all x1, blocking collectives: 18.2 us -> 14.1 us  [on_device(): lax.all_to_all(sums, 'row', 0, 0, tiled=True, axis_index_groups=ranks)]
    all_to_all x1, starting transfers between devices: 5.95 us -> 7.58 us  [on_device(): lax.all_to_all(parts, ('row', 'col'), 0, 0, tiled=True, axis_index_groups...]
    all_to_all x1, waiting for transfers between devices: 9.8 us -> 11 us  [on_device(): lax.all_to_all(parts, ('row', 'col'), 0, 0, tiled=True, axis_index_groups...]
  transfers between devices with their start and end apart: 19 -> 15, of which waited for: 11 -> 10; matrix products, arithmetic and copies ran while one was open for 0% -> 0% of each run, Pallas kernels for 8% -> 8%
where the time goes in v11:
time: 101 us
  waiting for transfers between devices  42 us (42%)
  starting transfers between devices  30.5 us (30%)
  blocking collectives  14.1 us (14%)
  Pallas kernels  11.4 us (11%)
  local copies, waits for them, and re-layouts  1.87 us (2%)
    ppermute x13, waiting for transfers between devices, send(): return lax.ppermute(share, axis, [(i, to(i)) for i in range(size)])  29.9 us
    ppermute x13, starting transfers between devices, send(): return lax.ppermute(share, axis, [(i, to(i)) for i in range(size)])  18.9 us
    all_to_all x1, blocking collectives, on_device(): lax.all_to_all(sums, 'row', 0, 0, tiled=True, axis_index_groups=ranks)  14.1 us
    all_to_all x1, waiting for transfers between devices, on_device(): lax.all_to_all(parts, ('row', 'col'), 0, 0, tiled=True, axis_index_groups...  11 us
    pallas_call x6, Pallas kernels, contract(): pl.pallas_call(kernel, out_shape=jax.ShapeDtypeStruct((2, blocks, ij, LAN...  7.92 us
    all_to_all x1, starting transfers between devices, on_device(): lax.all_to_all(parts, ('row', 'col'), 0, 0, tiled=True, axis_index_groups...  7.58 us
    ppermute x1, starting transfers between devices, on_device(): sums = sums[0] + lax.ppermute(sums[1], 'layer', [(0, 1), (1, 0)])  4.02 us
  transfers between devices with their start and end apart: 15, of which 10 were waited for; matrix products, arithmetic and copies ran while one was open for 0% of the time, Pallas kernels for 8%

profile of v11, /device:TPU:1, one launch (start us, length us, event | category | flops | bytes accessed | tf_op | source)
XLA Modules:
  0.0 100.9 jit_solution(15435539478288447878)
XLA Ops:
  0.0 0.0 copy-start
  0.0 0.0 copy-start.1
  0.0 1.1 %copy-done.1 = f32[2,1,1,16,4096]{4,3,2,1,0:T(8,128)S(1)} copy-done((f32[2,1,1,16,4096]{4,3,2,1,0:T(8,128)S(1)}, f32[2,1,1,16,4096]{4,3,2,1,0:T(8,128)}, u32[]{:S(2)}) %copy-start.1) | copy-done | bytes 524312
  1.1 0.0 copy-start.2
  1.1 0.7 copy-done.2
  1.8 1.5 %shard_map.37 = f32[16,72,128]{2,1,0:T(8,128)} custom-call(s32[2,16]{1,0:T(2,128)S(1)} %bitcast.24, f32[2,2,256,128]{3,2,1,0:T(8,128)S(1)} %bitcast.17), custom_call_target="tpu_custom_call" | custom-call | bytes 1048576 | tf_op jit(solution)/shard_map/pallas_call | solution.py:43
  3.3 7.6 %all-to-all-start = ((f32[16,72,128]{2,1,0:T(8,128)}), f32[16,72,128]{2,1,0:T(8,128)S(1)}, u32[]{:S(2)}, u32[]{:S(2)}) async-start(f32[16,72,128]{2,1,0:T(8,128)} %shard_map.37), calls=%async_computation | async-start | bytes 1179648 | tf_op jit(solution)/shard_map/all_to_all | solution.py:245
  10.9 0.1 pad_add_fusion.place.refs_0_
  11.0 11.0 %all-to-all-done.parts = f32[16,72,128]{2,1,0:T(8,128)S(1)} async-done(((f32[16,72,128]{2,1,0:T(8,128)}), f32[16,72,128]{2,1,0:T(8,128)S(1)}, u32[]{:S(2)}, u32[]{:S(2)}) %all-to-all-start) | async-done | bytes 589856 | tf_op jit(solution)/shard_map/all_to_all | solution.py:245
  22.0 0.6 shard_map.38
  22.5 4.4 %collective-permute-start = (f32[264,128]{1,0:T(8,128)S(1)}, f32[264,128]{1,0:T(8,128)S(1)}, u32[]{:S(2)}, u32[]{:S(2)}) collective-permute-start(f32[264,128]{1,0:T(8,128)S(1)} %get-tuple-element.21), channel_id=1, source_target_pairs={{0,96},{16,112},{32,64},{48,80},{64,32},{80,48},{96,0},{112,16},{1... | collective-permute-start | bytes 405512 | tf_op jit(solution)/shard_map/ppermute | solution.py:236
  27.0 2.9 %collective-permute-start.1 = (f32[264,128]{1,0:T(8,128)S(1)}, f32[264,128]{1,0:T(8,128)S(1)}, u32[]{:S(2)}, u32[]{:S(2)}) collective-permute-start(f32[264,128]{1,0:T(8,128)S(1)} %get-tuple-element.22), channel_id=1, source_target_pairs={{0,160},{16,176},{32,128},{48,144},{64,224},{80,240},{96,192},{112... | collective-permute-start | bytes 405512 | tf_op jit(solution)/shard_map/ppermute | solution.py:236
  29.8 0.0 collective-permute-start.2
  29.8 0.0 collective-permute-done.refs_1_
  29.8 10.4 %collective-permute-done.1.refs_2_ = f32[264,128]{1,0:T(8,128)S(1)} collective-permute-done((f32[264,128]{1,0:T(8,128)S(1)}, f32[264,128]{1,0:T(8,128)S(1)}, u32[]{:S(2)}, u32[]{:S(2)}) %collective-permute-start.1) | collective-permute-done | bytes 135200 | tf_op jit(solution)/shard_map/ppermute | solution.py:236
  40.2 0.2 collective-permute-done.2.refs_3_
  40.4 0.0 copy-done
  40.5 3.7 %collective-permute-start.3 = (f32[64,4096]{1,0:T(8,128)S(1)}, f32[64,4096]{1,0:T(8,128)S(1)}, u32[]{:S(2)}, u32[]{:S(2)}) collective-permute-start(f32[64,4096]{1,0:T(8,128)S(1)} %copy-done), channel_id=1, source_target_pairs={{0,32},{16,48},{32,0},{48,16},{64,96},{80,112},{96,64},{112,80},{1... | collective-permute-start | bytes 3145736 | tf_op jit(solution)/shard_map/ppermute | solution.py:236
  44.1 2.3 %collective-permute-start.6 = (f32[1024,128]{1,0:T(8,128)S(1)}, f32[1024,128]{1,0:T(8,128)S(1)}, u32[]{:S(2)}, u32[]{:S(2)}) collective-permute-start(f32[1024,128]{1,0:T(8,128)S(1)} %get-tuple-element.27.refs_3_), channel_id=1, source_target_pairs={{0,12},{2,14},{4,0},{6,2},{8,4},{10,6},{12,8},{14,10},{1,13},{3,15... | collective-permute-start | bytes 1572872 | tf_op jit(solution)/shard_map/ppermute | solution.py:236
  46.4 0.0 collective-permute-start.5
  46.4 0.2 collective-permute-start.4
  46.6 0.7 shard_map.40.refs_2_
  47.4 1.1 %shard_map.42.refs_6_ = f32[2,8,64,128]{3,2,1,0:T(8,128)S(1)} custom-call(s32[4]{0:T(128)S(1)} %pad_add_fusion.place.refs_0_, s32[16,16]{1,0:T(8,128)S(1)} %bitcast.18, bf16[64,128,128]{2,1,0:T(8,128)(2,1)S(1)} %shard_map.40.refs_2_, f32[1024,128]{1,0:T(8,128)S(1)} %get-tuple-element.27.refs_3_), custom_call_target="tpu_custom_call" | custom-call | flops 1048576 | bytes 65536 | tf_op jit(solution)/shard_map/pallas_call | solution.py:154
  48.4 8.0 %collective-permute-done.6.refs_5_.refs_6_ = f32[1024,128]{1,0:T(8,128)S(1)} collective-permute-done((f32[1024,128]{1,0:T(8,128)S(1)}, f32[1024,128]{1,0:T(8,128)S(1)}, u32[]{:S(2)}, u32[]{:S(2)}) %collective-permute-start.6) | collective-permute-done | bytes 524320 | tf_op jit(solution)/shard_map/ppermute | solution.py:236
  56.4 3.1 %collective-permute-done.5.refs_4_.refs_5_ = f32[1024,128]{1,0:T(8,128)S(1)} collective-permute-done((f32[1024,128]{1,0:T(8,128)S(1)}, f32[1024,128]{1,0:T(8,128)S(1)}, u32[]{:S(2)}, u32[]{:S(2)}) %collective-permute-start.5) | collective-permute-done | bytes 524320 | tf_op jit(solution)/shard_map/ppermute | solution.py:236
  59.5 0.0 collective-permute-done.4.refs_3_.refs_4_
  59.6 1.3 %collective-permute-start.8 = (f32[512,128]{1,0:T(8,128)S(1)}, f32[512,128]{1,0:T(8,128)S(1)}, u32[]{:S(2)}, u32[]{:S(2)}) collective-permute-start(f32[512,128]{1,0:T(8,128)S(1)} %slice.17), channel_id=1, source_target_pairs={{0,12},{2,14},{4,0},{6,2},{8,4},{10,6},{12,8},{14,10},{1,13},{3,15... | collective-permute-start | bytes 786440 | tf_op jit(solution)/shard_map/ppermute | solution.py:236
  60.8 0.3 collective-permute-start.7
  61.1 2.4 %collective-permute-start.12 = (f32[1024,128]{1,0:T(8,128)S(1)}, f32[1024,128]{1,0:T(8,128)S(1)}, u32[]{:S(2)}, u32[]{:S(2)}) collective-permute-start(f32[1024,128]{1,0:T(8,128)S(1)} %collective-permute-done.4.refs_3_.refs_4_), channel_id=1, source_target_pairs={{0,12},{2,14},{4,0},{6,2},{8,4},{10,6},{12,8},{14,10},{1,13},{3,15... | collective-permute-start | bytes 1572872 | tf_op jit(solution)/shard_map/ppermute | solution.py:236
  63.5 0.0 collective-permute-start.11
  63.5 1.4 %shard_map.43.refs_7_ = f32[2,8,64,128]{3,2,1,0:T(8,128)S(1)} custom-call(s32[4]{0:T(128)S(1)} %pad_add_fusion.place.refs_0_, s32[16,16]{1,0:T(8,128)S(1)} %bitcast.19, bf16[64,128,128]{2,1,0:T(8,128)(2,1)S(1)} %shard_map.40.refs_2_, f32[1024,128]{1,0:T(8,128)S(1)} %collective-permute-done.4.refs_3_.refs_4_, ...), custom_call_target="tpu_custom_call", output_to_operand_aliasing={{}: (6, {})} | custom-call | flops 1048576 | bytes 65536 | tf_op jit(solution)/shard_map/pallas_call | solution.py:154
  64.9 0.3 collective-permute-done.8.refs_5_
  65.2 2.1 %collective-permute-done.7.refs_4_ = f32[512,128]{1,0:T(8,128)S(1)} collective-permute-done((f32[512,128]{1,0:T(8,128)S(1)}, f32[512,128]{1,0:T(8,128)S(1)}, u32[]{:S(2)}, u32[]{:S(2)}) %collective-permute-start.7) | collective-permute-done | bytes 262176 | tf_op jit(solution)/shard_map/ppermute | solution.py:236
  67.3 0.2 collective-permute-start.9
  67.5 1.2 %collective-permute-start.10 = (f32[512,128]{1,0:T(8,128)S(1)}, f32[512,128]{1,0:T(8,128)S(1)}, u32[]{:S(2)}, u32[]{:S(2)}) collective-permute-start(f32[512,128]{1,0:T(8,128)S(1)} %collective-permute-done.8.refs_5_), channel_id=1, source_target_pairs={{0,2},{2,0},{4,6},{6,4},{8,10},{10,8},{12,14},{14,12},{1,3},{3,1},... | collective-permute-start | bytes 786440 | tf_op jit(solution)/shard_map/ppermute | solution.py:236
  68.7 0.0 collective-permute-done.3.refs_0_
  68.7 0.7 shard_map.41.refs_2_.refs_3_
  69.4 1.5 %shard_map.44.refs_6_ = f32[2,8,64,128]{3,2,1,0:T(8,128)S(1)} custom-call(s32[4]{0:T(128)S(1)} %pad_add_fusion.place.refs_0_, s32[16,16]{1,0:T(8,128)S(1)} %bitcast.20, bf16[64,128,128]{2,1,0:T(8,128)(2,1)S(1)} %shard_map.41.refs_2_.refs_3_, f32[1024,128]{1,0:T(8,128)S(1)} %get-tuple-element.27.refs_3_, ...), custom_call_target="tpu_custom_call", output_to_operand_aliasing={{}: (7, {})} | custom-call | flops 1048576 | bytes 65536 | tf_op jit(solution)/shard_map/pallas_call | solution.py:154
  71.0 1.2 %shard_map.45.refs_6_ = f32[2,8,64,128]{3,2,1,0:T(8,128)S(1)} custom-call(s32[4]{0:T(128)S(1)} %pad_add_fusion.place.refs_0_, s32[16,16]{1,0:T(8,128)S(1)} %bitcast.21, bf16[64,128,128]{2,1,0:T(8,128)(2,1)S(1)} %shard_map.40.refs_2_, bf16[64,128,128]{2,1,0:T(8,128)(2,1)S(1)} %shard_map.41.refs_2_.refs_3_, ...), custom_call_target="tpu_custom_call", output_to_operand_aliasing={{}: (6, {})} | custom-call | flops 1048576 | bytes 65536 | tf_op jit(solution)/shard_map/pallas_call | solution.py:154
  72.2 4.0 %collective-permute-done.12.refs_5_ = f32[1024,128]{1,0:T(8,128)S(1)} collective-permute-done((f32[1024,128]{1,0:T(8,128)S(1)}, f32[1024,128]{1,0:T(8,128)S(1)}, u32[]{:S(2)}, u32[]{:S(2)}) %collective-permute-start.12) | collective-permute-done | bytes 524320 | tf_op jit(solution)/shard_map/ppermute | solution.py:236
  76.2 1.8 %collective-permute-done.11.refs_4_ = f32[1024,128]{1,0:T(8,128)S(1)} collective-permute-done((f32[1024,128]{1,0:T(8,128)S(1)}, f32[1024,128]{1,0:T(8,128)S(1)}, u32[]{:S(2)}, u32[]{:S(2)}) %collective-permute-start.11) | collective-permute-done | bytes 524320 | tf_op jit(solution)/shard_map/ppermute | solution.py:236
  78.1 1.5 %shard_map.46.refs_6_ = f32[2,8,64,128]{3,2,1,0:T(8,128)S(1)} custom-call(s32[4]{0:T(128)S(1)} %pad_add_fusion.place.refs_0_, s32[16,16]{1,0:T(8,128)S(1)} %bitcast.22, bf16[64,128,128]{2,1,0:T(8,128)(2,1)S(1)} %shard_map.40.refs_2_, bf16[64,128,128]{2,1,0:T(8,128)(2,1)S(1)} %shard_map.41.refs_2_.refs_3_, ...), custom_call_target="tpu_custom_call", output_to_operand_aliasing={{}: (6, {})} | custom-call | flops 1048576 | bytes 65536 | tf_op jit(solution)/shard_map/pallas_call | solution.py:154
  79.6 0.0 collective-permute-done.9.refs_4_
  79.6 0.0 collective-permute-done.10.refs_5_
  79.6 1.2 %shard_map.47 = f32[2,8,64,128]{3,2,1,0:T(8,128)S(1)} custom-call(s32[4]{0:T(128)S(1)} %pad_add_fusion.place.refs_0_, s32[16,16]{1,0:T(8,128)S(1)} %bitcast.23, bf16[64,128,128]{2,1,0:T(8,128)(2,1)S(1)} %shard_map.40.refs_2_, bf16[64,128,128]{2,1,0:T(8,128)(2,1)S(1)} %shard_map.41.refs_2_.refs_3_, ...), custom_call_target="tpu_custom_call", output_to_operand_aliasing={{}: (6, {})} | custom-call | flops 1048576 | bytes 65536 | tf_op jit(solution)/shard_map/pallas_call | solution.py:154
  80.9 4.0 %collective-permute-start.13 = (f32[8,64,128]{2,1,0:T(8,128)S(1)}, f32[8,64,128]{2,1,0:T(8,128)S(1)}, u32[]{:S(2)}, u32[]{:S(2)}) collective-permute-start(f32[8,64,128]{2,1,0:T(8,128)S(1)} %slice_bitcast_fusion), channel_id=1, source_target_pairs={{0,1},{1,0},{2,3},{3,2},{4,5},{5,4},{6,7},{7,6},{8,9},{9,8},{10,11... | collective-permute-start | bytes 786440 | tf_op jit(solution)/shard_map/ppermute | solution.py:291
  84.9 1.2 %collective-permute-done.13 = f32[8,64,128]{2,1,0:T(8,128)S(1)} collective-permute-done((f32[8,64,128]{2,1,0:T(8,128)S(1)}, f32[8,64,128]{2,1,0:T(8,128)S(1)}, u32[]{:S(2)}, u32[]{:S(2)}) %collective-permute-start.13) | collective-permute-done | bytes 262176 | tf_op jit(solution)/shard_map/ppermute | solution.py:291
  86.1 14.1 %all_to_all.10 = f32[8,64,128]{2,1,0:T(8,128)S(1)} all-to-all(f32[8,64,128]{2,1,0:T(8,128)S(1)} %fusion), channel_id=1, replica_groups={{0,16,96,112,160,176,192,208},{32,48,64,80,128,144,224,240},{1,17,97,11..., dimensions={0} | all-to-all | bytes 524288 | tf_op jit(solution)/shard_map/all_to_all | solution.py:292
  100.2 0.6 reduce_sum.9
  (6 shorter events, 0.1 us)
Async XLA Ops:
  0.0 40.4 %copy-start = (f32[64,4096]{1,0:T(8,128)S(1)}, f32[64,4096]{1,0:T(8,128)}, u32[]{:S(2)}) copy-start(f32[64,4096]{1,0:T(8,128)} %refs_0_.1) | copy-start | bytes 3145732
  0.0 1.1 %copy-start.1 = (f32[2,1,1,16,4096]{4,3,2,1,0:T(8,128)S(1)}, f32[2,1,1,16,4096]{4,3,2,1,0:T(8,128)}, u32[]{:S(2)}) copy-start(f32[2,1,1,16,4096]{4,3,2,1,0:T(8,128)} %param.4) | copy-start | bytes 1572868
  1.1 0.7 copy-start.2
  3.3 18.7 %all-to-all-start = ((f32[16,72,128]{2,1,0:T(8,128)}), f32[16,72,128]{2,1,0:T(8,128)S(1)}, u32[]{:S(2)}, u32[]{:S(2)}) async-start(f32[16,72,128]{2,1,0:T(8,128)} %shard_map.37), calls=%async_computation | async-start | bytes 1179648 | tf_op jit(solution)/shard_map/all_to_all | solution.py:245
  22.5 7.3 %collective-permute-start = (f32[264,128]{1,0:T(8,128)S(1)}, f32[264,128]{1,0:T(8,128)S(1)}, u32[]{:S(2)}, u32[]{:S(2)}) collective-permute-start(f32[264,128]{1,0:T(8,128)S(1)} %get-tuple-element.21), channel_id=1, source_target_pairs={{0,96},{16,112},{32,64},{48,80},{64,32},{80,48},{96,0},{112,16},{1... | collective-permute-start | bytes 405512 | tf_op jit(solution)/shard_map/ppermute | solution.py:236
  27.0 13.2 %collective-permute-start.1 = (f32[264,128]{1,0:T(8,128)S(1)}, f32[264,128]{1,0:T(8,128)S(1)}, u32[]{:S(2)}, u32[]{:S(2)}) collective-permute-start(f32[264,128]{1,0:T(8,128)S(1)} %get-tuple-element.22), channel_id=1, source_target_pairs={{0,160},{16,176},{32,128},{48,144},{64,224},{80,240},{96,192},{112... | collective-permute-start | bytes 405512 | tf_op jit(solution)/shard_map/ppermute | solution.py:236
  29.8 10.6 %collective-permute-start.2 = (f32[264,128]{1,0:T(8,128)S(1)}, f32[264,128]{1,0:T(8,128)S(1)}, u32[]{:S(2)}, u32[]{:S(2)}) collective-permute-start(f32[264,128]{1,0:T(8,128)S(1)} %get-tuple-element.23), channel_id=1, source_target_pairs={{0,192},{16,208},{32,224},{48,240},{64,128},{80,144},{96,160},{112... | collective-permute-start | bytes 405512 | tf_op jit(solution)/shard_map/ppermute | solution.py:236
  40.5 28.3 %collective-permute-start.3 = (f32[64,4096]{1,0:T(8,128)S(1)}, f32[64,4096]{1,0:T(8,128)S(1)}, u32[]{:S(2)}, u32[]{:S(2)}) collective-permute-start(f32[64,4096]{1,0:T(8,128)S(1)} %copy-done), channel_id=1, source_target_pairs={{0,32},{16,48},{32,0},{48,16},{64,96},{80,112},{96,64},{112,80},{1... | collective-permute-start | bytes 3145736 | tf_op jit(solution)/shard_map/ppermute | solution.py:236
  44.1 12.2 %collective-permute-start.6 = (f32[1024,128]{1,0:T(8,128)S(1)}, f32[1024,128]{1,0:T(8,128)S(1)}, u32[]{:S(2)}, u32[]{:S(2)}) collective-permute-start(f32[1024,128]{1,0:T(8,128)S(1)} %get-tuple-element.27.refs_3_), channel_id=1, source_target_pairs={{0,12},{2,14},{4,0},{6,2},{8,4},{10,6},{12,8},{14,10},{1,13},{3,15... | collective-permute-start | bytes 1572872 | tf_op jit(solution)/shard_map/ppermute | solution.py:236
  46.4 13.1 %collective-permute-start.5 = (f32[1024,128]{1,0:T(8,128)S(1)}, f32[1024,128]{1,0:T(8,128)S(1)}, u32[]{:S(2)}, u32[]{:S(2)}) collective-permute-start(f32[1024,128]{1,0:T(8,128)S(1)} %get-tuple-element.27.refs_3_), channel_id=1, source_target_pairs={{0,4},{2,6},{4,8},{6,10},{8,12},{10,14},{12,0},{14,2},{1,5},{3,7},... | collective-permute-start | bytes 1572872 | tf_op jit(solution)/shard_map/ppermute | solution.py:236
  46.4 13.1 %collective-permute-start.4 = (f32[1024,128]{1,0:T(8,128)S(1)}, f32[1024,128]{1,0:T(8,128)S(1)}, u32[]{:S(2)}, u32[]{:S(2)}) collective-permute-start(f32[1024,128]{1,0:T(8,128)S(1)} %get-tuple-element.27.refs_3_), channel_id=1, source_target_pairs={{0,2},{2,0},{4,6},{6,4},{8,10},{10,8},{12,14},{14,12},{1,3},{3,1},... | collective-permute-start | bytes 1572872 | tf_op jit(solution)/shard_map/ppermute | solution.py:236
  59.6 5.6 %collective-permute-start.8 = (f32[512,128]{1,0:T(8,128)S(1)}, f32[512,128]{1,0:T(8,128)S(1)}, u32[]{:S(2)}, u32[]{:S(2)}) collective-permute-start(f32[512,128]{1,0:T(8,128)S(1)} %slice.17), channel_id=1, source_target_pairs={{0,12},{2,14},{4,0},{6,2},{8,4},{10,6},{12,8},{14,10},{1,13},{3,15... | collective-permute-start | bytes 786440 | tf_op jit(solution)/shard_map/ppermute | solution.py:236
  60.8 6.4 %collective-permute-start.7 = (f32[512,128]{1,0:T(8,128)S(1)}, f32[512,128]{1,0:T(8,128)S(1)}, u32[]{:S(2)}, u32[]{:S(2)}) collective-permute-start(f32[512,128]{1,0:T(8,128)S(1)} %slice.16), channel_id=1, source_target_pairs={{0,4},{2,6},{4,8},{6,10},{8,12},{10,14},{12,0},{14,2},{1,5},{3,7},... | collective-permute-start | bytes 786440 | tf_op jit(solution)/shard_map/ppermute | solution.py:236
  61.1 15.1 %collective-permute-start.12 = (f32[1024,128]{1,0:T(8,128)S(1)}, f32[1024,128]{1,0:T(8,128)S(1)}, u32[]{:S(2)}, u32[]{:S(2)}) collective-permute-start(f32[1024,128]{1,0:T(8,128)S(1)} %collective-permute-done.4.refs_3_.refs_4_), channel_id=1, source_target_pairs={{0,12},{2,14},{4,0},{6,2},{8,4},{10,6},{12,8},{14,10},{1,13},{3,15... | collective-permute-start | bytes 1572872 | tf_op jit(solution)/shard_map/ppermute | solution.py:236
  63.5 14.6 %collective-permute-start.11 = (f32[1024,128]{1,0:T(8,128)S(1)}, f32[1024,128]{1,0:T(8,128)S(1)}, u32[]{:S(2)}, u32[]{:S(2)}) collective-permute-start(f32[1024,128]{1,0:T(8,128)S(1)} %collective-permute-done.4.refs_3_.refs_4_), channel_id=1, source_target_pairs={{0,4},{2,6},{4,8},{6,10},{8,12},{10,14},{12,0},{14,2},{1,5},{3,7},... | collective-permute-start | bytes 1572872 | tf_op jit(solution)/shard_map/ppermute | solution.py:236
  67.3 12.3 %collective-permute-start.9 = (f32[512,128]{1,0:T(8,128)S(1)}, f32[512,128]{1,0:T(8,128)S(1)}, u32[]{:S(2)}, u32[]{:S(2)}) collective-permute-start(f32[512,128]{1,0:T(8,128)S(1)} %collective-permute-done.7.refs_4_), channel_id=1, source_target_pairs={{0,2},{2,0},{4,6},{6,4},{8,10},{10,8},{12,14},{14,12},{1,3},{3,1},... | collective-permute-start | bytes 786440 | tf_op jit(solution)/shard_map/ppermute | solution.py:236
  67.5 12.1 %collective-permute-start.10 = (f32[512,128]{1,0:T(8,128)S(1)}, f32[512,128]{1,0:T(8,128)S(1)}, u32[]{:S(2)}, u32[]{:S(2)}) collective-permute-start(f32[512,128]{1,0:T(8,128)S(1)} %collective-permute-done.8.refs_5_), channel_id=1, source_target_pairs={{0,2},{2,0},{4,6},{6,4},{8,10},{10,8},{12,14},{14,12},{1,3},{3,1},... | collective-permute-start | bytes 786440 | tf_op jit(solution)/shard_map/ppermute | solution.py:236
  80.9 5.2 %collective-permute-start.13 = (f32[8,64,128]{2,1,0:T(8,128)S(1)}, f32[8,64,128]{2,1,0:T(8,128)S(1)}, u32[]{:S(2)}, u32[]{:S(2)}) collective-permute-start(f32[8,64,128]{2,1,0:T(8,128)S(1)} %slice_bitcast_fusion), channel_id=1, source_target_pairs={{0,1},{1,0},{2,3},{3,2},{4,5},{5,4},{6,7},{7,6},{8,9},{9,8},{10,11... | collective-permute-start | bytes 786440 | tf_op jit(solution)/shard_map/ppermute | solution.py:291

commit v12 on v11

--- a/solution.py
+++ b/solution.py
@@ -159,8 +159,8 @@
         input_output_aliases={} if sums is None else {len(given) - 1: 0},
         compiler_params=pltpu.CompilerParams(vmem_limit_bytes=14 * 2**20),
         cost_estimate=pl.CostEstimate(
-            flops=2**20,
-            bytes_accessed=2**16,
+            flops=2**12,
+            bytes_accessed=2**10,
             transcendentals=0,
         ),
     )(*given)
@@ -194,10 +194,12 @@
 
 
 def join_kernel(*refs):
-    *chunks, own, spots = refs
+    *chunks, low, high, spots = refs
+    half = len(chunks) // 2
     for k, chunk in enumerate(chunks):
         size = chunk.shape[0] - 8
-        own[k * size : (k + 1) * size] = chunk[:size]
+        own, at = (low, high)[k // half], k % half * size
+        own[at : at + size] = chunk[:size]
         spots[k] = chunk[size:].astype(jnp.int32)
 
 
@@ -206,11 +208,12 @@
     return pl.pallas_call(
         join_kernel,
         out_shape=[
-            jax.ShapeDtypeStruct((len(chunks) * size, LANES), jnp.float32),
+            jax.ShapeDtypeStruct((len(chunks) // 2 * size, LANES), jnp.float32),
+            jax.ShapeDtypeStruct((len(chunks) // 2 * size, LANES), jnp.float32),
             jax.ShapeDtypeStruct((len(chunks), 8, LANES), jnp.int32),
         ],
         in_specs=[VMEM] * len(chunks),
-        out_specs=[VMEM] * 2,
+        out_specs=[VMEM] * 3,
         compiler_params=pltpu.CompilerParams(vmem_limit_bytes=14 * 2**20),
         cost_estimate=pl.CostEstimate(flops=0, bytes_accessed=2**16, transcendentals=0),
     )(*chunks)
@@ -241,16 +244,17 @@
     planes = [
         [(2 * z + x) * cols + c for x in range(2) for c in range(cols)] for z in range(rows_axis // 2)
     ]
+    t_other = send_t(t_amps)
     parts = pack(v_tiles, v_where, cols)
     parts = lax.all_to_all(parts, ("row", "col"), 0, 0, tiled=True, axis_index_groups=planes)
+    parts, t_other = lax.optimization_barrier((parts, t_other))
     chunks = sort(place, parts, blocks // 2)
 
     def send_m(chunk, k):
         return send(chunk, lambda i: i ^ (2 * GROUP * k) ^ (2 * (k.bit_count() % 2)), "row", rows_axis)
 
-    own, spots = join([chunks[0]] + [send_m(chunks[k], k) for k in range(1, blocks // 2)])
+    low, high, spots = join([chunks[0]] + [send_m(chunks[k], k) for k in range(1, blocks // 2)])
     spots = spots[:, : 2 * GROUP, :slots].reshape(blocks * GROUP, slots)
-    own, t_other = lax.optimization_barrier((own, t_amps))
 
     def up(i):
         return (i + 2) % cols
@@ -264,30 +268,44 @@
     def add(sums, held, *shares):
         return contract(sums, place, spots, held, shares, pair)
 
-    half, middle = own.shape[0] // 2, blocks // 2
-    partner = send(own, across)
-    below = send(own, up)
-    above = send(own, down)
-    t_other = send_t(t_other)
-    tiles = {0: prepare(t_amps)}
-    sums = add(None, tiles, ((0, 0, 0), own))
-    sums, partner, below, above = lax.optimization_barrier((sums, partner, below, above))
-    far_low = send(below[:half], up)
-    far_high = send(above[half:], down)
-    partner_below = send(partner, up)
-    partner_above = send(partner, down)
-    near = [((0, 0, 0), own), ((0, 0, 1), partner), ((0, -2, 0), below), ((0, 2, 0), above)]
-    sums = add(sums, tiles, *near[1:])
+    middle = blocks // 2
+
+    def halves(shift, flip, low, high):
+        return [((0, shift, flip), low), ((middle, shift, flip), high)]
+
+    below_low, above_high = send(low, up), send(high, down)
+    partner_low = send(low, across)
+    below_high, above_low = send(high, up), send(low, down)
+    partner_high = send(high, across)
+    tiles = {0: prepare(t_amps), 1: prepare(t_other)}
+    sums = add(None, tiles, *halves(0, 0, low, high))
+    sums, below_low, above_high = lax.optimization_barrier((sums, below_low, above_high))
+    far_low, far_high = send(below_low, up), send(above_high, down)
+    partner_below_low, partner_above_low = send(partner_low, up), send(partner_low, down)
+    partner_below_high, partner_above_high = send(partner_high, up), send(partner_high, down)
+    sums = add(
+        sums,
+        tiles,
+        *halves(0, 1, partner_low, partner_high),
+        *halves(-2, 0, below_low, below_high),
+        *halves(2, 0, above_low, above_high),
+    )
     sums, far_low, far_high = lax.optimization_barrier((sums, far_low, far_high))
-    partner_far_low = send(far_low, across)
-    partner_far_high = send(far_high, across)
-    other = {1: prepare(t_other)}
-    sums = add(sums, other, *near)
-    both = {**tiles, **other}
-    sums = add(sums, both, ((0, 4, 0), far_low), ((middle, 4, 0), far_high))
-    sums = add(sums, both, ((0, -2, 1), partner_below), ((0, 2, 1), partner_above))
-    sums = add(sums, both, ((0, 4, 1), partner_far_low), ((middle, 4, 1), partner_far_high))
-
+    partner_far_low, partner_far_high = send(far_low, across), send(far_high, across)
+    sums = add(
+        sums,
+        tiles,
+        *halves(4, 0, far_low, far_high),
+        ((0, -2, 1), partner_below_low),
+        ((0, 2, 1), partner_above_low),
+    )
+    sums = add(
+        sums,
+        tiles,
+        ((middle, -2, 1), partner_below_high),
+        ((middle, 2, 1), partner_above_high),
+        *halves(4, 1, partner_far_low, partner_far_high),
+    )
     sums = sums[0] + lax.ppermute(sums[1], "layer", [(0, 1), (1, 0)])
     sums = lax.all_to_all(sums, "row", 0, 0, tiled=True, axis_index_groups=ranks)
     return jnp.sum(sums, axis=0)

time: 101 us -> 104 us (1.030)
  waiting for transfers between devices: 42 us -> 31.5 us
  starting transfers between devices: 30.5 us -> 40.7 us
  blocking collectives: 14.1 us -> 19.1 us
  Pallas kernels: 11.4 us -> 9.62 us
    ppermute x13 -> x18, waiting for transfers between devices: 29.9 us -> 19.6 us  [send(): return lax.ppermute(share, axis, [(i, to(i)) for i in range(size)])]
    ppermute x13 -> x18, starting transfers between devices: 18.9 us -> 26.4 us  [send(): return lax.ppermute(share, axis, [(i, to(i)) for i in range(size)])]
    all_to_all x1, blocking collectives: 14.1 us -> 19.1 us  [on_device(): lax.all_to_all(sums, 'row', 0, 0, tiled=True, axis_index_groups=ranks)]
    ppermute x1, starting transfers between devices: 4.02 us -> 7.62 us  [on_device(): sums = sums[0] + lax.ppermute(sums[1], 'layer', [(0, 1), (1, 0)])]
    pallas_call x6 -> x4, Pallas kernels: 7.92 us -> 6.12 us  [contract(): pl.pallas_call(kernel, out_shape=jax.ShapeDtypeStruct((2, blocks, ij, LAN...]
  transfers between devices with their start and end apart: 15 -> 20, of which waited for: 10 -> 9; matrix products, arithmetic and copies ran while one was open for 0% -> 0% of each run, Pallas kernels for 8% -> 7%
where the time goes in v12:
time: 104 us
  starting transfers between devices  40.7 us (39%)
  waiting for transfers between devices  31.5 us (30%)
  blocking collectives  19.1 us (18%)
  Pallas kernels  9.62 us (9%)
  local copies, waits for them, and re-layouts  1.74 us (2%)
    ppermute x18, starting transfers between devices, send(): return lax.ppermute(share, axis, [(i, to(i)) for i in range(size)])  26.4 us
    ppermute x18, waiting for transfers between devices, send(): return lax.ppermute(share, axis, [(i, to(i)) for i in range(size)])  19.6 us
    all_to_all x1, blocking collectives, on_device(): lax.all_to_all(sums, 'row', 0, 0, tiled=True, axis_index_groups=ranks)  19.1 us
    all_to_all x1, waiting for transfers between devices, on_device(): lax.all_to_all(parts, ('row', 'col'), 0, 0, tiled=True, axis_index_groups...  10.7 us
    ppermute x1, starting transfers between devices, on_device(): sums = sums[0] + lax.ppermute(sums[1], 'layer', [(0, 1), (1, 0)])  7.62 us
    all_to_all x1, starting transfers between devices, on_device(): lax.all_to_all(parts, ('row', 'col'), 0, 0, tiled=True, axis_index_groups...  6.75 us
    pallas_call x4, Pallas kernels, contract(): pl.pallas_call(kernel, out_shape=jax.ShapeDtypeStruct((2, blocks, ij, LAN...  6.12 us
  transfers between devices with their start and end apart: 20, of which 9 were waited for; matrix products, arithmetic and copies ran while one was open for 0% of the time, Pallas kernels for 7%

profile of v12, /device:TPU:1, one launch (start us, length us, event | category | flops | bytes accessed | tf_op | source)
XLA Modules:
  0.0 103.6 jit_solution(8867793580097753851)
XLA Ops:
  0.0 0.0 copy-start
  0.0 2.5 %collective-permute-start = (f32[64,4096]{1,0:T(8,128)}, f32[64,4096]{1,0:T(8,128)S(1)}, u32[]{:S(2)}, u32[]{:S(2)}) collective-permute-start(f32[64,4096]{1,0:T(8,128)} %refs_0_.1), channel_id=1, source_target_pairs={{0,32},{16,48},{32,0},{48,16},{64,96},{80,112},{96,64},{112,80},{1... | collective-permute-start | bytes 3145736 | tf_op jit(solution)/shard_map/ppermute | solution.py:239
  2.5 0.0 copy-start.1
  2.5 1.0 %copy-done.1 = f32[2,1,1,16,4096]{4,3,2,1,0:T(8,128)S(1)} copy-done((f32[2,1,1,16,4096]{4,3,2,1,0:T(8,128)S(1)}, f32[2,1,1,16,4096]{4,3,2,1,0:T(8,128)}, u32[]{:S(2)}) %copy-start.1) | copy-done | bytes 524312
  3.5 0.0 copy-start.2
  3.5 0.7 copy-done.2
  4.2 1.5 %shard_map.37 = f32[16,72,128]{2,1,0:T(8,128)} custom-call(s32[2,16]{1,0:T(2,128)S(1)} %bitcast.22, f32[2,2,256,128]{3,2,1,0:T(8,128)S(1)} %bitcast.17), custom_call_target="tpu_custom_call" | custom-call | bytes 1048576 | tf_op jit(solution)/shard_map/pallas_call | solution.py:43
  5.7 6.8 %all-to-all-start = ((f32[16,72,128]{2,1,0:T(8,128)}), f32[16,72,128]{2,1,0:T(8,128)S(1)}, u32[]{:S(2)}, u32[]{:S(2)}) async-start(f32[16,72,128]{2,1,0:T(8,128)} %shard_map.37), calls=%async_computation | async-start | bytes 1179648 | tf_op jit(solution)/shard_map/all_to_all | solution.py:249
  12.5 0.1 pad_add_fusion.place.refs_0_
  12.5 10.7 %all-to-all-done.parts = f32[16,72,128]{2,1,0:T(8,128)S(1)} async-done(((f32[16,72,128]{2,1,0:T(8,128)}), f32[16,72,128]{2,1,0:T(8,128)S(1)}, u32[]{:S(2)}, u32[]{:S(2)}) %all-to-all-start) | async-done | bytes 589856 | tf_op jit(solution)/shard_map/all_to_all | solution.py:249
  23.3 1.3 %collective-permute-done.refs_0_ = f32[64,4096]{1,0:T(8,128)S(1)} collective-permute-done((f32[64,4096]{1,0:T(8,128)}, f32[64,4096]{1,0:T(8,128)S(1)}, u32[]{:S(2)}, u32[]{:S(2)}) %collective-permute-start) | collective-permute-done | bytes 1048608 | tf_op jit(solution)/shard_map/ppermute | solution.py:239
  24.6 0.6 shard_map.38
  25.2 4.9 %collective-permute-start.1 = (f32[264,128]{1,0:T(8,128)S(1)}, f32[264,128]{1,0:T(8,128)S(1)}, u32[]{:S(2)}, u32[]{:S(2)}) collective-permute-start(f32[264,128]{1,0:T(8,128)S(1)} %get-tuple-element.22), channel_id=1, source_target_pairs={{0,96},{16,112},{32,64},{48,80},{64,32},{80,48},{96,0},{112,16},{1... | collective-permute-start | bytes 405512 | tf_op jit(solution)/shard_map/ppermute | solution.py:239
  30.1 2.9 %collective-permute-start.2 = (f32[264,128]{1,0:T(8,128)S(1)}, f32[264,128]{1,0:T(8,128)S(1)}, u32[]{:S(2)}, u32[]{:S(2)}) collective-permute-start(f32[264,128]{1,0:T(8,128)S(1)} %get-tuple-element.23), channel_id=1, source_target_pairs={{0,160},{16,176},{32,128},{48,144},{64,224},{80,240},{96,192},{112... | collective-permute-start | bytes 405512 | tf_op jit(solution)/shard_map/ppermute | solution.py:239
  33.0 0.0 collective-permute-start.3
  33.0 0.0 collective-permute-done.1.refs_1_
  33.0 10.1 %collective-permute-done.2.refs_2_ = f32[264,128]{1,0:T(8,128)S(1)} collective-permute-done((f32[264,128]{1,0:T(8,128)S(1)}, f32[264,128]{1,0:T(8,128)S(1)}, u32[]{:S(2)}, u32[]{:S(2)}) %collective-permute-start.2) | collective-permute-done | bytes 135200 | tf_op jit(solution)/shard_map/ppermute | solution.py:239
  43.1 0.4 collective-permute-done.3.refs_3_
  43.6 1.4 %collective-permute-start.8 = (f32[512,128]{1,0:T(8,128)S(1)}, f32[512,128]{1,0:T(8,128)S(1)}, u32[]{:S(2)}, u32[]{:S(2)}) collective-permute-start(f32[512,128]{1,0:T(8,128)S(1)} %get-tuple-element.28.refs_4_), channel_id=1, source_target_pairs={{0,4},{2,6},{4,8},{6,10},{8,12},{10,14},{12,0},{14,2},{1,5},{3,7},... | collective-permute-start | bytes 786440 | tf_op jit(solution)/shard_map/ppermute | solution.py:239
  44.9 1.5 %collective-permute-start.9 = (f32[512,128]{1,0:T(8,128)S(1)}, f32[512,128]{1,0:T(8,128)S(1)}, u32[]{:S(2)}, u32[]{:S(2)}) collective-permute-start(f32[512,128]{1,0:T(8,128)S(1)} %get-tuple-element.27.refs_5_), channel_id=1, source_target_pairs={{0,12},{2,14},{4,0},{6,2},{8,4},{10,6},{12,8},{14,10},{1,13},{3,15... | collective-permute-start | bytes 786440 | tf_op jit(solution)/shard_map/ppermute | solution.py:239
  46.5 0.0 collective-permute-start.10
  46.5 1.2 %collective-permute-start.7 = (f32[512,128]{1,0:T(8,128)S(1)}, f32[512,128]{1,0:T(8,128)S(1)}, u32[]{:S(2)}, u32[]{:S(2)}) collective-permute-start(f32[512,128]{1,0:T(8,128)S(1)} %get-tuple-element.28.refs_4_), channel_id=1, source_target_pairs={{0,2},{2,0},{4,6},{6,4},{8,10},{10,8},{12,14},{14,12},{1,3},{3,1},... | collective-permute-start | bytes 786440 | tf_op jit(solution)/shard_map/ppermute | solution.py:239
  47.7 0.0 copy-done
  47.7 0.7 shard_map.40.refs_2_
  48.4 0.7 shard_map.41.refs_3_
  49.1 2.8 %collective-permute-start.11 = (f32[512,128]{1,0:T(8,128)S(1)}, f32[512,128]{1,0:T(8,128)S(1)}, u32[]{:S(2)}, u32[]{:S(2)}) collective-permute-start(f32[512,128]{1,0:T(8,128)S(1)} %get-tuple-element.28.refs_4_), channel_id=1, source_target_pairs={{0,12},{2,14},{4,0},{6,2},{8,4},{10,6},{12,8},{14,10},{1,13},{3,15... | collective-permute-start | bytes 786440 | tf_op jit(solution)/shard_map/ppermute | solution.py:239
  51.9 1.2 %shard_map.42.refs_10_ = f32[2,8,64,128]{3,2,1,0:T(8,128)S(1)} custom-call(s32[4]{0:T(128)S(1)} %pad_add_fusion.place.refs_0_, s32[16,16]{1,0:T(8,128)S(1)} %bitcast.18, bf16[64,128,128]{2,1,0:T(8,128)(2,1)S(1)} %shard_map.40.refs_2_, bf16[64,128,128]{2,1,0:T(8,128)(2,1)S(1)} %shard_map.41.refs_3_, f32[512,128]{1,0:T(8,128)S(1)} %get-tuple-element.28.refs_4_, ...), custom_call_target="tpu_custom_call" | custom-call | flops 4096 | bytes 1024 | tf_op jit(solution)/shard_map/pallas_call | solution.py:154
  53.1 0.0 collective-permute-done.8.refs_6_
  53.1 0.3 collective-permute-start.4
  53.4 0.0 collective-permute-done.9.refs_9_
  53.4 0.0 collective-permute-start.12
  53.4 3.0 %collective-permute-done.10.refs_7_ = f32[512,128]{1,0:T(8,128)S(1)} collective-permute-done((f32[512,128]{1,0:T(8,128)S(1)}, f32[512,128]{1,0:T(8,128)S(1)}, u32[]{:S(2)}, u32[]{:S(2)}) %collective-permute-start.10) | collective-permute-done | bytes 262176 | tf_op jit(solution)/shard_map/ppermute | solution.py:239
  56.5 1.4 %collective-permute-start.13 = (f32[512,128]{1,0:T(8,128)S(1)}, f32[512,128]{1,0:T(8,128)S(1)}, u32[]{:S(2)}, u32[]{:S(2)}) collective-permute-start(f32[512,128]{1,0:T(8,128)S(1)} %collective-permute-done.9.refs_9_), channel_id=1, source_target_pairs={{0,12},{2,14},{4,0},{6,2},{8,4},{10,6},{12,8},{14,10},{1,13},{3,15... | collective-permute-start | bytes 786440 | tf_op jit(solution)/shard_map/ppermute | solution.py:239
  57.9 0.0 collective-permute-done.7.refs_4_
  57.9 0.1 collective-permute-start.16
  57.9 0.0 collective-permute-done.11.refs_8_
  57.9 2.6 %collective-permute-start.17 = (f32[512,128]{1,0:T(8,128)S(1)}, f32[512,128]{1,0:T(8,128)S(1)}, u32[]{:S(2)}, u32[]{:S(2)}) collective-permute-start(f32[512,128]{1,0:T(8,128)S(1)} %collective-permute-done.7.refs_4_), channel_id=1, source_target_pairs={{0,12},{2,14},{4,0},{6,2},{8,4},{10,6},{12,8},{14,10},{1,13},{3,15... | collective-permute-start | bytes 786440 | tf_op jit(solution)/shard_map/ppermute | solution.py:239
  60.6 0.0 collective-permute-done.4.refs_5_
  60.6 0.0 collective-permute-start.5
  60.6 1.8 %shard_map.43.refs_8_ = f32[2,8,64,128]{3,2,1,0:T(8,128)S(1)} custom-call(s32[4]{0:T(128)S(1)} %pad_add_fusion.place.refs_0_, s32[16,16]{1,0:T(8,128)S(1)} %bitcast.19, bf16[64,128,128]{2,1,0:T(8,128)(2,1)S(1)} %shard_map.40.refs_2_, bf16[64,128,128]{2,1,0:T(8,128)(2,1)S(1)} %shard_map.41.refs_3_, ...), custom_call_target="tpu_custom_call", output_to_operand_aliasing={{}: (10, {})} | custom-call | flops 4096 | bytes 1024 | tf_op jit(solution)/shard_map/pallas_call | solution.py:154
  62.4 0.0 collective-permute-done.12.refs_4_
  62.4 2.8 %collective-permute-start.6 = (f32[512,128]{1,0:T(8,128)S(1)}, f32[512,128]{1,0:T(8,128)S(1)}, u32[]{:S(2)}, u32[]{:S(2)}) collective-permute-start(f32[512,128]{1,0:T(8,128)S(1)} %collective-permute-done.4.refs_5_), channel_id=1, source_target_pairs={{0,12},{2,14},{4,0},{6,2},{8,4},{10,6},{12,8},{14,10},{1,13},{3,15... | collective-permute-start | bytes 786440 | tf_op jit(solution)/shard_map/ppermute | solution.py:239
  65.2 0.0 collective-permute-done.13.refs_5_
  65.2 1.2 %collective-permute-start.14 = (f32[512,128]{1,0:T(8,128)S(1)}, f32[512,128]{1,0:T(8,128)S(1)}, u32[]{:S(2)}, u32[]{:S(2)}) collective-permute-start(f32[512,128]{1,0:T(8,128)S(1)} %collective-permute-done.12.refs_4_), channel_id=1, source_target_pairs={{0,2},{2,0},{4,6},{6,4},{8,10},{10,8},{12,14},{14,12},{1,3},{3,1},... | collective-permute-start | bytes 786440 | tf_op jit(solution)/shard_map/ppermute | solution.py:239
  66.4 0.9 collective-permute-done.16.refs_6_
  67.3 0.9 collective-permute-start.15
  68.2 0.0 collective-permute-done.17.refs_7_
  68.2 1.5 %shard_map.44.refs_8_ = f32[2,8,64,128]{3,2,1,0:T(8,128)S(1)} custom-call(s32[4]{0:T(128)S(1)} %pad_add_fusion.place.refs_0_, s32[16,16]{1,0:T(8,128)S(1)} %bitcast.20, bf16[64,128,128]{2,1,0:T(8,128)(2,1)S(1)} %shard_map.40.refs_2_, bf16[64,128,128]{2,1,0:T(8,128)(2,1)S(1)} %shard_map.41.refs_3_, ...), custom_call_target="tpu_custom_call", output_to_operand_aliasing={{}: (8, {})} | custom-call | flops 4096 | bytes 1024 | tf_op jit(solution)/shard_map/pallas_call | solution.py:154
  69.7 2.8 %collective-permute-done.5.refs_4_ = f32[512,128]{1,0:T(8,128)S(1)} collective-permute-done((f32[512,128]{1,0:T(8,128)S(1)}, f32[512,128]{1,0:T(8,128)S(1)}, u32[]{:S(2)}, u32[]{:S(2)}) %collective-permute-start.5) | collective-permute-done | bytes 262176 | tf_op jit(solution)/shard_map/ppermute | solution.py:239
  72.6 0.0 collective-permute-done.6.refs_5_
  72.6 0.0 collective-permute-done.14.refs_6_
  72.6 0.9 collective-permute-done.15.refs_7_
  73.5 1.5 %shard_map.45 = f32[2,8,64,128]{3,2,1,0:T(8,128)S(1)} custom-call(s32[4]{0:T(128)S(1)} %pad_add_fusion.place.refs_0_, s32[16,16]{1,0:T(8,128)S(1)} %bitcast.21, bf16[64,128,128]{2,1,0:T(8,128)(2,1)S(1)} %shard_map.40.refs_2_, bf16[64,128,128]{2,1,0:T(8,128)(2,1)S(1)} %shard_map.41.refs_3_, ...), custom_call_target="tpu_custom_call", output_to_operand_aliasing={{}: (8, {})} | custom-call | flops 4096 | bytes 1024 | tf_op jit(solution)/shard_map/pallas_call | solution.py:154
  75.1 7.6 %collective-permute-start.18 = (f32[8,64,128]{2,1,0:T(8,128)S(1)}, f32[8,64,128]{2,1,0:T(8,128)S(1)}, u32[]{:S(2)}, u32[]{:S(2)}) collective-permute-start(f32[8,64,128]{2,1,0:T(8,128)S(1)} %slice_bitcast_fusion), channel_id=1, source_target_pairs={{0,1},{1,0},{2,3},{3,2},{4,5},{5,4},{6,7},{7,6},{8,9},{9,8},{10,11... | collective-permute-start | bytes 786440 | tf_op jit(solution)/shard_map/ppermute | solution.py:309
  82.7 1.2 %collective-permute-done.18 = f32[8,64,128]{2,1,0:T(8,128)S(1)} collective-permute-done((f32[8,64,128]{2,1,0:T(8,128)S(1)}, f32[8,64,128]{2,1,0:T(8,128)S(1)}, u32[]{:S(2)}, u32[]{:S(2)}) %collective-permute-start.18) | collective-permute-done | bytes 262176 | tf_op jit(solution)/shard_map/ppermute | solution.py:309
  83.9 19.1 %all_to_all.10 = f32[8,64,128]{2,1,0:T(8,128)S(1)} all-to-all(f32[8,64,128]{2,1,0:T(8,128)S(1)} %fusion), channel_id=1, replica_groups={{0,16,96,112,160,176,192,208},{32,48,64,80,128,144,224,240},{1,17,97,11..., dimensions={0} | all-to-all | bytes 524288 | tf_op jit(solution)/shard_map/all_to_all | solution.py:310
  103.0 0.6 reduce_sum.9
  (4 shorter events, 0.1 us)
Async XLA Ops:
  0.0 47.7 %copy-start = (f32[64,4096]{1,0:T(8,128)S(1)}, f32[64,4096]{1,0:T(8,128)}, u32[]{:S(2)}) copy-start(f32[64,4096]{1,0:T(8,128)} %refs_0_.1) | copy-start | bytes 3145732
  0.0 24.6 %collective-permute-start = (f32[64,4096]{1,0:T(8,128)}, f32[64,4096]{1,0:T(8,128)S(1)}, u32[]{:S(2)}, u32[]{:S(2)}) collective-permute-start(f32[64,4096]{1,0:T(8,128)} %refs_0_.1), channel_id=1, source_target_pairs={{0,32},{16,48},{32,0},{48,16},{64,96},{80,112},{96,64},{112,80},{1... | collective-permute-start | bytes 3145736 | tf_op jit(solution)/shard_map/ppermute | solution.py:239
  2.5 1.0 %copy-start.1 = (f32[2,1,1,16,4096]{4,3,2,1,0:T(8,128)S(1)}, f32[2,1,1,16,4096]{4,3,2,1,0:T(8,128)}, u32[]{:S(2)}) copy-start(f32[2,1,1,16,4096]{4,3,2,1,0:T(8,128)} %param.4) | copy-start | bytes 1572868
  3.5 0.7 copy-start.2
  5.7 17.6 %all-to-all-start = ((f32[16,72,128]{2,1,0:T(8,128)}), f32[16,72,128]{2,1,0:T(8,128)S(1)}, u32[]{:S(2)}, u32[]{:S(2)}) async-start(f32[16,72,128]{2,1,0:T(8,128)} %shard_map.37), calls=%async_computation | async-start | bytes 1179648 | tf_op jit(solution)/shard_map/all_to_all | solution.py:249
  25.2 7.8 %collective-permute-start.1 = (f32[264,128]{1,0:T(8,128)S(1)}, f32[264,128]{1,0:T(8,128)S(1)}, u32[]{:S(2)}, u32[]{:S(2)}) collective-permute-start(f32[264,128]{1,0:T(8,128)S(1)} %get-tuple-element.22), channel_id=1, source_target_pairs={{0,96},{16,112},{32,64},{48,80},{64,32},{80,48},{96,0},{112,16},{1... | collective-permute-start | bytes 405512 | tf_op jit(solution)/shard_map/ppermute | solution.py:239
  30.1 13.0 %collective-permute-start.2 = (f32[264,128]{1,0:T(8,128)S(1)}, f32[264,128]{1,0:T(8,128)S(1)}, u32[]{:S(2)}, u32[]{:S(2)}) collective-permute-start(f32[264,128]{1,0:T(8,128)S(1)} %get-tuple-element.23), channel_id=1, source_target_pairs={{0,160},{16,176},{32,128},{48,144},{64,224},{80,240},{96,192},{112... | collective-permute-start | bytes 405512 | tf_op jit(solution)/shard_map/ppermute | solution.py:239
  33.0 10.6 %collective-permute-start.3 = (f32[264,128]{1,0:T(8,128)S(1)}, f32[264,128]{1,0:T(8,128)S(1)}, u32[]{:S(2)}, u32[]{:S(2)}) collective-permute-start(f32[264,128]{1,0:T(8,128)S(1)} %get-tuple-element.24), channel_id=1, source_target_pairs={{0,192},{16,208},{32,224},{48,240},{64,128},{80,144},{96,160},{112... | collective-permute-start | bytes 405512 | tf_op jit(solution)/shard_map/ppermute | solution.py:239
  43.6 9.5 %collective-permute-start.8 = (f32[512,128]{1,0:T(8,128)S(1)}, f32[512,128]{1,0:T(8,128)S(1)}, u32[]{:S(2)}, u32[]{:S(2)}) collective-permute-start(f32[512,128]{1,0:T(8,128)S(1)} %get-tuple-element.28.refs_4_), channel_id=1, source_target_pairs={{0,4},{2,6},{4,8},{6,10},{8,12},{10,14},{12,0},{14,2},{1,5},{3,7},... | collective-permute-start | bytes 786440 | tf_op jit(solution)/shard_map/ppermute | solution.py:239
  44.9 8.5 %collective-permute-start.9 = (f32[512,128]{1,0:T(8,128)S(1)}, f32[512,128]{1,0:T(8,128)S(1)}, u32[]{:S(2)}, u32[]{:S(2)}) collective-permute-start(f32[512,128]{1,0:T(8,128)S(1)} %get-tuple-element.27.refs_5_), channel_id=1, source_target_pairs={{0,12},{2,14},{4,0},{6,2},{8,4},{10,6},{12,8},{14,10},{1,13},{3,15... | collective-permute-start | bytes 786440 | tf_op jit(solution)/shard_map/ppermute | solution.py:239
  46.5 10.0 %collective-permute-start.10 = (f32[512,128]{1,0:T(8,128)S(1)}, f32[512,128]{1,0:T(8,128)S(1)}, u32[]{:S(2)}, u32[]{:S(2)}) collective-permute-start(f32[512,128]{1,0:T(8,128)S(1)} %get-tuple-element.27.refs_5_), channel_id=1, source_target_pairs={{0,4},{2,6},{4,8},{6,10},{8,12},{10,14},{12,0},{14,2},{1,5},{3,7},... | collective-permute-start | bytes 786440 | tf_op jit(solution)/shard_map/ppermute | solution.py:239
  46.5 11.4 %collective-permute-start.7 = (f32[512,128]{1,0:T(8,128)S(1)}, f32[512,128]{1,0:T(8,128)S(1)}, u32[]{:S(2)}, u32[]{:S(2)}) collective-permute-start(f32[512,128]{1,0:T(8,128)S(1)} %get-tuple-element.28.refs_4_), channel_id=1, source_target_pairs={{0,2},{2,0},{4,6},{6,4},{8,10},{10,8},{12,14},{14,12},{1,3},{3,1},... | collective-permute-start | bytes 786440 | tf_op jit(solution)/shard_map/ppermute | solution.py:239
  49.1 8.8 %collective-permute-start.11 = (f32[512,128]{1,0:T(8,128)S(1)}, f32[512,128]{1,0:T(8,128)S(1)}, u32[]{:S(2)}, u32[]{:S(2)}) collective-permute-start(f32[512,128]{1,0:T(8,128)S(1)} %get-tuple-element.28.refs_4_), channel_id=1, source_target_pairs={{0,12},{2,14},{4,0},{6,2},{8,4},{10,6},{12,8},{14,10},{1,13},{3,15... | collective-permute-start | bytes 786440 | tf_op jit(solution)/shard_map/ppermute | solution.py:239
  53.1 7.5 %collective-permute-start.4 = (f32[512,128]{1,0:T(8,128)S(1)}, f32[512,128]{1,0:T(8,128)S(1)}, u32[]{:S(2)}, u32[]{:S(2)}) collective-permute-start(f32[512,128]{1,0:T(8,128)S(1)} %get-tuple-element.27.refs_5_), channel_id=1, source_target_pairs={{0,2},{2,0},{4,6},{6,4},{8,10},{10,8},{12,14},{14,12},{1,3},{3,1},... | collective-permute-start | bytes 786440 | tf_op jit(solution)/shard_map/ppermute | solution.py:239
  53.4 9.0 %collective-permute-start.12 = (f32[512,128]{1,0:T(8,128)S(1)}, f32[512,128]{1,0:T(8,128)S(1)}, u32[]{:S(2)}, u32[]{:S(2)}) collective-permute-start(f32[512,128]{1,0:T(8,128)S(1)} %collective-permute-done.8.refs_6_), channel_id=1, source_target_pairs={{0,4},{2,6},{4,8},{6,10},{8,12},{10,14},{12,0},{14,2},{1,5},{3,7},... | collective-permute-start | bytes 786440 | tf_op jit(solution)/shard_map/ppermute | solution.py:239
  56.5 8.7 %collective-permute-start.13 = (f32[512,128]{1,0:T(8,128)S(1)}, f32[512,128]{1,0:T(8,128)S(1)}, u32[]{:S(2)}, u32[]{:S(2)}) collective-permute-start(f32[512,128]{1,0:T(8,128)S(1)} %collective-permute-done.9.refs_9_), channel_id=1, source_target_pairs={{0,12},{2,14},{4,0},{6,2},{8,4},{10,6},{12,8},{14,10},{1,13},{3,15... | collective-permute-start | bytes 786440 | tf_op jit(solution)/shard_map/ppermute | solution.py:239
  57.9 9.4 %collective-permute-start.16 = (f32[512,128]{1,0:T(8,128)S(1)}, f32[512,128]{1,0:T(8,128)S(1)}, u32[]{:S(2)}, u32[]{:S(2)}) collective-permute-start(f32[512,128]{1,0:T(8,128)S(1)} %collective-permute-done.7.refs_4_), channel_id=1, source_target_pairs={{0,4},{2,6},{4,8},{6,10},{8,12},{10,14},{12,0},{14,2},{1,5},{3,7},... | collective-permute-start | bytes 786440 | tf_op jit(solution)/shard_map/ppermute | solution.py:239
  57.9 10.3 %collective-permute-start.17 = (f32[512,128]{1,0:T(8,128)S(1)}, f32[512,128]{1,0:T(8,128)S(1)}, u32[]{:S(2)}, u32[]{:S(2)}) collective-permute-start(f32[512,128]{1,0:T(8,128)S(1)} %collective-permute-done.7.refs_4_), channel_id=1, source_target_pairs={{0,12},{2,14},{4,0},{6,2},{8,4},{10,6},{12,8},{14,10},{1,13},{3,15... | collective-permute-start | bytes 786440 | tf_op jit(solution)/shard_map/ppermute | solution.py:239
  60.6 12.0 %collective-permute-start.5 = (f32[512,128]{1,0:T(8,128)S(1)}, f32[512,128]{1,0:T(8,128)S(1)}, u32[]{:S(2)}, u32[]{:S(2)}) collective-permute-start(f32[512,128]{1,0:T(8,128)S(1)} %collective-permute-done.4.refs_5_), channel_id=1, source_target_pairs={{0,4},{2,6},{4,8},{6,10},{8,12},{10,14},{12,0},{14,2},{1,5},{3,7},... | collective-permute-start | bytes 786440 | tf_op jit(solution)/shard_map/ppermute | solution.py:239
  62.4 10.1 %collective-permute-start.6 = (f32[512,128]{1,0:T(8,128)S(1)}, f32[512,128]{1,0:T(8,128)S(1)}, u32[]{:S(2)}, u32[]{:S(2)}) collective-permute-start(f32[512,128]{1,0:T(8,128)S(1)} %collective-permute-done.4.refs_5_), channel_id=1, source_target_pairs={{0,12},{2,14},{4,0},{6,2},{8,4},{10,6},{12,8},{14,10},{1,13},{3,15... | collective-permute-start | bytes 786440 | tf_op jit(solution)/shard_map/ppermute | solution.py:239
  65.2 7.4 %collective-permute-start.14 = (f32[512,128]{1,0:T(8,128)S(1)}, f32[512,128]{1,0:T(8,128)S(1)}, u32[]{:S(2)}, u32[]{:S(2)}) collective-permute-start(f32[512,128]{1,0:T(8,128)S(1)} %collective-permute-done.12.refs_4_), channel_id=1, source_target_pairs={{0,2},{2,0},{4,6},{6,4},{8,10},{10,8},{12,14},{14,12},{1,3},{3,1},... | collective-permute-start | bytes 786440 | tf_op jit(solution)/shard_map/ppermute | solution.py:239
  67.3 6.2 %collective-permute-start.15 = (f32[512,128]{1,0:T(8,128)S(1)}, f32[512,128]{1,0:T(8,128)S(1)}, u32[]{:S(2)}, u32[]{:S(2)}) collective-permute-start(f32[512,128]{1,0:T(8,128)S(1)} %collective-permute-done.13.refs_5_), channel_id=1, source_target_pairs={{0,2},{2,0},{4,6},{6,4},{8,10},{10,8},{12,14},{14,12},{1,3},{3,1},... | collective-permute-start | bytes 786440 | tf_op jit(solution)/shard_map/ppermute | solution.py:239
  75.1 8.8 %collective-permute-start.18 = (f32[8,64,128]{2,1,0:T(8,128)S(1)}, f32[8,64,128]{2,1,0:T(8,128)S(1)}, u32[]{:S(2)}, u32[]{:S(2)}) collective-permute-start(f32[8,64,128]{2,1,0:T(8,128)S(1)} %slice_bitcast_fusion), channel_id=1, source_target_pairs={{0,1},{1,0},{2,3},{3,2},{4,5},{5,4},{6,7},{7,6},{8,9},{9,8},{10,11... | collective-permute-start | bytes 786440 | tf_op jit(solution)/shard_map/ppermute | solution.py:309

commit v13 on v11

--- a/solution.py
+++ b/solution.py
@@ -159,8 +159,8 @@
         input_output_aliases={} if sums is None else {len(given) - 1: 0},
         compiler_params=pltpu.CompilerParams(vmem_limit_bytes=14 * 2**20),
         cost_estimate=pl.CostEstimate(
-            flops=2**20,
-            bytes_accessed=2**16,
+            flops=2**12,
+            bytes_accessed=2**10,
             transcendentals=0,
         ),
     )(*given)
@@ -250,7 +250,6 @@
 
     own, spots = join([chunks[0]] + [send_m(chunks[k], k) for k in range(1, blocks // 2)])
     spots = spots[:, : 2 * GROUP, :slots].reshape(blocks * GROUP, slots)
-    own, t_other = lax.optimization_barrier((own, t_amps))
 
     def up(i):
         return (i + 2) % cols
@@ -268,9 +267,10 @@
     partner = send(own, across)
     below = send(own, up)
     above = send(own, down)
-    t_other = send_t(t_other)
     tiles = {0: prepare(t_amps)}
     sums = add(None, tiles, ((0, 0, 0), own))
+    sums, t_other = lax.optimization_barrier((sums, t_amps))
+    t_other = send_t(t_other)
     sums, partner, below, above = lax.optimization_barrier((sums, partner, below, above))
     far_low = send(below[:half], up)
     far_high = send(above[half:], down)

time: 101 us -> 99.5 us (0.985)
  waiting for transfers between devices: 42 us -> 37.2 us
  starting transfers between devices: 30.5 us -> 32.6 us
    ppermute x13, waiting for transfers between devices: 29.9 us -> 25.1 us  [send(): return lax.ppermute(share, axis, [(i, to(i)) for i in range(size)])]
    ppermute x13, starting transfers between devices: 18.9 us -> 21.1 us  [send(): return lax.ppermute(share, axis, [(i, to(i)) for i in range(size)])]
  transfers between devices with their start and end apart: 15 -> 15, of which waited for: 10 -> 9; matrix products, arithmetic and copies ran while one was open for 0% -> 0% of each run, Pallas kernels for 8% -> 7%
where the time goes in v13:
time: 99.5 us; the launch traced here: 98.9 us
  waiting for transfers between devices  37.2 us (37%)
  starting transfers between devices  32.6 us (33%)
  blocking collectives  14.8 us (15%)
  Pallas kernels  11.4 us (11%)
  local copies, waits for them, and re-layouts  1.87 us (2%)
    ppermute x13, waiting for transfers between devices, send(): return lax.ppermute(share, axis, [(i, to(i)) for i in range(size)])  25.1 us
    ppermute x13, starting transfers between devices, send(): return lax.ppermute(share, axis, [(i, to(i)) for i in range(size)])  21.1 us
    all_to_all x1, blocking collectives, on_device(): lax.all_to_all(sums, 'row', 0, 0, tiled=True, axis_index_groups=ranks)  14.8 us
    all_to_all x1, waiting for transfers between devices, on_device(): lax.all_to_all(parts, ('row', 'col'), 0, 0, tiled=True, axis_index_groups...  11 us
    pallas_call x6, Pallas kernels, contract(): pl.pallas_call(kernel, out_shape=jax.ShapeDtypeStruct((2, blocks, ij, LAN...  7.93 us
    all_to_all x1, starting transfers between devices, on_device(): lax.all_to_all(parts, ('row', 'col'), 0, 0, tiled=True, axis_index_groups...  7.58 us
    ppermute x1, starting transfers between devices, on_device(): sums = sums[0] + lax.ppermute(sums[1], 'layer', [(0, 1), (1, 0)])  3.88 us
  transfers between devices with their start and end apart: 15, of which 9 were waited for; matrix products, arithmetic and copies ran while one was open for 0% of the time, Pallas kernels for 7%

profile of v13, /device:TPU:1, one launch (start us, length us, event | category | flops | bytes accessed | tf_op | source)
XLA Modules:
  0.0 98.9 jit_solution(12539343154184332804)
XLA Ops:
  0.0 0.0 copy-start
  0.0 0.0 copy-start.1
  0.0 1.1 %copy-done.1 = f32[2,1,1,16,4096]{4,3,2,1,0:T(8,128)S(1)} copy-done((f32[2,1,1,16,4096]{4,3,2,1,0:T(8,128)S(1)}, f32[2,1,1,16,4096]{4,3,2,1,0:T(8,128)}, u32[]{:S(2)}) %copy-start.1) | copy-done | bytes 524312
  1.1 0.0 copy-start.2
  1.1 0.7 copy-done.2
  1.8 1.5 %shard_map.37 = f32[16,72,128]{2,1,0:T(8,128)} custom-call(s32[2,16]{1,0:T(2,128)S(1)} %bitcast.24, f32[2,2,256,128]{3,2,1,0:T(8,128)S(1)} %bitcast.17), custom_call_target="tpu_custom_call" | custom-call | bytes 1048576 | tf_op jit(solution)/shard_map/pallas_call | solution.py:43
  3.3 7.6 %all-to-all-start = ((f32[16,72,128]{2,1,0:T(8,128)}), f32[16,72,128]{2,1,0:T(8,128)S(1)}, u32[]{:S(2)}, u32[]{:S(2)}) async-start(f32[16,72,128]{2,1,0:T(8,128)} %shard_map.37), calls=%async_computation | async-start | bytes 1179648 | tf_op jit(solution)/shard_map/all_to_all | solution.py:245
  10.9 0.1 pad_add_fusion.place.refs_0_
  11.0 11.0 %all-to-all-done.parts = f32[16,72,128]{2,1,0:T(8,128)S(1)} async-done(((f32[16,72,128]{2,1,0:T(8,128)}), f32[16,72,128]{2,1,0:T(8,128)S(1)}, u32[]{:S(2)}, u32[]{:S(2)}) %all-to-all-start) | async-done | bytes 589856 | tf_op jit(solution)/shard_map/all_to_all | solution.py:245
  22.0 0.6 shard_map.38
  22.5 4.4 %collective-permute-start = (f32[264,128]{1,0:T(8,128)S(1)}, f32[264,128]{1,0:T(8,128)S(1)}, u32[]{:S(2)}, u32[]{:S(2)}) collective-permute-start(f32[264,128]{1,0:T(8,128)S(1)} %get-tuple-element.21), channel_id=1, source_target_pairs={{0,96},{16,112},{32,64},{48,80},{64,32},{80,48},{96,0},{112,16},{1... | collective-permute-start | bytes 405512 | tf_op jit(solution)/shard_map/ppermute | solution.py:236
  27.0 2.9 %collective-permute-start.1 = (f32[264,128]{1,0:T(8,128)S(1)}, f32[264,128]{1,0:T(8,128)S(1)}, u32[]{:S(2)}, u32[]{:S(2)}) collective-permute-start(f32[264,128]{1,0:T(8,128)S(1)} %get-tuple-element.22), channel_id=1, source_target_pairs={{0,160},{16,176},{32,128},{48,144},{64,224},{80,240},{96,192},{112... | collective-permute-start | bytes 405512 | tf_op jit(solution)/shard_map/ppermute | solution.py:236
  29.8 0.0 collective-permute-start.2
  29.8 0.0 copy-done
  29.8 0.7 shard_map.40.refs_2_
  30.6 0.0 collective-permute-done.refs_1_
  30.6 9.6 %collective-permute-done.1.refs_2_ = f32[264,128]{1,0:T(8,128)S(1)} collective-permute-done((f32[264,128]{1,0:T(8,128)S(1)}, f32[264,128]{1,0:T(8,128)S(1)}, u32[]{:S(2)}, u32[]{:S(2)}) %collective-permute-start.1) | collective-permute-done | bytes 135200 | tf_op jit(solution)/shard_map/ppermute | solution.py:236
  40.2 0.2 collective-permute-done.2.refs_3_
  40.5 1.1 %shard_map.41.refs_6_ = f32[2,8,64,128]{3,2,1,0:T(8,128)S(1)} custom-call(s32[4]{0:T(128)S(1)} %pad_add_fusion.place.refs_0_, s32[16,16]{1,0:T(8,128)S(1)} %bitcast.18, bf16[64,128,128]{2,1,0:T(8,128)(2,1)S(1)} %shard_map.40.refs_2_, f32[1024,128]{1,0:T(8,128)S(1)} %get-tuple-element.25.refs_3_), custom_call_target="tpu_custom_call" | custom-call | flops 4096 | bytes 1024 | tf_op jit(solution)/shard_map/pallas_call | solution.py:154
  41.5 3.7 %collective-permute-start.3 = (f32[64,4096]{1,0:T(8,128)S(1)}, f32[64,4096]{1,0:T(8,128)S(1)}, u32[]{:S(2)}, u32[]{:S(2)}) collective-permute-start(f32[64,4096]{1,0:T(8,128)S(1)} %copy-done), channel_id=1, source_target_pairs={{0,32},{16,48},{32,0},{48,16},{64,96},{80,112},{96,64},{112,80},{1... | collective-permute-start | bytes 3145736 | tf_op jit(solution)/shard_map/ppermute | solution.py:236
  45.2 0.2 collective-permute-start.4
  45.4 0.0 collective-permute-start.5
  45.4 2.7 %collective-permute-start.6 = (f32[1024,128]{1,0:T(8,128)S(1)}, f32[1024,128]{1,0:T(8,128)S(1)}, u32[]{:S(2)}, u32[]{:S(2)}) collective-permute-start(f32[1024,128]{1,0:T(8,128)S(1)} %get-tuple-element.25.refs_3_), channel_id=1, source_target_pairs={{0,12},{2,14},{4,0},{6,2},{8,4},{10,6},{12,8},{14,10},{1,13},{3,15... | collective-permute-start | bytes 1572872 | tf_op jit(solution)/shard_map/ppermute | solution.py:236
  48.1 8.9 %collective-permute-done.4.refs_3_.refs_4_ = f32[1024,128]{1,0:T(8,128)S(1)} collective-permute-done((f32[1024,128]{1,0:T(8,128)S(1)}, f32[1024,128]{1,0:T(8,128)S(1)}, u32[]{:S(2)}, u32[]{:S(2)}) %collective-permute-start.4) | collective-permute-done | bytes 524320 | tf_op jit(solution)/shard_map/ppermute | solution.py:236
  57.0 1.0 %collective-permute-done.5.refs_4_.refs_5_ = f32[1024,128]{1,0:T(8,128)S(1)} collective-permute-done((f32[1024,128]{1,0:T(8,128)S(1)}, f32[1024,128]{1,0:T(8,128)S(1)}, u32[]{:S(2)}, u32[]{:S(2)}) %collective-permute-start.5) | collective-permute-done | bytes 524320 | tf_op jit(solution)/shard_map/ppermute | solution.py:236
  58.0 0.0 collective-permute-done.6.refs_5_.refs_6_
  58.0 1.1 %collective-permute-start.7 = (f32[512,128]{1,0:T(8,128)S(1)}, f32[512,128]{1,0:T(8,128)S(1)}, u32[]{:S(2)}, u32[]{:S(2)}) collective-permute-start(f32[512,128]{1,0:T(8,128)S(1)} %slice.16), channel_id=1, source_target_pairs={{0,4},{2,6},{4,8},{6,10},{8,12},{10,14},{12,0},{14,2},{1,5},{3,7},... | collective-permute-start | bytes 786440 | tf_op jit(solution)/shard_map/ppermute | solution.py:236
  59.1 1.8 %collective-permute-start.8 = (f32[512,128]{1,0:T(8,128)S(1)}, f32[512,128]{1,0:T(8,128)S(1)}, u32[]{:S(2)}, u32[]{:S(2)}) collective-permute-start(f32[512,128]{1,0:T(8,128)S(1)} %slice.17), channel_id=1, source_target_pairs={{0,12},{2,14},{4,0},{6,2},{8,4},{10,6},{12,8},{14,10},{1,13},{3,15... | collective-permute-start | bytes 786440 | tf_op jit(solution)/shard_map/ppermute | solution.py:236
  60.9 0.0 collective-permute-start.11
  60.9 2.7 %collective-permute-start.12 = (f32[1024,128]{1,0:T(8,128)S(1)}, f32[1024,128]{1,0:T(8,128)S(1)}, u32[]{:S(2)}, u32[]{:S(2)}) collective-permute-start(f32[1024,128]{1,0:T(8,128)S(1)} %collective-permute-done.4.refs_3_.refs_4_), channel_id=1, source_target_pairs={{0,12},{2,14},{4,0},{6,2},{8,4},{10,6},{12,8},{14,10},{1,13},{3,15... | collective-permute-start | bytes 1572872 | tf_op jit(solution)/shard_map/ppermute | solution.py:236
  63.6 1.4 %shard_map.43.refs_7_ = f32[2,8,64,128]{3,2,1,0:T(8,128)S(1)} custom-call(s32[4]{0:T(128)S(1)} %pad_add_fusion.place.refs_0_, s32[16,16]{1,0:T(8,128)S(1)} %bitcast.19, bf16[64,128,128]{2,1,0:T(8,128)(2,1)S(1)} %shard_map.40.refs_2_, f32[1024,128]{1,0:T(8,128)S(1)} %collective-permute-done.4.refs_3_.refs_4_, ...), custom_call_target="tpu_custom_call", output_to_operand_aliasing={{}: (6, {})} | custom-call | flops 4096 | bytes 1024 | tf_op jit(solution)/shard_map/pallas_call | solution.py:154
  64.9 0.0 collective-permute-done.7.refs_4_
  65.0 0.0 collective-permute-done.8.refs_5_
  65.0 1.5 %collective-permute-start.10 = (f32[512,128]{1,0:T(8,128)S(1)}, f32[512,128]{1,0:T(8,128)S(1)}, u32[]{:S(2)}, u32[]{:S(2)}) collective-permute-start(f32[512,128]{1,0:T(8,128)S(1)} %collective-permute-done.8.refs_5_), channel_id=1, source_target_pairs={{0,2},{2,0},{4,6},{6,4},{8,10},{10,8},{12,14},{14,12},{1,3},{3,1},... | collective-permute-start | bytes 786440 | tf_op jit(solution)/shard_map/ppermute | solution.py:236
  66.4 0.3 collective-permute-start.9
  66.7 0.6 collective-permute-done.3.refs_0_
  67.3 0.7 shard_map.42.refs_2_.refs_3_
  68.0 1.5 %shard_map.44.refs_6_ = f32[2,8,64,128]{3,2,1,0:T(8,128)S(1)} custom-call(s32[4]{0:T(128)S(1)} %pad_add_fusion.place.refs_0_, s32[16,16]{1,0:T(8,128)S(1)} %bitcast.20, bf16[64,128,128]{2,1,0:T(8,128)(2,1)S(1)} %shard_map.42.refs_2_.refs_3_, f32[1024,128]{1,0:T(8,128)S(1)} %get-tuple-element.25.refs_3_, ...), custom_call_target="tpu_custom_call", output_to_operand_aliasing={{}: (7, {})} | custom-call | flops 4096 | bytes 1024 | tf_op jit(solution)/shard_map/pallas_call | solution.py:154
  69.6 1.2 %shard_map.45.refs_6_ = f32[2,8,64,128]{3,2,1,0:T(8,128)S(1)} custom-call(s32[4]{0:T(128)S(1)} %pad_add_fusion.place.refs_0_, s32[16,16]{1,0:T(8,128)S(1)} %bitcast.21, bf16[64,128,128]{2,1,0:T(8,128)(2,1)S(1)} %shard_map.40.refs_2_, bf16[64,128,128]{2,1,0:T(8,128)(2,1)S(1)} %shard_map.42.refs_2_.refs_3_, ...), custom_call_target="tpu_custom_call", output_to_operand_aliasing={{}: (6, {})} | custom-call | flops 4096 | bytes 1024 | tf_op jit(solution)/shard_map/pallas_call | solution.py:154
  70.8 4.6 %collective-permute-done.11.refs_4_ = f32[1024,128]{1,0:T(8,128)S(1)} collective-permute-done((f32[1024,128]{1,0:T(8,128)S(1)}, f32[1024,128]{1,0:T(8,128)S(1)}, u32[]{:S(2)}, u32[]{:S(2)}) %collective-permute-start.11) | collective-permute-done | bytes 524320 | tf_op jit(solution)/shard_map/ppermute | solution.py:236
  75.4 0.1 collective-permute-done.12.refs_5_
  75.5 1.5 %shard_map.46.refs_6_ = f32[2,8,64,128]{3,2,1,0:T(8,128)S(1)} custom-call(s32[4]{0:T(128)S(1)} %pad_add_fusion.place.refs_0_, s32[16,16]{1,0:T(8,128)S(1)} %bitcast.22, bf16[64,128,128]{2,1,0:T(8,128)(2,1)S(1)} %shard_map.40.refs_2_, bf16[64,128,128]{2,1,0:T(8,128)(2,1)S(1)} %shard_map.42.refs_2_.refs_3_, ...), custom_call_target="tpu_custom_call", output_to_operand_aliasing={{}: (6, {})} | custom-call | flops 4096 | bytes 1024 | tf_op jit(solution)/shard_map/pallas_call | solution.py:154
  77.0 0.0 collective-permute-done.10.refs_5_
  77.0 0.0 collective-permute-done.9.refs_4_
  77.1 1.2 %shard_map.47 = f32[2,8,64,128]{3,2,1,0:T(8,128)S(1)} custom-call(s32[4]{0:T(128)S(1)} %pad_add_fusion.place.refs_0_, s32[16,16]{1,0:T(8,128)S(1)} %bitcast.23, bf16[64,128,128]{2,1,0:T(8,128)(2,1)S(1)} %shard_map.40.refs_2_, bf16[64,128,128]{2,1,0:T(8,128)(2,1)S(1)} %shard_map.42.refs_2_.refs_3_, ...), custom_call_target="tpu_custom_call", output_to_operand_aliasing={{}: (6, {})} | custom-call | flops 4096 | bytes 1024 | tf_op jit(solution)/shard_map/pallas_call | solution.py:154
  78.3 3.9 %collective-permute-start.13 = (f32[8,64,128]{2,1,0:T(8,128)S(1)}, f32[8,64,128]{2,1,0:T(8,128)S(1)}, u32[]{:S(2)}, u32[]{:S(2)}) collective-permute-start(f32[8,64,128]{2,1,0:T(8,128)S(1)} %slice_bitcast_fusion), channel_id=1, source_target_pairs={{0,1},{1,0},{2,3},{3,2},{4,5},{5,4},{6,7},{7,6},{8,9},{9,8},{10,11... | collective-permute-start | bytes 786440 | tf_op jit(solution)/shard_map/ppermute | solution.py:291
  82.2 1.2 %collective-permute-done.13 = f32[8,64,128]{2,1,0:T(8,128)S(1)} collective-permute-done((f32[8,64,128]{2,1,0:T(8,128)S(1)}, f32[8,64,128]{2,1,0:T(8,128)S(1)}, u32[]{:S(2)}, u32[]{:S(2)}) %collective-permute-start.13) | collective-permute-done | bytes 262176 | tf_op jit(solution)/shard_map/ppermute | solution.py:291
  83.4 14.8 %all_to_all.10 = f32[8,64,128]{2,1,0:T(8,128)S(1)} all-to-all(f32[8,64,128]{2,1,0:T(8,128)S(1)} %fusion), channel_id=1, replica_groups={{0,16,96,112,160,176,192,208},{32,48,64,80,128,144,224,240},{1,17,97,11..., dimensions={0} | all-to-all | bytes 524288 | tf_op jit(solution)/shard_map/all_to_all | solution.py:292
  98.2 0.6 reduce_sum.9
  (6 shorter events, 0.1 us)
Async XLA Ops:
  0.0 29.8 %copy-start = (f32[64,4096]{1,0:T(8,128)S(1)}, f32[64,4096]{1,0:T(8,128)}, u32[]{:S(2)}) copy-start(f32[64,4096]{1,0:T(8,128)} %refs_0_.1) | copy-start | bytes 3145732
  0.0 1.1 %copy-start.1 = (f32[2,1,1,16,4096]{4,3,2,1,0:T(8,128)S(1)}, f32[2,1,1,16,4096]{4,3,2,1,0:T(8,128)}, u32[]{:S(2)}) copy-start(f32[2,1,1,16,4096]{4,3,2,1,0:T(8,128)} %param.4) | copy-start | bytes 1572868
  1.1 0.7 copy-start.2
  3.3 18.7 %all-to-all-start = ((f32[16,72,128]{2,1,0:T(8,128)}), f32[16,72,128]{2,1,0:T(8,128)S(1)}, u32[]{:S(2)}, u32[]{:S(2)}) async-start(f32[16,72,128]{2,1,0:T(8,128)} %shard_map.37), calls=%async_computation | async-start | bytes 1179648 | tf_op jit(solution)/shard_map/all_to_all | solution.py:245
  22.5 8.0 %collective-permute-start = (f32[264,128]{1,0:T(8,128)S(1)}, f32[264,128]{1,0:T(8,128)S(1)}, u32[]{:S(2)}, u32[]{:S(2)}) collective-permute-start(f32[264,128]{1,0:T(8,128)S(1)} %get-tuple-element.21), channel_id=1, source_target_pairs={{0,96},{16,112},{32,64},{48,80},{64,32},{80,48},{96,0},{112,16},{1... | collective-permute-start | bytes 405512 | tf_op jit(solution)/shard_map/ppermute | solution.py:236
  27.0 13.2 %collective-permute-start.1 = (f32[264,128]{1,0:T(8,128)S(1)}, f32[264,128]{1,0:T(8,128)S(1)}, u32[]{:S(2)}, u32[]{:S(2)}) collective-permute-start(f32[264,128]{1,0:T(8,128)S(1)} %get-tuple-element.22), channel_id=1, source_target_pairs={{0,160},{16,176},{32,128},{48,144},{64,224},{80,240},{96,192},{112... | collective-permute-start | bytes 405512 | tf_op jit(solution)/shard_map/ppermute | solution.py:236
  29.8 10.6 %collective-permute-start.2 = (f32[264,128]{1,0:T(8,128)S(1)}, f32[264,128]{1,0:T(8,128)S(1)}, u32[]{:S(2)}, u32[]{:S(2)}) collective-permute-start(f32[264,128]{1,0:T(8,128)S(1)} %get-tuple-element.23), channel_id=1, source_target_pairs={{0,192},{16,208},{32,224},{48,240},{64,128},{80,144},{96,160},{112... | collective-permute-start | bytes 405512 | tf_op jit(solution)/shard_map/ppermute | solution.py:236
  41.5 25.8 %collective-permute-start.3 = (f32[64,4096]{1,0:T(8,128)S(1)}, f32[64,4096]{1,0:T(8,128)S(1)}, u32[]{:S(2)}, u32[]{:S(2)}) collective-permute-start(f32[64,4096]{1,0:T(8,128)S(1)} %copy-done), channel_id=1, source_target_pairs={{0,32},{16,48},{32,0},{48,16},{64,96},{80,112},{96,64},{112,80},{1... | collective-permute-start | bytes 3145736 | tf_op jit(solution)/shard_map/ppermute | solution.py:236
  45.2 11.8 %collective-permute-start.4 = (f32[1024,128]{1,0:T(8,128)S(1)}, f32[1024,128]{1,0:T(8,128)S(1)}, u32[]{:S(2)}, u32[]{:S(2)}) collective-permute-start(f32[1024,128]{1,0:T(8,128)S(1)} %get-tuple-element.25.refs_3_), channel_id=1, source_target_pairs={{0,2},{2,0},{4,6},{6,4},{8,10},{10,8},{12,14},{14,12},{1,3},{3,1},... | collective-permute-start | bytes 1572872 | tf_op jit(solution)/shard_map/ppermute | solution.py:236
  45.4 12.6 %collective-permute-start.5 = (f32[1024,128]{1,0:T(8,128)S(1)}, f32[1024,128]{1,0:T(8,128)S(1)}, u32[]{:S(2)}, u32[]{:S(2)}) collective-permute-start(f32[1024,128]{1,0:T(8,128)S(1)} %get-tuple-element.25.refs_3_), channel_id=1, source_target_pairs={{0,4},{2,6},{4,8},{6,10},{8,12},{10,14},{12,0},{14,2},{1,5},{3,7},... | collective-permute-start | bytes 1572872 | tf_op jit(solution)/shard_map/ppermute | solution.py:236
  45.4 12.6 %collective-permute-start.6 = (f32[1024,128]{1,0:T(8,128)S(1)}, f32[1024,128]{1,0:T(8,128)S(1)}, u32[]{:S(2)}, u32[]{:S(2)}) collective-permute-start(f32[1024,128]{1,0:T(8,128)S(1)} %get-tuple-element.25.refs_3_), channel_id=1, source_target_pairs={{0,12},{2,14},{4,0},{6,2},{8,4},{10,6},{12,8},{14,10},{1,13},{3,15... | collective-permute-start | bytes 1572872 | tf_op jit(solution)/shard_map/ppermute | solution.py:236
  58.0 6.9 %collective-permute-start.7 = (f32[512,128]{1,0:T(8,128)S(1)}, f32[512,128]{1,0:T(8,128)S(1)}, u32[]{:S(2)}, u32[]{:S(2)}) collective-permute-start(f32[512,128]{1,0:T(8,128)S(1)} %slice.16), channel_id=1, source_target_pairs={{0,4},{2,6},{4,8},{6,10},{8,12},{10,14},{12,0},{14,2},{1,5},{3,7},... | collective-permute-start | bytes 786440 | tf_op jit(solution)/shard_map/ppermute | solution.py:236
  59.1 5.8 %collective-permute-start.8 = (f32[512,128]{1,0:T(8,128)S(1)}, f32[512,128]{1,0:T(8,128)S(1)}, u32[]{:S(2)}, u32[]{:S(2)}) collective-permute-start(f32[512,128]{1,0:T(8,128)S(1)} %slice.17), channel_id=1, source_target_pairs={{0,12},{2,14},{4,0},{6,2},{8,4},{10,6},{12,8},{14,10},{1,13},{3,15... | collective-permute-start | bytes 786440 | tf_op jit(solution)/shard_map/ppermute | solution.py:236
  60.9 14.5 %collective-permute-start.11 = (f32[1024,128]{1,0:T(8,128)S(1)}, f32[1024,128]{1,0:T(8,128)S(1)}, u32[]{:S(2)}, u32[]{:S(2)}) collective-permute-start(f32[1024,128]{1,0:T(8,128)S(1)} %collective-permute-done.4.refs_3_.refs_4_), channel_id=1, source_target_pairs={{0,4},{2,6},{4,8},{6,10},{8,12},{10,14},{12,0},{14,2},{1,5},{3,7},... | collective-permute-start | bytes 1572872 | tf_op jit(solution)/shard_map/ppermute | solution.py:236
  60.9 14.6 %collective-permute-start.12 = (f32[1024,128]{1,0:T(8,128)S(1)}, f32[1024,128]{1,0:T(8,128)S(1)}, u32[]{:S(2)}, u32[]{:S(2)}) collective-permute-start(f32[1024,128]{1,0:T(8,128)S(1)} %collective-permute-done.4.refs_3_.refs_4_), channel_id=1, source_target_pairs={{0,12},{2,14},{4,0},{6,2},{8,4},{10,6},{12,8},{14,10},{1,13},{3,15... | collective-permute-start | bytes 1572872 | tf_op jit(solution)/shard_map/ppermute | solution.py:236
  65.0 12.1 %collective-permute-start.10 = (f32[512,128]{1,0:T(8,128)S(1)}, f32[512,128]{1,0:T(8,128)S(1)}, u32[]{:S(2)}, u32[]{:S(2)}) collective-permute-start(f32[512,128]{1,0:T(8,128)S(1)} %collective-permute-done.8.refs_5_), channel_id=1, source_target_pairs={{0,2},{2,0},{4,6},{6,4},{8,10},{10,8},{12,14},{14,12},{1,3},{3,1},... | collective-permute-start | bytes 786440 | tf_op jit(solution)/shard_map/ppermute | solution.py:236
  66.4 10.6 %collective-permute-start.9 = (f32[512,128]{1,0:T(8,128)S(1)}, f32[512,128]{1,0:T(8,128)S(1)}, u32[]{:S(2)}, u32[]{:S(2)}) collective-permute-start(f32[512,128]{1,0:T(8,128)S(1)} %collective-permute-done.7.refs_4_), channel_id=1, source_target_pairs={{0,2},{2,0},{4,6},{6,4},{8,10},{10,8},{12,14},{14,12},{1,3},{3,1},... | collective-permute-start | bytes 786440 | tf_op jit(solution)/shard_map/ppermute | solution.py:236
  78.3 5.0 %collective-permute-start.13 = (f32[8,64,128]{2,1,0:T(8,128)S(1)}, f32[8,64,128]{2,1,0:T(8,128)S(1)}, u32[]{:S(2)}, u32[]{:S(2)}) collective-permute-start(f32[8,64,128]{2,1,0:T(8,128)S(1)} %slice_bitcast_fusion), channel_id=1, source_target_pairs={{0,1},{1,0},{2,3},{3,2},{4,5},{5,4},{6,7},{7,6},{8,9},{9,8},{10,11... | collective-permute-start | bytes 786440 | tf_op jit(solution)/shard_map/ppermute | solution.py:291

commit v14 on v13

--- a/solution.py
+++ b/solution.py
@@ -250,6 +250,7 @@
 
     own, spots = join([chunks[0]] + [send_m(chunks[k], k) for k in range(1, blocks // 2)])
     spots = spots[:, : 2 * GROUP, :slots].reshape(blocks * GROUP, slots)
+    own, t_other, t_own = lax.optimization_barrier((own, t_amps, t_amps))
 
     def up(i):
         return (i + 2) % cols
@@ -267,10 +268,9 @@
     partner = send(own, across)
     below = send(own, up)
     above = send(own, down)
-    tiles = {0: prepare(t_amps)}
+    t_other = send_t(t_other)
+    tiles = {0: prepare(t_own)}
     sums = add(None, tiles, ((0, 0, 0), own))
-    sums, t_other = lax.optimization_barrier((sums, t_amps))
-    t_other = send_t(t_other)
     sums, partner, below, above = lax.optimization_barrier((sums, partner, below, above))
     far_low = send(below[:half], up)
     far_high = send(above[half:], down)

time: 99.5 us -> 101 us (1.015)
  waiting for transfers between devices: 37.2 us -> 42 us
  starting transfers between devices: 32.6 us -> 30.5 us
    ppermute x13, waiting for transfers between devices: 25.1 us -> 29.9 us  [send(): return lax.ppermute(share, axis, [(i, to(i)) for i in range(size)])]
    ppermute x13, starting transfers between devices: 21.1 us -> 18.9 us  [send(): return lax.ppermute(share, axis, [(i, to(i)) for i in range(size)])]
  transfers between devices with their start and end apart: 15 -> 15, of which waited for: 9 -> 10; matrix products, arithmetic and copies ran while one was open for 0% -> 0% of each run, Pallas kernels for 7% -> 8%
where the time goes in v14:
time: 101 us
  waiting for transfers between devices  42 us (42%)
  starting transfers between devices  30.5 us (30%)
  blocking collectives  14.1 us (14%)
  Pallas kernels  11.4 us (11%)
  local copies, waits for them, and re-layouts  1.87 us (2%)
    ppermute x13, waiting for transfers between devices, send(): return lax.ppermute(share, axis, [(i, to(i)) for i in range(size)])  29.9 us
    ppermute x13, starting transfers between devices, send(): return lax.ppermute(share, axis, [(i, to(i)) for i in range(size)])  18.9 us
    all_to_all x1, blocking collectives, on_device(): lax.all_to_all(sums, 'row', 0, 0, tiled=True, axis_index_groups=ranks)  14.1 us
    all_to_all x1, waiting for transfers between devices, on_device(): lax.all_to_all(parts, ('row', 'col'), 0, 0, tiled=True, axis_index_groups...  11 us
    pallas_call x6, Pallas kernels, contract(): pl.pallas_call(kernel, out_shape=jax.ShapeDtypeStruct((2, blocks, ij, LAN...  7.93 us
    all_to_all x1, starting transfers between devices, on_device(): lax.all_to_all(parts, ('row', 'col'), 0, 0, tiled=True, axis_index_groups...  7.58 us
    ppermute x1, starting transfers between devices, on_device(): sums = sums[0] + lax.ppermute(sums[1], 'layer', [(0, 1), (1, 0)])  4.02 us
  transfers between devices with their start and end apart: 15, of which 10 were waited for; matrix products, arithmetic and copies ran while one was open for 0% of the time, Pallas kernels for 8%

profile of v14, /device:TPU:1, one launch (start us, length us, event | category | flops | bytes accessed | tf_op | source)
XLA Modules:
  0.0 100.9 jit_solution(12946229045167774748)
XLA Ops:
  0.0 0.0 copy-start
  0.0 0.0 copy-start.1
  0.0 1.1 %copy-done.1 = f32[2,1,1,16,4096]{4,3,2,1,0:T(8,128)S(1)} copy-done((f32[2,1,1,16,4096]{4,3,2,1,0:T(8,128)S(1)}, f32[2,1,1,16,4096]{4,3,2,1,0:T(8,128)}, u32[]{:S(2)}) %copy-start.1) | copy-done | bytes 524312
  1.1 0.0 copy-start.2
  1.1 0.7 copy-done.2
  1.8 1.5 %shard_map.37 = f32[16,72,128]{2,1,0:T(8,128)} custom-call(s32[2,16]{1,0:T(2,128)S(1)} %bitcast.24, f32[2,2,256,128]{3,2,1,0:T(8,128)S(1)} %bitcast.17), custom_call_target="tpu_custom_call" | custom-call | bytes 1048576 | tf_op jit(solution)/shard_map/pallas_call | solution.py:43
  3.3 7.6 %all-to-all-start = ((f32[16,72,128]{2,1,0:T(8,128)}), f32[16,72,128]{2,1,0:T(8,128)S(1)}, u32[]{:S(2)}, u32[]{:S(2)}) async-start(f32[16,72,128]{2,1,0:T(8,128)} %shard_map.37), calls=%async_computation | async-start | bytes 1179648 | tf_op jit(solution)/shard_map/all_to_all | solution.py:245
  10.9 0.1 pad_add_fusion.place.refs_0_
  11.0 11.0 %all-to-all-done.parts = f32[16,72,128]{2,1,0:T(8,128)S(1)} async-done(((f32[16,72,128]{2,1,0:T(8,128)}), f32[16,72,128]{2,1,0:T(8,128)S(1)}, u32[]{:S(2)}, u32[]{:S(2)}) %all-to-all-start) | async-done | bytes 589856 | tf_op jit(solution)/shard_map/all_to_all | solution.py:245
  22.0 0.6 shard_map.38
  22.5 4.4 %collective-permute-start = (f32[264,128]{1,0:T(8,128)S(1)}, f32[264,128]{1,0:T(8,128)S(1)}, u32[]{:S(2)}, u32[]{:S(2)}) collective-permute-start(f32[264,128]{1,0:T(8,128)S(1)} %get-tuple-element.22), channel_id=1, source_target_pairs={{0,96},{16,112},{32,64},{48,80},{64,32},{80,48},{96,0},{112,16},{1... | collective-permute-start | bytes 405512 | tf_op jit(solution)/shard_map/ppermute | solution.py:236
  27.0 2.9 %collective-permute-start.1 = (f32[264,128]{1,0:T(8,128)S(1)}, f32[264,128]{1,0:T(8,128)S(1)}, u32[]{:S(2)}, u32[]{:S(2)}) collective-permute-start(f32[264,128]{1,0:T(8,128)S(1)} %get-tuple-element.23), channel_id=1, source_target_pairs={{0,160},{16,176},{32,128},{48,144},{64,224},{80,240},{96,192},{112... | collective-permute-start | bytes 405512 | tf_op jit(solution)/shard_map/ppermute | solution.py:236
  29.8 0.0 collective-permute-start.2
  29.8 0.0 collective-permute-done.refs_1_
  29.8 10.4 %collective-permute-done.1.refs_2_ = f32[264,128]{1,0:T(8,128)S(1)} collective-permute-done((f32[264,128]{1,0:T(8,128)S(1)}, f32[264,128]{1,0:T(8,128)S(1)}, u32[]{:S(2)}, u32[]{:S(2)}) %collective-permute-start.1) | collective-permute-done | bytes 135200 | tf_op jit(solution)/shard_map/ppermute | solution.py:236
  40.2 0.2 collective-permute-done.2.refs_3_
  40.4 0.0 copy-done
  40.5 3.7 %collective-permute-start.3 = (f32[64,4096]{1,0:T(8,128)S(1)}, f32[64,4096]{1,0:T(8,128)S(1)}, u32[]{:S(2)}, u32[]{:S(2)}) collective-permute-start(f32[64,4096]{1,0:T(8,128)S(1)} %copy-done), channel_id=1, source_target_pairs={{0,32},{16,48},{32,0},{48,16},{64,96},{80,112},{96,64},{112,80},{1... | collective-permute-start | bytes 3145736 | tf_op jit(solution)/shard_map/ppermute | solution.py:236
  44.1 2.3 %collective-permute-start.6 = (f32[1024,128]{1,0:T(8,128)S(1)}, f32[1024,128]{1,0:T(8,128)S(1)}, u32[]{:S(2)}, u32[]{:S(2)}) collective-permute-start(f32[1024,128]{1,0:T(8,128)S(1)} %get-tuple-element.29.refs_3_), channel_id=1, source_target_pairs={{0,12},{2,14},{4,0},{6,2},{8,4},{10,6},{12,8},{14,10},{1,13},{3,15... | collective-permute-start | bytes 1572872 | tf_op jit(solution)/shard_map/ppermute | solution.py:236
  46.4 0.0 collective-permute-start.5
  46.4 0.2 collective-permute-start.4
  46.6 0.7 shard_map.40.refs_2_
  47.4 1.1 %shard_map.42.refs_6_ = f32[2,8,64,128]{3,2,1,0:T(8,128)S(1)} custom-call(s32[4]{0:T(128)S(1)} %pad_add_fusion.place.refs_0_, s32[16,16]{1,0:T(8,128)S(1)} %bitcast.18, bf16[64,128,128]{2,1,0:T(8,128)(2,1)S(1)} %shard_map.40.refs_2_, f32[1024,128]{1,0:T(8,128)S(1)} %get-tuple-element.29.refs_3_), custom_call_target="tpu_custom_call" | custom-call | flops 4096 | bytes 1024 | tf_op jit(solution)/shard_map/pallas_call | solution.py:154
  48.4 8.0 %collective-permute-done.6.refs_5_.refs_6_ = f32[1024,128]{1,0:T(8,128)S(1)} collective-permute-done((f32[1024,128]{1,0:T(8,128)S(1)}, f32[1024,128]{1,0:T(8,128)S(1)}, u32[]{:S(2)}, u32[]{:S(2)}) %collective-permute-start.6) | collective-permute-done | bytes 524320 | tf_op jit(solution)/shard_map/ppermute | solution.py:236
  56.4 3.1 %collective-permute-done.5.refs_4_.refs_5_ = f32[1024,128]{1,0:T(8,128)S(1)} collective-permute-done((f32[1024,128]{1,0:T(8,128)S(1)}, f32[1024,128]{1,0:T(8,128)S(1)}, u32[]{:S(2)}, u32[]{:S(2)}) %collective-permute-start.5) | collective-permute-done | bytes 524320 | tf_op jit(solution)/shard_map/ppermute | solution.py:236
  59.5 0.0 collective-permute-done.4.refs_3_.refs_4_
  59.6 1.3 %collective-permute-start.8 = (f32[512,128]{1,0:T(8,128)S(1)}, f32[512,128]{1,0:T(8,128)S(1)}, u32[]{:S(2)}, u32[]{:S(2)}) collective-permute-start(f32[512,128]{1,0:T(8,128)S(1)} %slice.17), channel_id=1, source_target_pairs={{0,12},{2,14},{4,0},{6,2},{8,4},{10,6},{12,8},{14,10},{1,13},{3,15... | collective-permute-start | bytes 786440 | tf_op jit(solution)/shard_map/ppermute | solution.py:236
  60.8 0.3 collective-permute-start.7
  61.1 2.4 %collective-permute-start.12 = (f32[1024,128]{1,0:T(8,128)S(1)}, f32[1024,128]{1,0:T(8,128)S(1)}, u32[]{:S(2)}, u32[]{:S(2)}) collective-permute-start(f32[1024,128]{1,0:T(8,128)S(1)} %collective-permute-done.4.refs_3_.refs_4_), channel_id=1, source_target_pairs={{0,12},{2,14},{4,0},{6,2},{8,4},{10,6},{12,8},{14,10},{1,13},{3,15... | collective-permute-start | bytes 1572872 | tf_op jit(solution)/shard_map/ppermute | solution.py:236
  63.5 0.0 collective-permute-start.11
  63.5 1.4 %shard_map.43.refs_7_ = f32[2,8,64,128]{3,2,1,0:T(8,128)S(1)} custom-call(s32[4]{0:T(128)S(1)} %pad_add_fusion.place.refs_0_, s32[16,16]{1,0:T(8,128)S(1)} %bitcast.19, bf16[64,128,128]{2,1,0:T(8,128)(2,1)S(1)} %shard_map.40.refs_2_, f32[1024,128]{1,0:T(8,128)S(1)} %collective-permute-done.4.refs_3_.refs_4_, ...), custom_call_target="tpu_custom_call", output_to_operand_aliasing={{}: (6, {})} | custom-call | flops 4096 | bytes 1024 | tf_op jit(solution)/shard_map/pallas_call | solution.py:154
  64.9 0.3 collective-permute-done.8.refs_5_
  65.2 2.1 %collective-permute-done.7.refs_4_ = f32[512,128]{1,0:T(8,128)S(1)} collective-permute-done((f32[512,128]{1,0:T(8,128)S(1)}, f32[512,128]{1,0:T(8,128)S(1)}, u32[]{:S(2)}, u32[]{:S(2)}) %collective-permute-start.7) | collective-permute-done | bytes 262176 | tf_op jit(solution)/shard_map/ppermute | solution.py:236
  67.3 0.2 collective-permute-start.9
  67.5 1.2 %collective-permute-start.10 = (f32[512,128]{1,0:T(8,128)S(1)}, f32[512,128]{1,0:T(8,128)S(1)}, u32[]{:S(2)}, u32[]{:S(2)}) collective-permute-start(f32[512,128]{1,0:T(8,128)S(1)} %collective-permute-done.8.refs_5_), channel_id=1, source_target_pairs={{0,2},{2,0},{4,6},{6,4},{8,10},{10,8},{12,14},{14,12},{1,3},{3,1},... | collective-permute-start | bytes 786440 | tf_op jit(solution)/shard_map/ppermute | solution.py:236
  68.7 0.0 collective-permute-done.3.refs_0_
  68.7 0.7 shard_map.41.refs_2_.refs_3_
  69.4 1.5 %shard_map.44.refs_6_ = f32[2,8,64,128]{3,2,1,0:T(8,128)S(1)} custom-call(s32[4]{0:T(128)S(1)} %pad_add_fusion.place.refs_0_, s32[16,16]{1,0:T(8,128)S(1)} %bitcast.20, bf16[64,128,128]{2,1,0:T(8,128)(2,1)S(1)} %shard_map.41.refs_2_.refs_3_, f32[1024,128]{1,0:T(8,128)S(1)} %get-tuple-element.29.refs_3_, ...), custom_call_target="tpu_custom_call", output_to_operand_aliasing={{}: (7, {})} | custom-call | flops 4096 | bytes 1024 | tf_op jit(solution)/shard_map/pallas_call | solution.py:154
  71.0 1.2 %shard_map.45.refs_6_ = f32[2,8,64,128]{3,2,1,0:T(8,128)S(1)} custom-call(s32[4]{0:T(128)S(1)} %pad_add_fusion.place.refs_0_, s32[16,16]{1,0:T(8,128)S(1)} %bitcast.21, bf16[64,128,128]{2,1,0:T(8,128)(2,1)S(1)} %shard_map.40.refs_2_, bf16[64,128,128]{2,1,0:T(8,128)(2,1)S(1)} %shard_map.41.refs_2_.refs_3_, ...), custom_call_target="tpu_custom_call", output_to_operand_aliasing={{}: (6, {})} | custom-call | flops 4096 | bytes 1024 | tf_op jit(solution)/shard_map/pallas_call | solution.py:154
  72.2 4.0 %collective-permute-done.12.refs_5_ = f32[1024,128]{1,0:T(8,128)S(1)} collective-permute-done((f32[1024,128]{1,0:T(8,128)S(1)}, f32[1024,128]{1,0:T(8,128)S(1)}, u32[]{:S(2)}, u32[]{:S(2)}) %collective-permute-start.12) | collective-permute-done | bytes 524320 | tf_op jit(solution)/shard_map/ppermute | solution.py:236
  76.2 1.8 %collective-permute-done.11.refs_4_ = f32[1024,128]{1,0:T(8,128)S(1)} collective-permute-done((f32[1024,128]{1,0:T(8,128)S(1)}, f32[1024,128]{1,0:T(8,128)S(1)}, u32[]{:S(2)}, u32[]{:S(2)}) %collective-permute-start.11) | collective-permute-done | bytes 524320 | tf_op jit(solution)/shard_map/ppermute | solution.py:236
  78.1 1.5 %shard_map.46.refs_6_ = f32[2,8,64,128]{3,2,1,0:T(8,128)S(1)} custom-call(s32[4]{0:T(128)S(1)} %pad_add_fusion.place.refs_0_, s32[16,16]{1,0:T(8,128)S(1)} %bitcast.22, bf16[64,128,128]{2,1,0:T(8,128)(2,1)S(1)} %shard_map.40.refs_2_, bf16[64,128,128]{2,1,0:T(8,128)(2,1)S(1)} %shard_map.41.refs_2_.refs_3_, ...), custom_call_target="tpu_custom_call", output_to_operand_aliasing={{}: (6, {})} | custom-call | flops 4096 | bytes 1024 | tf_op jit(solution)/shard_map/pallas_call | solution.py:154
  79.6 0.0 collective-permute-done.9.refs_4_
  79.6 0.0 collective-permute-done.10.refs_5_
  79.6 1.2 %shard_map.47 = f32[2,8,64,128]{3,2,1,0:T(8,128)S(1)} custom-call(s32[4]{0:T(128)S(1)} %pad_add_fusion.place.refs_0_, s32[16,16]{1,0:T(8,128)S(1)} %bitcast.23, bf16[64,128,128]{2,1,0:T(8,128)(2,1)S(1)} %shard_map.40.refs_2_, bf16[64,128,128]{2,1,0:T(8,128)(2,1)S(1)} %shard_map.41.refs_2_.refs_3_, ...), custom_call_target="tpu_custom_call", output_to_operand_aliasing={{}: (6, {})} | custom-call | flops 4096 | bytes 1024 | tf_op jit(solution)/shard_map/pallas_call | solution.py:154
  80.9 4.0 %collective-permute-start.13 = (f32[8,64,128]{2,1,0:T(8,128)S(1)}, f32[8,64,128]{2,1,0:T(8,128)S(1)}, u32[]{:S(2)}, u32[]{:S(2)}) collective-permute-start(f32[8,64,128]{2,1,0:T(8,128)S(1)} %slice_bitcast_fusion), channel_id=1, source_target_pairs={{0,1},{1,0},{2,3},{3,2},{4,5},{5,4},{6,7},{7,6},{8,9},{9,8},{10,11... | collective-permute-start | bytes 786440 | tf_op jit(solution)/shard_map/ppermute | solution.py:291
  84.9 1.2 %collective-permute-done.13 = f32[8,64,128]{2,1,0:T(8,128)S(1)} collective-permute-done((f32[8,64,128]{2,1,0:T(8,128)S(1)}, f32[8,64,128]{2,1,0:T(8,128)S(1)}, u32[]{:S(2)}, u32[]{:S(2)}) %collective-permute-start.13) | collective-permute-done | bytes 262176 | tf_op jit(solution)/shard_map/ppermute | solution.py:291
  86.1 14.1 %all_to_all.10 = f32[8,64,128]{2,1,0:T(8,128)S(1)} all-to-all(f32[8,64,128]{2,1,0:T(8,128)S(1)} %fusion), channel_id=1, replica_groups={{0,16,96,112,160,176,192,208},{32,48,64,80,128,144,224,240},{1,17,97,11..., dimensions={0} | all-to-all | bytes 524288 | tf_op jit(solution)/shard_map/all_to_all | solution.py:292
  100.2 0.6 reduce_sum.9
  (6 shorter events, 0.1 us)
Async XLA Ops:
  0.0 40.4 %copy-start = (f32[64,4096]{1,0:T(8,128)S(1)}, f32[64,4096]{1,0:T(8,128)}, u32[]{:S(2)}) copy-start(f32[64,4096]{1,0:T(8,128)} %refs_0_) | copy-start | bytes 3145732
  0.0 1.1 %copy-start.1 = (f32[2,1,1,16,4096]{4,3,2,1,0:T(8,128)S(1)}, f32[2,1,1,16,4096]{4,3,2,1,0:T(8,128)}, u32[]{:S(2)}) copy-start(f32[2,1,1,16,4096]{4,3,2,1,0:T(8,128)} %param.4) | copy-start | bytes 1572868
  1.1 0.7 copy-start.2
  3.3 18.7 %all-to-all-start = ((f32[16,72,128]{2,1,0:T(8,128)}), f32[16,72,128]{2,1,0:T(8,128)S(1)}, u32[]{:S(2)}, u32[]{:S(2)}) async-start(f32[16,72,128]{2,1,0:T(8,128)} %shard_map.37), calls=%async_computation | async-start | bytes 1179648 | tf_op jit(solution)/shard_map/all_to_all | solution.py:245
  22.5 7.3 %collective-permute-start = (f32[264,128]{1,0:T(8,128)S(1)}, f32[264,128]{1,0:T(8,128)S(1)}, u32[]{:S(2)}, u32[]{:S(2)}) collective-permute-start(f32[264,128]{1,0:T(8,128)S(1)} %get-tuple-element.22), channel_id=1, source_target_pairs={{0,96},{16,112},{32,64},{48,80},{64,32},{80,48},{96,0},{112,16},{1... | collective-permute-start | bytes 405512 | tf_op jit(solution)/shard_map/ppermute | solution.py:236
  27.0 13.2 %collective-permute-start.1 = (f32[264,128]{1,0:T(8,128)S(1)}, f32[264,128]{1,0:T(8,128)S(1)}, u32[]{:S(2)}, u32[]{:S(2)}) collective-permute-start(f32[264,128]{1,0:T(8,128)S(1)} %get-tuple-element.23), channel_id=1, source_target_pairs={{0,160},{16,176},{32,128},{48,144},{64,224},{80,240},{96,192},{112... | collective-permute-start | bytes 405512 | tf_op jit(solution)/shard_map/ppermute | solution.py:236
  29.8 10.6 %collective-permute-start.2 = (f32[264,128]{1,0:T(8,128)S(1)}, f32[264,128]{1,0:T(8,128)S(1)}, u32[]{:S(2)}, u32[]{:S(2)}) collective-permute-start(f32[264,128]{1,0:T(8,128)S(1)} %get-tuple-element.24), channel_id=1, source_target_pairs={{0,192},{16,208},{32,224},{48,240},{64,128},{80,144},{96,160},{112... | collective-permute-start | bytes 405512 | tf_op jit(solution)/shard_map/ppermute | solution.py:236
  40.5 28.3 %collective-permute-start.3 = (f32[64,4096]{1,0:T(8,128)S(1)}, f32[64,4096]{1,0:T(8,128)S(1)}, u32[]{:S(2)}, u32[]{:S(2)}) collective-permute-start(f32[64,4096]{1,0:T(8,128)S(1)} %copy-done), channel_id=1, source_target_pairs={{0,32},{16,48},{32,0},{48,16},{64,96},{80,112},{96,64},{112,80},{1... | collective-permute-start | bytes 3145736 | tf_op jit(solution)/shard_map/ppermute | solution.py:236
  44.1 12.2 %collective-permute-start.6 = (f32[1024,128]{1,0:T(8,128)S(1)}, f32[1024,128]{1,0:T(8,128)S(1)}, u32[]{:S(2)}, u32[]{:S(2)}) collective-permute-start(f32[1024,128]{1,0:T(8,128)S(1)} %get-tuple-element.29.refs_3_), channel_id=1, source_target_pairs={{0,12},{2,14},{4,0},{6,2},{8,4},{10,6},{12,8},{14,10},{1,13},{3,15... | collective-permute-start | bytes 1572872 | tf_op jit(solution)/shard_map/ppermute | solution.py:236
  46.4 13.1 %collective-permute-start.5 = (f32[1024,128]{1,0:T(8,128)S(1)}, f32[1024,128]{1,0:T(8,128)S(1)}, u32[]{:S(2)}, u32[]{:S(2)}) collective-permute-start(f32[1024,128]{1,0:T(8,128)S(1)} %get-tuple-element.29.refs_3_), channel_id=1, source_target_pairs={{0,4},{2,6},{4,8},{6,10},{8,12},{10,14},{12,0},{14,2},{1,5},{3,7},... | collective-permute-start | bytes 1572872 | tf_op jit(solution)/shard_map/ppermute | solution.py:236
  46.4 13.1 %collective-permute-start.4 = (f32[1024,128]{1,0:T(8,128)S(1)}, f32[1024,128]{1,0:T(8,128)S(1)}, u32[]{:S(2)}, u32[]{:S(2)}) collective-permute-start(f32[1024,128]{1,0:T(8,128)S(1)} %get-tuple-element.29.refs_3_), channel_id=1, source_target_pairs={{0,2},{2,0},{4,6},{6,4},{8,10},{10,8},{12,14},{14,12},{1,3},{3,1},... | collective-permute-start | bytes 1572872 | tf_op jit(solution)/shard_map/ppermute | solution.py:236
  59.6 5.6 %collective-permute-start.8 = (f32[512,128]{1,0:T(8,128)S(1)}, f32[512,128]{1,0:T(8,128)S(1)}, u32[]{:S(2)}, u32[]{:S(2)}) collective-permute-start(f32[512,128]{1,0:T(8,128)S(1)} %slice.17), channel_id=1, source_target_pairs={{0,12},{2,14},{4,0},{6,2},{8,4},{10,6},{12,8},{14,10},{1,13},{3,15... | collective-permute-start | bytes 786440 | tf_op jit(solution)/shard_map/ppermute | solution.py:236
  60.8 6.4 %collective-permute-start.7 = (f32[512,128]{1,0:T(8,128)S(1)}, f32[512,128]{1,0:T(8,128)S(1)}, u32[]{:S(2)}, u32[]{:S(2)}) collective-permute-start(f32[512,128]{1,0:T(8,128)S(1)} %slice.16), channel_id=1, source_target_pairs={{0,4},{2,6},{4,8},{6,10},{8,12},{10,14},{12,0},{14,2},{1,5},{3,7},... | collective-permute-start | bytes 786440 | tf_op jit(solution)/shard_map/ppermute | solution.py:236
  61.1 15.1 %collective-permute-start.12 = (f32[1024,128]{1,0:T(8,128)S(1)}, f32[1024,128]{1,0:T(8,128)S(1)}, u32[]{:S(2)}, u32[]{:S(2)}) collective-permute-start(f32[1024,128]{1,0:T(8,128)S(1)} %collective-permute-done.4.refs_3_.refs_4_), channel_id=1, source_target_pairs={{0,12},{2,14},{4,0},{6,2},{8,4},{10,6},{12,8},{14,10},{1,13},{3,15... | collective-permute-start | bytes 1572872 | tf_op jit(solution)/shard_map/ppermute | solution.py:236
  63.5 14.6 %collective-permute-start.11 = (f32[1024,128]{1,0:T(8,128)S(1)}, f32[1024,128]{1,0:T(8,128)S(1)}, u32[]{:S(2)}, u32[]{:S(2)}) collective-permute-start(f32[1024,128]{1,0:T(8,128)S(1)} %collective-permute-done.4.refs_3_.refs_4_), channel_id=1, source_target_pairs={{0,4},{2,6},{4,8},{6,10},{8,12},{10,14},{12,0},{14,2},{1,5},{3,7},... | collective-permute-start | bytes 1572872 | tf_op jit(solution)/shard_map/ppermute | solution.py:236
  67.3 12.3 %collective-permute-start.9 = (f32[512,128]{1,0:T(8,128)S(1)}, f32[512,128]{1,0:T(8,128)S(1)}, u32[]{:S(2)}, u32[]{:S(2)}) collective-permute-start(f32[512,128]{1,0:T(8,128)S(1)} %collective-permute-done.7.refs_4_), channel_id=1, source_target_pairs={{0,2},{2,0},{4,6},{6,4},{8,10},{10,8},{12,14},{14,12},{1,3},{3,1},... | collective-permute-start | bytes 786440 | tf_op jit(solution)/shard_map/ppermute | solution.py:236
  67.5 12.1 %collective-permute-start.10 = (f32[512,128]{1,0:T(8,128)S(1)}, f32[512,128]{1,0:T(8,128)S(1)}, u32[]{:S(2)}, u32[]{:S(2)}) collective-permute-start(f32[512,128]{1,0:T(8,128)S(1)} %collective-permute-done.8.refs_5_), channel_id=1, source_target_pairs={{0,2},{2,0},{4,6},{6,4},{8,10},{10,8},{12,14},{14,12},{1,3},{3,1},... | collective-permute-start | bytes 786440 | tf_op jit(solution)/shard_map/ppermute | solution.py:236
  80.9 5.2 %collective-permute-start.13 = (f32[8,64,128]{2,1,0:T(8,128)S(1)}, f32[8,64,128]{2,1,0:T(8,128)S(1)}, u32[]{:S(2)}, u32[]{:S(2)}) collective-permute-start(f32[8,64,128]{2,1,0:T(8,128)S(1)} %slice_bitcast_fusion), channel_id=1, source_target_pairs={{0,1},{1,0},{2,3},{3,2},{4,5},{5,4},{6,7},{7,6},{8,9},{9,8},{10,11... | collective-permute-start | bytes 786440 | tf_op jit(solution)/shard_map/ppermute | solution.py:291

commit v15 on v13

--- a/solution.py
+++ b/solution.py
@@ -12,6 +12,7 @@
 HALF = TILE // 2
 VMEM = pl.BlockSpec(memory_space=pltpu.VMEM)
 SMEM = pl.BlockSpec(memory_space=pltpu.SMEM)
+ANYWHERE = pl.BlockSpec(memory_space=pl.ANY)
 
 
 def split_rows(x):
@@ -19,13 +20,20 @@
     return hi, (x - hi.astype(jnp.float32)).astype(jnp.bfloat16)
 
 
-def pack_kernel(spots, lists, out):
+def pack_kernel(spots_in, lists_in, out, spots, lists, arrived):
+    copies = [pltpu.make_async_copy(spots_in, spots, arrived.at[0])]
+    for b in range(lists.shape[0]):
+        copies.append(pltpu.make_async_copy(lists_in.at[b], lists.at[b], arrived.at[1 + b]))
+    for copy in copies:
+        copy.start()
+    copies[0].wait()
     held, slots = spots.shape
     cols = out.shape[0] // held
     pair = slots // cols
     rows = pair * HALF
     lane = lax.broadcasted_iota(jnp.int32, (8, LANES), 1)
     for b in range(held):
+        copies[1 + b].wait()
         row = jnp.zeros((8, LANES), jnp.float32)
         for s in range(slots):
             row = jnp.where(lane == s, spots[b, s].astype(jnp.float32), row)
@@ -43,9 +51,14 @@
     return pl.pallas_call(
         pack_kernel,
         out_shape=jax.ShapeDtypeStruct((held * cols, slots // cols * HALF + 8, LANES), jnp.float32),
-        in_specs=[SMEM, VMEM],
+        in_specs=[ANYWHERE, ANYWHERE],
         out_specs=VMEM,
-        compiler_params=pltpu.CompilerParams(vmem_limit_bytes=14 * 2**20),
+        scratch_shapes=[
+            pltpu.SMEM((held, slots), jnp.int32),
+            pltpu.VMEM(lists.shape, jnp.float32),
+            pltpu.SemaphoreType.DMA((1 + held,)),
+        ],
+        compiler_params=pltpu.CompilerParams(vmem_limit_bytes=60 * 2**20),
         cost_estimate=pl.CostEstimate(flops=0, bytes_accessed=2**20, transcendentals=0),
     )(v_where.reshape(held, slots), lists)
 

time: 99.5 us -> 98.3 us (0.988)
  local copies, waits for them, and re-layouts: 1.87 us -> 0.06 us
    unnamed x6 -> x2, local copies, waits for them, and re-layouts: 1.81 us -> 0.01 us
where the time goes in v15:
time: 98.3 us; the launch traced here: 97.6 us
  waiting for transfers between devices  37.2 us (38%)
  starting transfers between devices  32.6 us (33%)
  blocking collectives  14.8 us (15%)
  Pallas kernels  12 us (12%)
    ppermute x13, waiting for transfers between devices, send(): return lax.ppermute(share, axis, [(i, to(i)) for i in range(size)])  25.1 us
    ppermute x13, starting transfers between devices, send(): return lax.ppermute(share, axis, [(i, to(i)) for i in range(size)])  21.1 us
    all_to_all x1, blocking collectives, on_device(): lax.all_to_all(sums, 'row', 0, 0, tiled=True, axis_index_groups=ranks)  14.8 us
    all_to_all x1, waiting for transfers between devices, on_device(): lax.all_to_all(parts, ('row', 'col'), 0, 0, tiled=True, axis_index_groups...  11 us
    pallas_call x6, Pallas kernels, contract(): pl.pallas_call(kernel, out_shape=jax.ShapeDtypeStruct((2, blocks, ij, LAN...  7.91 us
    all_to_all x1, starting transfers between devices, on_device(): lax.all_to_all(parts, ('row', 'col'), 0, 0, tiled=True, axis_index_groups...  7.6 us
    ppermute x1, starting transfers between devices, on_device(): sums = sums[0] + lax.ppermute(sums[1], 'layer', [(0, 1), (1, 0)])  3.87 us
    pallas_call x1, Pallas kernels, pack(): pl.pallas_call(pack_kernel, out_shape=jax.ShapeDtypeStruct((held * cols,...  2.01 us
  transfers between devices with their start and end apart: 15, of which 9 were waited for; matrix products, arithmetic and copies ran while one was open for 0% of the time, Pallas kernels for 7%

profile of v15, /device:TPU:1, one launch (start us, length us, event | category | flops | bytes accessed | tf_op | source)
XLA Modules:
  0.0 97.6 jit_solution(11718530554176845308)
XLA Ops:
  0.0 0.0 copy-start
  0.0 2.0 %shard_map.37 = f32[16,72,128]{2,1,0:T(8,128)} custom-call(s32[2,16]{1,0:T(2,128)} %bitcast.24, f32[2,2,256,128]{3,2,1,0:T(8,128)} %bitcast.23), custom_call_target="tpu_custom_call" | custom-call | bytes 1048576 | tf_op jit(solution)/shard_map/pallas_call | solution.py:51
  2.0 7.6 %all-to-all-start = ((f32[16,72,128]{2,1,0:T(8,128)}), f32[16,72,128]{2,1,0:T(8,128)S(1)}, u32[]{:S(2)}, u32[]{:S(2)}) async-start(f32[16,72,128]{2,1,0:T(8,128)} %shard_map.37), calls=%async_computation | async-start | bytes 1179648 | tf_op jit(solution)/shard_map/all_to_all | solution.py:258
  9.7 0.1 pad_add_fusion.place.refs_0_
  9.7 11.0 %all-to-all-done.parts = f32[16,72,128]{2,1,0:T(8,128)S(1)} async-done(((f32[16,72,128]{2,1,0:T(8,128)}), f32[16,72,128]{2,1,0:T(8,128)S(1)}, u32[]{:S(2)}, u32[]{:S(2)}) %all-to-all-start) | async-done | bytes 589856 | tf_op jit(solution)/shard_map/all_to_all | solution.py:258
  20.7 0.6 shard_map.38
  21.3 4.4 %collective-permute-start = (f32[264,128]{1,0:T(8,128)S(1)}, f32[264,128]{1,0:T(8,128)S(1)}, u32[]{:S(2)}, u32[]{:S(2)}) collective-permute-start(f32[264,128]{1,0:T(8,128)S(1)} %get-tuple-element.21), channel_id=1, source_target_pairs={{0,96},{16,112},{32,64},{48,80},{64,32},{80,48},{96,0},{112,16},{1... | collective-permute-start | bytes 405512 | tf_op jit(solution)/shard_map/ppermute | solution.py:249
  25.7 2.9 %collective-permute-start.1 = (f32[264,128]{1,0:T(8,128)S(1)}, f32[264,128]{1,0:T(8,128)S(1)}, u32[]{:S(2)}, u32[]{:S(2)}) collective-permute-start(f32[264,128]{1,0:T(8,128)S(1)} %get-tuple-element.22), channel_id=1, source_target_pairs={{0,160},{16,176},{32,128},{48,144},{64,224},{80,240},{96,192},{112... | collective-permute-start | bytes 405512 | tf_op jit(solution)/shard_map/ppermute | solution.py:249
  28.6 0.0 collective-permute-start.2
  28.6 0.0 copy-done
  28.6 0.7 shard_map.40.refs_2_
  29.3 0.0 collective-permute-done.refs_1_
  29.3 9.6 %collective-permute-done.1.refs_2_ = f32[264,128]{1,0:T(8,128)S(1)} collective-permute-done((f32[264,128]{1,0:T(8,128)S(1)}, f32[264,128]{1,0:T(8,128)S(1)}, u32[]{:S(2)}, u32[]{:S(2)}) %collective-permute-start.1) | collective-permute-done | bytes 135200 | tf_op jit(solution)/shard_map/ppermute | solution.py:249
  39.0 0.2 collective-permute-done.2.refs_3_
  39.2 1.1 %shard_map.41.refs_6_ = f32[2,8,64,128]{3,2,1,0:T(8,128)S(1)} custom-call(s32[4]{0:T(128)S(1)} %pad_add_fusion.place.refs_0_, s32[16,16]{1,0:T(8,128)S(1)} %bitcast.17, bf16[64,128,128]{2,1,0:T(8,128)(2,1)S(1)} %shard_map.40.refs_2_, f32[1024,128]{1,0:T(8,128)S(1)} %get-tuple-element.25.refs_3_), custom_call_target="tpu_custom_call" | custom-call | flops 4096 | bytes 1024 | tf_op jit(solution)/shard_map/pallas_call | solution.py:167
  40.3 3.7 %collective-permute-start.3 = (f32[64,4096]{1,0:T(8,128)S(1)}, f32[64,4096]{1,0:T(8,128)S(1)}, u32[]{:S(2)}, u32[]{:S(2)}) collective-permute-start(f32[64,4096]{1,0:T(8,128)S(1)} %copy-done), channel_id=1, source_target_pairs={{0,32},{16,48},{32,0},{48,16},{64,96},{80,112},{96,64},{112,80},{1... | collective-permute-start | bytes 3145736 | tf_op jit(solution)/shard_map/ppermute | solution.py:249
  44.0 0.2 collective-permute-start.4
  44.1 0.0 collective-permute-start.5
  44.2 2.7 %collective-permute-start.6 = (f32[1024,128]{1,0:T(8,128)S(1)}, f32[1024,128]{1,0:T(8,128)S(1)}, u32[]{:S(2)}, u32[]{:S(2)}) collective-permute-start(f32[1024,128]{1,0:T(8,128)S(1)} %get-tuple-element.25.refs_3_), channel_id=1, source_target_pairs={{0,12},{2,14},{4,0},{6,2},{8,4},{10,6},{12,8},{14,10},{1,13},{3,15... | collective-permute-start | bytes 1572872 | tf_op jit(solution)/shard_map/ppermute | solution.py:249
  46.8 8.9 %collective-permute-done.4.refs_3_.refs_4_ = f32[1024,128]{1,0:T(8,128)S(1)} collective-permute-done((f32[1024,128]{1,0:T(8,128)S(1)}, f32[1024,128]{1,0:T(8,128)S(1)}, u32[]{:S(2)}, u32[]{:S(2)}) %collective-permute-start.4) | collective-permute-done | bytes 524320 | tf_op jit(solution)/shard_map/ppermute | solution.py:249
  55.7 1.0 %collective-permute-done.5.refs_4_.refs_5_ = f32[1024,128]{1,0:T(8,128)S(1)} collective-permute-done((f32[1024,128]{1,0:T(8,128)S(1)}, f32[1024,128]{1,0:T(8,128)S(1)}, u32[]{:S(2)}, u32[]{:S(2)}) %collective-permute-start.5) | collective-permute-done | bytes 524320 | tf_op jit(solution)/shard_map/ppermute | solution.py:249
  56.8 0.0 collective-permute-done.6.refs_5_.refs_6_
  56.8 1.1 %collective-permute-start.7 = (f32[512,128]{1,0:T(8,128)S(1)}, f32[512,128]{1,0:T(8,128)S(1)}, u32[]{:S(2)}, u32[]{:S(2)}) collective-permute-start(f32[512,128]{1,0:T(8,128)S(1)} %slice.16), channel_id=1, source_target_pairs={{0,4},{2,6},{4,8},{6,10},{8,12},{10,14},{12,0},{14,2},{1,5},{3,7},... | collective-permute-start | bytes 786440 | tf_op jit(solution)/shard_map/ppermute | solution.py:249
  57.9 1.8 %collective-permute-start.8 = (f32[512,128]{1,0:T(8,128)S(1)}, f32[512,128]{1,0:T(8,128)S(1)}, u32[]{:S(2)}, u32[]{:S(2)}) collective-permute-start(f32[512,128]{1,0:T(8,128)S(1)} %slice.17), channel_id=1, source_target_pairs={{0,12},{2,14},{4,0},{6,2},{8,4},{10,6},{12,8},{14,10},{1,13},{3,15... | collective-permute-start | bytes 786440 | tf_op jit(solution)/shard_map/ppermute | solution.py:249
  59.6 0.0 collective-permute-start.11
  59.6 2.7 %collective-permute-start.12 = (f32[1024,128]{1,0:T(8,128)S(1)}, f32[1024,128]{1,0:T(8,128)S(1)}, u32[]{:S(2)}, u32[]{:S(2)}) collective-permute-start(f32[1024,128]{1,0:T(8,128)S(1)} %collective-permute-done.4.refs_3_.refs_4_), channel_id=1, source_target_pairs={{0,12},{2,14},{4,0},{6,2},{8,4},{10,6},{12,8},{14,10},{1,13},{3,15... | collective-permute-start | bytes 1572872 | tf_op jit(solution)/shard_map/ppermute | solution.py:249
  62.3 1.4 %shard_map.43.refs_7_ = f32[2,8,64,128]{3,2,1,0:T(8,128)S(1)} custom-call(s32[4]{0:T(128)S(1)} %pad_add_fusion.place.refs_0_, s32[16,16]{1,0:T(8,128)S(1)} %bitcast.18, bf16[64,128,128]{2,1,0:T(8,128)(2,1)S(1)} %shard_map.40.refs_2_, f32[1024,128]{1,0:T(8,128)S(1)} %collective-permute-done.4.refs_3_.refs_4_, ...), custom_call_target="tpu_custom_call", output_to_operand_aliasing={{}: (6, {})} | custom-call | flops 4096 | bytes 1024 | tf_op jit(solution)/shard_map/pallas_call | solution.py:167
  63.7 0.0 collective-permute-done.7.refs_4_
  63.7 0.0 collective-permute-done.8.refs_5_
  63.7 1.5 %collective-permute-start.10 = (f32[512,128]{1,0:T(8,128)S(1)}, f32[512,128]{1,0:T(8,128)S(1)}, u32[]{:S(2)}, u32[]{:S(2)}) collective-permute-start(f32[512,128]{1,0:T(8,128)S(1)} %collective-permute-done.8.refs_5_), channel_id=1, source_target_pairs={{0,2},{2,0},{4,6},{6,4},{8,10},{10,8},{12,14},{14,12},{1,3},{3,1},... | collective-permute-start | bytes 786440 | tf_op jit(solution)/shard_map/ppermute | solution.py:249
  65.2 0.3 collective-permute-start.9
  65.5 0.6 collective-permute-done.3.refs_0_
  66.1 0.7 shard_map.42.refs_2_.refs_3_
  66.8 1.5 %shard_map.44.refs_6_ = f32[2,8,64,128]{3,2,1,0:T(8,128)S(1)} custom-call(s32[4]{0:T(128)S(1)} %pad_add_fusion.place.refs_0_, s32[16,16]{1,0:T(8,128)S(1)} %bitcast.19, bf16[64,128,128]{2,1,0:T(8,128)(2,1)S(1)} %shard_map.42.refs_2_.refs_3_, f32[1024,128]{1,0:T(8,128)S(1)} %get-tuple-element.25.refs_3_, ...), custom_call_target="tpu_custom_call", output_to_operand_aliasing={{}: (7, {})} | custom-call | flops 4096 | bytes 1024 | tf_op jit(solution)/shard_map/pallas_call | solution.py:167
  68.3 1.2 %shard_map.45.refs_6_ = f32[2,8,64,128]{3,2,1,0:T(8,128)S(1)} custom-call(s32[4]{0:T(128)S(1)} %pad_add_fusion.place.refs_0_, s32[16,16]{1,0:T(8,128)S(1)} %bitcast.20, bf16[64,128,128]{2,1,0:T(8,128)(2,1)S(1)} %shard_map.40.refs_2_, bf16[64,128,128]{2,1,0:T(8,128)(2,1)S(1)} %shard_map.42.refs_2_.refs_3_, ...), custom_call_target="tpu_custom_call", output_to_operand_aliasing={{}: (6, {})} | custom-call | flops 4096 | bytes 1024 | tf_op jit(solution)/shard_map/pallas_call | solution.py:167
  69.5 4.6 %collective-permute-done.11.refs_4_ = f32[1024,128]{1,0:T(8,128)S(1)} collective-permute-done((f32[1024,128]{1,0:T(8,128)S(1)}, f32[1024,128]{1,0:T(8,128)S(1)}, u32[]{:S(2)}, u32[]{:S(2)}) %collective-permute-start.11) | collective-permute-done | bytes 524320 | tf_op jit(solution)/shard_map/ppermute | solution.py:249
  74.2 0.1 collective-permute-done.12.refs_5_
  74.2 1.5 %shard_map.46.refs_6_ = f32[2,8,64,128]{3,2,1,0:T(8,128)S(1)} custom-call(s32[4]{0:T(128)S(1)} %pad_add_fusion.place.refs_0_, s32[16,16]{1,0:T(8,128)S(1)} %bitcast.21, bf16[64,128,128]{2,1,0:T(8,128)(2,1)S(1)} %shard_map.40.refs_2_, bf16[64,128,128]{2,1,0:T(8,128)(2,1)S(1)} %shard_map.42.refs_2_.refs_3_, ...), custom_call_target="tpu_custom_call", output_to_operand_aliasing={{}: (6, {})} | custom-call | flops 4096 | bytes 1024 | tf_op jit(solution)/shard_map/pallas_call | solution.py:167
  75.8 0.0 collective-permute-done.10.refs_5_
  75.8 0.0 collective-permute-done.9.refs_4_
  75.8 1.2 %shard_map.47 = f32[2,8,64,128]{3,2,1,0:T(8,128)S(1)} custom-call(s32[4]{0:T(128)S(1)} %pad_add_fusion.place.refs_0_, s32[16,16]{1,0:T(8,128)S(1)} %bitcast.22, bf16[64,128,128]{2,1,0:T(8,128)(2,1)S(1)} %shard_map.40.refs_2_, bf16[64,128,128]{2,1,0:T(8,128)(2,1)S(1)} %shard_map.42.refs_2_.refs_3_, ...), custom_call_target="tpu_custom_call", output_to_operand_aliasing={{}: (6, {})} | custom-call | flops 4096 | bytes 1024 | tf_op jit(solution)/shard_map/pallas_call | solution.py:167
  77.0 3.9 %collective-permute-start.13 = (f32[8,64,128]{2,1,0:T(8,128)S(1)}, f32[8,64,128]{2,1,0:T(8,128)S(1)}, u32[]{:S(2)}, u32[]{:S(2)}) collective-permute-start(f32[8,64,128]{2,1,0:T(8,128)S(1)} %slice_bitcast_fusion), channel_id=1, source_target_pairs={{0,1},{1,0},{2,3},{3,2},{4,5},{5,4},{6,7},{7,6},{8,9},{9,8},{10,11... | collective-permute-start | bytes 786440 | tf_op jit(solution)/shard_map/ppermute | solution.py:304
  80.9 1.2 %collective-permute-done.13 = f32[8,64,128]{2,1,0:T(8,128)S(1)} collective-permute-done((f32[8,64,128]{2,1,0:T(8,128)S(1)}, f32[8,64,128]{2,1,0:T(8,128)S(1)}, u32[]{:S(2)}, u32[]{:S(2)}) %collective-permute-start.13) | collective-permute-done | bytes 262176 | tf_op jit(solution)/shard_map/ppermute | solution.py:304
  82.1 14.8 %all_to_all.10 = f32[8,64,128]{2,1,0:T(8,128)S(1)} all-to-all(f32[8,64,128]{2,1,0:T(8,128)S(1)} %fusion), channel_id=1, replica_groups={{0,16,96,112,160,176,192,208},{32,48,64,80,128,144,224,240},{1,17,97,11..., dimensions={0} | all-to-all | bytes 524288 | tf_op jit(solution)/shard_map/all_to_all | solution.py:305
  96.9 0.6 reduce_sum.9
  (6 shorter events, 0.1 us)
Async XLA Ops:
  0.0 28.6 %copy-start = (f32[64,4096]{1,0:T(8,128)S(1)}, f32[64,4096]{1,0:T(8,128)}, u32[]{:S(2)}) copy-start(f32[64,4096]{1,0:T(8,128)} %refs_0_.1) | copy-start | bytes 3145732
  2.0 18.7 %all-to-all-start = ((f32[16,72,128]{2,1,0:T(8,128)}), f32[16,72,128]{2,1,0:T(8,128)S(1)}, u32[]{:S(2)}, u32[]{:S(2)}) async-start(f32[16,72,128]{2,1,0:T(8,128)} %shard_map.37), calls=%async_computation | async-start | bytes 1179648 | tf_op jit(solution)/shard_map/all_to_all | solution.py:258
  21.3 8.0 %collective-permute-start = (f32[264,128]{1,0:T(8,128)S(1)}, f32[264,128]{1,0:T(8,128)S(1)}, u32[]{:S(2)}, u32[]{:S(2)}) collective-permute-start(f32[264,128]{1,0:T(8,128)S(1)} %get-tuple-element.21), channel_id=1, source_target_pairs={{0,96},{16,112},{32,64},{48,80},{64,32},{80,48},{96,0},{112,16},{1... | collective-permute-start | bytes 405512 | tf_op jit(solution)/shard_map/ppermute | solution.py:249
  25.7 13.2 %collective-permute-start.1 = (f32[264,128]{1,0:T(8,128)S(1)}, f32[264,128]{1,0:T(8,128)S(1)}, u32[]{:S(2)}, u32[]{:S(2)}) collective-permute-start(f32[264,128]{1,0:T(8,128)S(1)} %get-tuple-element.22), channel_id=1, source_target_pairs={{0,160},{16,176},{32,128},{48,144},{64,224},{80,240},{96,192},{112... | collective-permute-start | bytes 405512 | tf_op jit(solution)/shard_map/ppermute | solution.py:249
  28.6 10.6 %collective-permute-start.2 = (f32[264,128]{1,0:T(8,128)S(1)}, f32[264,128]{1,0:T(8,128)S(1)}, u32[]{:S(2)}, u32[]{:S(2)}) collective-permute-start(f32[264,128]{1,0:T(8,128)S(1)} %get-tuple-element.23), channel_id=1, source_target_pairs={{0,192},{16,208},{32,224},{48,240},{64,128},{80,144},{96,160},{112... | collective-permute-start | bytes 405512 | tf_op jit(solution)/shard_map/ppermute | solution.py:249
  40.3 25.8 %collective-permute-start.3 = (f32[64,4096]{1,0:T(8,128)S(1)}, f32[64,4096]{1,0:T(8,128)S(1)}, u32[]{:S(2)}, u32[]{:S(2)}) collective-permute-start(f32[64,4096]{1,0:T(8,128)S(1)} %copy-done), channel_id=1, source_target_pairs={{0,32},{16,48},{32,0},{48,16},{64,96},{80,112},{96,64},{112,80},{1... | collective-permute-start | bytes 3145736 | tf_op jit(solution)/shard_map/ppermute | solution.py:249
  44.0 11.8 %collective-permute-start.4 = (f32[1024,128]{1,0:T(8,128)S(1)}, f32[1024,128]{1,0:T(8,128)S(1)}, u32[]{:S(2)}, u32[]{:S(2)}) collective-permute-start(f32[1024,128]{1,0:T(8,128)S(1)} %get-tuple-element.25.refs_3_), channel_id=1, source_target_pairs={{0,2},{2,0},{4,6},{6,4},{8,10},{10,8},{12,14},{14,12},{1,3},{3,1},... | collective-permute-start | bytes 1572872 | tf_op jit(solution)/shard_map/ppermute | solution.py:249
  44.1 12.6 %collective-permute-start.5 = (f32[1024,128]{1,0:T(8,128)S(1)}, f32[1024,128]{1,0:T(8,128)S(1)}, u32[]{:S(2)}, u32[]{:S(2)}) collective-permute-start(f32[1024,128]{1,0:T(8,128)S(1)} %get-tuple-element.25.refs_3_), channel_id=1, source_target_pairs={{0,4},{2,6},{4,8},{6,10},{8,12},{10,14},{12,0},{14,2},{1,5},{3,7},... | collective-permute-start | bytes 1572872 | tf_op jit(solution)/shard_map/ppermute | solution.py:249
  44.2 12.6 %collective-permute-start.6 = (f32[1024,128]{1,0:T(8,128)S(1)}, f32[1024,128]{1,0:T(8,128)S(1)}, u32[]{:S(2)}, u32[]{:S(2)}) collective-permute-start(f32[1024,128]{1,0:T(8,128)S(1)} %get-tuple-element.25.refs_3_), channel_id=1, source_target_pairs={{0,12},{2,14},{4,0},{6,2},{8,4},{10,6},{12,8},{14,10},{1,13},{3,15... | collective-permute-start | bytes 1572872 | tf_op jit(solution)/shard_map/ppermute | solution.py:249
  56.8 6.9 %collective-permute-start.7 = (f32[512,128]{1,0:T(8,128)S(1)}, f32[512,128]{1,0:T(8,128)S(1)}, u32[]{:S(2)}, u32[]{:S(2)}) collective-permute-start(f32[512,128]{1,0:T(8,128)S(1)} %slice.16), channel_id=1, source_target_pairs={{0,4},{2,6},{4,8},{6,10},{8,12},{10,14},{12,0},{14,2},{1,5},{3,7},... | collective-permute-start | bytes 786440 | tf_op jit(solution)/shard_map/ppermute | solution.py:249
  57.9 5.8 %collective-permute-start.8 = (f32[512,128]{1,0:T(8,128)S(1)}, f32[512,128]{1,0:T(8,128)S(1)}, u32[]{:S(2)}, u32[]{:S(2)}) collective-permute-start(f32[512,128]{1,0:T(8,128)S(1)} %slice.17), channel_id=1, source_target_pairs={{0,12},{2,14},{4,0},{6,2},{8,4},{10,6},{12,8},{14,10},{1,13},{3,15... | collective-permute-start | bytes 786440 | tf_op jit(solution)/shard_map/ppermute | solution.py:249
  59.6 14.5 %collective-permute-start.11 = (f32[1024,128]{1,0:T(8,128)S(1)}, f32[1024,128]{1,0:T(8,128)S(1)}, u32[]{:S(2)}, u32[]{:S(2)}) collective-permute-start(f32[1024,128]{1,0:T(8,128)S(1)} %collective-permute-done.4.refs_3_.refs_4_), channel_id=1, source_target_pairs={{0,4},{2,6},{4,8},{6,10},{8,12},{10,14},{12,0},{14,2},{1,5},{3,7},... | collective-permute-start | bytes 1572872 | tf_op jit(solution)/shard_map/ppermute | solution.py:249
  59.6 14.6 %collective-permute-start.12 = (f32[1024,128]{1,0:T(8,128)S(1)}, f32[1024,128]{1,0:T(8,128)S(1)}, u32[]{:S(2)}, u32[]{:S(2)}) collective-permute-start(f32[1024,128]{1,0:T(8,128)S(1)} %collective-permute-done.4.refs_3_.refs_4_), channel_id=1, source_target_pairs={{0,12},{2,14},{4,0},{6,2},{8,4},{10,6},{12,8},{14,10},{1,13},{3,15... | collective-permute-start | bytes 1572872 | tf_op jit(solution)/shard_map/ppermute | solution.py:249
  63.7 12.1 %collective-permute-start.10 = (f32[512,128]{1,0:T(8,128)S(1)}, f32[512,128]{1,0:T(8,128)S(1)}, u32[]{:S(2)}, u32[]{:S(2)}) collective-permute-start(f32[512,128]{1,0:T(8,128)S(1)} %collective-permute-done.8.refs_5_), channel_id=1, source_target_pairs={{0,2},{2,0},{4,6},{6,4},{8,10},{10,8},{12,14},{14,12},{1,3},{3,1},... | collective-permute-start | bytes 786440 | tf_op jit(solution)/shard_map/ppermute | solution.py:249
  65.2 10.6 %collective-permute-start.9 = (f32[512,128]{1,0:T(8,128)S(1)}, f32[512,128]{1,0:T(8,128)S(1)}, u32[]{:S(2)}, u32[]{:S(2)}) collective-permute-start(f32[512,128]{1,0:T(8,128)S(1)} %collective-permute-done.7.refs_4_), channel_id=1, source_target_pairs={{0,2},{2,0},{4,6},{6,4},{8,10},{10,8},{12,14},{14,12},{1,3},{3,1},... | collective-permute-start | bytes 786440 | tf_op jit(solution)/shard_map/ppermute | solution.py:249
  77.0 5.0 %collective-permute-start.13 = (f32[8,64,128]{2,1,0:T(8,128)S(1)}, f32[8,64,128]{2,1,0:T(8,128)S(1)}, u32[]{:S(2)}, u32[]{:S(2)}) collective-permute-start(f32[8,64,128]{2,1,0:T(8,128)S(1)} %slice_bitcast_fusion), channel_id=1, source_target_pairs={{0,1},{1,0},{2,3},{3,2},{4,5},{5,4},{6,7},{7,6},{8,9},{9,8},{10,11... | collective-permute-start | bytes 786440 | tf_op jit(solution)/shard_map/ppermute | solution.py:304

commit v16 on v15

--- a/solution.py
+++ b/solution.py
@@ -207,10 +207,11 @@
 
 
 def join_kernel(*refs):
-    *chunks, own, spots = refs
+    *chunks, rest, spots = refs
+    size = chunks[0].shape[0] - 8
     for k, chunk in enumerate(chunks):
-        size = chunk.shape[0] - 8
-        own[k * size : (k + 1) * size] = chunk[:size]
+        if k:
+            rest[(k - 1) * size : k * size] = chunk[:size]
         spots[k] = chunk[size:].astype(jnp.int32)
 
 
@@ -219,7 +220,7 @@
     return pl.pallas_call(
         join_kernel,
         out_shape=[
-            jax.ShapeDtypeStruct((len(chunks) * size, LANES), jnp.float32),
+            jax.ShapeDtypeStruct(((len(chunks) - 1) * size, LANES), jnp.float32),
             jax.ShapeDtypeStruct((len(chunks), 8, LANES), jnp.int32),
         ],
         in_specs=[VMEM] * len(chunks),
@@ -261,9 +262,6 @@
     def send_m(chunk, k):
         return send(chunk, lambda i: i ^ (2 * GROUP * k) ^ (2 * (k.bit_count() % 2)), "row", rows_axis)
 
-    own, spots = join([chunks[0]] + [send_m(chunks[k], k) for k in range(1, blocks // 2)])
-    spots = spots[:, : 2 * GROUP, :slots].reshape(blocks * GROUP, slots)
-
     def up(i):
         return (i + 2) % cols
 
@@ -273,15 +271,26 @@
     def across(i):
         return i ^ 1
 
+    first = chunks[0]
+    others = [send_m(chunks[k], k) for k in range(1, blocks // 2)]
+    first_partner, first_below, first_above = send(first, across), send(first, up), send(first, down)
+    first_far = send(first_below, up)
+    first_partner_below, first_partner_above = send(first_partner, up), send(first_partner, down)
+    own, spots = join([first] + others)
+    own, first_above, first_far, first_partner_below, first_partner_above = lax.optimization_barrier(
+        (own, first_above, first_far, first_partner_below, first_partner_above)
+    )
+    spots = spots[:, : 2 * GROUP, :slots].reshape(blocks * GROUP, slots)
+
     def add(sums, held, *shares):
         return contract(sums, place, spots, held, shares, pair)
 
-    half, middle = own.shape[0] // 2, blocks // 2
+    half, low, middle = own.shape[0] // 2, 2, 1 + blocks // 2
     partner = send(own, across)
     below = send(own, up)
     above = send(own, down)
     tiles = {0: prepare(t_amps)}
-    sums = add(None, tiles, ((0, 0, 0), own))
+    sums = add(None, tiles, ((0, 0, 0), first), ((low, 0, 0), own))
     sums, t_other = lax.optimization_barrier((sums, t_amps))
     t_other = send_t(t_other)
     sums, partner, below, above = lax.optimization_barrier((sums, partner, below, above))
@@ -289,17 +298,40 @@
     far_high = send(above[half:], down)
     partner_below = send(partner, up)
     partner_above = send(partner, down)
-    near = [((0, 0, 0), own), ((0, 0, 1), partner), ((0, -2, 0), below), ((0, 2, 0), above)]
-    sums = add(sums, tiles, *near[1:])
-    sums, far_low, far_high = lax.optimization_barrier((sums, far_low, far_high))
+    near = [
+        ((0, 0, 0), first),
+        ((low, 0, 0), own),
+        ((0, 0, 1), first_partner),
+        ((low, 0, 1), partner),
+        ((0, -2, 0), first_below),
+        ((low, -2, 0), below),
+        ((0, 2, 0), first_above),
+        ((low, 2, 0), above),
+    ]
+    sums = add(sums, tiles, *near[2:])
+    sums, far_low, far_high, first_far = lax.optimization_barrier((sums, far_low, far_high, first_far))
     partner_far_low = send(far_low, across)
     partner_far_high = send(far_high, across)
+    first_partner_far = send(first_far, across)
     other = {1: prepare(t_other)}
     sums = add(sums, other, *near)
     both = {**tiles, **other}
-    sums = add(sums, both, ((0, 4, 0), far_low), ((middle, 4, 0), far_high))
-    sums = add(sums, both, ((0, -2, 1), partner_below), ((0, 2, 1), partner_above))
-    sums = add(sums, both, ((0, 4, 1), partner_far_low), ((middle, 4, 1), partner_far_high))
+    sums = add(sums, both, ((0, 4, 0), first_far), ((low, 4, 0), far_low), ((middle, 4, 0), far_high))
+    sums = add(
+        sums,
+        both,
+        ((0, -2, 1), first_partner_below),
+        ((low, -2, 1), partner_below),
+        ((0, 2, 1), first_partner_above),
+        ((low, 2, 1), partner_above),
+    )
+    sums = add(
+        sums,
+        both,
+        ((0, 4, 1), first_partner_far),
+        ((low, 4, 1), partner_far_low),
+        ((middle, 4, 1), partner_far_high),
+    )
 
     sums = sums[0] + lax.ppermute(sums[1], "layer", [(0, 1), (1, 0)])
     sums = lax.all_to_all(sums, "row", 0, 0, tiled=True, axis_index_groups=ranks)

time: 98.3 us -> 100 us (1.017)
  the two profiles are of different devices: /device:TPU:1 before, /device:TPU:2 now
where the time goes in v16:
time: 100 us
  starting transfers between devices  41.8 us (42%)
  waiting for transfers between devices  28.5 us (28%)
  blocking collectives  17 us (17%)
  Pallas kernels  12 us (12%)
    ppermute x20, starting transfers between devices, send(): return lax.ppermute(share, axis, [(i, to(i)) for i in range(size)])  34.2 us
    all_to_all x1, blocking collectives, on_device(): lax.all_to_all(sums, 'row', 0, 0, tiled=True, axis_index_groups=ranks)  17 us
    ppermute x20, waiting for transfers between devices, send(): return lax.ppermute(share, axis, [(i, to(i)) for i in range(size)])  16.1 us
    all_to_all x1, waiting for transfers between devices, on_device(): lax.all_to_all(parts, ('row', 'col'), 0, 0, tiled=True, axis_index_groups...  10.8 us
    pallas_call x6, Pallas kernels, contract(): pl.pallas_call(kernel, out_shape=jax.ShapeDtypeStruct((2, blocks, ij, LAN...  7.9 us
    all_to_all x1, starting transfers between devices, on_device(): lax.all_to_all(parts, ('row', 'col'), 0, 0, tiled=True, axis_index_groups...  7.49 us
    pallas_call x1, Pallas kernels, pack(): pl.pallas_call(pack_kernel, out_shape=jax.ShapeDtypeStruct((held * cols,...  2.02 us
  transfers between devices with their start and end apart: 22, of which 7 were waited for; matrix products, arithmetic and copies ran while one was open for 0% of the time, Pallas kernels for 7%

profile of v16, /device:TPU:2, one launch (start us, length us, event | category | flops | bytes accessed | tf_op | source)
XLA Modules:
  0.0 100.2 jit_solution(17392864005604427631)
XLA Ops:
  0.0 0.0 copy-start
  0.0 2.0 %shard_map.37 = f32[16,72,128]{2,1,0:T(8,128)} custom-call(s32[2,16]{1,0:T(2,128)} %bitcast.24, f32[2,2,256,128]{3,2,1,0:T(8,128)} %bitcast.23), custom_call_target="tpu_custom_call" | custom-call | bytes 1048576 | tf_op jit(solution)/shard_map/pallas_call | solution.py:51
  2.0 7.5 %all-to-all-start = ((f32[16,72,128]{2,1,0:T(8,128)}), f32[16,72,128]{2,1,0:T(8,128)S(1)}, u32[]{:S(2)}, u32[]{:S(2)}) async-start(f32[16,72,128]{2,1,0:T(8,128)} %shard_map.37), calls=%async_computation | async-start | bytes 1179648 | tf_op jit(solution)/shard_map/all_to_all | solution.py:259
  9.5 0.1 pad_add_fusion.place.refs_0_
  9.6 10.8 %all-to-all-done.parts = f32[16,72,128]{2,1,0:T(8,128)S(1)} async-done(((f32[16,72,128]{2,1,0:T(8,128)}), f32[16,72,128]{2,1,0:T(8,128)S(1)}, u32[]{:S(2)}, u32[]{:S(2)}) %all-to-all-start) | async-done | bytes 589856 | tf_op jit(solution)/shard_map/all_to_all | solution.py:259
  20.4 0.6 shard_map.38
  21.0 4.7 %collective-permute-start = (f32[264,128]{1,0:T(8,128)S(1)}, f32[264,128]{1,0:T(8,128)S(1)}, u32[]{:S(2)}, u32[]{:S(2)}) collective-permute-start(f32[264,128]{1,0:T(8,128)S(1)} %get-tuple-element.27), channel_id=1, source_target_pairs={{0,96},{16,112},{32,64},{48,80},{64,32},{80,48},{96,0},{112,16},{1... | collective-permute-start | bytes 405512 | tf_op jit(solution)/shard_map/ppermute | solution.py:250
  25.7 0.0 collective-permute-start.4
  25.7 1.5 %collective-permute-start.6 = (f32[264,128]{1,0:T(8,128)S(1)}, f32[264,128]{1,0:T(8,128)S(1)}, u32[]{:S(2)}, u32[]{:S(2)}) collective-permute-start(f32[264,128]{1,0:T(8,128)S(1)} %get-tuple-element.26.refs_0_.refs_3_), channel_id=1, source_target_pairs={{0,2},{2,0},{4,6},{6,4},{8,10},{10,8},{12,14},{14,12},{1,3},{3,1},... | collective-permute-start | bytes 405512 | tf_op jit(solution)/shard_map/ppermute | solution.py:250
  27.2 3.1 %collective-permute-start.1 = (f32[264,128]{1,0:T(8,128)S(1)}, f32[264,128]{1,0:T(8,128)S(1)}, u32[]{:S(2)}, u32[]{:S(2)}) collective-permute-start(f32[264,128]{1,0:T(8,128)S(1)} %get-tuple-element.28), channel_id=1, source_target_pairs={{0,160},{16,176},{32,128},{48,144},{64,224},{80,240},{96,192},{112... | collective-permute-start | bytes 405512 | tf_op jit(solution)/shard_map/ppermute | solution.py:250
  30.3 0.0 collective-permute-start.2
  30.3 0.0 collective-permute-done.refs_1_
  30.3 3.2 %collective-permute-start.3 = (f32[264,128]{1,0:T(8,128)S(1)}, f32[264,128]{1,0:T(8,128)S(1)}, u32[]{:S(2)}, u32[]{:S(2)}) collective-permute-start(f32[264,128]{1,0:T(8,128)S(1)} %get-tuple-element.26.refs_0_.refs_3_), channel_id=1, source_target_pairs={{0,12},{2,14},{4,0},{6,2},{8,4},{10,6},{12,8},{14,10},{1,13},{3,15... | collective-permute-start | bytes 405512 | tf_op jit(solution)/shard_map/ppermute | solution.py:250
  33.5 0.0 collective-permute-done.4.refs_5_.refs_7_
  33.6 0.0 collective-permute-start.5
  33.6 0.0 collective-permute-done.6.refs_3_.refs_5_
  33.6 0.1 collective-permute-start.7
  33.7 4.8 %collective-permute-done.1.refs_2_ = f32[264,128]{1,0:T(8,128)S(1)} collective-permute-done((f32[264,128]{1,0:T(8,128)S(1)}, f32[264,128]{1,0:T(8,128)S(1)}, u32[]{:S(2)}, u32[]{:S(2)}) %collective-permute-start.1) | collective-permute-done | bytes 135200 | tf_op jit(solution)/shard_map/ppermute | solution.py:250
  38.4 3.0 %collective-permute-start.8 = (f32[264,128]{1,0:T(8,128)S(1)}, f32[264,128]{1,0:T(8,128)S(1)}, u32[]{:S(2)}, u32[]{:S(2)}) collective-permute-start(f32[264,128]{1,0:T(8,128)S(1)} %collective-permute-done.6.refs_3_.refs_5_), channel_id=1, source_target_pairs={{0,12},{2,14},{4,0},{6,2},{8,4},{10,6},{12,8},{14,10},{1,13},{3,15... | collective-permute-start | bytes 405512 | tf_op jit(solution)/shard_map/ppermute | solution.py:250
  41.4 0.0 copy-done
  41.4 0.7 shard_map.40.refs_2_
  42.1 0.0 collective-permute-done.2.refs_3_
  42.1 0.0 collective-permute-done.3.refs_7_.refs_9_
  42.1 0.0 collective-permute-done.5.refs_4_
  42.2 0.0 collective-permute-done.7.refs_4_
  42.2 1.8 %collective-permute-done.8.refs_6_ = f32[264,128]{1,0:T(8,128)S(1)} collective-permute-done((f32[264,128]{1,0:T(8,128)S(1)}, f32[264,128]{1,0:T(8,128)S(1)}, u32[]{:S(2)}, u32[]{:S(2)}) %collective-permute-start.8) | collective-permute-done | bytes 135200 | tf_op jit(solution)/shard_map/ppermute | solution.py:250
  43.9 1.1 %shard_map.41.refs_9_ = f32[2,8,64,128]{3,2,1,0:T(8,128)S(1)} custom-call(s32[4]{0:T(128)S(1)} %pad_add_fusion.place.refs_0_, s32[16,16]{1,0:T(8,128)S(1)} %bitcast.17, bf16[64,128,128]{2,1,0:T(8,128)(2,1)S(1)} %shard_map.40.refs_2_, f32[264,128]{1,0:T(8,128)S(1)} %get-tuple-element.26.refs_0_.refs_3_, f32[768,128]{1,0:T(8,128)S(1)} %get-tuple-element.32.refs_4_), custom_call_target="tpu_custom_call" | custom-call | flops 4096 | bytes 1024 | tf_op jit(solution)/shard_map/pallas_call | solution.py:167
  45.0 3.7 %collective-permute-start.9 = (f32[64,4096]{1,0:T(8,128)S(1)}, f32[64,4096]{1,0:T(8,128)S(1)}, u32[]{:S(2)}, u32[]{:S(2)}) collective-permute-start(f32[64,4096]{1,0:T(8,128)S(1)} %copy-done), channel_id=1, source_target_pairs={{0,32},{16,48},{32,0},{48,16},{64,96},{80,112},{96,64},{112,80},{1... | collective-permute-start | bytes 3145736 | tf_op jit(solution)/shard_map/ppermute | solution.py:250
  48.7 0.8 collective-permute-start.10
  49.6 0.0 collective-permute-start.11
  49.6 3.7 %collective-permute-start.12 = (f32[768,128]{1,0:T(8,128)S(1)}, f32[768,128]{1,0:T(8,128)S(1)}, u32[]{:S(2)}, u32[]{:S(2)}) collective-permute-start(f32[768,128]{1,0:T(8,128)S(1)} %get-tuple-element.32.refs_4_), channel_id=1, source_target_pairs={{0,12},{2,14},{4,0},{6,2},{8,4},{10,6},{12,8},{14,10},{1,13},{3,15... | collective-permute-start | bytes 1179656 | tf_op jit(solution)/shard_map/ppermute | solution.py:250
  53.2 3.3 %collective-permute-done.10.refs_4_.refs_6_ = f32[768,128]{1,0:T(8,128)S(1)} collective-permute-done((f32[768,128]{1,0:T(8,128)S(1)}, f32[768,128]{1,0:T(8,128)S(1)}, u32[]{:S(2)}, u32[]{:S(2)}) %collective-permute-start.10) | collective-permute-done | bytes 393248 | tf_op jit(solution)/shard_map/ppermute | solution.py:250
  56.5 5.6 %collective-permute-done.11.refs_6_.refs_8_ = f32[768,128]{1,0:T(8,128)S(1)} collective-permute-done((f32[768,128]{1,0:T(8,128)S(1)}, f32[768,128]{1,0:T(8,128)S(1)}, u32[]{:S(2)}, u32[]{:S(2)}) %collective-permute-start.11) | collective-permute-done | bytes 393248 | tf_op jit(solution)/shard_map/ppermute | solution.py:250
  62.1 0.0 collective-permute-done.12.refs_8_.refs_10_
  62.1 1.1 %collective-permute-start.13 = (f32[384,128]{1,0:T(8,128)S(1)}, f32[384,128]{1,0:T(8,128)S(1)}, u32[]{:S(2)}, u32[]{:S(2)}) collective-permute-start(f32[384,128]{1,0:T(8,128)S(1)} %slice.16), channel_id=1, source_target_pairs={{0,4},{2,6},{4,8},{6,10},{8,12},{10,14},{12,0},{14,2},{1,5},{3,7},... | collective-permute-start | bytes 589832 | tf_op jit(solution)/shard_map/ppermute | solution.py:250
  63.2 2.5 %collective-permute-start.14 = (f32[384,128]{1,0:T(8,128)S(1)}, f32[384,128]{1,0:T(8,128)S(1)}, u32[]{:S(2)}, u32[]{:S(2)}) collective-permute-start(f32[384,128]{1,0:T(8,128)S(1)} %slice.17), channel_id=1, source_target_pairs={{0,12},{2,14},{4,0},{6,2},{8,4},{10,6},{12,8},{14,10},{1,13},{3,15... | collective-permute-start | bytes 589832 | tf_op jit(solution)/shard_map/ppermute | solution.py:250
  65.7 0.8 collective-permute-start.18
  66.5 2.4 %collective-permute-start.19 = (f32[768,128]{1,0:T(8,128)S(1)}, f32[768,128]{1,0:T(8,128)S(1)}, u32[]{:S(2)}, u32[]{:S(2)}) collective-permute-start(f32[768,128]{1,0:T(8,128)S(1)} %collective-permute-done.10.refs_4_.refs_6_), channel_id=1, source_target_pairs={{0,12},{2,14},{4,0},{6,2},{8,4},{10,6},{12,8},{14,10},{1,13},{3,15... | collective-permute-start | bytes 1179656 | tf_op jit(solution)/shard_map/ppermute | solution.py:250
  69.0 1.4 %shard_map.43.refs_11_ = f32[2,8,64,128]{3,2,1,0:T(8,128)S(1)} custom-call(s32[4]{0:T(128)S(1)} %pad_add_fusion.place.refs_0_, s32[16,16]{1,0:T(8,128)S(1)} %bitcast.18, bf16[64,128,128]{2,1,0:T(8,128)(2,1)S(1)} %shard_map.40.refs_2_, f32[264,128]{1,0:T(8,128)S(1)} %collective-permute-done.6.refs_3_.refs_5_, ...), custom_call_target="tpu_custom_call", output_to_operand_aliasing={{}: (9, {})} | custom-call | flops 4096 | bytes 1024 | tf_op jit(solution)/shard_map/pallas_call | solution.py:167
  70.3 0.0 collective-permute-done.13.refs_5_
  70.3 0.0 collective-permute-done.14.refs_6_
  70.3 1.5 %collective-permute-start.16 = (f32[384,128]{1,0:T(8,128)S(1)}, f32[384,128]{1,0:T(8,128)S(1)}, u32[]{:S(2)}, u32[]{:S(2)}) collective-permute-start(f32[384,128]{1,0:T(8,128)S(1)} %collective-permute-done.13.refs_5_), channel_id=1, source_target_pairs={{0,2},{2,0},{4,6},{6,4},{8,10},{10,8},{12,14},{14,12},{1,3},{3,1},... | collective-permute-start | bytes 589832 | tf_op jit(solution)/shard_map/ppermute | solution.py:250
  71.8 0.6 collective-permute-start.17
  72.5 0.0 collective-permute-done.9.refs_0_
  72.5 1.4 %collective-permute-start.15 = (f32[264,128]{1,0:T(8,128)S(1)}, f32[264,128]{1,0:T(8,128)S(1)}, u32[]{:S(2)}, u32[]{:S(2)}) collective-permute-start(f32[264,128]{1,0:T(8,128)S(1)} %collective-permute-done.5.refs_4_), channel_id=1, source_target_pairs={{0,2},{2,0},{4,6},{6,4},{8,10},{10,8},{12,14},{14,12},{1,3},{3,1},... | collective-permute-start | bytes 405512 | tf_op jit(solution)/shard_map/ppermute | solution.py:250
  73.9 0.7 shard_map.42.refs_2_.refs_3_
  74.6 1.5 %shard_map.44.refs_7_ = f32[2,8,64,128]{3,2,1,0:T(8,128)S(1)} custom-call(s32[4]{0:T(128)S(1)} %pad_add_fusion.place.refs_0_, s32[16,16]{1,0:T(8,128)S(1)} %bitcast.19, bf16[64,128,128]{2,1,0:T(8,128)(2,1)S(1)} %shard_map.42.refs_2_.refs_3_, f32[264,128]{1,0:T(8,128)S(1)} %get-tuple-element.26.refs_0_.refs_3_, ...), custom_call_target="tpu_custom_call", output_to_operand_aliasing={{}: (11, {})} | custom-call | flops 4096 | bytes 1024 | tf_op jit(solution)/shard_map/pallas_call | solution.py:167
  76.1 1.2 %shard_map.45.refs_8_ = f32[2,8,64,128]{3,2,1,0:T(8,128)S(1)} custom-call(s32[4]{0:T(128)S(1)} %pad_add_fusion.place.refs_0_, s32[16,16]{1,0:T(8,128)S(1)} %bitcast.20, bf16[64,128,128]{2,1,0:T(8,128)(2,1)S(1)} %shard_map.40.refs_2_, bf16[64,128,128]{2,1,0:T(8,128)(2,1)S(1)} %shard_map.42.refs_2_.refs_3_, ...), custom_call_target="tpu_custom_call", output_to_operand_aliasing={{}: (7, {})} | custom-call | flops 4096 | bytes 1024 | tf_op jit(solution)/shard_map/pallas_call | solution.py:167
  77.3 0.0 collective-permute-done.18.refs_5_
  77.4 0.0 collective-permute-done.19.refs_7_
  77.4 1.5 %shard_map.46.refs_7_ = f32[2,8,64,128]{3,2,1,0:T(8,128)S(1)} custom-call(s32[4]{0:T(128)S(1)} %pad_add_fusion.place.refs_0_, s32[16,16]{1,0:T(8,128)S(1)} %bitcast.21, bf16[64,128,128]{2,1,0:T(8,128)(2,1)S(1)} %shard_map.40.refs_2_, bf16[64,128,128]{2,1,0:T(8,128)(2,1)S(1)} %shard_map.42.refs_2_.refs_3_, ...), custom_call_target="tpu_custom_call", output_to_operand_aliasing={{}: (8, {})} | custom-call | flops 4096 | bytes 1024 | tf_op jit(solution)/shard_map/pallas_call | solution.py:167
  78.9 0.8 collective-permute-done.15.refs_4_
  79.7 0.0 collective-permute-done.16.refs_5_
  79.7 0.0 collective-permute-done.17.refs_6_
  79.7 1.2 %shard_map.47 = f32[2,8,64,128]{3,2,1,0:T(8,128)S(1)} custom-call(s32[4]{0:T(128)S(1)} %pad_add_fusion.place.refs_0_, s32[16,16]{1,0:T(8,128)S(1)} %bitcast.22, bf16[64,128,128]{2,1,0:T(8,128)(2,1)S(1)} %shard_map.40.refs_2_, bf16[64,128,128]{2,1,0:T(8,128)(2,1)S(1)} %shard_map.42.refs_2_.refs_3_, ...), custom_call_target="tpu_custom_call", output_to_operand_aliasing={{}: (7, {})} | custom-call | flops 4096 | bytes 1024 | tf_op jit(solution)/shard_map/pallas_call | solution.py:167
  80.9 0.1 collective-permute-start.20
  81.0 1.5 %collective-permute-done.20 = f32[8,64,128]{2,1,0:T(8,128)S(1)} collective-permute-done((f32[8,64,128]{2,1,0:T(8,128)S(1)}, f32[8,64,128]{2,1,0:T(8,128)S(1)}, u32[]{:S(2)}, u32[]{:S(2)}) %collective-permute-start.20) | collective-permute-done | bytes 262176 | tf_op jit(solution)/shard_map/ppermute | solution.py:336
  82.6 17.0 %all_to_all.10 = f32[8,64,128]{2,1,0:T(8,128)S(1)} all-to-all(f32[8,64,128]{2,1,0:T(8,128)S(1)} %fusion), channel_id=1, replica_groups={{0,16,96,112,160,176,192,208},{32,48,64,80,128,144,224,240},{1,17,97,11..., dimensions={0} | all-to-all | bytes 524288 | tf_op jit(solution)/shard_map/all_to_all | solution.py:337
  99.5 0.6 reduce_sum.9
  (6 shorter events, 0.1 us)
Async XLA Ops:
  0.0 41.4 %copy-start = (f32[64,4096]{1,0:T(8,128)S(1)}, f32[64,4096]{1,0:T(8,128)}, u32[]{:S(2)}) copy-start(f32[64,4096]{1,0:T(8,128)} %refs_0_.1) | copy-start | bytes 3145732
  2.0 18.4 %all-to-all-start = ((f32[16,72,128]{2,1,0:T(8,128)}), f32[16,72,128]{2,1,0:T(8,128)S(1)}, u32[]{:S(2)}, u32[]{:S(2)}) async-start(f32[16,72,128]{2,1,0:T(8,128)} %shard_map.37), calls=%async_computation | async-start | bytes 1179648 | tf_op jit(solution)/shard_map/all_to_all | solution.py:259
  21.0 9.3 %collective-permute-start = (f32[264,128]{1,0:T(8,128)S(1)}, f32[264,128]{1,0:T(8,128)S(1)}, u32[]{:S(2)}, u32[]{:S(2)}) collective-permute-start(f32[264,128]{1,0:T(8,128)S(1)} %get-tuple-element.27), channel_id=1, source_target_pairs={{0,96},{16,112},{32,64},{48,80},{64,32},{80,48},{96,0},{112,16},{1... | collective-permute-start | bytes 405512 | tf_op jit(solution)/shard_map/ppermute | solution.py:250
  25.7 7.8 %collective-permute-start.4 = (f32[264,128]{1,0:T(8,128)S(1)}, f32[264,128]{1,0:T(8,128)S(1)}, u32[]{:S(2)}, u32[]{:S(2)}) collective-permute-start(f32[264,128]{1,0:T(8,128)S(1)} %get-tuple-element.26.refs_0_.refs_3_), channel_id=1, source_target_pairs={{0,4},{2,6},{4,8},{6,10},{8,12},{10,14},{12,0},{14,2},{1,5},{3,7},... | collective-permute-start | bytes 405512 | tf_op jit(solution)/shard_map/ppermute | solution.py:250
  25.7 7.9 %collective-permute-start.6 = (f32[264,128]{1,0:T(8,128)S(1)}, f32[264,128]{1,0:T(8,128)S(1)}, u32[]{:S(2)}, u32[]{:S(2)}) collective-permute-start(f32[264,128]{1,0:T(8,128)S(1)} %get-tuple-element.26.refs_0_.refs_3_), channel_id=1, source_target_pairs={{0,2},{2,0},{4,6},{6,4},{8,10},{10,8},{12,14},{14,12},{1,3},{3,1},... | collective-permute-start | bytes 405512 | tf_op jit(solution)/shard_map/ppermute | solution.py:250
  27.2 11.2 %collective-permute-start.1 = (f32[264,128]{1,0:T(8,128)S(1)}, f32[264,128]{1,0:T(8,128)S(1)}, u32[]{:S(2)}, u32[]{:S(2)}) collective-permute-start(f32[264,128]{1,0:T(8,128)S(1)} %get-tuple-element.28), channel_id=1, source_target_pairs={{0,160},{16,176},{32,128},{48,144},{64,224},{80,240},{96,192},{112... | collective-permute-start | bytes 405512 | tf_op jit(solution)/shard_map/ppermute | solution.py:250
  30.3 11.8 %collective-permute-start.2 = (f32[264,128]{1,0:T(8,128)S(1)}, f32[264,128]{1,0:T(8,128)S(1)}, u32[]{:S(2)}, u32[]{:S(2)}) collective-permute-start(f32[264,128]{1,0:T(8,128)S(1)} %get-tuple-element.29), channel_id=1, source_target_pairs={{0,192},{16,208},{32,224},{48,240},{64,128},{80,144},{96,160},{112... | collective-permute-start | bytes 405512 | tf_op jit(solution)/shard_map/ppermute | solution.py:250
  30.3 11.8 %collective-permute-start.3 = (f32[264,128]{1,0:T(8,128)S(1)}, f32[264,128]{1,0:T(8,128)S(1)}, u32[]{:S(2)}, u32[]{:S(2)}) collective-permute-start(f32[264,128]{1,0:T(8,128)S(1)} %get-tuple-element.26.refs_0_.refs_3_), channel_id=1, source_target_pairs={{0,12},{2,14},{4,0},{6,2},{8,4},{10,6},{12,8},{14,10},{1,13},{3,15... | collective-permute-start | bytes 405512 | tf_op jit(solution)/shard_map/ppermute | solution.py:250
  33.6 8.6 %collective-permute-start.5 = (f32[264,128]{1,0:T(8,128)S(1)}, f32[264,128]{1,0:T(8,128)S(1)}, u32[]{:S(2)}, u32[]{:S(2)}) collective-permute-start(f32[264,128]{1,0:T(8,128)S(1)} %collective-permute-done.4.refs_5_.refs_7_), channel_id=1, source_target_pairs={{0,4},{2,6},{4,8},{6,10},{8,12},{10,14},{12,0},{14,2},{1,5},{3,7},... | collective-permute-start | bytes 405512 | tf_op jit(solution)/shard_map/ppermute | solution.py:250
  33.6 8.6 %collective-permute-start.7 = (f32[264,128]{1,0:T(8,128)S(1)}, f32[264,128]{1,0:T(8,128)S(1)}, u32[]{:S(2)}, u32[]{:S(2)}) collective-permute-start(f32[264,128]{1,0:T(8,128)S(1)} %collective-permute-done.6.refs_3_.refs_5_), channel_id=1, source_target_pairs={{0,4},{2,6},{4,8},{6,10},{8,12},{10,14},{12,0},{14,2},{1,5},{3,7},... | collective-permute-start | bytes 405512 | tf_op jit(solution)/shard_map/ppermute | solution.py:250
  38.4 5.5 %collective-permute-start.8 = (f32[264,128]{1,0:T(8,128)S(1)}, f32[264,128]{1,0:T(8,128)S(1)}, u32[]{:S(2)}, u32[]{:S(2)}) collective-permute-start(f32[264,128]{1,0:T(8,128)S(1)} %collective-permute-done.6.refs_3_.refs_5_), channel_id=1, source_target_pairs={{0,12},{2,14},{4,0},{6,2},{8,4},{10,6},{12,8},{14,10},{1,13},{3,15... | collective-permute-start | bytes 405512 | tf_op jit(solution)/shard_map/ppermute | solution.py:250
  45.0 27.5 %collective-permute-start.9 = (f32[64,4096]{1,0:T(8,128)S(1)}, f32[64,4096]{1,0:T(8,128)S(1)}, u32[]{:S(2)}, u32[]{:S(2)}) collective-permute-start(f32[64,4096]{1,0:T(8,128)S(1)} %copy-done), channel_id=1, source_target_pairs={{0,32},{16,48},{32,0},{48,16},{64,96},{80,112},{96,64},{112,80},{1... | collective-permute-start | bytes 3145736 | tf_op jit(solution)/shard_map/ppermute | solution.py:250
  48.7 7.8 %collective-permute-start.10 = (f32[768,128]{1,0:T(8,128)S(1)}, f32[768,128]{1,0:T(8,128)S(1)}, u32[]{:S(2)}, u32[]{:S(2)}) collective-permute-start(f32[768,128]{1,0:T(8,128)S(1)} %get-tuple-element.32.refs_4_), channel_id=1, source_target_pairs={{0,2},{2,0},{4,6},{6,4},{8,10},{10,8},{12,14},{14,12},{1,3},{3,1},... | collective-permute-start | bytes 1179656 | tf_op jit(solution)/shard_map/ppermute | solution.py:250
  49.6 12.5 %collective-permute-start.11 = (f32[768,128]{1,0:T(8,128)S(1)}, f32[768,128]{1,0:T(8,128)S(1)}, u32[]{:S(2)}, u32[]{:S(2)}) collective-permute-start(f32[768,128]{1,0:T(8,128)S(1)} %get-tuple-element.32.refs_4_), channel_id=1, source_target_pairs={{0,4},{2,6},{4,8},{6,10},{8,12},{10,14},{12,0},{14,2},{1,5},{3,7},... | collective-permute-start | bytes 1179656 | tf_op jit(solution)/shard_map/ppermute | solution.py:250
  49.6 12.5 %collective-permute-start.12 = (f32[768,128]{1,0:T(8,128)S(1)}, f32[768,128]{1,0:T(8,128)S(1)}, u32[]{:S(2)}, u32[]{:S(2)}) collective-permute-start(f32[768,128]{1,0:T(8,128)S(1)} %get-tuple-element.32.refs_4_), channel_id=1, source_target_pairs={{0,12},{2,14},{4,0},{6,2},{8,4},{10,6},{12,8},{14,10},{1,13},{3,15... | collective-permute-start | bytes 1179656 | tf_op jit(solution)/shard_map/ppermute | solution.py:250
  62.1 8.2 %collective-permute-start.13 = (f32[384,128]{1,0:T(8,128)S(1)}, f32[384,128]{1,0:T(8,128)S(1)}, u32[]{:S(2)}, u32[]{:S(2)}) collective-permute-start(f32[384,128]{1,0:T(8,128)S(1)} %slice.16), channel_id=1, source_target_pairs={{0,4},{2,6},{4,8},{6,10},{8,12},{10,14},{12,0},{14,2},{1,5},{3,7},... | collective-permute-start | bytes 589832 | tf_op jit(solution)/shard_map/ppermute | solution.py:250
  63.2 7.1 %collective-permute-start.14 = (f32[384,128]{1,0:T(8,128)S(1)}, f32[384,128]{1,0:T(8,128)S(1)}, u32[]{:S(2)}, u32[]{:S(2)}) collective-permute-start(f32[384,128]{1,0:T(8,128)S(1)} %slice.17), channel_id=1, source_target_pairs={{0,12},{2,14},{4,0},{6,2},{8,4},{10,6},{12,8},{14,10},{1,13},{3,15... | collective-permute-start | bytes 589832 | tf_op jit(solution)/shard_map/ppermute | solution.py:250
  65.7 11.6 %collective-permute-start.18 = (f32[768,128]{1,0:T(8,128)S(1)}, f32[768,128]{1,0:T(8,128)S(1)}, u32[]{:S(2)}, u32[]{:S(2)}) collective-permute-start(f32[768,128]{1,0:T(8,128)S(1)} %collective-permute-done.10.refs_4_.refs_6_), channel_id=1, source_target_pairs={{0,4},{2,6},{4,8},{6,10},{8,12},{10,14},{12,0},{14,2},{1,5},{3,7},... | collective-permute-start | bytes 1179656 | tf_op jit(solution)/shard_map/ppermute | solution.py:250
  66.5 10.8 %collective-permute-start.19 = (f32[768,128]{1,0:T(8,128)S(1)}, f32[768,128]{1,0:T(8,128)S(1)}, u32[]{:S(2)}, u32[]{:S(2)}) collective-permute-start(f32[768,128]{1,0:T(8,128)S(1)} %collective-permute-done.10.refs_4_.refs_6_), channel_id=1, source_target_pairs={{0,12},{2,14},{4,0},{6,2},{8,4},{10,6},{12,8},{14,10},{1,13},{3,15... | collective-permute-start | bytes 1179656 | tf_op jit(solution)/shard_map/ppermute | solution.py:250
  70.3 9.3 %collective-permute-start.16 = (f32[384,128]{1,0:T(8,128)S(1)}, f32[384,128]{1,0:T(8,128)S(1)}, u32[]{:S(2)}, u32[]{:S(2)}) collective-permute-start(f32[384,128]{1,0:T(8,128)S(1)} %collective-permute-done.13.refs_5_), channel_id=1, source_target_pairs={{0,2},{2,0},{4,6},{6,4},{8,10},{10,8},{12,14},{14,12},{1,3},{3,1},... | collective-permute-start | bytes 589832 | tf_op jit(solution)/shard_map/ppermute | solution.py:250
  71.8 7.8 %collective-permute-start.17 = (f32[384,128]{1,0:T(8,128)S(1)}, f32[384,128]{1,0:T(8,128)S(1)}, u32[]{:S(2)}, u32[]{:S(2)}) collective-permute-start(f32[384,128]{1,0:T(8,128)S(1)} %collective-permute-done.14.refs_6_), channel_id=1, source_target_pairs={{0,2},{2,0},{4,6},{6,4},{8,10},{10,8},{12,14},{14,12},{1,3},{3,1},... | collective-permute-start | bytes 589832 | tf_op jit(solution)/shard_map/ppermute | solution.py:250
  72.5 7.2 %collective-permute-start.15 = (f32[264,128]{1,0:T(8,128)S(1)}, f32[264,128]{1,0:T(8,128)S(1)}, u32[]{:S(2)}, u32[]{:S(2)}) collective-permute-start(f32[264,128]{1,0:T(8,128)S(1)} %collective-permute-done.5.refs_4_), channel_id=1, source_target_pairs={{0,2},{2,0},{4,6},{6,4},{8,10},{10,8},{12,14},{14,12},{1,3},{3,1},... | collective-permute-start | bytes 405512 | tf_op jit(solution)/shard_map/ppermute | solution.py:250
  80.9 1.6 %collective-permute-start.20 = (f32[8,64,128]{2,1,0:T(8,128)S(1)}, f32[8,64,128]{2,1,0:T(8,128)S(1)}, u32[]{:S(2)}, u32[]{:S(2)}) collective-permute-start(f32[8,64,128]{2,1,0:T(8,128)S(1)} %slice_bitcast_fusion), channel_id=1, source_target_pairs={{0,1},{1,0},{2,3},{3,2},{4,5},{5,4},{6,7},{7,6},{8,9},{9,8},{10,11... | collective-permute-start | bytes 786440 | tf_op jit(solution)/shard_map/ppermute | solution.py:336
